TPU v7x, 256 devices: a whole 4x4x8 slice. The times are simulated.
256 devices in a mesh: batch: 8 (over x, core), branch: 32 (over z, y).
Axes of the slice: x: 4, y: 4, z: 8, core: 2. Of those that a mesh axis runs over, the one named last changes fastest.
Arguments:
- queries: bfloat16 [256, 128, 16, 128], P(('batch', 'branch')), parts along dimension 0, may hold values from -6 to 6
- response_keys: bfloat16 [256, 128, 4, 128], P(('batch', 'branch')), parts along dimension 0, may hold values from -6 to 6
- response_values: bfloat16 [256, 128, 4, 128], P(('batch', 'branch')), parts along dimension 0, may hold values from -6 to 6
- prompt_keys: bfloat16 [16384, 4, 128], P(('batch', 'branch')), parts along dimension 0, may hold values from -6 to 6
- prompt_value_rows: bfloat16 [16384, 4, 128], P(('batch', 'branch')), parts along dimension 0, may hold values from -6 to 6
- lengths: int32 [256], P(('batch', 'branch')), parts along dimension 0, may hold values from 16 to 128, as said below
- grad_out: bfloat16 [256, 128, 16, 128], P(('batch', 'branch')), parts along dimension 0, may hold values from -6 to 6
Outputs:
- attended: bfloat16 [256, 128, 16, 128], P(('batch', 'branch')), parts along dimension 0
- grad_query: bfloat16 [256, 128, 16, 128], P(('batch', 'branch')), parts along dimension 0
- grad_resp_keys: bfloat16 [256, 128, 4, 128], P(('batch', 'branch')), parts along dimension 0
- grad_resp_values: bfloat16 [256, 128, 4, 128], P(('batch', 'branch')), parts along dimension 0
- grad_prompt_keys: bfloat16 [16384, 4, 128], P(('batch', 'branch')), parts along dimension 0
- grad_prompt_values: bfloat16 [16384, 4, 128], P(('batch', 'branch')), parts along dimension 0
There are 8 independent parts, one for each index of `batch`. A program takes and returns all parts, laid end to end along the dimension named above; each array names one. Nothing has to cross between parts.
Inputs may be any that keep to these rules, and one draw needn't show every extreme that they name: `lengths`: some response of every prompt has all 128 slots live.
All inputs are finite; a program needn't handle non-finite values.
Results may differ from a plain program's by a relative error of at most 0.034.
Values may be sent and summed in bfloat16 or wider, within the bound.
No kernel may reach another device: no remote copies, remote signals or barrier semaphores. Data moves between devices by JAX's collectives and lax.ppermute only.
A program may use at most 192 MiB of HBM per device.

v0:
```python
import jax
import jax.numpy as jnp
from jax import lax
from jax.experimental import pallas as pl
from jax.experimental.pallas import tpu as pltpu
from jax.sharding import Mesh, PartitionSpec as P

LOG2E = 1.4426950408889634
CHUNK = 512
f32 = jnp.float32
bf16 = jnp.bfloat16
NT = (((1,), (1,)), ((), ()))
NN = (((1,), (0,)), ((), ()))


def dot(a, b, dims):
    return lax.dot_general(a, b, dims, preferred_element_type=f32)


def attention_kernel(*refs, rows_per, own_len, head_dim, group, spots):
    pack = refs[0]
    kvs = refs[1:9]
    out_pack = refs[9]
    out_kvs = refs[10:18]
    K, V, S, Pm, KT, VT, Qn, On, stat, dqt = refs[18:]
    R = rows_per
    T = own_len
    D = head_dim
    C = D ** (-0.5)
    nk = K.shape[0]
    nch = nk // CHUNK
    for i in range(8):
        for j in range(4):
            at = (4 * i + j) * spots
            K[at:at + spots, :] = kvs[i][j, 0]
            V[at:at + spots, :] = kvs[i][j, 1]
    for c in range(nch):
        KT[:, c * CHUNK:(c + 1) * CHUNK] = K[c * CHUNK:(c + 1) * CHUNK, :].T
        VT[0:D, c * CHUNK:(c + 1) * CHUNK] = V[c * CHUNK:(c + 1) * CHUNK, :].T
    VT[D:D + 16, :] = jnp.ones((16, nk), bf16)
    key_pos = lax.broadcasted_iota(jnp.int32, (T, R), 0)
    row_pos = lax.broadcasted_iota(jnp.int32, (T, R), 1) // group
    for r in range(4):
        rows = slice(r * R, (r + 1) * R)
        qr = pack[r, 0:R, :]
        dor = pack[r, R:2 * R, :]
        kr = pack[r, 2 * R:2 * R + T, :]
        vr = pack[r, 2 * R + T:2 * R + 2 * T, :]
        top = jnp.full((8, R), -jnp.inf, f32)
        for c in range(nch):
            s = dot(K[c * CHUNK:(c + 1) * CHUNK, :], qr, NT)
            S[c * CHUNK:(c + 1) * CHUNK, :] = s
            top = jnp.maximum(top, jnp.max(s.reshape(CHUNK // 8, 8, R), axis=0))
        s = dot(kr, qr, NT)
        s = jnp.where(key_pos <= row_pos, s, -1e30)
        S[nk:nk + T, :] = s
        top = jnp.maximum(top, jnp.max(s.reshape(T // 8, 8, R), axis=0))
        top = jnp.max(top, axis=0, keepdims=True) * (C * LOG2E)
        acc = jnp.zeros((D + 16, R), f32)
        for c in range(nch):
            p = jnp.exp2(S[c * CHUNK:(c + 1) * CHUNK, :] * (C * LOG2E) - top).astype(bf16)
            Pm[c * CHUNK:(c + 1) * CHUNK, rows] = p
            acc = acc + dot(VT[:, c * CHUNK:(c + 1) * CHUNK], p, NN)
        p = jnp.exp2(S[nk:nk + T, :] * (C * LOG2E) - top).astype(bf16)
        Pm[nk:nk + T, rows] = p
        acc = acc + dot(jnp.concatenate([vr.T, jnp.ones((16, T), bf16)], axis=0), p, NN)
        inv = 1.0 / acc[D:D + 1, :]
        o = (acc[0:D, :] * inv).T.astype(bf16)
        out_pack[r, 0:R, :] = o
        dof = dor.astype(f32)
        delta = jnp.sum(dof * o.astype(f32), axis=1, keepdims=True)
        stat[0:1, rows] = jnp.broadcast_to(delta, (R, D)).T[0:1, :]
        stat[1:2, rows] = inv
        inv_col = jnp.broadcast_to(inv, (D, R)).T
        Qn[rows, :] = (qr.astype(f32) * (inv_col * C)).astype(bf16)
        On[rows, :] = (dof * inv_col).astype(bf16)
    for r in range(4):
        rows = slice(r * R, (r + 1) * R)
        dor = pack[r, R:2 * R, :]
        kr = pack[r, 2 * R:2 * R + T, :]
        vr = pack[r, 2 * R + T:2 * R + 2 * T, :]
        p = Pm[nk:nk + T, rows]
        ds = (p.astype(f32) * (dot(vr, dor, NT) - stat[0:1, rows])).astype(bf16)
        out_pack[r, 2 * R:2 * R + T, :] = dot(ds, Qn[rows, :], NN).astype(bf16)
        out_pack[r, 2 * R + T:2 * R + 2 * T, :] = dot(p, On[rows, :], NN).astype(bf16)
        dqt[:, rows] = dot(kr.T, ds, NN)
    for c in range(nch):
        ks = slice(c * CHUNK, (c + 1) * CHUNK)
        dk = jnp.zeros((CHUNK, D), f32)
        dv = jnp.zeros((CHUNK, D), f32)
        for r in range(4):
            rows = slice(r * R, (r + 1) * R)
            p = Pm[ks, rows]
            dp = dot(V[ks, :], pack[r, R:2 * R, :], NT)
            ds = (p.astype(f32) * (dp - stat[0:1, rows])).astype(bf16)
            dk = dk + dot(ds, Qn[rows, :], NN)
            dv = dv + dot(p, On[rows, :], NN)
            dqt[:, rows] += dot(KT[:, ks], ds, NN)
        for j in range(CHUNK // spots):
            block = c * (CHUNK // spots) + j
            part = slice(j * spots, (j + 1) * spots)
            out_kvs[block // 4][block % 4, 0] = dk[part, :].astype(bf16)
            out_kvs[block // 4][block % 4, 1] = dv[part, :].astype(bf16)
    for r in range(4):
        rows = slice(r * R, (r + 1) * R)
        out_pack[r, R:2 * R, :] = (dqt[:, rows] * (stat[1:2, rows] * C)).T.astype(bf16)


def attention_call(pack, kvs, rows_per, own_len, head_dim, group):
    spots = kvs[0].shape[2]
    nk = spots * 32
    shapes = [jax.ShapeDtypeStruct(x.shape, bf16) for x in [pack] + list(kvs)]
    rows = 4 * rows_per

    def body(*refs):
        attention_kernel(
            *refs, rows_per=rows_per, own_len=own_len, head_dim=head_dim, group=group, spots=spots
        )

    outs = pl.pallas_call(
        body,
        out_shape=shapes,
        scratch_shapes=[
            pltpu.VMEM((nk, head_dim), bf16),
            pltpu.VMEM((nk, head_dim), bf16),
            pltpu.VMEM((nk + own_len, rows_per), f32),
            pltpu.VMEM((nk + own_len, rows), bf16),
            pltpu.VMEM((head_dim, nk), bf16),
            pltpu.VMEM((head_dim + 16, nk), bf16),
            pltpu.VMEM((rows, head_dim), bf16),
            pltpu.VMEM((rows, head_dim), bf16),
            pltpu.VMEM((8, rows), f32),
            pltpu.VMEM((head_dim, rows), f32),
        ],
        compiler_params=pltpu.CompilerParams(vmem_limit_bytes=40 * 2**20),
        name="attention",
    )(pack, *kvs)
    return outs[0], outs[1:]


def on_device(
    queries, response_keys, response_values, prompt_keys, prompt_value_rows, lengths, grad_out
):
    _, T, H, D = queries.shape
    KH = prompt_keys.shape[1]
    G = H // KH
    R = T * G

    def over_z(x, k):
        return lax.ppermute(x, "z", [(i, (i + k) % 8) for i in range(8)])

    def swap_y(x):
        return lax.all_to_all(x, "y", 0, 0, tiled=True)

    kv = jnp.stack([prompt_keys, prompt_value_rows], axis=0)
    kv = swap_y(jnp.transpose(kv, (2, 0, 1, 3)))

    live = (jnp.arange(T) < lengths[0])[:, None, None]
    masked = jnp.where(live, grad_out[0], jnp.zeros((), bf16))

    def by_head(x, n):
        x = x.reshape(T, KH, n, D)
        return jnp.transpose(x, (1, 0, 2, 3)).reshape(KH, T * n, D)

    pack = jnp.concatenate(
        [
            by_head(queries, G),
            by_head(masked, G),
            by_head(response_keys, 1),
            by_head(response_values, 1),
        ],
        axis=1,
    )
    kv, pack = lax.optimization_barrier((kv, pack))
    pack = swap_y(pack)
    from_2 = over_z(kv, 2)
    from_m2 = over_z(kv, -2)
    from_1 = over_z(kv, 1)
    from_m1 = over_z(kv, -1)
    from_4 = over_z(from_2, 2)
    from_3 = over_z(from_2, 1)
    from_m3 = over_z(from_m2, -1)

    kvs = [kv, from_1, from_m1, from_2, from_m2, from_3, from_m3, from_4]
    pack, dkv = attention_call(pack, kvs, R, T, D, G)

    d0, d1, dm1, d2, dm2, d3, dm3, d4 = dkv
    home = swap_y(pack)
    via_2 = over_z(d4, -2)
    via_1 = over_z(d3, -1)
    via_m1 = over_z(dm3, 1)
    far = (d2.astype(f32) + via_1.astype(f32) + via_2.astype(f32)).astype(bf16)
    far_m = (dm2.astype(f32) + via_m1.astype(f32)).astype(bf16)
    parts = [over_z(d1, -1), over_z(dm1, 1), over_z(far, -2), over_z(far_m, 2)]
    total = d0.astype(f32)
    for x in parts:
        total = total + x.astype(f32)
    total = swap_y(total.astype(bf16))

    def by_token(x, n):
        x = x.reshape(KH, T, n, D)
        return jnp.transpose(x, (1, 0, 2, 3)).reshape(1, T, KH * n, D)

    attended = by_token(home[:, 0:R], G)
    attended = jnp.where(live, attended, jnp.zeros((), bf16))
    return (
        attended,
        by_token(home[:, R:2 * R], G),
        by_token(home[:, 2 * R:2 * R + T], 1),
        by_token(home[:, 2 * R + T:2 * R + 2 * T], 1),
        jnp.transpose(total[:, 0], (1, 0, 2)),
        jnp.transpose(total[:, 1], (1, 0, 2)),
    )


def solution(mesh):
    split = Mesh(mesh.devices.reshape(8, 8, 4), ("batch", "z", "y"))
    spec = P(("batch", "z", "y"))
    return jax.shard_map(
        on_device,
        mesh=split,
        in_specs=(spec,) * 7,
        out_specs=(spec,) * 6,
        check_vma=False,
    )
```

profile of v0, /device:TPU:4, one launch (start us, length us, event | category | flops | bytes accessed | tf_op | source)
XLA Modules:
  0.0 110.2 jit_solution(5037738064394221551)
XLA Ops:
  0.7 1.0 copy_bitcast_fusion.2
  1.6 0.7 maximum_bitcast_fusion
  2.3 4.5 %all-to-all-start = ((bf16[4,2,64,128]{3,2,1,0:T(8,128)(2,1)}), bf16[4,2,64,128]{3,2,1,0:T(8,128)(2,1)S(1)}, u32[]{:S(2)}, u32[]{:S(2)}) async-start(bf16[4,2,64,128]{3,2,1,0:T(8,128)(2,1)} %maximum_bitcast_fusion), calls=%async_computation | async-start | bytes 262144 | tf_op jit(solution)/shard_map/all_to_all | solution.py:153
  7.4 1.2 %copy.15 = bf16[128,4,4,128]{3,2,0,1:T(4,128)(2,1)S(1)} copy(bf16[128,4,4,128]{3,2,1,0:T(4,128)(2,1)} %bitcast.61) | data formatting | bytes 1048576 | tf_op jit(solution)/shard_map/reshape | solution.py:162
  8.7 0.3 copy_select_fusion
  9.0 1.2 %pad_maximum_fusion = bf16[4,1280,128]{2,1,0:T(8,128)(2,1)} fusion(bf16[4,128,128]{2,1,0:T(8,128)(2,1)S(1)} %get-tuple-element.42, bf16[4,128,128]{2,1,0:T(8,128)(2,1)S(1)} %get-tuple-element.43, bf16[4,512,128]{2,1,0:T(8,128)(2,1)S(1)} %bitcast.57, bf16[4,512,128]{2,1,0:T(8,128)(2,1)S(1)} %bitcast.56), kind=kLoop, calls=%fused_computation | loop fusion | flops 5242880 | bytes 2621440 | tf_op jit(solution)/shard_map/concatenate | solution.py:165
  10.2 2.6 %all-to-all-done.refs_1_ = bf16[4,2,64,128]{3,2,1,0:T(8,128)(2,1)S(1)} async-done(((bf16[4,2,64,128]{3,2,1,0:T(8,128)(2,1)}), bf16[4,2,64,128]{3,2,1,0:T(8,128)(2,1)S(1)}, u32[]{:S(2)}, u32[]{:S(2)}) %all-to-all-start) | async-done | bytes 131104 | tf_op jit(solution)/shard_map/all_to_all | solution.py:153
  12.7 3.5 %all-to-all-start.1 = ((bf16[4,1280,128]{2,1,0:T(8,128)(2,1)}), bf16[4,1280,128]{2,1,0:T(8,128)(2,1)S(1)}, u32[]{:S(2)}, u32[]{:S(2)}) async-start(bf16[4,1280,128]{2,1,0:T(8,128)(2,1)} %pad_maximum_fusion), calls=%async_computation.1 | async-start | bytes 2621440 | tf_op jit(solution)/shard_map/all_to_all | solution.py:153
  16.3 6.4 %collective-permute-start.3 = (bf16[4,2,64,128]{3,2,1,0:T(8,128)(2,1)S(1)}, bf16[4,2,64,128]{3,2,1,0:T(8,128)(2,1)S(1)}, u32[]{:S(2)}, u32[]{:S(2)}) collective-permute-start(bf16[4,2,64,128]{3,2,1,0:T(8,128)(2,1)S(1)} %all-to-all-done.refs_1_), channel_id=1, source_target_pairs={{0,24},{4,28},{8,0},{12,4},{16,8},{20,12},{24,16},{28,20},{1,25},{... | collective-permute-start | bytes 393224 | tf_op jit(solution)/shard_map/ppermute | solution.py:150
  22.7 0.0 collective-permute-start.2
  22.7 3.7 %collective-permute-start.1 = (bf16[4,2,64,128]{3,2,1,0:T(8,128)(2,1)S(1)}, bf16[4,2,64,128]{3,2,1,0:T(8,128)(2,1)S(1)}, u32[]{:S(2)}, u32[]{:S(2)}) collective-permute-start(bf16[4,2,64,128]{3,2,1,0:T(8,128)(2,1)S(1)} %all-to-all-done.refs_1_), channel_id=1, source_target_pairs={{0,28},{4,0},{8,4},{12,8},{16,12},{20,16},{24,20},{28,24},{1,29},{... | collective-permute-start | bytes 393224 | tf_op jit(solution)/shard_map/ppermute | solution.py:150
  26.4 0.0 collective-permute-start
  26.4 1.4 %collective-permute-done.3.refs_5_ = bf16[4,2,64,128]{3,2,1,0:T(8,128)(2,1)S(1)} collective-permute-done((bf16[4,2,64,128]{3,2,1,0:T(8,128)(2,1)S(1)}, bf16[4,2,64,128]{3,2,1,0:T(8,128)(2,1)S(1)}, u32[]{:S(2)}, u32[]{:S(2)}) %collective-permute-start.3) | collective-permute-done | bytes 131104 | tf_op jit(solution)/shard_map/ppermute | solution.py:150
  27.8 2.8 %collective-permute-start.5 = (bf16[4,2,64,128]{3,2,1,0:T(8,128)(2,1)S(1)}, bf16[4,2,64,128]{3,2,1,0:T(8,128)(2,1)S(1)}, u32[]{:S(2)}, u32[]{:S(2)}) collective-permute-start(bf16[4,2,64,128]{3,2,1,0:T(8,128)(2,1)S(1)} %collective-permute-done.3.refs_5_), channel_id=1, source_target_pairs={{0,28},{4,0},{8,4},{12,8},{16,12},{20,16},{24,20},{28,24},{1,29},{... | collective-permute-start | bytes 393224 | tf_op jit(solution)/shard_map/ppermute | solution.py:150
  30.6 1.4 %collective-permute-done.2.refs_4_ = bf16[4,2,64,128]{3,2,1,0:T(8,128)(2,1)S(1)} collective-permute-done((bf16[4,2,64,128]{3,2,1,0:T(8,128)(2,1)S(1)}, bf16[4,2,64,128]{3,2,1,0:T(8,128)(2,1)S(1)}, u32[]{:S(2)}, u32[]{:S(2)}) %collective-permute-start.2) | collective-permute-done | bytes 131104 | tf_op jit(solution)/shard_map/ppermute | solution.py:150
  32.0 0.0 collective-permute-start.6
  32.0 1.6 %collective-permute-start.4 = (bf16[4,2,64,128]{3,2,1,0:T(8,128)(2,1)S(1)}, bf16[4,2,64,128]{3,2,1,0:T(8,128)(2,1)S(1)}, u32[]{:S(2)}, u32[]{:S(2)}) collective-permute-start(bf16[4,2,64,128]{3,2,1,0:T(8,128)(2,1)S(1)} %collective-permute-done.2.refs_4_), channel_id=1, source_target_pairs={{0,4},{4,8},{8,12},{12,16},{16,20},{20,24},{24,28},{28,0},{1,5},{5... | collective-permute-start | bytes 393224 | tf_op jit(solution)/shard_map/ppermute | solution.py:150
  33.5 0.0 collective-permute-done.1.refs_3_
  33.5 2.2 %collective-permute-done.refs_2_ = bf16[4,2,64,128]{3,2,1,0:T(8,128)(2,1)S(1)} collective-permute-done((bf16[4,2,64,128]{3,2,1,0:T(8,128)(2,1)S(1)}, bf16[4,2,64,128]{3,2,1,0:T(8,128)(2,1)S(1)}, u32[]{:S(2)}, u32[]{:S(2)}) %collective-permute-start) | collective-permute-done | bytes 131104 | tf_op jit(solution)/shard_map/ppermute | solution.py:150
  35.8 0.0 collective-permute-done.5.refs_7_
  35.8 4.6 %collective-permute-done.6.refs_8_ = bf16[4,2,64,128]{3,2,1,0:T(8,128)(2,1)S(1)} collective-permute-done((bf16[4,2,64,128]{3,2,1,0:T(8,128)(2,1)S(1)}, bf16[4,2,64,128]{3,2,1,0:T(8,128)(2,1)S(1)}, u32[]{:S(2)}, u32[]{:S(2)}) %collective-permute-start.6) | collective-permute-done | bytes 131104 | tf_op jit(solution)/shard_map/ppermute | solution.py:150
  40.4 1.6 %collective-permute-done.4.refs_6_ = bf16[4,2,64,128]{3,2,1,0:T(8,128)(2,1)S(1)} collective-permute-done((bf16[4,2,64,128]{3,2,1,0:T(8,128)(2,1)S(1)}, bf16[4,2,64,128]{3,2,1,0:T(8,128)(2,1)S(1)}, u32[]{:S(2)}, u32[]{:S(2)}) %collective-permute-start.4) | collective-permute-done | bytes 131104 | tf_op jit(solution)/shard_map/ppermute | solution.py:150
  42.0 0.0 all-to-all-done.1.refs_0_
  42.0 17.2 %attention.1 = (bf16[4,1280,128]{2,1,0:T(8,128)(2,1)}, bf16[4,2,64,128]{3,2,1,0:T(8,128)(2,1)S(1)}, bf16[4,2,64,128]{3,2,1,0:T(8,128)(2,1)S(1)}, bf16[4,2,64,128...) custom-call(bf16[4,1280,128]{2,1,0:T(8,128)(2,1)S(1)} %all-to-all-do, ...), custom_call_target="tpu_custom_call" | custom-call | tf_op jit(solution)/shard_map/attention/pallas_call | solution.py:120
  59.1 0.4 collective-permute-start.9
  59.5 0.8 collective-permute-start.10
  60.3 1.3 %collective-permute-start.7 = (bf16[4,2,64,128]{3,2,1,0:T(8,128)(2,1)S(1)}, bf16[4,2,64,128]{3,2,1,0:T(8,128)(2,1)S(1)}, u32[]{:S(2)}, u32[]{:S(2)}) collective-permute-start(bf16[4,2,64,128]{3,2,1,0:T(8,128)(2,1)S(1)} %get-tuple-element.21), channel_id=1, source_target_pairs={{0,28},{4,0},{8,4},{12,8},{16,12},{20,16},{24,20},{28,24},{1,29},{... | collective-permute-start | bytes 393224 | tf_op jit(solution)/shard_map/ppermute | solution.py:150
  61.6 0.7 collective-permute-start.8
  62.3 1.0 collective-permute-start.12
  63.4 0.9 collective-permute-done.9
  64.3 5.6 %collective-permute-done.10 = bf16[4,2,64,128]{3,2,1,0:T(8,128)(2,1)S(1)} collective-permute-done((bf16[4,2,64,128]{3,2,1,0:T(8,128)(2,1)S(1)}, bf16[4,2,64,128]{3,2,1,0:T(8,128)(2,1)S(1)}, u32[]{:S(2)}, u32[]{:S(2)}) %collective-permute-start.10) | collective-permute-done | bytes 131104 | tf_op jit(solution)/shard_map/ppermute | solution.py:150
  69.9 0.1 add_convert_fusion.2
  69.9 2.3 %collective-permute-start.11 = (bf16[4,2,64,128]{3,2,1,0:T(8,128)(2,1)S(1)}, bf16[4,2,64,128]{3,2,1,0:T(8,128)(2,1)S(1)}, u32[]{:S(2)}, u32[]{:S(2)}) collective-permute-start(bf16[4,2,64,128]{3,2,1,0:T(8,128)(2,1)S(1)} %add_convert_fusion.2), channel_id=1, source_target_pairs={{0,24},{4,28},{8,0},{12,4},{16,8},{20,12},{24,16},{28,20},{1,25},{... | collective-permute-start | bytes 393224 | tf_op jit(solution)/shard_map/ppermute | solution.py:150
  72.2 0.8 collective-permute-start.13
  73.1 2.8 %collective-permute-done.11 = bf16[4,2,64,128]{3,2,1,0:T(8,128)(2,1)S(1)} collective-permute-done((bf16[4,2,64,128]{3,2,1,0:T(8,128)(2,1)S(1)}, bf16[4,2,64,128]{3,2,1,0:T(8,128)(2,1)S(1)}, u32[]{:S(2)}, u32[]{:S(2)}) %collective-permute-start.11) | collective-permute-done | bytes 131104 | tf_op jit(solution)/shard_map/ppermute | solution.py:150
  75.9 3.5 %collective-permute-done.13 = bf16[4,2,64,128]{3,2,1,0:T(8,128)(2,1)S(1)} collective-permute-done((bf16[4,2,64,128]{3,2,1,0:T(8,128)(2,1)S(1)}, bf16[4,2,64,128]{3,2,1,0:T(8,128)(2,1)S(1)}, u32[]{:S(2)}, u32[]{:S(2)}) %collective-permute-start.13) | collective-permute-done | bytes 131104 | tf_op jit(solution)/shard_map/ppermute | solution.py:150
  79.4 0.1 add_convert_fusion
  79.5 11.1 %all_to_all.20 = bf16[4,2,64,128]{3,2,1,0:T(8,128)(2,1)S(1)} all-to-all(bf16[4,2,64,128]{3,2,1,0:T(8,128)(2,1)S(1)} %add_convert_fusion), channel_id=1, replica_groups=mesh['batch'=8,'z'=8,'y'=4] {'y'}, dimensions={0} | all-to-all | bytes 262144 | tf_op jit(solution)/shard_map/all_to_all | solution.py:153
  90.6 3.5 %all-to-all-start.2 = ((bf16[4,1280,128]{2,1,0:T(8,128)(2,1)}), bf16[4,1280,128]{2,1,0:T(8,128)(2,1)S(1)}, u32[]{:S(2)}, u32[]{:S(2)}) async-start(bf16[4,1280,128]{2,1,0:T(8,128)(2,1)} %get-tuple-element.19), calls=%async_computation.2 | async-start | bytes 2621440 | tf_op jit(solution)/shard_map/all_to_all | solution.py:153
  94.2 0.7 copy.24
  94.9 0.7 copy.23
  95.6 10.9 %all-to-all-done.2 = bf16[4,1280,128]{2,1,0:T(8,128)(2,1)S(1)} async-done(((bf16[4,1280,128]{2,1,0:T(8,128)(2,1)}), bf16[4,1280,128]{2,1,0:T(8,128)(2,1)S(1)}, u32[]{:S(2)}, u32[]{:S(2)}) %all-to-all-start.2) | async-done | bytes 1310752 | tf_op jit(solution)/shard_map/all_to_all | solution.py:153
  106.4 0.1 fusion
  106.5 1.0 copy.20
  107.5 0.2 copy.19
  107.7 1.0 broadcast_select_fusion
  108.7 0.8 copy.22
  109.5 0.8 copy.21
  (14 shorter events, 0.1 us)
Async XLA Ops:
  0.6 8.0 %copy-start.1 = (bf16[1,128,4,128]{3,2,1,0:T(4,128)(2,1)S(1)}, bf16[1,128,4,128]{3,2,1,0:T(4,128)(2,1)}, u32[]{:S(2)}) copy-start(bf16[1,128,4,128]{3,2,1,0:T(4,128)(2,1)} %param.9) | copy-start | bytes 393220
  0.6 8.0 %copy-start.2 = (bf16[1,128,4,128]{3,2,1,0:T(4,128)(2,1)S(1)}, bf16[1,128,4,128]{3,2,1,0:T(4,128)(2,1)}, u32[]{:S(2)}) copy-start(bf16[1,128,4,128]{3,2,1,0:T(4,128)(2,1)} %param.8) | copy-start | bytes 393220
  0.7 8.1 %copy-start = (bf16[1,128,16,128]{3,2,1,0:T(8,128)(2,1)S(1)}, bf16[1,128,16,128]{3,2,1,0:T(8,128)(2,1)}, u32[]{:S(2)}) copy-start(bf16[1,128,16,128]{3,2,1,0:T(8,128)(2,1)} %param.13) | copy-start | bytes 1572868
  2.3 10.4 %all-to-all-start = ((bf16[4,2,64,128]{3,2,1,0:T(8,128)(2,1)}), bf16[4,2,64,128]{3,2,1,0:T(8,128)(2,1)S(1)}, u32[]{:S(2)}, u32[]{:S(2)}) async-start(bf16[4,2,64,128]{3,2,1,0:T(8,128)(2,1)} %maximum_bitcast_fusion), calls=%async_computation | async-start | bytes 262144 | tf_op jit(solution)/shard_map/all_to_all | solution.py:153
  12.7 29.2 %all-to-all-start.1 = ((bf16[4,1280,128]{2,1,0:T(8,128)(2,1)}), bf16[4,1280,128]{2,1,0:T(8,128)(2,1)S(1)}, u32[]{:S(2)}, u32[]{:S(2)}) async-start(bf16[4,1280,128]{2,1,0:T(8,128)(2,1)} %pad_maximum_fusion), calls=%async_computation.1 | async-start | bytes 2621440 | tf_op jit(solution)/shard_map/all_to_all | solution.py:153
  16.3 11.5 %collective-permute-start.3 = (bf16[4,2,64,128]{3,2,1,0:T(8,128)(2,1)S(1)}, bf16[4,2,64,128]{3,2,1,0:T(8,128)(2,1)S(1)}, u32[]{:S(2)}, u32[]{:S(2)}) collective-permute-start(bf16[4,2,64,128]{3,2,1,0:T(8,128)(2,1)S(1)} %all-to-all-done.refs_1_), channel_id=1, source_target_pairs={{0,24},{4,28},{8,0},{12,4},{16,8},{20,12},{24,16},{28,20},{1,25},{... | collective-permute-start | bytes 393224 | tf_op jit(solution)/shard_map/ppermute | solution.py:150
  22.7 9.3 %collective-permute-start.2 = (bf16[4,2,64,128]{3,2,1,0:T(8,128)(2,1)S(1)}, bf16[4,2,64,128]{3,2,1,0:T(8,128)(2,1)S(1)}, u32[]{:S(2)}, u32[]{:S(2)}) collective-permute-start(bf16[4,2,64,128]{3,2,1,0:T(8,128)(2,1)S(1)} %all-to-all-done.refs_1_), channel_id=1, source_target_pairs={{0,8},{4,12},{8,16},{12,20},{16,24},{20,28},{24,0},{28,4},{1,9},{5... | collective-permute-start | bytes 393224 | tf_op jit(solution)/shard_map/ppermute | solution.py:150
  22.7 10.9 %collective-permute-start.1 = (bf16[4,2,64,128]{3,2,1,0:T(8,128)(2,1)S(1)}, bf16[4,2,64,128]{3,2,1,0:T(8,128)(2,1)S(1)}, u32[]{:S(2)}, u32[]{:S(2)}) collective-permute-start(bf16[4,2,64,128]{3,2,1,0:T(8,128)(2,1)S(1)} %all-to-all-done.refs_1_), channel_id=1, source_target_pairs={{0,28},{4,0},{8,4},{12,8},{16,12},{20,16},{24,20},{28,24},{1,29},{... | collective-permute-start | bytes 393224 | tf_op jit(solution)/shard_map/ppermute | solution.py:150
  26.4 9.4 %collective-permute-start = (bf16[4,2,64,128]{3,2,1,0:T(8,128)(2,1)S(1)}, bf16[4,2,64,128]{3,2,1,0:T(8,128)(2,1)S(1)}, u32[]{:S(2)}, u32[]{:S(2)}) collective-permute-start(bf16[4,2,64,128]{3,2,1,0:T(8,128)(2,1)S(1)} %all-to-all-done.refs_1_), channel_id=1, source_target_pairs={{0,4},{4,8},{8,12},{12,16},{16,20},{20,24},{24,28},{28,0},{1,5},{5... | collective-permute-start | bytes 393224 | tf_op jit(solution)/shard_map/ppermute | solution.py:150
  27.8 8.0 %collective-permute-start.5 = (bf16[4,2,64,128]{3,2,1,0:T(8,128)(2,1)S(1)}, bf16[4,2,64,128]{3,2,1,0:T(8,128)(2,1)S(1)}, u32[]{:S(2)}, u32[]{:S(2)}) collective-permute-start(bf16[4,2,64,128]{3,2,1,0:T(8,128)(2,1)S(1)} %collective-permute-done.3.refs_5_), channel_id=1, source_target_pairs={{0,28},{4,0},{8,4},{12,8},{16,12},{20,16},{24,20},{28,24},{1,29},{... | collective-permute-start | bytes 393224 | tf_op jit(solution)/shard_map/ppermute | solution.py:150
  32.0 8.4 %collective-permute-start.6 = (bf16[4,2,64,128]{3,2,1,0:T(8,128)(2,1)S(1)}, bf16[4,2,64,128]{3,2,1,0:T(8,128)(2,1)S(1)}, u32[]{:S(2)}, u32[]{:S(2)}) collective-permute-start(bf16[4,2,64,128]{3,2,1,0:T(8,128)(2,1)S(1)} %collective-permute-done.2.refs_4_), channel_id=1, source_target_pairs={{0,8},{4,12},{8,16},{12,20},{16,24},{20,28},{24,0},{28,4},{1,9},{5... | collective-permute-start | bytes 393224 | tf_op jit(solution)/shard_map/ppermute | solution.py:150
  32.0 10.0 %collective-permute-start.4 = (bf16[4,2,64,128]{3,2,1,0:T(8,128)(2,1)S(1)}, bf16[4,2,64,128]{3,2,1,0:T(8,128)(2,1)S(1)}, u32[]{:S(2)}, u32[]{:S(2)}) collective-permute-start(bf16[4,2,64,128]{3,2,1,0:T(8,128)(2,1)S(1)} %collective-permute-done.2.refs_4_), channel_id=1, source_target_pairs={{0,4},{4,8},{8,12},{12,16},{16,20},{20,24},{24,28},{28,0},{1,5},{5... | collective-permute-start | bytes 393224 | tf_op jit(solution)/shard_map/ppermute | solution.py:150
  59.1 5.2 %collective-permute-start.9 = (bf16[4,2,64,128]{3,2,1,0:T(8,128)(2,1)S(1)}, bf16[4,2,64,128]{3,2,1,0:T(8,128)(2,1)S(1)}, u32[]{:S(2)}, u32[]{:S(2)}) collective-permute-start(bf16[4,2,64,128]{3,2,1,0:T(8,128)(2,1)S(1)} %get-tuple-element.24), channel_id=1, source_target_pairs={{0,28},{4,0},{8,4},{12,8},{16,12},{20,16},{24,20},{28,24},{1,29},{... | collective-permute-start | bytes 393224 | tf_op jit(solution)/shard_map/ppermute | solution.py:150
  59.5 10.4 %collective-permute-start.10 = (bf16[4,2,64,128]{3,2,1,0:T(8,128)(2,1)S(1)}, bf16[4,2,64,128]{3,2,1,0:T(8,128)(2,1)S(1)}, u32[]{:S(2)}, u32[]{:S(2)}) collective-permute-start(bf16[4,2,64,128]{3,2,1,0:T(8,128)(2,1)S(1)} %get-tuple-element.25), channel_id=1, source_target_pairs={{0,24},{4,28},{8,0},{12,4},{16,8},{20,12},{24,16},{28,20},{1,25},{... | collective-permute-start | bytes 393224 | tf_op jit(solution)/shard_map/ppermute | solution.py:150
  60.3 12.8 %collective-permute-start.7 = (bf16[4,2,64,128]{3,2,1,0:T(8,128)(2,1)S(1)}, bf16[4,2,64,128]{3,2,1,0:T(8,128)(2,1)S(1)}, u32[]{:S(2)}, u32[]{:S(2)}) collective-permute-start(bf16[4,2,64,128]{3,2,1,0:T(8,128)(2,1)S(1)} %get-tuple-element.21), channel_id=1, source_target_pairs={{0,28},{4,0},{8,4},{12,8},{16,12},{20,16},{24,20},{28,24},{1,29},{... | collective-permute-start | bytes 393224 | tf_op jit(solution)/shard_map/ppermute | solution.py:150
  61.6 11.4 %collective-permute-start.8 = (bf16[4,2,64,128]{3,2,1,0:T(8,128)(2,1)S(1)}, bf16[4,2,64,128]{3,2,1,0:T(8,128)(2,1)S(1)}, u32[]{:S(2)}, u32[]{:S(2)}) collective-permute-start(bf16[4,2,64,128]{3,2,1,0:T(8,128)(2,1)S(1)} %get-tuple-element.22), channel_id=1, source_target_pairs={{0,4},{4,8},{8,12},{12,16},{16,20},{20,24},{24,28},{28,0},{1,5},{5... | collective-permute-start | bytes 393224 | tf_op jit(solution)/shard_map/ppermute | solution.py:150
  62.3 9.9 %collective-permute-start.12 = (bf16[4,2,64,128]{3,2,1,0:T(8,128)(2,1)S(1)}, bf16[4,2,64,128]{3,2,1,0:T(8,128)(2,1)S(1)}, u32[]{:S(2)}, u32[]{:S(2)}) collective-permute-start(bf16[4,2,64,128]{3,2,1,0:T(8,128)(2,1)S(1)} %get-tuple-element.27), channel_id=1, source_target_pairs={{0,4},{4,8},{8,12},{12,16},{16,20},{20,24},{24,28},{28,0},{1,5},{5... | collective-permute-start | bytes 393224 | tf_op jit(solution)/shard_map/ppermute | solution.py:150
  69.9 5.9 %collective-permute-start.11 = (bf16[4,2,64,128]{3,2,1,0:T(8,128)(2,1)S(1)}, bf16[4,2,64,128]{3,2,1,0:T(8,128)(2,1)S(1)}, u32[]{:S(2)}, u32[]{:S(2)}) collective-permute-start(bf16[4,2,64,128]{3,2,1,0:T(8,128)(2,1)S(1)} %add_convert_fusion.2), channel_id=1, source_target_pairs={{0,24},{4,28},{8,0},{12,4},{16,8},{20,12},{24,16},{28,20},{1,25},{... | collective-permute-start | bytes 393224 | tf_op jit(solution)/shard_map/ppermute | solution.py:150
  72.2 7.2 %collective-permute-start.13 = (bf16[4,2,64,128]{3,2,1,0:T(8,128)(2,1)S(1)}, bf16[4,2,64,128]{3,2,1,0:T(8,128)(2,1)S(1)}, u32[]{:S(2)}, u32[]{:S(2)}) collective-permute-start(bf16[4,2,64,128]{3,2,1,0:T(8,128)(2,1)S(1)} %add_convert_fusion.1), channel_id=1, source_target_pairs={{0,8},{4,12},{8,16},{12,20},{16,24},{20,28},{24,0},{28,4},{1,9},{5... | collective-permute-start | bytes 393224 | tf_op jit(solution)/shard_map/ppermute | solution.py:150
  90.6 15.8 %all-to-all-start.2 = ((bf16[4,1280,128]{2,1,0:T(8,128)(2,1)}), bf16[4,1280,128]{2,1,0:T(8,128)(2,1)S(1)}, u32[]{:S(2)}, u32[]{:S(2)}) async-start(bf16[4,1280,128]{2,1,0:T(8,128)(2,1)} %get-tuple-element.19), calls=%async_computation.2 | async-start | bytes 2621440 | tf_op jit(solution)/shard_map/all_to_all | solution.py:153
where the time goes:
time: 111 us; the launch traced here: 110 us
  waiting for transfers between devices  37.5 us (34%)
  starting transfers between devices  33.3 us (30%)
  Pallas kernels  17.2 us (15%)
  blocking collectives  11.1 us (10%)
  local copies, waits for them, and re-layouts  6.38 us (6%)
  other arithmetic  3.31 us (3%)
  between operations  1.43 us (1%)
    ppermute x14, waiting for transfers between devices, over_z(): return lax.ppermute(x, 'z', [(i, (i + k) % 8) for i in range(8)])  24 us
    ppermute x14, starting transfers between devices, over_z(): return lax.ppermute(x, 'z', [(i, (i + k) % 8) for i in range(8)])  21.8 us
    pallas_call x1, Pallas kernels, attention_call(): pl.pallas_call(body, out_shape=shapes, scratch_shapes=[pltpu.VMEM((nk, he...  17.2 us
    all_to_all x3, waiting for transfers between devices, swap_y(): return lax.all_to_all(x, 'y', 0, 0, tiled=True)  13.4 us
    all_to_all x3, starting transfers between devices, swap_y(): return lax.all_to_all(x, 'y', 0, 0, tiled=True)  11.5 us
    all_to_all x1, blocking collectives, swap_y(): return lax.all_to_all(x, 'y', 0, 0, tiled=True)  11.1 us
    unnamed x10, local copies, waits for them, and re-layouts  2.9 us
  transfers between devices with their start and end apart: 17, of which 11 were waited for; matrix products, arithmetic and copies ran while one was open for 4% of the time, Pallas kernels for 0%

commit v1 on v0

--- a/solution.py
+++ b/solution.py
@@ -195,7 +195,8 @@
     total = d0.astype(f32)
     for x in parts:
         total = total + x.astype(f32)
-    total = swap_y(total.astype(bf16))
+    total, home = lax.optimization_barrier((total.astype(bf16), home))
+    total = swap_y(total)
 
     def by_token(x, n):
         x = x.reshape(KH, T, n, D)

time: 111 us -> 97 us (0.87)
  blocking collectives: 11.1 us -> 0 us
  waiting for transfers between devices: 37.5 us -> 28.7 us
  starting transfers between devices: 33.3 us -> 38.9 us
    all_to_all x1 -> x0, blocking collectives: 11.1 us -> none  [swap_y(): return lax.all_to_all(x, 'y', 0, 0, tiled=True)]
    all_to_all x3 -> x4, waiting for transfers between devices: 13.4 us -> 4.75 us  [swap_y(): return lax.all_to_all(x, 'y', 0, 0, tiled=True)]
    all_to_all x3 -> x4, starting transfers between devices: 11.5 us -> 17.1 us  [swap_y(): return lax.all_to_all(x, 'y', 0, 0, tiled=True)]
  transfers between devices with their start and end apart: 17 -> 18, of which waited for: 11 -> 11; matrix products, arithmetic and copies ran while one was open for 4% -> 8% of each run, Pallas kernels for 0% -> 0%
where the time goes in v1:
time: 97 us; the launch traced here: 96.5 us
  starting transfers between devices  38.9 us (40%)
  waiting for transfers between devices  28.7 us (30%)
  Pallas kernels  17.2 us (18%)
  local copies, waits for them, and re-layouts  6.37 us (7%)
  other arithmetic  3.97 us (4%)
  between operations  1.42 us (1%)
    ppermute x14, waiting for transfers between devices, over_z(): return lax.ppermute(x, 'z', [(i, (i + k) % 8) for i in range(8)])  23.9 us
    ppermute x14, starting transfers between devices, over_z(): return lax.ppermute(x, 'z', [(i, (i + k) % 8) for i in range(8)])  21.8 us
    pallas_call x1, Pallas kernels, attention_call(): pl.pallas_call(body, out_shape=shapes, scratch_shapes=[pltpu.VMEM((nk, he...  17.2 us
    all_to_all x4, starting transfers between devices, swap_y(): return lax.all_to_all(x, 'y', 0, 0, tiled=True)  17.1 us
    all_to_all x4, waiting for transfers between devices, swap_y(): return lax.all_to_all(x, 'y', 0, 0, tiled=True)  4.75 us
    unnamed x10, local copies, waits for them, and re-layouts  2.89 us
  transfers between devices with their start and end apart: 18, of which 11 were waited for; matrix products, arithmetic and copies ran while one was open for 8% of the time, Pallas kernels for 0%

profile of v1, /device:TPU:4, one launch (start us, length us, event | category | flops | bytes accessed | tf_op | source)
XLA Modules:
  0.0 96.5 jit_solution(3187428485902451824)
XLA Ops:
  0.7 1.0 copy_bitcast_fusion.2
  1.6 0.7 maximum_bitcast_fusion
  2.3 4.5 %all-to-all-start = ((bf16[4,2,64,128]{3,2,1,0:T(8,128)(2,1)}), bf16[4,2,64,128]{3,2,1,0:T(8,128)(2,1)S(1)}, u32[]{:S(2)}, u32[]{:S(2)}) async-start(bf16[4,2,64,128]{3,2,1,0:T(8,128)(2,1)} %maximum_bitcast_fusion), calls=%async_computation | async-start | bytes 262144 | tf_op jit(solution)/shard_map/all_to_all | solution.py:153
  7.4 1.2 %copy.15 = bf16[128,4,4,128]{3,2,0,1:T(4,128)(2,1)S(1)} copy(bf16[128,4,4,128]{3,2,1,0:T(4,128)(2,1)} %bitcast.61) | data formatting | bytes 1048576 | tf_op jit(solution)/shard_map/reshape | solution.py:162
  8.7 0.3 copy_select_fusion
  9.0 1.2 %pad_maximum_fusion = bf16[4,1280,128]{2,1,0:T(8,128)(2,1)} fusion(bf16[4,128,128]{2,1,0:T(8,128)(2,1)S(1)} %get-tuple-element.46, bf16[4,128,128]{2,1,0:T(8,128)(2,1)S(1)} %get-tuple-element.47, bf16[4,512,128]{2,1,0:T(8,128)(2,1)S(1)} %bitcast.57, bf16[4,512,128]{2,1,0:T(8,128)(2,1)S(1)} %bitcast.56), kind=kLoop, calls=%fused_computation | loop fusion | flops 5242880 | bytes 2621440 | tf_op jit(solution)/shard_map/concatenate | solution.py:165
  10.2 2.5 %all-to-all-done.refs_1_ = bf16[4,2,64,128]{3,2,1,0:T(8,128)(2,1)S(1)} async-done(((bf16[4,2,64,128]{3,2,1,0:T(8,128)(2,1)}), bf16[4,2,64,128]{3,2,1,0:T(8,128)(2,1)S(1)}, u32[]{:S(2)}, u32[]{:S(2)}) %all-to-all-start) | async-done | bytes 131104 | tf_op jit(solution)/shard_map/all_to_all | solution.py:153
  12.7 3.5 %all-to-all-start.1 = ((bf16[4,1280,128]{2,1,0:T(8,128)(2,1)}), bf16[4,1280,128]{2,1,0:T(8,128)(2,1)S(1)}, u32[]{:S(2)}, u32[]{:S(2)}) async-start(bf16[4,1280,128]{2,1,0:T(8,128)(2,1)} %pad_maximum_fusion), calls=%async_computation.1 | async-start | bytes 2621440 | tf_op jit(solution)/shard_map/all_to_all | solution.py:153
  16.3 6.4 %collective-permute-start.3 = (bf16[4,2,64,128]{3,2,1,0:T(8,128)(2,1)S(1)}, bf16[4,2,64,128]{3,2,1,0:T(8,128)(2,1)S(1)}, u32[]{:S(2)}, u32[]{:S(2)}) collective-permute-start(bf16[4,2,64,128]{3,2,1,0:T(8,128)(2,1)S(1)} %all-to-all-done.refs_1_), channel_id=1, source_target_pairs={{0,24},{4,28},{8,0},{12,4},{16,8},{20,12},{24,16},{28,20},{1,25},{... | collective-permute-start | bytes 393224 | tf_op jit(solution)/shard_map/ppermute | solution.py:150
  22.7 0.0 collective-permute-start.2
  22.7 3.7 %collective-permute-start.1 = (bf16[4,2,64,128]{3,2,1,0:T(8,128)(2,1)S(1)}, bf16[4,2,64,128]{3,2,1,0:T(8,128)(2,1)S(1)}, u32[]{:S(2)}, u32[]{:S(2)}) collective-permute-start(bf16[4,2,64,128]{3,2,1,0:T(8,128)(2,1)S(1)} %all-to-all-done.refs_1_), channel_id=1, source_target_pairs={{0,28},{4,0},{8,4},{12,8},{16,12},{20,16},{24,20},{28,24},{1,29},{... | collective-permute-start | bytes 393224 | tf_op jit(solution)/shard_map/ppermute | solution.py:150
  26.4 0.0 collective-permute-start
  26.4 1.4 %collective-permute-done.3.refs_5_ = bf16[4,2,64,128]{3,2,1,0:T(8,128)(2,1)S(1)} collective-permute-done((bf16[4,2,64,128]{3,2,1,0:T(8,128)(2,1)S(1)}, bf16[4,2,64,128]{3,2,1,0:T(8,128)(2,1)S(1)}, u32[]{:S(2)}, u32[]{:S(2)}) %collective-permute-start.3) | collective-permute-done | bytes 131104 | tf_op jit(solution)/shard_map/ppermute | solution.py:150
  27.8 2.8 %collective-permute-start.5 = (bf16[4,2,64,128]{3,2,1,0:T(8,128)(2,1)S(1)}, bf16[4,2,64,128]{3,2,1,0:T(8,128)(2,1)S(1)}, u32[]{:S(2)}, u32[]{:S(2)}) collective-permute-start(bf16[4,2,64,128]{3,2,1,0:T(8,128)(2,1)S(1)} %collective-permute-done.3.refs_5_), channel_id=1, source_target_pairs={{0,28},{4,0},{8,4},{12,8},{16,12},{20,16},{24,20},{28,24},{1,29},{... | collective-permute-start | bytes 393224 | tf_op jit(solution)/shard_map/ppermute | solution.py:150
  30.6 1.4 %collective-permute-done.2.refs_4_ = bf16[4,2,64,128]{3,2,1,0:T(8,128)(2,1)S(1)} collective-permute-done((bf16[4,2,64,128]{3,2,1,0:T(8,128)(2,1)S(1)}, bf16[4,2,64,128]{3,2,1,0:T(8,128)(2,1)S(1)}, u32[]{:S(2)}, u32[]{:S(2)}) %collective-permute-start.2) | collective-permute-done | bytes 131104 | tf_op jit(solution)/shard_map/ppermute | solution.py:150
  32.0 0.0 collective-permute-start.6
  32.0 1.6 %collective-permute-start.4 = (bf16[4,2,64,128]{3,2,1,0:T(8,128)(2,1)S(1)}, bf16[4,2,64,128]{3,2,1,0:T(8,128)(2,1)S(1)}, u32[]{:S(2)}, u32[]{:S(2)}) collective-permute-start(bf16[4,2,64,128]{3,2,1,0:T(8,128)(2,1)S(1)} %collective-permute-done.2.refs_4_), channel_id=1, source_target_pairs={{0,4},{4,8},{8,12},{12,16},{16,20},{20,24},{24,28},{28,0},{1,5},{5... | collective-permute-start | bytes 393224 | tf_op jit(solution)/shard_map/ppermute | solution.py:150
  33.5 0.0 collective-permute-done.1.refs_3_
  33.5 2.2 %collective-permute-done.refs_2_ = bf16[4,2,64,128]{3,2,1,0:T(8,128)(2,1)S(1)} collective-permute-done((bf16[4,2,64,128]{3,2,1,0:T(8,128)(2,1)S(1)}, bf16[4,2,64,128]{3,2,1,0:T(8,128)(2,1)S(1)}, u32[]{:S(2)}, u32[]{:S(2)}) %collective-permute-start) | collective-permute-done | bytes 131104 | tf_op jit(solution)/shard_map/ppermute | solution.py:150
  35.8 0.0 collective-permute-done.5.refs_7_
  35.8 4.6 %collective-permute-done.6.refs_8_ = bf16[4,2,64,128]{3,2,1,0:T(8,128)(2,1)S(1)} collective-permute-done((bf16[4,2,64,128]{3,2,1,0:T(8,128)(2,1)S(1)}, bf16[4,2,64,128]{3,2,1,0:T(8,128)(2,1)S(1)}, u32[]{:S(2)}, u32[]{:S(2)}) %collective-permute-start.6) | collective-permute-done | bytes 131104 | tf_op jit(solution)/shard_map/ppermute | solution.py:150
  40.4 1.6 %collective-permute-done.4.refs_6_ = bf16[4,2,64,128]{3,2,1,0:T(8,128)(2,1)S(1)} collective-permute-done((bf16[4,2,64,128]{3,2,1,0:T(8,128)(2,1)S(1)}, bf16[4,2,64,128]{3,2,1,0:T(8,128)(2,1)S(1)}, u32[]{:S(2)}, u32[]{:S(2)}) %collective-permute-start.4) | collective-permute-done | bytes 131104 | tf_op jit(solution)/shard_map/ppermute | solution.py:150
  42.0 17.2 %attention.1 = (bf16[4,1280,128]{2,1,0:T(8,128)(2,1)}, bf16[4,2,64,128]{3,2,1,0:T(8,128)(2,1)S(1)}, bf16[4,2,64,128]{3,2,1,0:T(8,128)(2,1)S(1)}, bf16[4,2,64,128...) custom-call(bf16[4,1280,128]{2,1,0:T(8,128)(2,1)S(1)} %all-to-all-do, ...), custom_call_target="tpu_custom_call" | custom-call | tf_op jit(solution)/shard_map/attention/pallas_call | solution.py:120
  59.1 4.4 %all-to-all-start.2 = ((bf16[4,1280,128]{2,1,0:T(8,128)(2,1)}), bf16[4,1280,128]{2,1,0:T(8,128)(2,1)S(1)}, u32[]{:S(2)}, u32[]{:S(2)}) async-start(bf16[4,1280,128]{2,1,0:T(8,128)(2,1)} %get-tuple-element.29), calls=%async_computation.2 | async-start | bytes 2621440 | tf_op jit(solution)/shard_map/all_to_all | solution.py:153
  63.5 0.4 collective-permute-start.9
  63.9 0.8 collective-permute-start.10
  64.7 1.3 %collective-permute-start.7 = (bf16[4,2,64,128]{3,2,1,0:T(8,128)(2,1)S(1)}, bf16[4,2,64,128]{3,2,1,0:T(8,128)(2,1)S(1)}, u32[]{:S(2)}, u32[]{:S(2)}) collective-permute-start(bf16[4,2,64,128]{3,2,1,0:T(8,128)(2,1)S(1)} %get-tuple-element.22), channel_id=1, source_target_pairs={{0,28},{4,0},{8,4},{12,8},{16,12},{20,16},{24,20},{28,24},{1,29},{... | collective-permute-start | bytes 393224 | tf_op jit(solution)/shard_map/ppermute | solution.py:150
  66.0 0.7 collective-permute-start.8
  66.7 1.0 %collective-permute-start.12 = (bf16[4,2,64,128]{3,2,1,0:T(8,128)(2,1)S(1)}, bf16[4,2,64,128]{3,2,1,0:T(8,128)(2,1)S(1)}, u32[]{:S(2)}, u32[]{:S(2)}) collective-permute-start(bf16[4,2,64,128]{3,2,1,0:T(8,128)(2,1)S(1)} %get-tuple-element.28), channel_id=1, source_target_pairs={{0,4},{4,8},{8,12},{12,16},{16,20},{20,24},{24,28},{28,0},{1,5},{5... | collective-permute-start | bytes 393224 | tf_op jit(solution)/shard_map/ppermute | solution.py:150
  67.8 0.7 collective-permute-done.9
  68.5 6.0 %collective-permute-done.10 = bf16[4,2,64,128]{3,2,1,0:T(8,128)(2,1)S(1)} collective-permute-done((bf16[4,2,64,128]{3,2,1,0:T(8,128)(2,1)S(1)}, bf16[4,2,64,128]{3,2,1,0:T(8,128)(2,1)S(1)}, u32[]{:S(2)}, u32[]{:S(2)}) %collective-permute-start.10) | collective-permute-done | bytes 131104 | tf_op jit(solution)/shard_map/ppermute | solution.py:150
  74.5 0.1 add_convert_fusion.2
  74.5 2.0 %collective-permute-start.11 = (bf16[4,2,64,128]{3,2,1,0:T(8,128)(2,1)S(1)}, bf16[4,2,64,128]{3,2,1,0:T(8,128)(2,1)S(1)}, u32[]{:S(2)}, u32[]{:S(2)}) collective-permute-start(bf16[4,2,64,128]{3,2,1,0:T(8,128)(2,1)S(1)} %add_convert_fusion.2), channel_id=1, source_target_pairs={{0,24},{4,28},{8,0},{12,4},{16,8},{20,12},{24,16},{28,20},{1,25},{... | collective-permute-start | bytes 393224 | tf_op jit(solution)/shard_map/ppermute | solution.py:150
  76.5 1.1 %collective-permute-start.13 = (bf16[4,2,64,128]{3,2,1,0:T(8,128)(2,1)S(1)}, bf16[4,2,64,128]{3,2,1,0:T(8,128)(2,1)S(1)}, u32[]{:S(2)}, u32[]{:S(2)}) collective-permute-start(bf16[4,2,64,128]{3,2,1,0:T(8,128)(2,1)S(1)} %add_convert_fusion.1), channel_id=1, source_target_pairs={{0,8},{4,12},{8,16},{12,20},{16,24},{20,28},{24,0},{28,4},{1,9},{5... | collective-permute-start | bytes 393224 | tf_op jit(solution)/shard_map/ppermute | solution.py:150
  77.7 2.8 %collective-permute-done.11 = bf16[4,2,64,128]{3,2,1,0:T(8,128)(2,1)S(1)} collective-permute-done((bf16[4,2,64,128]{3,2,1,0:T(8,128)(2,1)S(1)}, bf16[4,2,64,128]{3,2,1,0:T(8,128)(2,1)S(1)}, u32[]{:S(2)}, u32[]{:S(2)}) %collective-permute-start.11) | collective-permute-done | bytes 131104 | tf_op jit(solution)/shard_map/ppermute | solution.py:150
  80.5 3.2 %collective-permute-done.13 = bf16[4,2,64,128]{3,2,1,0:T(8,128)(2,1)S(1)} collective-permute-done((bf16[4,2,64,128]{3,2,1,0:T(8,128)(2,1)S(1)}, bf16[4,2,64,128]{3,2,1,0:T(8,128)(2,1)S(1)}, u32[]{:S(2)}, u32[]{:S(2)}) %collective-permute-start.13) | collective-permute-done | bytes 131104 | tf_op jit(solution)/shard_map/ppermute | solution.py:150
  83.7 0.7 add_convert_fusion
  84.4 0.0 all-to-all-done.2
  84.4 4.7 %all-to-all-start.3 = ((bf16[4,2,64,128]{3,2,1,0:T(8,128)(2,1)}), bf16[4,2,64,128]{3,2,1,0:T(8,128)(2,1)S(1)}, u32[]{:S(2)}, u32[]{:S(2)}) async-start(bf16[4,2,64,128]{3,2,1,0:T(8,128)(2,1)} %add_convert_fusion), calls=%async_computation.3 | async-start | bytes 262144 | tf_op jit(solution)/shard_map/all_to_all | solution.py:153
  89.2 0.1 fusion
  89.2 0.2 copy.19
  89.4 1.0 %broadcast_select_fusion = bf16[1,128,16,128]{3,2,1,0:T(8,128)(2,1)} fusion(bf16[1,128,16,128]{3,2,1,0:T(8,128)(2,1)S(1)} %bitcast.58, pred[128]{0:T(512)(128)(4,1)S(1)} %iota_compare_fusion), kind=kLoop, calls=%fused_computation.2 | loop fusion | flops 262144 | bytes 1048704 | tf_op jit(solution)/shard_map/jit(_where)/select_n | solution.py:206
  90.5 1.0 %copy.20 = bf16[128,4,4,128]{3,2,1,0:T(4,128)(2,1)} copy(bf16[128,4,4,128]{3,2,0,1:T(4,128)(2,1)S(1)} %bitcast.59) | data formatting | bytes 1048576 | tf_op jit(solution)/shard_map/transpose | solution.py:203
  91.4 0.8 copy.22
  92.2 0.8 copy.21
  93.0 2.2 %all-to-all-done.3 = bf16[4,2,64,128]{3,2,1,0:T(8,128)(2,1)S(1)} async-done(((bf16[4,2,64,128]{3,2,1,0:T(8,128)(2,1)}), bf16[4,2,64,128]{3,2,1,0:T(8,128)(2,1)S(1)}, u32[]{:S(2)}, u32[]{:S(2)}) %all-to-all-start.3) | async-done | bytes 131104 | tf_op jit(solution)/shard_map/all_to_all | solution.py:153
  95.2 0.7 copy.24
  95.9 0.7 copy.23
  (15 shorter events, 0.1 us)
Async XLA Ops:
  0.6 8.0 %copy-start.1 = (bf16[1,128,4,128]{3,2,1,0:T(4,128)(2,1)S(1)}, bf16[1,128,4,128]{3,2,1,0:T(4,128)(2,1)}, u32[]{:S(2)}) copy-start(bf16[1,128,4,128]{3,2,1,0:T(4,128)(2,1)} %param.9) | copy-start | bytes 393220
  0.6 8.0 %copy-start.2 = (bf16[1,128,4,128]{3,2,1,0:T(4,128)(2,1)S(1)}, bf16[1,128,4,128]{3,2,1,0:T(4,128)(2,1)}, u32[]{:S(2)}) copy-start(bf16[1,128,4,128]{3,2,1,0:T(4,128)(2,1)} %param.8) | copy-start | bytes 393220
  0.7 8.1 %copy-start = (bf16[1,128,16,128]{3,2,1,0:T(8,128)(2,1)S(1)}, bf16[1,128,16,128]{3,2,1,0:T(8,128)(2,1)}, u32[]{:S(2)}) copy-start(bf16[1,128,16,128]{3,2,1,0:T(8,128)(2,1)} %param.13) | copy-start | bytes 1572868
  2.3 10.4 %all-to-all-start = ((bf16[4,2,64,128]{3,2,1,0:T(8,128)(2,1)}), bf16[4,2,64,128]{3,2,1,0:T(8,128)(2,1)S(1)}, u32[]{:S(2)}, u32[]{:S(2)}) async-start(bf16[4,2,64,128]{3,2,1,0:T(8,128)(2,1)} %maximum_bitcast_fusion), calls=%async_computation | async-start | bytes 262144 | tf_op jit(solution)/shard_map/all_to_all | solution.py:153
  12.7 29.2 %all-to-all-start.1 = ((bf16[4,1280,128]{2,1,0:T(8,128)(2,1)}), bf16[4,1280,128]{2,1,0:T(8,128)(2,1)S(1)}, u32[]{:S(2)}, u32[]{:S(2)}) async-start(bf16[4,1280,128]{2,1,0:T(8,128)(2,1)} %pad_maximum_fusion), calls=%async_computation.1 | async-start | bytes 2621440 | tf_op jit(solution)/shard_map/all_to_all | solution.py:153
  16.3 11.5 %collective-permute-start.3 = (bf16[4,2,64,128]{3,2,1,0:T(8,128)(2,1)S(1)}, bf16[4,2,64,128]{3,2,1,0:T(8,128)(2,1)S(1)}, u32[]{:S(2)}, u32[]{:S(2)}) collective-permute-start(bf16[4,2,64,128]{3,2,1,0:T(8,128)(2,1)S(1)} %all-to-all-done.refs_1_), channel_id=1, source_target_pairs={{0,24},{4,28},{8,0},{12,4},{16,8},{20,12},{24,16},{28,20},{1,25},{... | collective-permute-start | bytes 393224 | tf_op jit(solution)/shard_map/ppermute | solution.py:150
  22.7 9.3 %collective-permute-start.2 = (bf16[4,2,64,128]{3,2,1,0:T(8,128)(2,1)S(1)}, bf16[4,2,64,128]{3,2,1,0:T(8,128)(2,1)S(1)}, u32[]{:S(2)}, u32[]{:S(2)}) collective-permute-start(bf16[4,2,64,128]{3,2,1,0:T(8,128)(2,1)S(1)} %all-to-all-done.refs_1_), channel_id=1, source_target_pairs={{0,8},{4,12},{8,16},{12,20},{16,24},{20,28},{24,0},{28,4},{1,9},{5... | collective-permute-start | bytes 393224 | tf_op jit(solution)/shard_map/ppermute | solution.py:150
  22.7 10.9 %collective-permute-start.1 = (bf16[4,2,64,128]{3,2,1,0:T(8,128)(2,1)S(1)}, bf16[4,2,64,128]{3,2,1,0:T(8,128)(2,1)S(1)}, u32[]{:S(2)}, u32[]{:S(2)}) collective-permute-start(bf16[4,2,64,128]{3,2,1,0:T(8,128)(2,1)S(1)} %all-to-all-done.refs_1_), channel_id=1, source_target_pairs={{0,28},{4,0},{8,4},{12,8},{16,12},{20,16},{24,20},{28,24},{1,29},{... | collective-permute-start | bytes 393224 | tf_op jit(solution)/shard_map/ppermute | solution.py:150
  26.4 9.4 %collective-permute-start = (bf16[4,2,64,128]{3,2,1,0:T(8,128)(2,1)S(1)}, bf16[4,2,64,128]{3,2,1,0:T(8,128)(2,1)S(1)}, u32[]{:S(2)}, u32[]{:S(2)}) collective-permute-start(bf16[4,2,64,128]{3,2,1,0:T(8,128)(2,1)S(1)} %all-to-all-done.refs_1_), channel_id=1, source_target_pairs={{0,4},{4,8},{8,12},{12,16},{16,20},{20,24},{24,28},{28,0},{1,5},{5... | collective-permute-start | bytes 393224 | tf_op jit(solution)/shard_map/ppermute | solution.py:150
  27.8 8.0 %collective-permute-start.5 = (bf16[4,2,64,128]{3,2,1,0:T(8,128)(2,1)S(1)}, bf16[4,2,64,128]{3,2,1,0:T(8,128)(2,1)S(1)}, u32[]{:S(2)}, u32[]{:S(2)}) collective-permute-start(bf16[4,2,64,128]{3,2,1,0:T(8,128)(2,1)S(1)} %collective-permute-done.3.refs_5_), channel_id=1, source_target_pairs={{0,28},{4,0},{8,4},{12,8},{16,12},{20,16},{24,20},{28,24},{1,29},{... | collective-permute-start | bytes 393224 | tf_op jit(solution)/shard_map/ppermute | solution.py:150
  32.0 8.4 %collective-permute-start.6 = (bf16[4,2,64,128]{3,2,1,0:T(8,128)(2,1)S(1)}, bf16[4,2,64,128]{3,2,1,0:T(8,128)(2,1)S(1)}, u32[]{:S(2)}, u32[]{:S(2)}) collective-permute-start(bf16[4,2,64,128]{3,2,1,0:T(8,128)(2,1)S(1)} %collective-permute-done.2.refs_4_), channel_id=1, source_target_pairs={{0,8},{4,12},{8,16},{12,20},{16,24},{20,28},{24,0},{28,4},{1,9},{5... | collective-permute-start | bytes 393224 | tf_op jit(solution)/shard_map/ppermute | solution.py:150
  32.0 10.0 %collective-permute-start.4 = (bf16[4,2,64,128]{3,2,1,0:T(8,128)(2,1)S(1)}, bf16[4,2,64,128]{3,2,1,0:T(8,128)(2,1)S(1)}, u32[]{:S(2)}, u32[]{:S(2)}) collective-permute-start(bf16[4,2,64,128]{3,2,1,0:T(8,128)(2,1)S(1)} %collective-permute-done.2.refs_4_), channel_id=1, source_target_pairs={{0,4},{4,8},{8,12},{12,16},{16,20},{20,24},{24,28},{28,0},{1,5},{5... | collective-permute-start | bytes 393224 | tf_op jit(solution)/shard_map/ppermute | solution.py:150
  59.1 25.3 %all-to-all-start.2 = ((bf16[4,1280,128]{2,1,0:T(8,128)(2,1)}), bf16[4,1280,128]{2,1,0:T(8,128)(2,1)S(1)}, u32[]{:S(2)}, u32[]{:S(2)}) async-start(bf16[4,1280,128]{2,1,0:T(8,128)(2,1)} %get-tuple-element.29), calls=%async_computation.2 | async-start | bytes 2621440 | tf_op jit(solution)/shard_map/all_to_all | solution.py:153
  63.5 5.0 %collective-permute-start.9 = (bf16[4,2,64,128]{3,2,1,0:T(8,128)(2,1)S(1)}, bf16[4,2,64,128]{3,2,1,0:T(8,128)(2,1)S(1)}, u32[]{:S(2)}, u32[]{:S(2)}) collective-permute-start(bf16[4,2,64,128]{3,2,1,0:T(8,128)(2,1)S(1)} %get-tuple-element.25), channel_id=1, source_target_pairs={{0,28},{4,0},{8,4},{12,8},{16,12},{20,16},{24,20},{28,24},{1,29},{... | collective-permute-start | bytes 393224 | tf_op jit(solution)/shard_map/ppermute | solution.py:150
  63.9 10.5 %collective-permute-start.10 = (bf16[4,2,64,128]{3,2,1,0:T(8,128)(2,1)S(1)}, bf16[4,2,64,128]{3,2,1,0:T(8,128)(2,1)S(1)}, u32[]{:S(2)}, u32[]{:S(2)}) collective-permute-start(bf16[4,2,64,128]{3,2,1,0:T(8,128)(2,1)S(1)} %get-tuple-element.26), channel_id=1, source_target_pairs={{0,24},{4,28},{8,0},{12,4},{16,8},{20,12},{24,16},{28,20},{1,25},{... | collective-permute-start | bytes 393224 | tf_op jit(solution)/shard_map/ppermute | solution.py:150
  64.7 12.9 %collective-permute-start.7 = (bf16[4,2,64,128]{3,2,1,0:T(8,128)(2,1)S(1)}, bf16[4,2,64,128]{3,2,1,0:T(8,128)(2,1)S(1)}, u32[]{:S(2)}, u32[]{:S(2)}) collective-permute-start(bf16[4,2,64,128]{3,2,1,0:T(8,128)(2,1)S(1)} %get-tuple-element.22), channel_id=1, source_target_pairs={{0,28},{4,0},{8,4},{12,8},{16,12},{20,16},{24,20},{28,24},{1,29},{... | collective-permute-start | bytes 393224 | tf_op jit(solution)/shard_map/ppermute | solution.py:150
  66.0 11.6 %collective-permute-start.8 = (bf16[4,2,64,128]{3,2,1,0:T(8,128)(2,1)S(1)}, bf16[4,2,64,128]{3,2,1,0:T(8,128)(2,1)S(1)}, u32[]{:S(2)}, u32[]{:S(2)}) collective-permute-start(bf16[4,2,64,128]{3,2,1,0:T(8,128)(2,1)S(1)} %get-tuple-element.23), channel_id=1, source_target_pairs={{0,4},{4,8},{8,12},{12,16},{16,20},{20,24},{24,28},{28,0},{1,5},{5... | collective-permute-start | bytes 393224 | tf_op jit(solution)/shard_map/ppermute | solution.py:150
  66.7 9.8 %collective-permute-start.12 = (bf16[4,2,64,128]{3,2,1,0:T(8,128)(2,1)S(1)}, bf16[4,2,64,128]{3,2,1,0:T(8,128)(2,1)S(1)}, u32[]{:S(2)}, u32[]{:S(2)}) collective-permute-start(bf16[4,2,64,128]{3,2,1,0:T(8,128)(2,1)S(1)} %get-tuple-element.28), channel_id=1, source_target_pairs={{0,4},{4,8},{8,12},{12,16},{16,20},{20,24},{24,28},{28,0},{1,5},{5... | collective-permute-start | bytes 393224 | tf_op jit(solution)/shard_map/ppermute | solution.py:150
  74.5 5.9 %collective-permute-start.11 = (bf16[4,2,64,128]{3,2,1,0:T(8,128)(2,1)S(1)}, bf16[4,2,64,128]{3,2,1,0:T(8,128)(2,1)S(1)}, u32[]{:S(2)}, u32[]{:S(2)}) collective-permute-start(bf16[4,2,64,128]{3,2,1,0:T(8,128)(2,1)S(1)} %add_convert_fusion.2), channel_id=1, source_target_pairs={{0,24},{4,28},{8,0},{12,4},{16,8},{20,12},{24,16},{28,20},{1,25},{... | collective-permute-start | bytes 393224 | tf_op jit(solution)/shard_map/ppermute | solution.py:150
  76.5 7.2 %collective-permute-start.13 = (bf16[4,2,64,128]{3,2,1,0:T(8,128)(2,1)S(1)}, bf16[4,2,64,128]{3,2,1,0:T(8,128)(2,1)S(1)}, u32[]{:S(2)}, u32[]{:S(2)}) collective-permute-start(bf16[4,2,64,128]{3,2,1,0:T(8,128)(2,1)S(1)} %add_convert_fusion.1), channel_id=1, source_target_pairs={{0,8},{4,12},{8,16},{12,20},{16,24},{20,28},{24,0},{28,4},{1,9},{5... | collective-permute-start | bytes 393224 | tf_op jit(solution)/shard_map/ppermute | solution.py:150
  84.4 10.7 %all-to-all-start.3 = ((bf16[4,2,64,128]{3,2,1,0:T(8,128)(2,1)}), bf16[4,2,64,128]{3,2,1,0:T(8,128)(2,1)S(1)}, u32[]{:S(2)}, u32[]{:S(2)}) async-start(bf16[4,2,64,128]{3,2,1,0:T(8,128)(2,1)} %add_convert_fusion), calls=%async_computation.3 | async-start | bytes 262144 | tf_op jit(solution)/shard_map/all_to_all | solution.py:153

commit v2 on v1

v2 whole, which is shorter than its diff:
```python
import functools

import jax
import jax.numpy as jnp
from jax import lax
from jax.experimental import pallas as pl
from jax.experimental.pallas import tpu as pltpu
from jax.sharding import Mesh, PartitionSpec as P

LOG2E = 1.4426950408889634
CHUNK = 512
f32 = jnp.float32
bf16 = jnp.bfloat16
NT = (((1,), (1,)), ((), ()))
NN = (((1,), (0,)), ((), ()))


def dot(a, b, dims):
    return lax.dot_general(a, b, dims, preferred_element_type=f32)


def spans(total, size):
    return [slice(i, min(i + size, total)) for i in range(0, total, size)]


def load_blocks(kvs, K, V, KT, VT):
    spots, D = kvs[0].shape[2], kvs[0].shape[3]
    for i in range(len(kvs)):
        for j in range(4):
            at = (4 * i + j) * spots
            K[at:at + spots, :] = kvs[i][j, 0]
            V[at:at + spots, :] = kvs[i][j, 1]
    for ks in spans(K.shape[0], CHUNK):
        if KT is not None:
            KT[:, ks] = K[ks, :].T
        if VT is not None:
            VT[0:D, ks] = V[ks, :].T
    if VT is not None:
        VT[D:D + 16, :] = jnp.ones((16, K.shape[0]), bf16)


def store_blocks(out_kvs, ks, dk, dv):
    spots = out_kvs[0].shape[2]
    for j in range((ks.stop - ks.start) // spots):
        block = ks.start // spots + j
        part = slice(j * spots, (j + 1) * spots)
        out_kvs[block // 4][block % 4, 0] = dk[part, :].astype(bf16)
        out_kvs[block // 4][block % 4, 1] = dv[part, :].astype(bf16)


def scores_into(S, at, s, top):
    S[at, :] = s
    return jnp.maximum(top, jnp.max(s.reshape(s.shape[0] // 8, 8, s.shape[1]), axis=0))


def near_forward(pack, kv0, kv1, kv2, kv3, kv4, Pm, acc_ref, top_ref, K, V, S, VT, *, T, G):
    D = K.shape[1]
    R = T * G
    C = D ** (-0.5)
    nk = K.shape[0]
    load_blocks((kv0, kv1, kv2, kv3, kv4), K, V, None, VT)
    key_pos = lax.broadcasted_iota(jnp.int32, (T, R), 0)
    row_pos = lax.broadcasted_iota(jnp.int32, (T, R), 1) // G
    own = slice(nk, nk + T)
    for r in range(4):
        rows = slice(r * R, (r + 1) * R)
        qr = pack[r, 0:R, :]
        kr = pack[r, 2 * R:2 * R + T, :]
        vr = pack[r, 2 * R + T:2 * R + 2 * T, :]
        top = jnp.full((8, R), -jnp.inf, f32)
        for ks in spans(nk, CHUNK):
            top = scores_into(S, ks, dot(K[ks, :], qr, NT), top)
        s = jnp.where(key_pos <= row_pos, dot(kr, qr, NT), -1e30)
        top = scores_into(S, own, s, top)
        top = jnp.max(top, axis=0, keepdims=True) * (C * LOG2E)
        top_ref[0:1, rows] = top
        p = jnp.exp2(S[own, :] * (C * LOG2E) - top).astype(bf16)
        Pm[own, rows] = p
        acc = dot(jnp.concatenate([vr.T, jnp.ones((16, T), bf16)], axis=0), p, NN)
        for ks in spans(nk, CHUNK):
            p = jnp.exp2(S[ks, :] * (C * LOG2E) - top).astype(bf16)
            Pm[ks, rows] = p
            acc = acc + dot(VT[:, ks], p, NN)
        acc_ref[:, rows] = acc


def far_both(
    pack, kv0, kv1, kv2, acc_ref, top_ref, o_ref, stat, Qs, Os, dqt, d0, d1, d2,
    K, V, S, Pm, KT, VT, Qn, On, *, T, G
):
    D = K.shape[1]
    R = T * G
    C = D ** (-0.5)
    nk = K.shape[0]
    load_blocks((kv0, kv1, kv2), K, V, KT, VT)
    for r in range(4):
        rows = slice(r * R, (r + 1) * R)
        qr = pack[r, 0:R, :]
        dof = pack[r, R:2 * R, :].astype(f32)
        top = jnp.full((8, R), -jnp.inf, f32)
        for ks in spans(nk, CHUNK):
            top = scores_into(S, ks, dot(K[ks, :], qr, NT), top)
        near_top = top_ref[0:1, rows]
        top = jnp.maximum(near_top, jnp.max(top, axis=0, keepdims=True) * (C * LOG2E))
        near = jnp.exp2(near_top - top)
        acc = acc_ref[:, rows] * near
        for ks in spans(nk, CHUNK):
            p = jnp.exp2(S[ks, :] * (C * LOG2E) - top).astype(bf16)
            Pm[ks, rows] = p
            acc = acc + dot(VT[:, ks], p, NN)
        inv = 1.0 / acc[D:D + 1, :]
        o = (acc[0:D, :] * inv).T.astype(bf16)
        o_ref[r] = o
        delta = jnp.sum(dof * o.astype(f32), axis=1, keepdims=True)
        stat[0:1, rows] = jnp.broadcast_to(delta, (R, D)).T[0:1, :]
        stat[1:2, rows] = inv
        stat[2:3, rows] = inv * near
        inv_col = jnp.broadcast_to(inv, (D, R)).T
        near_col = jnp.broadcast_to(inv * near, (D, R)).T
        qf = qr.astype(f32) * C
        Qn[rows, :] = (qf * inv_col).astype(bf16)
        On[rows, :] = (dof * inv_col).astype(bf16)
        Qs[rows, :] = (qf * near_col).astype(bf16)
        Os[rows, :] = (dof * near_col).astype(bf16)
    for i, ks in enumerate(spans(nk, CHUNK)):
        dk = jnp.zeros((ks.stop - ks.start, D), f32)
        dv = jnp.zeros((ks.stop - ks.start, D), f32)
        for r in range(4):
            rows = slice(r * R, (r + 1) * R)
            p = Pm[ks, rows]
            dp = dot(V[ks, :], pack[r, R:2 * R, :], NT)
            ds = (p.astype(f32) * (dp - stat[0:1, rows])).astype(bf16)
            dk = dk + dot(ds, Qn[rows, :], NN)
            dv = dv + dot(p, On[rows, :], NN)
            part = dot(KT[:, ks], ds, NN) * stat[1:2, rows]
            if i == 0:
                dqt[:, rows] = part
            else:
                dqt[:, rows] += part
        store_blocks((d0, d1, d2), ks, dk, dv)


def near_backward(
    pack, kv0, kv1, kv2, kv3, kv4, Pm, o_ref, stat, Qs, Os, dqt, out, d0, d1, d2, d3, d4,
    K, V, KT, acc, *, T, G
):
    D = K.shape[1]
    R = T * G
    C = D ** (-0.5)
    nk = K.shape[0]
    load_blocks((kv0, kv1, kv2, kv3, kv4), K, V, KT, None)
    own = slice(nk, nk + T)
    for r in range(4):
        rows = slice(r * R, (r + 1) * R)
        kr = pack[r, 2 * R:2 * R + T, :]
        vr = pack[r, 2 * R + T:2 * R + 2 * T, :]
        p = Pm[own, rows]
        ds = (p.astype(f32) * (dot(vr, pack[r, R:2 * R, :], NT) - stat[0:1, rows])).astype(bf16)
        out[r, 0:R, :] = o_ref[r]
        out[r, 2 * R:2 * R + T, :] = dot(ds, Qs[rows, :], NN).astype(bf16)
        out[r, 2 * R + T:2 * R + 2 * T, :] = dot(p, Os[rows, :], NN).astype(bf16)
        acc[:, rows] = dot(kr.T, ds, NN)
    for ks in spans(nk, CHUNK):
        dk = jnp.zeros((ks.stop - ks.start, D), f32)
        dv = jnp.zeros((ks.stop - ks.start, D), f32)
        for r in range(4):
            rows = slice(r * R, (r + 1) * R)
            p = Pm[ks, rows]
            dp = dot(V[ks, :], pack[r, R:2 * R, :], NT)
            ds = (p.astype(f32) * (dp - stat[0:1, rows])).astype(bf16)
            dk = dk + dot(ds, Qs[rows, :], NN)
            dv = dv + dot(p, Os[rows, :], NN)
            acc[:, rows] += dot(KT[:, ks], ds, NN)
        store_blocks((d0, d1, d2, d3, d4), ks, dk, dv)
    for r in range(4):
        rows = slice(r * R, (r + 1) * R)
        dq = (dqt[:, rows] + acc[:, rows] * stat[2:3, rows]) * C
        out[r, R:2 * R, :] = dq.T.astype(bf16)


def call(body, name, out_shape, scratch, flops, *args):
    return pl.pallas_call(
        body,
        out_shape=out_shape,
        scratch_shapes=scratch,
        compiler_params=pltpu.CompilerParams(vmem_limit_bytes=32 * 2**20),
        cost_estimate=pl.CostEstimate(flops=flops, bytes_accessed=4 * 2**20, transcendentals=0),
        name=name,
    )(*args)


def on_device(
    queries, response_keys, response_values, prompt_keys, prompt_value_rows, lengths, grad_out
):
    _, T, H, D = queries.shape
    KH = prompt_keys.shape[1]
    G = H // KH
    R = T * G

    def over_z(x, k):
        return lax.ppermute(x, "z", [(i, (i + k) % 8) for i in range(8)])

    def swap_y(x):
        return lax.all_to_all(x, "y", 0, 0, tiled=True)

    kv = jnp.stack([prompt_keys, prompt_value_rows], axis=0)
    kv = swap_y(jnp.transpose(kv, (2, 0, 1, 3)))

    live = (jnp.arange(T) < lengths[0])[:, None, None]
    masked = jnp.where(live, grad_out[0], jnp.zeros((), bf16))

    def by_head(x, n):
        x = x.reshape(T, KH, n, D)
        return jnp.transpose(x, (1, 0, 2, 3)).reshape(KH, T * n, D)

    pack = jnp.concatenate(
        [
            by_head(queries, G),
            by_head(masked, G),
            by_head(response_keys, 1),
            by_head(response_values, 1),
        ],
        axis=1,
    )
    kv, pack = lax.optimization_barrier((kv, pack))
    pack = swap_y(pack)
    from_2 = over_z(kv, 2)
    from_m2 = over_z(kv, -2)
    from_1 = over_z(kv, 1)
    from_m1 = over_z(kv, -1)
    from_4 = over_z(from_2, 2)
    from_3 = over_z(from_2, 1)
    from_m3 = over_z(from_m2, -1)

    near = (kv, from_1, from_m1, from_2, from_m2)
    far = (from_3, from_m3, from_4)
    block = jax.ShapeDtypeStruct(kv.shape, bf16)
    spots = kv.shape[2]
    near_keys = 5 * 4 * spots
    far_keys = 3 * 4 * spots
    rows = 4 * R

    def shape(dims, kind):
        return jax.ShapeDtypeStruct(dims, kind)

    def cost(products, keys):
        return products * 2 * rows * keys * D

    weights, acc, top = call(
        functools.partial(near_forward, T=T, G=G),
        "near_forward",
        (
            shape((near_keys + T, rows), bf16),
            shape((D + 16, rows), f32),
            shape((8, rows), f32),
        ),
        [
            pltpu.VMEM((near_keys, D), bf16),
            pltpu.VMEM((near_keys, D), bf16),
            pltpu.VMEM((near_keys + T, R), f32),
            pltpu.VMEM((D + 16, near_keys), bf16),
        ],
        cost(2, near_keys + T),
        pack, *near,
    )
    out, stat, q_near, g_near, dqt, d3, dm3, d4 = call(
        functools.partial(far_both, T=T, G=G),
        "far_both",
        (
            shape((4, R, D), bf16),
            shape((8, rows), f32),
            shape((rows, D), bf16),
            shape((rows, D), bf16),
            shape((D, rows), f32),
            block, block, block,
        ),
        [
            pltpu.VMEM((far_keys, D), bf16),
            pltpu.VMEM((far_keys, D), bf16),
            pltpu.VMEM((far_keys, R), f32),
            pltpu.VMEM((far_keys, rows), bf16),
            pltpu.VMEM((D, far_keys), bf16),
            pltpu.VMEM((D + 16, far_keys), bf16),
            pltpu.VMEM((rows, D), bf16),
            pltpu.VMEM((rows, D), bf16),
        ],
        cost(6, far_keys),
        pack, *far, acc, top,
    )
    home, d0, d1, dm1, d2, dm2 = call(
        functools.partial(near_backward, T=T, G=G),
        "near_backward",
        (shape(pack.shape, bf16), block, block, block, block, block),
        [
            pltpu.VMEM((near_keys, D), bf16),
            pltpu.VMEM((near_keys, D), bf16),
            pltpu.VMEM((D, near_keys), bf16),
            pltpu.VMEM((D, rows), f32),
        ],
        cost(4, near_keys + T),
        pack, *near, weights, out, stat, q_near, g_near, dqt,
    )
    home = swap_y(home)
    via_2 = over_z(d4, -2)
    via_1 = over_z(d3, -1)
    via_m1 = over_z(dm3, 1)
    far = (d2.astype(f32) + via_1.astype(f32) + via_2.astype(f32)).astype(bf16)
    far_m = (dm2.astype(f32) + via_m1.astype(f32)).astype(bf16)
    parts = [over_z(d1, -1), over_z(dm1, 1), over_z(far, -2), over_z(far_m, 2)]
    total = d0.astype(f32)
    for x in parts:
        total = total + x.astype(f32)
    total, home = lax.optimization_barrier((total.astype(bf16), home))
    total = swap_y(total)

    def by_token(x, n):
        x = x.reshape(KH, T, n, D)
        return jnp.transpose(x, (1, 0, 2, 3)).reshape(1, T, KH * n, D)

    attended = by_token(home[:, 0:R], G)
    attended = jnp.where(live, attended, jnp.zeros((), bf16))
    return (
        attended,
        by_token(home[:, R:2 * R], G),
        by_token(home[:, 2 * R:2 * R + T], 1),
        by_token(home[:, 2 * R + T:2 * R + 2 * T], 1),
        jnp.transpose(total[:, 0], (1, 0, 2)),
        jnp.transpose(total[:, 1], (1, 0, 2)),
    )


def solution(mesh):
    split = Mesh(mesh.devices.reshape(8, 8, 4), ("batch", "z", "y"))
    spec = P(("batch", "z", "y"))
    return jax.shard_map(
        on_device,
        mesh=split,
        in_specs=(spec,) * 7,
        out_specs=(spec,) * 6,
        check_vma=False,
    )
```

time: 97 us -> 96.1 us (level)
  waiting for transfers between devices: 28.7 us -> 20 us
  starting transfers between devices: 38.9 us -> 44.3 us
  Pallas kernels: 17.2 us -> 19.5 us
    ppermute x14, waiting for transfers between devices: 23.9 us -> 15.1 us  [over_z(): return lax.ppermute(x, 'z', [(i, (i + k) % 8) for i in range(8)])]
    ppermute x14, starting transfers between devices: 21.8 us -> 27.7 us  [over_z(): return lax.ppermute(x, 'z', [(i, (i + k) % 8) for i in range(8)])]
    pallas_call x1 -> x3, Pallas kernels: 17.2 us -> 19.5 us  [call(): pl.pallas_call(body, out_shape=out_shape, scratch_shapes=scratch, compile...]
  transfers between devices with their start and end apart: 18 -> 18, of which waited for: 11 -> 10; matrix products, arithmetic and copies ran while one was open for 8% -> 8% of each run, Pallas kernels for 0% -> 5%
where the time goes in v2:
time: 96.1 us; the launch traced here: 95.6 us
  starting transfers between devices  44.3 us (46%)
  waiting for transfers between devices  20 us (21%)
  Pallas kernels  19.5 us (20%)
  local copies, waits for them, and re-layouts  6.37 us (7%)
  other arithmetic  3.96 us (4%)
  between operations  1.47 us (2%)
    ppermute x14, starting transfers between devices, over_z(): return lax.ppermute(x, 'z', [(i, (i + k) % 8) for i in range(8)])  27.7 us
    pallas_call x3, Pallas kernels, call(): pl.pallas_call(body, out_shape=out_shape, scratch_shapes=scratch, compile...  19.5 us
    all_to_all x4, starting transfers between devices, swap_y(): return lax.all_to_all(x, 'y', 0, 0, tiled=True)  16.6 us
    ppermute x14, waiting for transfers between devices, over_z(): return lax.ppermute(x, 'z', [(i, (i + k) % 8) for i in range(8)])  15.1 us
    all_to_all x4, waiting for transfers between devices, swap_y(): return lax.all_to_all(x, 'y', 0, 0, tiled=True)  4.88 us
    unnamed x10, local copies, waits for them, and re-layouts  2.89 us
  transfers between devices with their start and end apart: 18, of which 10 were waited for; matrix products, arithmetic and copies ran while one was open for 8% of the time, Pallas kernels for 5%

profile of v2, /device:TPU:4, one launch (start us, length us, event | category | flops | bytes accessed | tf_op | source)
XLA Modules:
  0.0 95.6 jit_solution(7291349971908022837)
XLA Ops:
  0.7 1.0 %copy_bitcast_fusion.2 = (bf16[1,64,4,128]{3,1,0,2:T(8,128)(2,1)S(1)}, bf16[1,64,4,128]{3,1,0,2:T(8,128)(2,1)S(1)}) fusion(bf16[64,4,128]{2,1,0:T(4,128)(2,1)} %param.11, bf16[64,4,128]{2,1,0:T(4,128)(2,1)} %param.10), kind=kLoop, calls=%fused_computation.13 | loop fusion | bytes 262144 | tf_op jit(solution)/shard_map/stack | solution.py:206
  1.6 0.7 maximum_bitcast_fusion
  2.3 4.5 %all-to-all-start = ((bf16[4,2,64,128]{3,2,1,0:T(8,128)(2,1)}), bf16[4,2,64,128]{3,2,1,0:T(8,128)(2,1)S(1)}, u32[]{:S(2)}, u32[]{:S(2)}) async-start(bf16[4,2,64,128]{3,2,1,0:T(8,128)(2,1)} %maximum_bitcast_fusion), calls=%async_computation | async-start | bytes 262144 | tf_op jit(solution)/shard_map/all_to_all | solution.py:204
  7.4 1.2 %copy.15 = bf16[128,4,4,128]{3,2,0,1:T(4,128)(2,1)S(1)} copy(bf16[128,4,4,128]{3,2,1,0:T(4,128)(2,1)} %bitcast.61) | data formatting | bytes 1048576 | tf_op jit(solution)/shard_map/reshape | solution.py:213
  8.7 0.3 copy_select_fusion
  9.0 1.2 %pad_maximum_fusion = bf16[4,1280,128]{2,1,0:T(8,128)(2,1)} fusion(bf16[4,128,128]{2,1,0:T(8,128)(2,1)S(1)} %get-tuple-element.62, bf16[4,128,128]{2,1,0:T(8,128)(2,1)S(1)} %get-tuple-element.63, bf16[4,512,128]{2,1,0:T(8,128)(2,1)S(1)} %bitcast.57, bf16[4,512,128]{2,1,0:T(8,128)(2,1)S(1)} %bitcast.56), kind=kLoop, calls=%fused_computation | loop fusion | flops 5242880 | bytes 2621440 | tf_op jit(solution)/shard_map/concatenate | solution.py:216
  10.2 2.6 %all-to-all-done.kv0 = bf16[4,2,64,128]{3,2,1,0:T(8,128)(2,1)S(1)} async-done(((bf16[4,2,64,128]{3,2,1,0:T(8,128)(2,1)}), bf16[4,2,64,128]{3,2,1,0:T(8,128)(2,1)S(1)}, u32[]{:S(2)}, u32[]{:S(2)}) %all-to-all-start) | async-done | bytes 131104 | tf_op jit(solution)/shard_map/all_to_all | solution.py:204
  12.7 3.5 %all-to-all-start.1 = ((bf16[4,1280,128]{2,1,0:T(8,128)(2,1)}), bf16[4,1280,128]{2,1,0:T(8,128)(2,1)S(1)}, u32[]{:S(2)}, u32[]{:S(2)}) async-start(bf16[4,1280,128]{2,1,0:T(8,128)(2,1)} %pad_maximum_fusion), calls=%async_computation.1 | async-start | bytes 2621440 | tf_op jit(solution)/shard_map/all_to_all | solution.py:204
  16.3 3.3 %collective-permute-start.2 = (bf16[4,2,64,128]{3,2,1,0:T(8,128)(2,1)S(1)}, bf16[4,2,64,128]{3,2,1,0:T(8,128)(2,1)S(1)}, u32[]{:S(2)}, u32[]{:S(2)}) collective-permute-start(bf16[4,2,64,128]{3,2,1,0:T(8,128)(2,1)S(1)} %all-to-all-done.kv0), channel_id=1, source_target_pairs={{0,8},{4,12},{8,16},{12,20},{16,24},{20,28},{24,0},{28,4},{1,9},{5... | collective-permute-start | bytes 393224 | tf_op jit(solution)/shard_map/ppermute | solution.py:201
  19.6 3.1 %collective-permute-start.3 = (bf16[4,2,64,128]{3,2,1,0:T(8,128)(2,1)S(1)}, bf16[4,2,64,128]{3,2,1,0:T(8,128)(2,1)S(1)}, u32[]{:S(2)}, u32[]{:S(2)}) collective-permute-start(bf16[4,2,64,128]{3,2,1,0:T(8,128)(2,1)S(1)} %all-to-all-done.kv0), channel_id=1, source_target_pairs={{0,24},{4,28},{8,0},{12,4},{16,8},{20,12},{24,16},{28,20},{1,25},{... | collective-permute-start | bytes 393224 | tf_op jit(solution)/shard_map/ppermute | solution.py:201
  22.8 2.4 %collective-permute-start.1 = (bf16[4,2,64,128]{3,2,1,0:T(8,128)(2,1)S(1)}, bf16[4,2,64,128]{3,2,1,0:T(8,128)(2,1)S(1)}, u32[]{:S(2)}, u32[]{:S(2)}) collective-permute-start(bf16[4,2,64,128]{3,2,1,0:T(8,128)(2,1)S(1)} %all-to-all-done.kv0), channel_id=1, source_target_pairs={{0,28},{4,0},{8,4},{12,8},{16,12},{20,16},{24,20},{28,24},{1,29},{... | collective-permute-start | bytes 393224 | tf_op jit(solution)/shard_map/ppermute | solution.py:201
  25.1 1.9 %collective-permute-done.2.kv3 = bf16[4,2,64,128]{3,2,1,0:T(8,128)(2,1)S(1)} collective-permute-done((bf16[4,2,64,128]{3,2,1,0:T(8,128)(2,1)S(1)}, bf16[4,2,64,128]{3,2,1,0:T(8,128)(2,1)S(1)}, u32[]{:S(2)}, u32[]{:S(2)}) %collective-permute-start.2) | collective-permute-done | bytes 131104 | tf_op jit(solution)/shard_map/ppermute | solution.py:201
  27.0 1.9 %collective-permute-start.6 = (bf16[4,2,64,128]{3,2,1,0:T(8,128)(2,1)S(1)}, bf16[4,2,64,128]{3,2,1,0:T(8,128)(2,1)S(1)}, u32[]{:S(2)}, u32[]{:S(2)}) collective-permute-start(bf16[4,2,64,128]{3,2,1,0:T(8,128)(2,1)S(1)} %collective-permute-done.2.kv3), channel_id=1, source_target_pairs={{0,8},{4,12},{8,16},{12,20},{16,24},{20,28},{24,0},{28,4},{1,9},{5... | collective-permute-start | bytes 393224 | tf_op jit(solution)/shard_map/ppermute | solution.py:201
  28.9 1.0 %collective-permute-start.4 = (bf16[4,2,64,128]{3,2,1,0:T(8,128)(2,1)S(1)}, bf16[4,2,64,128]{3,2,1,0:T(8,128)(2,1)S(1)}, u32[]{:S(2)}, u32[]{:S(2)}) collective-permute-start(bf16[4,2,64,128]{3,2,1,0:T(8,128)(2,1)S(1)} %collective-permute-done.2.kv3), channel_id=1, source_target_pairs={{0,4},{4,8},{8,12},{12,16},{16,20},{20,24},{24,28},{28,0},{1,5},{5... | collective-permute-start | bytes 393224 | tf_op jit(solution)/shard_map/ppermute | solution.py:201
  30.0 0.0 collective-permute-done.3.kv4
  30.0 2.2 %collective-permute-start.5 = (bf16[4,2,64,128]{3,2,1,0:T(8,128)(2,1)S(1)}, bf16[4,2,64,128]{3,2,1,0:T(8,128)(2,1)S(1)}, u32[]{:S(2)}, u32[]{:S(2)}) collective-permute-start(bf16[4,2,64,128]{3,2,1,0:T(8,128)(2,1)S(1)} %collective-permute-done.3.kv4), channel_id=1, source_target_pairs={{0,28},{4,0},{8,4},{12,8},{16,12},{20,16},{24,20},{28,24},{1,29},{... | collective-permute-start | bytes 393224 | tf_op jit(solution)/shard_map/ppermute | solution.py:201
  32.2 0.0 collective-permute-done.1.kv2
  32.2 0.7 collective-permute-done.kv1
  32.9 0.1 all-to-all-done.1.pack
  33.0 5.1 %near_forward.1 = (bf16[1408,2048]{1,0:T(8,128)(2,1)S(1)}, f32[144,2048]{1,0:T(8,128)S(1)}, f32[8,2048]{1,0:T(8,128)S(1)}) custom-call(bf16[4,1280,128]{2,1,0:T(8,128)(2,1)S(1)} %all-to-all-done.1.pack, bf16[4,2,64,128]{3,2,1,0:T(8,128)(2,1)S(1)} %all-to-all-done.kv0, bf16[4,2,64,128]{3,2,1,0:T(8,128)(2,1)S(1)} %collective-permute-done.kv1, ...), custom_call_target="tpu_custom_call" | custom-call | flops 1476395008 | bytes 4194304 | tf_op jit(solution)/shard_map/near_forward/pallas_call | solution.py:182
  38.1 0.0 collective-permute-done.5.kv1
  38.1 1.1 %collective-permute-done.4.kv0 = bf16[4,2,64,128]{3,2,1,0:T(8,128)(2,1)S(1)} collective-permute-done((bf16[4,2,64,128]{3,2,1,0:T(8,128)(2,1)S(1)}, bf16[4,2,64,128]{3,2,1,0:T(8,128)(2,1)S(1)}, u32[]{:S(2)}, u32[]{:S(2)}) %collective-permute-start.4) | collective-permute-done | bytes 131104 | tf_op jit(solution)/shard_map/ppermute | solution.py:201
  39.2 6.4 %far_both.1 = (bf16[4,512,128]{2,1,0:T(8,128)(2,1)S(1)}, f32[8,2048]{1,0:T(8,128)S(1)}, bf16[2048,128]{1,0:T(8,128)(2,1)S(1)}, bf16[2048,128]{1,0:T(8,128)(2,1)S...) custom-call(bf16[4,1280,128]{2,1,0:T(8,128)(2,1)S(1)} %all-to-all-do, ...), custom_call_target="tpu_custom_call" | custom-call | flops 2415919104 | bytes 4194304 | tf_op jit(solution)/shard_map/far_both/pallas_call | solution.py:182
  45.6 8.0 %near_backward.1 = (bf16[4,1280,128]{2,1,0:T(8,128)(2,1)}, bf16[4,2,64,128]{3,2,1,0:T(8,128)(2,1)S(1)}, bf16[4,2,64,128]{3,2,1,0:T(8,128)(2,1)S(1)}, bf16[4,2,64...) custom-call(bf16[4,1280,128]{2,1,0:T(8,128)(2,1)S(1)} %all-to-all-done.1.pack, ...), custom_call_target="tpu_custom_call" | custom-call | flops 2952790016 | bytes 4194304 | tf_op jit(solution)/shard_map/near_backward/pallas_call | solution.py:182
  53.6 4.3 %all-to-all-start.2 = ((bf16[4,1280,128]{2,1,0:T(8,128)(2,1)}), bf16[4,1280,128]{2,1,0:T(8,128)(2,1)S(1)}, u32[]{:S(2)}, u32[]{:S(2)}) async-start(bf16[4,1280,128]{2,1,0:T(8,128)(2,1)} %get-tuple-element.45), calls=%async_computation.2 | async-start | bytes 2621440 | tf_op jit(solution)/shard_map/all_to_all | solution.py:204
  57.9 4.1 %collective-permute-start.9 = (bf16[4,2,64,128]{3,2,1,0:T(8,128)(2,1)S(1)}, bf16[4,2,64,128]{3,2,1,0:T(8,128)(2,1)S(1)}, u32[]{:S(2)}, u32[]{:S(2)}) collective-permute-start(bf16[4,2,64,128]{3,2,1,0:T(8,128)(2,1)S(1)} %get-tuple-element.41), channel_id=1, source_target_pairs={{0,28},{4,0},{8,4},{12,8},{16,12},{20,16},{24,20},{28,24},{1,29},{... | collective-permute-start | bytes 393224 | tf_op jit(solution)/shard_map/ppermute | solution.py:201
  62.0 1.4 %collective-permute-start.10 = (bf16[4,2,64,128]{3,2,1,0:T(8,128)(2,1)S(1)}, bf16[4,2,64,128]{3,2,1,0:T(8,128)(2,1)S(1)}, u32[]{:S(2)}, u32[]{:S(2)}) collective-permute-start(bf16[4,2,64,128]{3,2,1,0:T(8,128)(2,1)S(1)} %get-tuple-element.42), channel_id=1, source_target_pairs={{0,24},{4,28},{8,0},{12,4},{16,8},{20,12},{24,16},{28,20},{1,25},{... | collective-permute-start | bytes 393224 | tf_op jit(solution)/shard_map/ppermute | solution.py:201
  63.4 1.0 %collective-permute-start.7 = (bf16[4,2,64,128]{3,2,1,0:T(8,128)(2,1)S(1)}, bf16[4,2,64,128]{3,2,1,0:T(8,128)(2,1)S(1)}, u32[]{:S(2)}, u32[]{:S(2)}) collective-permute-start(bf16[4,2,64,128]{3,2,1,0:T(8,128)(2,1)S(1)} %get-tuple-element.38), channel_id=1, source_target_pairs={{0,28},{4,0},{8,4},{12,8},{16,12},{20,16},{24,20},{28,24},{1,29},{... | collective-permute-start | bytes 393224 | tf_op jit(solution)/shard_map/ppermute | solution.py:201
  64.4 1.0 %collective-permute-start.8 = (bf16[4,2,64,128]{3,2,1,0:T(8,128)(2,1)S(1)}, bf16[4,2,64,128]{3,2,1,0:T(8,128)(2,1)S(1)}, u32[]{:S(2)}, u32[]{:S(2)}) collective-permute-start(bf16[4,2,64,128]{3,2,1,0:T(8,128)(2,1)S(1)} %get-tuple-element.39), channel_id=1, source_target_pairs={{0,4},{4,8},{8,12},{12,16},{16,20},{20,24},{24,28},{28,0},{1,5},{5... | collective-permute-start | bytes 393224 | tf_op jit(solution)/shard_map/ppermute | solution.py:201
  65.5 1.0 %collective-permute-start.12 = (bf16[4,2,64,128]{3,2,1,0:T(8,128)(2,1)S(1)}, bf16[4,2,64,128]{3,2,1,0:T(8,128)(2,1)S(1)}, u32[]{:S(2)}, u32[]{:S(2)}) collective-permute-start(bf16[4,2,64,128]{3,2,1,0:T(8,128)(2,1)S(1)} %get-tuple-element.44), channel_id=1, source_target_pairs={{0,4},{4,8},{8,12},{12,16},{16,20},{20,24},{24,28},{28,0},{1,5},{5... | collective-permute-start | bytes 393224 | tf_op jit(solution)/shard_map/ppermute | solution.py:201
  66.5 0.7 collective-permute-done.9
  67.2 3.8 %collective-permute-done.10 = bf16[4,2,64,128]{3,2,1,0:T(8,128)(2,1)S(1)} collective-permute-done((bf16[4,2,64,128]{3,2,1,0:T(8,128)(2,1)S(1)}, bf16[4,2,64,128]{3,2,1,0:T(8,128)(2,1)S(1)}, u32[]{:S(2)}, u32[]{:S(2)}) %collective-permute-start.10) | collective-permute-done | bytes 131104 | tf_op jit(solution)/shard_map/ppermute | solution.py:201
  70.9 0.1 add_convert_fusion.2
  71.0 5.0 %collective-permute-start.11 = (bf16[4,2,64,128]{3,2,1,0:T(8,128)(2,1)S(1)}, bf16[4,2,64,128]{3,2,1,0:T(8,128)(2,1)S(1)}, u32[]{:S(2)}, u32[]{:S(2)}) collective-permute-start(bf16[4,2,64,128]{3,2,1,0:T(8,128)(2,1)S(1)} %add_convert_fusion.2), channel_id=1, source_target_pairs={{0,24},{4,28},{8,0},{12,4},{16,8},{20,12},{24,16},{28,20},{1,25},{... | collective-permute-start | bytes 393224 | tf_op jit(solution)/shard_map/ppermute | solution.py:201
  76.0 0.1 collective-permute-start.13
  76.2 3.5 %collective-permute-done.11 = bf16[4,2,64,128]{3,2,1,0:T(8,128)(2,1)S(1)} collective-permute-done((bf16[4,2,64,128]{3,2,1,0:T(8,128)(2,1)S(1)}, bf16[4,2,64,128]{3,2,1,0:T(8,128)(2,1)S(1)}, u32[]{:S(2)}, u32[]{:S(2)}) %collective-permute-start.11) | collective-permute-done | bytes 131104 | tf_op jit(solution)/shard_map/ppermute | solution.py:201
  79.6 3.6 %collective-permute-done.13 = bf16[4,2,64,128]{3,2,1,0:T(8,128)(2,1)S(1)} collective-permute-done((bf16[4,2,64,128]{3,2,1,0:T(8,128)(2,1)S(1)}, bf16[4,2,64,128]{3,2,1,0:T(8,128)(2,1)S(1)}, u32[]{:S(2)}, u32[]{:S(2)}) %collective-permute-start.13) | collective-permute-done | bytes 131104 | tf_op jit(solution)/shard_map/ppermute | solution.py:201
  83.2 0.7 add_convert_fusion
  83.9 4.3 %all-to-all-start.3 = ((bf16[4,2,64,128]{3,2,1,0:T(8,128)(2,1)}), bf16[4,2,64,128]{3,2,1,0:T(8,128)(2,1)S(1)}, u32[]{:S(2)}, u32[]{:S(2)}) async-start(bf16[4,2,64,128]{3,2,1,0:T(8,128)(2,1)} %add_convert_fusion), calls=%async_computation.3 | async-start | bytes 262144 | tf_op jit(solution)/shard_map/all_to_all | solution.py:204
  88.2 0.1 fusion
  88.3 0.2 copy.19
  88.5 1.0 %broadcast_select_fusion = bf16[1,128,16,128]{3,2,1,0:T(8,128)(2,1)} fusion(bf16[1,128,16,128]{3,2,1,0:T(8,128)(2,1)S(1)} %bitcast.58, pred[128]{0:T(512)(128)(4,1)S(1)} %iota_compare_fusion), kind=kLoop, calls=%fused_computation.2 | loop fusion | flops 262144 | bytes 1048704 | tf_op jit(solution)/shard_map/jit(_where)/select_n | solution.py:321
  89.5 1.0 %copy.20 = bf16[128,4,4,128]{3,2,1,0:T(4,128)(2,1)} copy(bf16[128,4,4,128]{3,2,0,1:T(4,128)(2,1)S(1)} %bitcast.59) | data formatting | bytes 1048576 | tf_op jit(solution)/shard_map/transpose | solution.py:318
  90.5 0.8 copy.22
  91.2 0.8 copy.21
  92.0 2.2 %all-to-all-done.3 = bf16[4,2,64,128]{3,2,1,0:T(8,128)(2,1)S(1)} async-done(((bf16[4,2,64,128]{3,2,1,0:T(8,128)(2,1)}), bf16[4,2,64,128]{3,2,1,0:T(8,128)(2,1)S(1)}, u32[]{:S(2)}, u32[]{:S(2)}) %all-to-all-start.3) | async-done | bytes 131104 | tf_op jit(solution)/shard_map/all_to_all | solution.py:204
  94.2 0.7 copy.24
  94.9 0.7 copy.23
  (17 shorter events, 0.1 us)
Async XLA Ops:
  0.6 8.0 %copy-start.1 = (bf16[1,128,4,128]{3,2,1,0:T(4,128)(2,1)S(1)}, bf16[1,128,4,128]{3,2,1,0:T(4,128)(2,1)}, u32[]{:S(2)}) copy-start(bf16[1,128,4,128]{3,2,1,0:T(4,128)(2,1)} %param.9) | copy-start | bytes 393220
  0.6 8.0 %copy-start.2 = (bf16[1,128,4,128]{3,2,1,0:T(4,128)(2,1)S(1)}, bf16[1,128,4,128]{3,2,1,0:T(4,128)(2,1)}, u32[]{:S(2)}) copy-start(bf16[1,128,4,128]{3,2,1,0:T(4,128)(2,1)} %param.8) | copy-start | bytes 393220
  0.7 8.1 %copy-start = (bf16[1,128,16,128]{3,2,1,0:T(8,128)(2,1)S(1)}, bf16[1,128,16,128]{3,2,1,0:T(8,128)(2,1)}, u32[]{:S(2)}) copy-start(bf16[1,128,16,128]{3,2,1,0:T(8,128)(2,1)} %param.13) | copy-start | bytes 1572868
  2.3 10.4 %all-to-all-start = ((bf16[4,2,64,128]{3,2,1,0:T(8,128)(2,1)}), bf16[4,2,64,128]{3,2,1,0:T(8,128)(2,1)S(1)}, u32[]{:S(2)}, u32[]{:S(2)}) async-start(bf16[4,2,64,128]{3,2,1,0:T(8,128)(2,1)} %maximum_bitcast_fusion), calls=%async_computation | async-start | bytes 262144 | tf_op jit(solution)/shard_map/all_to_all | solution.py:204
  12.7 20.3 %all-to-all-start.1 = ((bf16[4,1280,128]{2,1,0:T(8,128)(2,1)}), bf16[4,1280,128]{2,1,0:T(8,128)(2,1)S(1)}, u32[]{:S(2)}, u32[]{:S(2)}) async-start(bf16[4,1280,128]{2,1,0:T(8,128)(2,1)} %pad_maximum_fusion), calls=%async_computation.1 | async-start | bytes 2621440 | tf_op jit(solution)/shard_map/all_to_all | solution.py:204
  16.3 10.7 %collective-permute-start.2 = (bf16[4,2,64,128]{3,2,1,0:T(8,128)(2,1)S(1)}, bf16[4,2,64,128]{3,2,1,0:T(8,128)(2,1)S(1)}, u32[]{:S(2)}, u32[]{:S(2)}) collective-permute-start(bf16[4,2,64,128]{3,2,1,0:T(8,128)(2,1)S(1)} %all-to-all-done.kv0), channel_id=1, source_target_pairs={{0,8},{4,12},{8,16},{12,20},{16,24},{20,28},{24,0},{28,4},{1,9},{5... | collective-permute-start | bytes 393224 | tf_op jit(solution)/shard_map/ppermute | solution.py:201
  19.6 10.3 %collective-permute-start.3 = (bf16[4,2,64,128]{3,2,1,0:T(8,128)(2,1)S(1)}, bf16[4,2,64,128]{3,2,1,0:T(8,128)(2,1)S(1)}, u32[]{:S(2)}, u32[]{:S(2)}) collective-permute-start(bf16[4,2,64,128]{3,2,1,0:T(8,128)(2,1)S(1)} %all-to-all-done.kv0), channel_id=1, source_target_pairs={{0,24},{4,28},{8,0},{12,4},{16,8},{20,12},{24,16},{28,20},{1,25},{... | collective-permute-start | bytes 393224 | tf_op jit(solution)/shard_map/ppermute | solution.py:201
  22.8 9.5 %collective-permute-start.1 = (bf16[4,2,64,128]{3,2,1,0:T(8,128)(2,1)S(1)}, bf16[4,2,64,128]{3,2,1,0:T(8,128)(2,1)S(1)}, u32[]{:S(2)}, u32[]{:S(2)}) collective-permute-start(bf16[4,2,64,128]{3,2,1,0:T(8,128)(2,1)S(1)} %all-to-all-done.kv0), channel_id=1, source_target_pairs={{0,28},{4,0},{8,4},{12,8},{16,12},{20,16},{24,20},{28,24},{1,29},{... | collective-permute-start | bytes 393224 | tf_op jit(solution)/shard_map/ppermute | solution.py:201
  25.1 7.7 %collective-permute-start = (bf16[4,2,64,128]{3,2,1,0:T(8,128)(2,1)S(1)}, bf16[4,2,64,128]{3,2,1,0:T(8,128)(2,1)S(1)}, u32[]{:S(2)}, u32[]{:S(2)}) collective-permute-start(bf16[4,2,64,128]{3,2,1,0:T(8,128)(2,1)S(1)} %all-to-all-done.kv0), channel_id=1, source_target_pairs={{0,4},{4,8},{8,12},{12,16},{16,20},{20,24},{24,28},{28,0},{1,5},{5... | collective-permute-start | bytes 393224 | tf_op jit(solution)/shard_map/ppermute | solution.py:201
  27.0 11.1 %collective-permute-start.6 = (bf16[4,2,64,128]{3,2,1,0:T(8,128)(2,1)S(1)}, bf16[4,2,64,128]{3,2,1,0:T(8,128)(2,1)S(1)}, u32[]{:S(2)}, u32[]{:S(2)}) collective-permute-start(bf16[4,2,64,128]{3,2,1,0:T(8,128)(2,1)S(1)} %collective-permute-done.2.kv3), channel_id=1, source_target_pairs={{0,8},{4,12},{8,16},{12,20},{16,24},{20,28},{24,0},{28,4},{1,9},{5... | collective-permute-start | bytes 393224 | tf_op jit(solution)/shard_map/ppermute | solution.py:201
  28.9 10.2 %collective-permute-start.4 = (bf16[4,2,64,128]{3,2,1,0:T(8,128)(2,1)S(1)}, bf16[4,2,64,128]{3,2,1,0:T(8,128)(2,1)S(1)}, u32[]{:S(2)}, u32[]{:S(2)}) collective-permute-start(bf16[4,2,64,128]{3,2,1,0:T(8,128)(2,1)S(1)} %collective-permute-done.2.kv3), channel_id=1, source_target_pairs={{0,4},{4,8},{8,12},{12,16},{16,20},{20,24},{24,28},{28,0},{1,5},{5... | collective-permute-start | bytes 393224 | tf_op jit(solution)/shard_map/ppermute | solution.py:201
  30.0 8.1 %collective-permute-start.5 = (bf16[4,2,64,128]{3,2,1,0:T(8,128)(2,1)S(1)}, bf16[4,2,64,128]{3,2,1,0:T(8,128)(2,1)S(1)}, u32[]{:S(2)}, u32[]{:S(2)}) collective-permute-start(bf16[4,2,64,128]{3,2,1,0:T(8,128)(2,1)S(1)} %collective-permute-done.3.kv4), channel_id=1, source_target_pairs={{0,28},{4,0},{8,4},{12,8},{16,12},{20,16},{24,20},{28,24},{1,29},{... | collective-permute-start | bytes 393224 | tf_op jit(solution)/shard_map/ppermute | solution.py:201
  53.6 30.4 %all-to-all-start.2 = ((bf16[4,1280,128]{2,1,0:T(8,128)(2,1)}), bf16[4,1280,128]{2,1,0:T(8,128)(2,1)S(1)}, u32[]{:S(2)}, u32[]{:S(2)}) async-start(bf16[4,1280,128]{2,1,0:T(8,128)(2,1)} %get-tuple-element.45), calls=%async_computation.2 | async-start | bytes 2621440 | tf_op jit(solution)/shard_map/all_to_all | solution.py:204
  57.9 9.3 %collective-permute-start.9 = (bf16[4,2,64,128]{3,2,1,0:T(8,128)(2,1)S(1)}, bf16[4,2,64,128]{3,2,1,0:T(8,128)(2,1)S(1)}, u32[]{:S(2)}, u32[]{:S(2)}) collective-permute-start(bf16[4,2,64,128]{3,2,1,0:T(8,128)(2,1)S(1)} %get-tuple-element.41), channel_id=1, source_target_pairs={{0,28},{4,0},{8,4},{12,8},{16,12},{20,16},{24,20},{28,24},{1,29},{... | collective-permute-start | bytes 393224 | tf_op jit(solution)/shard_map/ppermute | solution.py:201
  62.0 8.9 %collective-permute-start.10 = (bf16[4,2,64,128]{3,2,1,0:T(8,128)(2,1)S(1)}, bf16[4,2,64,128]{3,2,1,0:T(8,128)(2,1)S(1)}, u32[]{:S(2)}, u32[]{:S(2)}) collective-permute-start(bf16[4,2,64,128]{3,2,1,0:T(8,128)(2,1)S(1)} %get-tuple-element.42), channel_id=1, source_target_pairs={{0,24},{4,28},{8,0},{12,4},{16,8},{20,12},{24,16},{28,20},{1,25},{... | collective-permute-start | bytes 393224 | tf_op jit(solution)/shard_map/ppermute | solution.py:201
  63.4 12.7 %collective-permute-start.7 = (bf16[4,2,64,128]{3,2,1,0:T(8,128)(2,1)S(1)}, bf16[4,2,64,128]{3,2,1,0:T(8,128)(2,1)S(1)}, u32[]{:S(2)}, u32[]{:S(2)}) collective-permute-start(bf16[4,2,64,128]{3,2,1,0:T(8,128)(2,1)S(1)} %get-tuple-element.38), channel_id=1, source_target_pairs={{0,28},{4,0},{8,4},{12,8},{16,12},{20,16},{24,20},{28,24},{1,29},{... | collective-permute-start | bytes 393224 | tf_op jit(solution)/shard_map/ppermute | solution.py:201
  64.4 11.7 %collective-permute-start.8 = (bf16[4,2,64,128]{3,2,1,0:T(8,128)(2,1)S(1)}, bf16[4,2,64,128]{3,2,1,0:T(8,128)(2,1)S(1)}, u32[]{:S(2)}, u32[]{:S(2)}) collective-permute-start(bf16[4,2,64,128]{3,2,1,0:T(8,128)(2,1)S(1)} %get-tuple-element.39), channel_id=1, source_target_pairs={{0,4},{4,8},{8,12},{12,16},{16,20},{20,24},{24,28},{28,0},{1,5},{5... | collective-permute-start | bytes 393224 | tf_op jit(solution)/shard_map/ppermute | solution.py:201
  65.5 10.5 %collective-permute-start.12 = (bf16[4,2,64,128]{3,2,1,0:T(8,128)(2,1)S(1)}, bf16[4,2,64,128]{3,2,1,0:T(8,128)(2,1)S(1)}, u32[]{:S(2)}, u32[]{:S(2)}) collective-permute-start(bf16[4,2,64,128]{3,2,1,0:T(8,128)(2,1)S(1)} %get-tuple-element.44), channel_id=1, source_target_pairs={{0,4},{4,8},{8,12},{12,16},{16,20},{20,24},{24,28},{28,0},{1,5},{5... | collective-permute-start | bytes 393224 | tf_op jit(solution)/shard_map/ppermute | solution.py:201
  71.0 8.7 %collective-permute-start.11 = (bf16[4,2,64,128]{3,2,1,0:T(8,128)(2,1)S(1)}, bf16[4,2,64,128]{3,2,1,0:T(8,128)(2,1)S(1)}, u32[]{:S(2)}, u32[]{:S(2)}) collective-permute-start(bf16[4,2,64,128]{3,2,1,0:T(8,128)(2,1)S(1)} %add_convert_fusion.2), channel_id=1, source_target_pairs={{0,24},{4,28},{8,0},{12,4},{16,8},{20,12},{24,16},{28,20},{1,25},{... | collective-permute-start | bytes 393224 | tf_op jit(solution)/shard_map/ppermute | solution.py:201
  76.0 7.2 %collective-permute-start.13 = (bf16[4,2,64,128]{3,2,1,0:T(8,128)(2,1)S(1)}, bf16[4,2,64,128]{3,2,1,0:T(8,128)(2,1)S(1)}, u32[]{:S(2)}, u32[]{:S(2)}) collective-permute-start(bf16[4,2,64,128]{3,2,1,0:T(8,128)(2,1)S(1)} %add_convert_fusion.1), channel_id=1, source_target_pairs={{0,8},{4,12},{8,16},{12,20},{16,24},{20,28},{24,0},{28,4},{1,9},{5... | collective-permute-start | bytes 393224 | tf_op jit(solution)/shard_map/ppermute | solution.py:201
  83.9 10.2 %all-to-all-start.3 = ((bf16[4,2,64,128]{3,2,1,0:T(8,128)(2,1)}), bf16[4,2,64,128]{3,2,1,0:T(8,128)(2,1)S(1)}, u32[]{:S(2)}, u32[]{:S(2)}) async-start(bf16[4,2,64,128]{3,2,1,0:T(8,128)(2,1)} %add_convert_fusion), calls=%async_computation.3 | async-start | bytes 262144 | tf_op jit(solution)/shard_map/all_to_all | solution.py:204

commit v3 on v2

--- a/solution.py
+++ b/solution.py
@@ -300,10 +300,13 @@
         cost(4, near_keys + T),
         pack, *near, weights, out, stat, q_near, g_near, dqt,
     )
-    home = swap_y(home)
     via_2 = over_z(d4, -2)
     via_1 = over_z(d3, -1)
     via_m1 = over_z(dm3, 1)
+    (via_2, via_1, via_m1, home, d1, dm1, d2, dm2) = lax.optimization_barrier(
+        (via_2, via_1, via_m1, home, d1, dm1, d2, dm2)
+    )
+    home = swap_y(home)
     far = (d2.astype(f32) + via_1.astype(f32) + via_2.astype(f32)).astype(bf16)
     far_m = (dm2.astype(f32) + via_m1.astype(f32)).astype(bf16)
     parts = [over_z(d1, -1), over_z(dm1, 1), over_z(far, -2), over_z(far_m, 2)]

time: 96.1 us -> 90.4 us (0.941)
  waiting for transfers between devices: 20 us -> 16.2 us
  starting transfers between devices: 44.3 us -> 42.6 us
    ppermute x14, waiting for transfers between devices: 15.1 us -> 8.76 us  [over_z(): return lax.ppermute(x, 'z', [(i, (i + k) % 8) for i in range(8)])]
    all_to_all x4, waiting for transfers between devices: 4.88 us -> 7.48 us  [swap_y(): return lax.all_to_all(x, 'y', 0, 0, tiled=True)]
    all_to_all x4, starting transfers between devices: 16.6 us -> 14.9 us  [swap_y(): return lax.all_to_all(x, 'y', 0, 0, tiled=True)]
  transfers between devices with their start and end apart: 18 -> 18, of which waited for: 10 -> 10; matrix products, arithmetic and copies ran while one was open for 8% -> 8% of each run, Pallas kernels for 5% -> 14%
where the time goes in v3:
time: 90.4 us; the launch traced here: 89.8 us
  starting transfers between devices  42.6 us (47%)
  Pallas kernels  19.2 us (21%)
  waiting for transfers between devices  16.2 us (18%)
  local copies, waits for them, and re-layouts  6.37 us (7%)
  other arithmetic  3.96 us (4%)
  between operations  1.47 us (2%)
    ppermute x14, starting transfers between devices, over_z(): return lax.ppermute(x, 'z', [(i, (i + k) % 8) for i in range(8)])  27.7 us
    pallas_call x3, Pallas kernels, call(): pl.pallas_call(body, out_shape=out_shape, scratch_shapes=scratch, compile...  19.2 us
    all_to_all x4, starting transfers between devices, swap_y(): return lax.all_to_all(x, 'y', 0, 0, tiled=True)  14.9 us
    ppermute x14, waiting for transfers between devices, over_z(): return lax.ppermute(x, 'z', [(i, (i + k) % 8) for i in range(8)])  8.76 us
    all_to_all x4, waiting for transfers between devices, swap_y(): return lax.all_to_all(x, 'y', 0, 0, tiled=True)  7.48 us
    unnamed x10, local copies, waits for them, and re-layouts  2.89 us
  transfers between devices with their start and end apart: 18, of which 10 were waited for; matrix products, arithmetic and copies ran while one was open for 8% of the time, Pallas kernels for 14%

profile of v3, /device:TPU:4, one launch (start us, length us, event | category | flops | bytes accessed | tf_op | source)
XLA Modules:
  0.0 89.8 jit_solution(104940156449612656)
XLA Ops:
  0.7 1.0 %copy_bitcast_fusion.2 = (bf16[1,64,4,128]{3,1,0,2:T(8,128)(2,1)S(1)}, bf16[1,64,4,128]{3,1,0,2:T(8,128)(2,1)S(1)}) fusion(bf16[64,4,128]{2,1,0:T(4,128)(2,1)} %param.11, bf16[64,4,128]{2,1,0:T(4,128)(2,1)} %param.10), kind=kLoop, calls=%fused_computation.13 | loop fusion | bytes 262144 | tf_op jit(solution)/shard_map/stack | solution.py:206
  1.6 0.7 maximum_bitcast_fusion
  2.3 4.5 %all-to-all-start = ((bf16[4,2,64,128]{3,2,1,0:T(8,128)(2,1)}), bf16[4,2,64,128]{3,2,1,0:T(8,128)(2,1)S(1)}, u32[]{:S(2)}, u32[]{:S(2)}) async-start(bf16[4,2,64,128]{3,2,1,0:T(8,128)(2,1)} %maximum_bitcast_fusion), calls=%async_computation | async-start | bytes 262144 | tf_op jit(solution)/shard_map/all_to_all | solution.py:204
  7.4 1.2 %copy.15 = bf16[128,4,4,128]{3,2,0,1:T(4,128)(2,1)S(1)} copy(bf16[128,4,4,128]{3,2,1,0:T(4,128)(2,1)} %bitcast.61) | data formatting | bytes 1048576 | tf_op jit(solution)/shard_map/reshape | solution.py:213
  8.7 0.3 copy_select_fusion
  9.0 1.2 %pad_maximum_fusion = bf16[4,1280,128]{2,1,0:T(8,128)(2,1)} fusion(bf16[4,128,128]{2,1,0:T(8,128)(2,1)S(1)} %get-tuple-element.78, bf16[4,128,128]{2,1,0:T(8,128)(2,1)S(1)} %get-tuple-element.79, bf16[4,512,128]{2,1,0:T(8,128)(2,1)S(1)} %bitcast.57, bf16[4,512,128]{2,1,0:T(8,128)(2,1)S(1)} %bitcast.56), kind=kLoop, calls=%fused_computation | loop fusion | flops 5242880 | bytes 2621440 | tf_op jit(solution)/shard_map/concatenate | solution.py:216
  10.2 2.6 %all-to-all-done.kv0 = bf16[4,2,64,128]{3,2,1,0:T(8,128)(2,1)S(1)} async-done(((bf16[4,2,64,128]{3,2,1,0:T(8,128)(2,1)}), bf16[4,2,64,128]{3,2,1,0:T(8,128)(2,1)S(1)}, u32[]{:S(2)}, u32[]{:S(2)}) %all-to-all-start) | async-done | bytes 131104 | tf_op jit(solution)/shard_map/all_to_all | solution.py:204
  12.7 3.5 %all-to-all-start.1 = ((bf16[4,1280,128]{2,1,0:T(8,128)(2,1)}), bf16[4,1280,128]{2,1,0:T(8,128)(2,1)S(1)}, u32[]{:S(2)}, u32[]{:S(2)}) async-start(bf16[4,1280,128]{2,1,0:T(8,128)(2,1)} %pad_maximum_fusion), calls=%async_computation.1 | async-start | bytes 2621440 | tf_op jit(solution)/shard_map/all_to_all | solution.py:204
  16.3 3.3 %collective-permute-start.2 = (bf16[4,2,64,128]{3,2,1,0:T(8,128)(2,1)S(1)}, bf16[4,2,64,128]{3,2,1,0:T(8,128)(2,1)S(1)}, u32[]{:S(2)}, u32[]{:S(2)}) collective-permute-start(bf16[4,2,64,128]{3,2,1,0:T(8,128)(2,1)S(1)} %all-to-all-done.kv0), channel_id=1, source_target_pairs={{0,8},{4,12},{8,16},{12,20},{16,24},{20,28},{24,0},{28,4},{1,9},{5... | collective-permute-start | bytes 393224 | tf_op jit(solution)/shard_map/ppermute | solution.py:201
  19.6 3.1 %collective-permute-start.3 = (bf16[4,2,64,128]{3,2,1,0:T(8,128)(2,1)S(1)}, bf16[4,2,64,128]{3,2,1,0:T(8,128)(2,1)S(1)}, u32[]{:S(2)}, u32[]{:S(2)}) collective-permute-start(bf16[4,2,64,128]{3,2,1,0:T(8,128)(2,1)S(1)} %all-to-all-done.kv0), channel_id=1, source_target_pairs={{0,24},{4,28},{8,0},{12,4},{16,8},{20,12},{24,16},{28,20},{1,25},{... | collective-permute-start | bytes 393224 | tf_op jit(solution)/shard_map/ppermute | solution.py:201
  22.8 2.4 %collective-permute-start.1 = (bf16[4,2,64,128]{3,2,1,0:T(8,128)(2,1)S(1)}, bf16[4,2,64,128]{3,2,1,0:T(8,128)(2,1)S(1)}, u32[]{:S(2)}, u32[]{:S(2)}) collective-permute-start(bf16[4,2,64,128]{3,2,1,0:T(8,128)(2,1)S(1)} %all-to-all-done.kv0), channel_id=1, source_target_pairs={{0,28},{4,0},{8,4},{12,8},{16,12},{20,16},{24,20},{28,24},{1,29},{... | collective-permute-start | bytes 393224 | tf_op jit(solution)/shard_map/ppermute | solution.py:201
  25.1 0.0 collective-permute-start
  25.1 1.9 %collective-permute-done.2.kv3 = bf16[4,2,64,128]{3,2,1,0:T(8,128)(2,1)S(1)} collective-permute-done((bf16[4,2,64,128]{3,2,1,0:T(8,128)(2,1)S(1)}, bf16[4,2,64,128]{3,2,1,0:T(8,128)(2,1)S(1)}, u32[]{:S(2)}, u32[]{:S(2)}) %collective-permute-start.2) | collective-permute-done | bytes 131104 | tf_op jit(solution)/shard_map/ppermute | solution.py:201
  27.0 1.9 %collective-permute-start.6 = (bf16[4,2,64,128]{3,2,1,0:T(8,128)(2,1)S(1)}, bf16[4,2,64,128]{3,2,1,0:T(8,128)(2,1)S(1)}, u32[]{:S(2)}, u32[]{:S(2)}) collective-permute-start(bf16[4,2,64,128]{3,2,1,0:T(8,128)(2,1)S(1)} %collective-permute-done.2.kv3), channel_id=1, source_target_pairs={{0,8},{4,12},{8,16},{12,20},{16,24},{20,28},{24,0},{28,4},{1,9},{5... | collective-permute-start | bytes 393224 | tf_op jit(solution)/shard_map/ppermute | solution.py:201
  28.9 1.0 %collective-permute-start.4 = (bf16[4,2,64,128]{3,2,1,0:T(8,128)(2,1)S(1)}, bf16[4,2,64,128]{3,2,1,0:T(8,128)(2,1)S(1)}, u32[]{:S(2)}, u32[]{:S(2)}) collective-permute-start(bf16[4,2,64,128]{3,2,1,0:T(8,128)(2,1)S(1)} %collective-permute-done.2.kv3), channel_id=1, source_target_pairs={{0,4},{4,8},{8,12},{12,16},{16,20},{20,24},{24,28},{28,0},{1,5},{5... | collective-permute-start | bytes 393224 | tf_op jit(solution)/shard_map/ppermute | solution.py:201
  30.0 0.0 collective-permute-done.3.kv4
  30.0 2.2 %collective-permute-start.5 = (bf16[4,2,64,128]{3,2,1,0:T(8,128)(2,1)S(1)}, bf16[4,2,64,128]{3,2,1,0:T(8,128)(2,1)S(1)}, u32[]{:S(2)}, u32[]{:S(2)}) collective-permute-start(bf16[4,2,64,128]{3,2,1,0:T(8,128)(2,1)S(1)} %collective-permute-done.3.kv4), channel_id=1, source_target_pairs={{0,28},{4,0},{8,4},{12,8},{16,12},{20,16},{24,20},{28,24},{1,29},{... | collective-permute-start | bytes 393224 | tf_op jit(solution)/shard_map/ppermute | solution.py:201
  32.2 0.0 collective-permute-done.1.kv2
  32.2 0.7 collective-permute-done.kv1
  32.9 0.1 all-to-all-done.1.pack
  33.0 5.1 %near_forward.1 = (bf16[1408,2048]{1,0:T(8,128)(2,1)S(1)}, f32[144,2048]{1,0:T(8,128)S(1)}, f32[8,2048]{1,0:T(8,128)S(1)}) custom-call(bf16[4,1280,128]{2,1,0:T(8,128)(2,1)S(1)} %all-to-all-done.1.pack, bf16[4,2,64,128]{3,2,1,0:T(8,128)(2,1)S(1)} %all-to-all-done.kv0, bf16[4,2,64,128]{3,2,1,0:T(8,128)(2,1)S(1)} %collective-permute-done.kv1, ...), custom_call_target="tpu_custom_call" | custom-call | flops 1476395008 | bytes 4194304 | tf_op jit(solution)/shard_map/near_forward/pallas_call | solution.py:182
  38.1 1.1 %collective-permute-done.4.kv0 = bf16[4,2,64,128]{3,2,1,0:T(8,128)(2,1)S(1)} collective-permute-done((bf16[4,2,64,128]{3,2,1,0:T(8,128)(2,1)S(1)}, bf16[4,2,64,128]{3,2,1,0:T(8,128)(2,1)S(1)}, u32[]{:S(2)}, u32[]{:S(2)}) %collective-permute-start.4) | collective-permute-done | bytes 131104 | tf_op jit(solution)/shard_map/ppermute | solution.py:201
  39.2 6.4 %far_both.1 = (bf16[4,512,128]{2,1,0:T(8,128)(2,1)S(1)}, f32[8,2048]{1,0:T(8,128)S(1)}, bf16[2048,128]{1,0:T(8,128)(2,1)S(1)}, bf16[2048,128]{1,0:T(8,128)(2,1)S...) custom-call(bf16[4,1280,128]{2,1,0:T(8,128)(2,1)S(1)} %all-to-all-do, ...), custom_call_target="tpu_custom_call" | custom-call | flops 2415919104 | bytes 4194304 | tf_op jit(solution)/shard_map/far_both/pallas_call | solution.py:182
  45.6 5.3 %collective-permute-start.7 = (bf16[4,2,64,128]{3,2,1,0:T(8,128)(2,1)S(1)}, bf16[4,2,64,128]{3,2,1,0:T(8,128)(2,1)S(1)}, u32[]{:S(2)}, u32[]{:S(2)}) collective-permute-start(bf16[4,2,64,128]{3,2,1,0:T(8,128)(2,1)S(1)} %get-tuple-element.46), channel_id=1, source_target_pairs={{0,24},{4,28},{8,0},{12,4},{16,8},{20,12},{24,16},{28,20},{1,25},{... | collective-permute-start | bytes 393224 | tf_op jit(solution)/shard_map/ppermute | solution.py:201
  50.9 1.0 %collective-permute-start.8 = (bf16[4,2,64,128]{3,2,1,0:T(8,128)(2,1)S(1)}, bf16[4,2,64,128]{3,2,1,0:T(8,128)(2,1)S(1)}, u32[]{:S(2)}, u32[]{:S(2)}) collective-permute-start(bf16[4,2,64,128]{3,2,1,0:T(8,128)(2,1)S(1)} %get-tuple-element.47), channel_id=1, source_target_pairs={{0,28},{4,0},{8,4},{12,8},{16,12},{20,16},{24,20},{28,24},{1,29},{... | collective-permute-start | bytes 393224 | tf_op jit(solution)/shard_map/ppermute | solution.py:201
  51.9 1.0 %collective-permute-start.9 = (bf16[4,2,64,128]{3,2,1,0:T(8,128)(2,1)S(1)}, bf16[4,2,64,128]{3,2,1,0:T(8,128)(2,1)S(1)}, u32[]{:S(2)}, u32[]{:S(2)}) collective-permute-start(bf16[4,2,64,128]{3,2,1,0:T(8,128)(2,1)S(1)} %get-tuple-element.48), channel_id=1, source_target_pairs={{0,4},{4,8},{8,12},{12,16},{16,20},{20,24},{24,28},{28,0},{1,5},{5... | collective-permute-start | bytes 393224 | tf_op jit(solution)/shard_map/ppermute | solution.py:201
  52.9 7.7 %near_backward.1 = (bf16[4,1280,128]{2,1,0:T(8,128)(2,1)}, bf16[4,2,64,128]{3,2,1,0:T(8,128)(2,1)S(1)}, bf16[4,2,64,128]{3,2,1,0:T(8,128)(2,1)S(1)}, bf16[4,2,64...) custom-call(bf16[4,1280,128]{2,1,0:T(8,128)(2,1)S(1)} %all-to-all-done.1.pack, ...), custom_call_target="tpu_custom_call" | custom-call | flops 2952790016 | bytes 4194304 | tf_op jit(solution)/shard_map/near_backward/pallas_call | solution.py:182
  60.7 3.6 %all-to-all-start.2 = ((bf16[4,1280,128]{2,1,0:T(8,128)(2,1)}), bf16[4,1280,128]{2,1,0:T(8,128)(2,1)S(1)}, u32[]{:S(2)}, u32[]{:S(2)}) async-start(bf16[4,1280,128]{2,1,0:T(8,128)(2,1)} %get-tuple-element.61), calls=%async_computation.2 | async-start | bytes 2621440 | tf_op jit(solution)/shard_map/all_to_all | solution.py:204
  64.3 0.5 collective-permute-start.13
  64.8 0.1 add_convert_fusion.2
  64.9 3.8 %collective-permute-start.12 = (bf16[4,2,64,128]{3,2,1,0:T(8,128)(2,1)S(1)}, bf16[4,2,64,128]{3,2,1,0:T(8,128)(2,1)S(1)}, u32[]{:S(2)}, u32[]{:S(2)}) collective-permute-start(bf16[4,2,64,128]{3,2,1,0:T(8,128)(2,1)S(1)} %add_convert_fusion.2), channel_id=1, source_target_pairs={{0,24},{4,28},{8,0},{12,4},{16,8},{20,12},{24,16},{28,20},{1,25},{... | collective-permute-start | bytes 393224 | tf_op jit(solution)/shard_map/ppermute | solution.py:201
  68.6 1.0 %collective-permute-start.10 = (bf16[4,2,64,128]{3,2,1,0:T(8,128)(2,1)S(1)}, bf16[4,2,64,128]{3,2,1,0:T(8,128)(2,1)S(1)}, u32[]{:S(2)}, u32[]{:S(2)}) collective-permute-start(bf16[4,2,64,128]{3,2,1,0:T(8,128)(2,1)S(1)} %get-tuple-element.54), channel_id=1, source_target_pairs={{0,28},{4,0},{8,4},{12,8},{16,12},{20,16},{24,20},{28,24},{1,29},{... | collective-permute-start | bytes 393224 | tf_op jit(solution)/shard_map/ppermute | solution.py:201
  69.6 1.0 %collective-permute-start.11 = (bf16[4,2,64,128]{3,2,1,0:T(8,128)(2,1)S(1)}, bf16[4,2,64,128]{3,2,1,0:T(8,128)(2,1)S(1)}, u32[]{:S(2)}, u32[]{:S(2)}) collective-permute-start(bf16[4,2,64,128]{3,2,1,0:T(8,128)(2,1)S(1)} %get-tuple-element.55), channel_id=1, source_target_pairs={{0,4},{4,8},{8,12},{12,16},{16,20},{20,24},{24,28},{28,0},{1,5},{5... | collective-permute-start | bytes 393224 | tf_op jit(solution)/shard_map/ppermute | solution.py:201
  70.7 2.2 %collective-permute-done.13 = bf16[4,2,64,128]{3,2,1,0:T(8,128)(2,1)S(1)} collective-permute-done((bf16[4,2,64,128]{3,2,1,0:T(8,128)(2,1)S(1)}, bf16[4,2,64,128]{3,2,1,0:T(8,128)(2,1)S(1)}, u32[]{:S(2)}, u32[]{:S(2)}) %collective-permute-start.13) | collective-permute-done | bytes 131104 | tf_op jit(solution)/shard_map/ppermute | solution.py:201
  72.8 2.2 %collective-permute-done.10 = bf16[4,2,64,128]{3,2,1,0:T(8,128)(2,1)S(1)} collective-permute-done((bf16[4,2,64,128]{3,2,1,0:T(8,128)(2,1)S(1)}, bf16[4,2,64,128]{3,2,1,0:T(8,128)(2,1)S(1)}, u32[]{:S(2)}, u32[]{:S(2)}) %collective-permute-start.10) | collective-permute-done | bytes 131104 | tf_op jit(solution)/shard_map/ppermute | solution.py:201
  75.1 0.7 collective-permute-done.11
  75.8 0.7 add_convert_fusion
  76.5 2.6 %all-to-all-done.2 = bf16[4,1280,128]{2,1,0:T(8,128)(2,1)S(1)} async-done(((bf16[4,1280,128]{2,1,0:T(8,128)(2,1)}), bf16[4,1280,128]{2,1,0:T(8,128)(2,1)S(1)}, u32[]{:S(2)}, u32[]{:S(2)}) %all-to-all-start.2) | async-done | bytes 1310752 | tf_op jit(solution)/shard_map/all_to_all | solution.py:204
  79.2 3.3 %all-to-all-start.3 = ((bf16[4,2,64,128]{3,2,1,0:T(8,128)(2,1)}), bf16[4,2,64,128]{3,2,1,0:T(8,128)(2,1)S(1)}, u32[]{:S(2)}, u32[]{:S(2)}) async-start(bf16[4,2,64,128]{3,2,1,0:T(8,128)(2,1)} %add_convert_fusion), calls=%async_computation.3 | async-start | bytes 262144 | tf_op jit(solution)/shard_map/all_to_all | solution.py:204
  82.5 0.1 fusion
  82.6 0.2 copy.19
  82.8 1.0 %broadcast_select_fusion = bf16[1,128,16,128]{3,2,1,0:T(8,128)(2,1)} fusion(bf16[1,128,16,128]{3,2,1,0:T(8,128)(2,1)S(1)} %bitcast.58, pred[128]{0:T(512)(128)(4,1)S(1)} %iota_compare_fusion), kind=kLoop, calls=%fused_computation.2 | loop fusion | flops 262144 | bytes 1048704 | tf_op jit(solution)/shard_map/jit(_where)/select_n | solution.py:324
  83.8 1.0 %copy.20 = bf16[128,4,4,128]{3,2,1,0:T(4,128)(2,1)} copy(bf16[128,4,4,128]{3,2,0,1:T(4,128)(2,1)S(1)} %bitcast.59) | data formatting | bytes 1048576 | tf_op jit(solution)/shard_map/transpose | solution.py:321
  84.8 0.8 copy.22
  85.5 0.8 copy.21
  86.3 2.2 %all-to-all-done.3 = bf16[4,2,64,128]{3,2,1,0:T(8,128)(2,1)S(1)} async-done(((bf16[4,2,64,128]{3,2,1,0:T(8,128)(2,1)}), bf16[4,2,64,128]{3,2,1,0:T(8,128)(2,1)S(1)}, u32[]{:S(2)}, u32[]{:S(2)}) %all-to-all-start.3) | async-done | bytes 131104 | tf_op jit(solution)/shard_map/all_to_all | solution.py:204
  88.5 0.7 copy.24
  89.2 0.7 copy.23
  (17 shorter events, 0.1 us)
Async XLA Ops:
  0.6 8.0 %copy-start.1 = (bf16[1,128,4,128]{3,2,1,0:T(4,128)(2,1)S(1)}, bf16[1,128,4,128]{3,2,1,0:T(4,128)(2,1)}, u32[]{:S(2)}) copy-start(bf16[1,128,4,128]{3,2,1,0:T(4,128)(2,1)} %param.9) | copy-start | bytes 393220
  0.6 8.0 %copy-start.2 = (bf16[1,128,4,128]{3,2,1,0:T(4,128)(2,1)S(1)}, bf16[1,128,4,128]{3,2,1,0:T(4,128)(2,1)}, u32[]{:S(2)}) copy-start(bf16[1,128,4,128]{3,2,1,0:T(4,128)(2,1)} %param.8) | copy-start | bytes 393220
  0.7 8.1 %copy-start = (bf16[1,128,16,128]{3,2,1,0:T(8,128)(2,1)S(1)}, bf16[1,128,16,128]{3,2,1,0:T(8,128)(2,1)}, u32[]{:S(2)}) copy-start(bf16[1,128,16,128]{3,2,1,0:T(8,128)(2,1)} %param.13) | copy-start | bytes 1572868
  2.3 10.4 %all-to-all-start = ((bf16[4,2,64,128]{3,2,1,0:T(8,128)(2,1)}), bf16[4,2,64,128]{3,2,1,0:T(8,128)(2,1)S(1)}, u32[]{:S(2)}, u32[]{:S(2)}) async-start(bf16[4,2,64,128]{3,2,1,0:T(8,128)(2,1)} %maximum_bitcast_fusion), calls=%async_computation | async-start | bytes 262144 | tf_op jit(solution)/shard_map/all_to_all | solution.py:204
  12.7 20.3 %all-to-all-start.1 = ((bf16[4,1280,128]{2,1,0:T(8,128)(2,1)}), bf16[4,1280,128]{2,1,0:T(8,128)(2,1)S(1)}, u32[]{:S(2)}, u32[]{:S(2)}) async-start(bf16[4,1280,128]{2,1,0:T(8,128)(2,1)} %pad_maximum_fusion), calls=%async_computation.1 | async-start | bytes 2621440 | tf_op jit(solution)/shard_map/all_to_all | solution.py:204
  16.3 10.7 %collective-permute-start.2 = (bf16[4,2,64,128]{3,2,1,0:T(8,128)(2,1)S(1)}, bf16[4,2,64,128]{3,2,1,0:T(8,128)(2,1)S(1)}, u32[]{:S(2)}, u32[]{:S(2)}) collective-permute-start(bf16[4,2,64,128]{3,2,1,0:T(8,128)(2,1)S(1)} %all-to-all-done.kv0), channel_id=1, source_target_pairs={{0,8},{4,12},{8,16},{12,20},{16,24},{20,28},{24,0},{28,4},{1,9},{5... | collective-permute-start | bytes 393224 | tf_op jit(solution)/shard_map/ppermute | solution.py:201
  19.6 10.3 %collective-permute-start.3 = (bf16[4,2,64,128]{3,2,1,0:T(8,128)(2,1)S(1)}, bf16[4,2,64,128]{3,2,1,0:T(8,128)(2,1)S(1)}, u32[]{:S(2)}, u32[]{:S(2)}) collective-permute-start(bf16[4,2,64,128]{3,2,1,0:T(8,128)(2,1)S(1)} %all-to-all-done.kv0), channel_id=1, source_target_pairs={{0,24},{4,28},{8,0},{12,4},{16,8},{20,12},{24,16},{28,20},{1,25},{... | collective-permute-start | bytes 393224 | tf_op jit(solution)/shard_map/ppermute | solution.py:201
  22.8 9.5 %collective-permute-start.1 = (bf16[4,2,64,128]{3,2,1,0:T(8,128)(2,1)S(1)}, bf16[4,2,64,128]{3,2,1,0:T(8,128)(2,1)S(1)}, u32[]{:S(2)}, u32[]{:S(2)}) collective-permute-start(bf16[4,2,64,128]{3,2,1,0:T(8,128)(2,1)S(1)} %all-to-all-done.kv0), channel_id=1, source_target_pairs={{0,28},{4,0},{8,4},{12,8},{16,12},{20,16},{24,20},{28,24},{1,29},{... | collective-permute-start | bytes 393224 | tf_op jit(solution)/shard_map/ppermute | solution.py:201
  25.1 7.7 %collective-permute-start = (bf16[4,2,64,128]{3,2,1,0:T(8,128)(2,1)S(1)}, bf16[4,2,64,128]{3,2,1,0:T(8,128)(2,1)S(1)}, u32[]{:S(2)}, u32[]{:S(2)}) collective-permute-start(bf16[4,2,64,128]{3,2,1,0:T(8,128)(2,1)S(1)} %all-to-all-done.kv0), channel_id=1, source_target_pairs={{0,4},{4,8},{8,12},{12,16},{16,20},{20,24},{24,28},{28,0},{1,5},{5... | collective-permute-start | bytes 393224 | tf_op jit(solution)/shard_map/ppermute | solution.py:201
  27.0 11.1 %collective-permute-start.6 = (bf16[4,2,64,128]{3,2,1,0:T(8,128)(2,1)S(1)}, bf16[4,2,64,128]{3,2,1,0:T(8,128)(2,1)S(1)}, u32[]{:S(2)}, u32[]{:S(2)}) collective-permute-start(bf16[4,2,64,128]{3,2,1,0:T(8,128)(2,1)S(1)} %collective-permute-done.2.kv3), channel_id=1, source_target_pairs={{0,8},{4,12},{8,16},{12,20},{16,24},{20,28},{24,0},{28,4},{1,9},{5... | collective-permute-start | bytes 393224 | tf_op jit(solution)/shard_map/ppermute | solution.py:201
  28.9 10.2 %collective-permute-start.4 = (bf16[4,2,64,128]{3,2,1,0:T(8,128)(2,1)S(1)}, bf16[4,2,64,128]{3,2,1,0:T(8,128)(2,1)S(1)}, u32[]{:S(2)}, u32[]{:S(2)}) collective-permute-start(bf16[4,2,64,128]{3,2,1,0:T(8,128)(2,1)S(1)} %collective-permute-done.2.kv3), channel_id=1, source_target_pairs={{0,4},{4,8},{8,12},{12,16},{16,20},{20,24},{24,28},{28,0},{1,5},{5... | collective-permute-start | bytes 393224 | tf_op jit(solution)/shard_map/ppermute | solution.py:201
  30.0 8.1 %collective-permute-start.5 = (bf16[4,2,64,128]{3,2,1,0:T(8,128)(2,1)S(1)}, bf16[4,2,64,128]{3,2,1,0:T(8,128)(2,1)S(1)}, u32[]{:S(2)}, u32[]{:S(2)}) collective-permute-start(bf16[4,2,64,128]{3,2,1,0:T(8,128)(2,1)S(1)} %collective-permute-done.3.kv4), channel_id=1, source_target_pairs={{0,28},{4,0},{8,4},{12,8},{16,12},{20,16},{24,20},{28,24},{1,29},{... | collective-permute-start | bytes 393224 | tf_op jit(solution)/shard_map/ppermute | solution.py:201
  45.6 15.1 %collective-permute-start.7 = (bf16[4,2,64,128]{3,2,1,0:T(8,128)(2,1)S(1)}, bf16[4,2,64,128]{3,2,1,0:T(8,128)(2,1)S(1)}, u32[]{:S(2)}, u32[]{:S(2)}) collective-permute-start(bf16[4,2,64,128]{3,2,1,0:T(8,128)(2,1)S(1)} %get-tuple-element.46), channel_id=1, source_target_pairs={{0,24},{4,28},{8,0},{12,4},{16,8},{20,12},{24,16},{28,20},{1,25},{... | collective-permute-start | bytes 393224 | tf_op jit(solution)/shard_map/ppermute | solution.py:201
  50.9 9.8 %collective-permute-start.8 = (bf16[4,2,64,128]{3,2,1,0:T(8,128)(2,1)S(1)}, bf16[4,2,64,128]{3,2,1,0:T(8,128)(2,1)S(1)}, u32[]{:S(2)}, u32[]{:S(2)}) collective-permute-start(bf16[4,2,64,128]{3,2,1,0:T(8,128)(2,1)S(1)} %get-tuple-element.47), channel_id=1, source_target_pairs={{0,28},{4,0},{8,4},{12,8},{16,12},{20,16},{24,20},{28,24},{1,29},{... | collective-permute-start | bytes 393224 | tf_op jit(solution)/shard_map/ppermute | solution.py:201
  51.9 8.8 %collective-permute-start.9 = (bf16[4,2,64,128]{3,2,1,0:T(8,128)(2,1)S(1)}, bf16[4,2,64,128]{3,2,1,0:T(8,128)(2,1)S(1)}, u32[]{:S(2)}, u32[]{:S(2)}) collective-permute-start(bf16[4,2,64,128]{3,2,1,0:T(8,128)(2,1)S(1)} %get-tuple-element.48), channel_id=1, source_target_pairs={{0,4},{4,8},{8,12},{12,16},{16,20},{20,24},{24,28},{28,0},{1,5},{5... | collective-permute-start | bytes 393224 | tf_op jit(solution)/shard_map/ppermute | solution.py:201
  60.7 18.5 %all-to-all-start.2 = ((bf16[4,1280,128]{2,1,0:T(8,128)(2,1)}), bf16[4,1280,128]{2,1,0:T(8,128)(2,1)S(1)}, u32[]{:S(2)}, u32[]{:S(2)}) async-start(bf16[4,1280,128]{2,1,0:T(8,128)(2,1)} %get-tuple-element.61), calls=%async_computation.2 | async-start | bytes 2621440 | tf_op jit(solution)/shard_map/all_to_all | solution.py:204
  64.3 8.6 %collective-permute-start.13 = (bf16[4,2,64,128]{3,2,1,0:T(8,128)(2,1)S(1)}, bf16[4,2,64,128]{3,2,1,0:T(8,128)(2,1)S(1)}, u32[]{:S(2)}, u32[]{:S(2)}) collective-permute-start(bf16[4,2,64,128]{3,2,1,0:T(8,128)(2,1)S(1)} %add_convert_fusion.1), channel_id=1, source_target_pairs={{0,8},{4,12},{8,16},{12,20},{16,24},{20,28},{24,0},{28,4},{1,9},{5... | collective-permute-start | bytes 393224 | tf_op jit(solution)/shard_map/ppermute | solution.py:201
  64.9 8.0 %collective-permute-start.12 = (bf16[4,2,64,128]{3,2,1,0:T(8,128)(2,1)S(1)}, bf16[4,2,64,128]{3,2,1,0:T(8,128)(2,1)S(1)}, u32[]{:S(2)}, u32[]{:S(2)}) collective-permute-start(bf16[4,2,64,128]{3,2,1,0:T(8,128)(2,1)S(1)} %add_convert_fusion.2), channel_id=1, source_target_pairs={{0,24},{4,28},{8,0},{12,4},{16,8},{20,12},{24,16},{28,20},{1,25},{... | collective-permute-start | bytes 393224 | tf_op jit(solution)/shard_map/ppermute | solution.py:201
  68.6 6.5 %collective-permute-start.10 = (bf16[4,2,64,128]{3,2,1,0:T(8,128)(2,1)S(1)}, bf16[4,2,64,128]{3,2,1,0:T(8,128)(2,1)S(1)}, u32[]{:S(2)}, u32[]{:S(2)}) collective-permute-start(bf16[4,2,64,128]{3,2,1,0:T(8,128)(2,1)S(1)} %get-tuple-element.54), channel_id=1, source_target_pairs={{0,28},{4,0},{8,4},{12,8},{16,12},{20,16},{24,20},{28,24},{1,29},{... | collective-permute-start | bytes 393224 | tf_op jit(solution)/shard_map/ppermute | solution.py:201
  69.6 6.2 %collective-permute-start.11 = (bf16[4,2,64,128]{3,2,1,0:T(8,128)(2,1)S(1)}, bf16[4,2,64,128]{3,2,1,0:T(8,128)(2,1)S(1)}, u32[]{:S(2)}, u32[]{:S(2)}) collective-permute-start(bf16[4,2,64,128]{3,2,1,0:T(8,128)(2,1)S(1)} %get-tuple-element.55), channel_id=1, source_target_pairs={{0,4},{4,8},{8,12},{12,16},{16,20},{20,24},{24,28},{28,0},{1,5},{5... | collective-permute-start | bytes 393224 | tf_op jit(solution)/shard_map/ppermute | solution.py:201
  79.2 9.3 %all-to-all-start.3 = ((bf16[4,2,64,128]{3,2,1,0:T(8,128)(2,1)}), bf16[4,2,64,128]{3,2,1,0:T(8,128)(2,1)S(1)}, u32[]{:S(2)}, u32[]{:S(2)}) async-start(bf16[4,2,64,128]{3,2,1,0:T(8,128)(2,1)} %add_convert_fusion), calls=%async_computation.3 | async-start | bytes 262144 | tf_op jit(solution)/shard_map/all_to_all | solution.py:204

commit v4 on v3

--- a/solution.py
+++ b/solution.py
@@ -203,8 +203,16 @@
     def swap_y(x):
         return lax.all_to_all(x, "y", 0, 0, tiled=True)
 
+    def over_y(x, k):
+        return lax.ppermute(x, "y", [(i, (i + k) % 4) for i in range(4)])
+
+    def turned(x, by):
+        return lax.dynamic_slice_in_dim(jnp.concatenate([x, x], axis=0), by, 4, 0)
+
+    my_y = lax.axis_index("y")
     kv = jnp.stack([prompt_keys, prompt_value_rows], axis=0)
-    kv = swap_y(jnp.transpose(kv, (2, 0, 1, 3)))
+    kv = turned(jnp.transpose(kv, (2, 0, 1, 3)), my_y)
+    kv = jnp.stack([kv[0]] + [over_y(kv[k], k) for k in (1, 2, 3)])
 
     live = (jnp.arange(T) < lengths[0])[:, None, None]
     masked = jnp.where(live, grad_out[0], jnp.zeros((), bf16))
@@ -222,7 +230,6 @@
         ],
         axis=1,
     )
-    kv, pack = lax.optimization_barrier((kv, pack))
     pack = swap_y(pack)
     from_2 = over_z(kv, 2)
     from_m2 = over_z(kv, -2)
@@ -313,8 +320,9 @@
     total = d0.astype(f32)
     for x in parts:
         total = total + x.astype(f32)
-    total, home = lax.optimization_barrier((total.astype(bf16), home))
-    total = swap_y(total)
+    total = total.astype(bf16)
+    total = jnp.stack([total[0]] + [over_y(total[k], -k) for k in (1, 2, 3)])
+    total = turned(total, (4 - my_y) % 4)
 
     def by_token(x, n):
         x = x.reshape(KH, T, n, D)

time: 90.4 us -> 105 us (1.16)
  waiting for transfers between devices: 16.2 us -> 28.7 us
  starting transfers between devices: 42.6 us -> 45.9 us
  other arithmetic: 3.96 us -> 2.75 us
    ppermute x0 -> x6, waiting for transfers between devices: none -> 22.8 us  [over_y(): return lax.ppermute(x, 'y', [(i, (i + k) % 4) for i in range(4)])]
    ppermute x0 -> x6, starting transfers between devices: none -> 11 us  [over_y(): return lax.ppermute(x, 'y', [(i, (i + k) % 4) for i in range(4)])]
    all_to_all x4 -> x2, waiting for transfers between devices: 7.48 us -> 0.01 us  [swap_y(): return lax.all_to_all(x, 'y', 0, 0, tiled=True)]
    all_to_all x4 -> x2, starting transfers between devices: 14.9 us -> 8.13 us  [swap_y(): return lax.all_to_all(x, 'y', 0, 0, tiled=True)]
    ppermute x14, waiting for transfers between devices: 8.76 us -> 5.88 us  [over_z(): return lax.ppermute(x, 'z', [(i, (i + k) % 8) for i in range(8)])]
    unnamed x10 -> x16, local copies, waits for them, and re-layouts: 2.89 us -> 2.96 us
  transfers between devices with their start and end apart: 18 -> 22, of which waited for: 10 -> 7; matrix products, arithmetic and copies ran while one was open for 8% -> 2% of each run, Pallas kernels for 14% -> 12%
where the time goes in v4:
time: 105 us
  starting transfers between devices  45.9 us (44%)
  waiting for transfers between devices  28.7 us (27%)
  Pallas kernels  19.2 us (18%)
  local copies, waits for them, and re-layouts  6.51 us (6%)
  other arithmetic  2.75 us (3%)
  between operations  1.54 us (1%)
    ppermute x14, starting transfers between devices, over_z(): return lax.ppermute(x, 'z', [(i, (i + k) % 8) for i in range(8)])  26.8 us
    ppermute x6, waiting for transfers between devices, over_y(): return lax.ppermute(x, 'y', [(i, (i + k) % 4) for i in range(4)])  22.8 us
    pallas_call x3, Pallas kernels, call(): pl.pallas_call(body, out_shape=out_shape, scratch_shapes=scratch, compile...  19.2 us
    ppermute x6, starting transfers between devices, over_y(): return lax.ppermute(x, 'y', [(i, (i + k) % 4) for i in range(4)])  11 us
    all_to_all x2, starting transfers between devices, swap_y(): return lax.all_to_all(x, 'y', 0, 0, tiled=True)  8.13 us
    ppermute x14, waiting for transfers between devices, over_z(): return lax.ppermute(x, 'z', [(i, (i + k) % 8) for i in range(8)])  5.88 us
    unnamed x16, local copies, waits for them, and re-layouts  2.96 us
  transfers between devices with their start and end apart: 22, of which 7 were waited for; matrix products, arithmetic and copies ran while one was open for 2% of the time, Pallas kernels for 12%

profile of v4, /device:TPU:4, one launch (start us, length us, event | category | flops | bytes accessed | tf_op | source)
XLA Modules:
  0.0 104.6 jit_solution(10098440632158854049)
XLA Ops:
  1.4 1.2 %copy.13 = bf16[128,4,4,128]{3,2,0,1:T(4,128)(2,1)S(1)} copy(bf16[128,4,4,128]{3,2,1,0:T(4,128)(2,1)} %bitcast.85) | data formatting | bytes 1048576 | tf_op jit(solution)/shard_map/reshape | solution.py:221
  2.6 1.0 copy_bitcast_fusion
  3.6 0.3 copy_select_fusion
  3.9 1.2 %pad_maximum_fusion = bf16[4,1280,128]{2,1,0:T(8,128)(2,1)} fusion(bf16[4,128,128]{2,1,0:T(8,128)(2,1)S(1)} %get-tuple-element.76, bf16[4,128,128]{2,1,0:T(8,128)(2,1)S(1)} %get-tuple-element.77, bf16[4,512,128]{2,1,0:T(8,128)(2,1)S(1)} %bitcast.81, bf16[4,512,128]{2,1,0:T(8,128)(2,1)S(1)} %bitcast.80), kind=kLoop, calls=%fused_computation | loop fusion | flops 5242880 | bytes 2621440 | tf_op jit(solution)/shard_map/concatenate | solution.py:224
  5.1 4.6 %all-to-all-start = ((bf16[4,1280,128]{2,1,0:T(8,128)(2,1)}), bf16[4,1280,128]{2,1,0:T(8,128)(2,1)S(1)}, u32[]{:S(2)}, u32[]{:S(2)}) async-start(bf16[4,1280,128]{2,1,0:T(8,128)(2,1)} %pad_maximum_fusion), calls=%async_computation | async-start | bytes 2621440 | tf_op jit(solution)/shard_map/all_to_all | solution.py:204
  9.7 0.1 fusion
  9.8 3.3 %collective-permute-start.2 = (bf16[2,64,128]{2,1,0:T(8,128)(2,1)S(1)}, bf16[2,64,128]{2,1,0:T(8,128)(2,1)S(1)}, u32[]{:S(2)}, u32[]{:S(2)}) collective-permute-start(bf16[2,64,128]{2,1,0:T(8,128)(2,1)S(1)} %get-tuple-element.75), channel_id=1, source_target_pairs={{0,3},{1,0},{2,1},{3,2},{4,7},{5,4},{6,5},{7,6},{8,11},{9,8},{10,9... | collective-permute-start | bytes 98312 | tf_op jit(solution)/shard_map/ppermute | solution.py:207
  13.1 0.9 collective-permute-start.1
  14.0 0.9 collective-permute-start
  14.8 12.3 %collective-permute-done.2 = bf16[2,64,128]{2,1,0:T(8,128)(2,1)S(1)} collective-permute-done((bf16[2,64,128]{2,1,0:T(8,128)(2,1)S(1)}, bf16[2,64,128]{2,1,0:T(8,128)(2,1)S(1)}, u32[]{:S(2)}, u32[]{:S(2)}) %collective-permute-start.2) | collective-permute-done | bytes 32800 | tf_op jit(solution)/shard_map/ppermute | solution.py:207
  27.1 1.6 %collective-permute-done.1 = bf16[2,64,128]{2,1,0:T(8,128)(2,1)S(1)} collective-permute-done((bf16[2,64,128]{2,1,0:T(8,128)(2,1)S(1)}, bf16[2,64,128]{2,1,0:T(8,128)(2,1)S(1)}, u32[]{:S(2)}, u32[]{:S(2)}) %collective-permute-start.1) | collective-permute-done | bytes 32800 | tf_op jit(solution)/shard_map/ppermute | solution.py:207
  28.7 0.0 collective-permute-done
  28.7 3.3 %collective-permute-start.3 = (bf16[4,2,64,128]{3,2,1,0:T(8,128)(2,1)S(1)}, bf16[4,2,64,128]{3,2,1,0:T(8,128)(2,1)S(1)}, u32[]{:S(2)}, u32[]{:S(2)}) collective-permute-start(bf16[4,2,64,128]{3,2,1,0:T(8,128)(2,1)S(1)} %pad_maximum_fusion.1.kv0), channel_id=1, source_target_pairs={{0,8},{4,12},{8,16},{12,20},{16,24},{20,28},{24,0},{28,4},{1,9},{5... | collective-permute-start | bytes 393224 | tf_op jit(solution)/shard_map/ppermute | solution.py:201
  32.1 3.1 %collective-permute-start.5 = (bf16[4,2,64,128]{3,2,1,0:T(8,128)(2,1)S(1)}, bf16[4,2,64,128]{3,2,1,0:T(8,128)(2,1)S(1)}, u32[]{:S(2)}, u32[]{:S(2)}) collective-permute-start(bf16[4,2,64,128]{3,2,1,0:T(8,128)(2,1)S(1)} %pad_maximum_fusion.1.kv0), channel_id=1, source_target_pairs={{0,24},{4,28},{8,0},{12,4},{16,8},{20,12},{24,16},{28,20},{1,25},{... | collective-permute-start | bytes 393224 | tf_op jit(solution)/shard_map/ppermute | solution.py:201
  35.2 1.0 collective-permute-start.8
  36.2 2.2 %collective-permute-start.9 = (bf16[4,2,64,128]{3,2,1,0:T(8,128)(2,1)S(1)}, bf16[4,2,64,128]{3,2,1,0:T(8,128)(2,1)S(1)}, u32[]{:S(2)}, u32[]{:S(2)}) collective-permute-start(bf16[4,2,64,128]{3,2,1,0:T(8,128)(2,1)S(1)} %pad_maximum_fusion.1.kv0), channel_id=1, source_target_pairs={{0,28},{4,0},{8,4},{12,8},{16,12},{20,16},{24,20},{28,24},{1,29},{... | collective-permute-start | bytes 393224 | tf_op jit(solution)/shard_map/ppermute | solution.py:201
  38.4 1.7 %collective-permute-done.3.kv3 = bf16[4,2,64,128]{3,2,1,0:T(8,128)(2,1)S(1)} collective-permute-done((bf16[4,2,64,128]{3,2,1,0:T(8,128)(2,1)S(1)}, bf16[4,2,64,128]{3,2,1,0:T(8,128)(2,1)S(1)}, u32[]{:S(2)}, u32[]{:S(2)}) %collective-permute-start.3) | collective-permute-done | bytes 131104 | tf_op jit(solution)/shard_map/ppermute | solution.py:201
  40.1 1.8 %collective-permute-start.4 = (bf16[4,2,64,128]{3,2,1,0:T(8,128)(2,1)S(1)}, bf16[4,2,64,128]{3,2,1,0:T(8,128)(2,1)S(1)}, u32[]{:S(2)}, u32[]{:S(2)}) collective-permute-start(bf16[4,2,64,128]{3,2,1,0:T(8,128)(2,1)S(1)} %collective-permute-done.3.kv3), channel_id=1, source_target_pairs={{0,4},{4,8},{8,12},{12,16},{16,20},{20,24},{24,28},{28,0},{1,5},{5... | collective-permute-start | bytes 393224 | tf_op jit(solution)/shard_map/ppermute | solution.py:201
  41.9 0.4 collective-permute-start.7
  42.4 2.4 %collective-permute-start.6 = (bf16[4,2,64,128]{3,2,1,0:T(8,128)(2,1)S(1)}, bf16[4,2,64,128]{3,2,1,0:T(8,128)(2,1)S(1)}, u32[]{:S(2)}, u32[]{:S(2)}) collective-permute-start(bf16[4,2,64,128]{3,2,1,0:T(8,128)(2,1)S(1)} %collective-permute-done.5.kv4), channel_id=1, source_target_pairs={{0,28},{4,0},{8,4},{12,8},{16,12},{20,16},{24,20},{28,24},{1,29},{... | collective-permute-start | bytes 393224 | tf_op jit(solution)/shard_map/ppermute | solution.py:201
  44.8 5.1 %near_forward.1 = (bf16[1408,2048]{1,0:T(8,128)(2,1)S(1)}, f32[144,2048]{1,0:T(8,128)S(1)}, f32[8,2048]{1,0:T(8,128)S(1)}) custom-call(bf16[4,1280,128]{2,1,0:T(8,128)(2,1)S(1)} %all-to-all-done.pack, bf16[4,2,64,128]{3,2,1,0:T(8,128)(2,1)S(1)} %pad_maximum_fusion.1.kv0, bf16[4,2,64,128]{3,2,1,0:T(8,128)(2,1)S(1)} %collective-permute-done.8.kv1, ...), custom_call_target="tpu_custom_call" | custom-call | flops 1476395008 | bytes 4194304 | tf_op jit(solution)/shard_map/near_forward/pallas_call | solution.py:182
  49.9 1.2 %collective-permute-done.7.kv2 = bf16[4,2,64,128]{3,2,1,0:T(8,128)(2,1)S(1)} collective-permute-done((bf16[4,2,64,128]{3,2,1,0:T(8,128)(2,1)S(1)}, bf16[4,2,64,128]{3,2,1,0:T(8,128)(2,1)S(1)}, u32[]{:S(2)}, u32[]{:S(2)}) %collective-permute-start.7) | collective-permute-done | bytes 131104 | tf_op jit(solution)/shard_map/ppermute | solution.py:201
  51.1 6.4 %far_both.1 = (bf16[4,512,128]{2,1,0:T(8,128)(2,1)S(1)}, f32[8,2048]{1,0:T(8,128)S(1)}, bf16[2048,128]{1,0:T(8,128)(2,1)S(1)}, bf16[2048,128]{1,0:T(8,128)(2,1)S...) custom-call(bf16[4,1280,128]{2,1,0:T(8,128)(2,1)S(1)} %all-to-all-do, ...), custom_call_target="tpu_custom_call" | custom-call | flops 2415919104 | bytes 4194304 | tf_op jit(solution)/shard_map/far_both/pallas_call | solution.py:182
  57.5 1.8 %collective-permute-start.10 = (bf16[4,2,64,128]{3,2,1,0:T(8,128)(2,1)S(1)}, bf16[4,2,64,128]{3,2,1,0:T(8,128)(2,1)S(1)}, u32[]{:S(2)}, u32[]{:S(2)}) collective-permute-start(bf16[4,2,64,128]{3,2,1,0:T(8,128)(2,1)S(1)} %get-tuple-element.33), channel_id=1, source_target_pairs={{0,24},{4,28},{8,0},{12,4},{16,8},{20,12},{24,16},{28,20},{1,25},{... | collective-permute-start | bytes 393224 | tf_op jit(solution)/shard_map/ppermute | solution.py:201
  59.2 3.2 %collective-permute-start.11 = (bf16[4,2,64,128]{3,2,1,0:T(8,128)(2,1)S(1)}, bf16[4,2,64,128]{3,2,1,0:T(8,128)(2,1)S(1)}, u32[]{:S(2)}, u32[]{:S(2)}) collective-permute-start(bf16[4,2,64,128]{3,2,1,0:T(8,128)(2,1)S(1)} %get-tuple-element.34), channel_id=1, source_target_pairs={{0,28},{4,0},{8,4},{12,8},{16,12},{20,16},{24,20},{28,24},{1,29},{... | collective-permute-start | bytes 393224 | tf_op jit(solution)/shard_map/ppermute | solution.py:201
  62.4 0.0 collective-permute-start.12
  62.4 7.8 %near_backward.1 = (bf16[4,1280,128]{2,1,0:T(8,128)(2,1)}, bf16[4,2,64,128]{3,2,1,0:T(8,128)(2,1)S(1)}, bf16[4,2,64,128]{3,2,1,0:T(8,128)(2,1)S(1)}, bf16[4,2,64...) custom-call(bf16[4,1280,128]{2,1,0:T(8,128)(2,1)S(1)} %all-to-all-done.pack, ...), custom_call_target="tpu_custom_call" | custom-call | flops 2952790016 | bytes 4194304 | tf_op jit(solution)/shard_map/near_backward/pallas_call | solution.py:182
  70.2 0.3 collective-permute-start.16
  70.6 0.1 add_convert_fusion.2
  70.6 4.0 %collective-permute-start.15 = (bf16[4,2,64,128]{3,2,1,0:T(8,128)(2,1)S(1)}, bf16[4,2,64,128]{3,2,1,0:T(8,128)(2,1)S(1)}, u32[]{:S(2)}, u32[]{:S(2)}) collective-permute-start(bf16[4,2,64,128]{3,2,1,0:T(8,128)(2,1)S(1)} %add_convert_fusion.2), channel_id=1, source_target_pairs={{0,24},{4,28},{8,0},{12,4},{16,8},{20,12},{24,16},{28,20},{1,25},{... | collective-permute-start | bytes 393224 | tf_op jit(solution)/shard_map/ppermute | solution.py:201
  74.6 0.8 collective-permute-start.14
  75.4 2.4 %collective-permute-start.13 = (bf16[4,2,64,128]{3,2,1,0:T(8,128)(2,1)S(1)}, bf16[4,2,64,128]{3,2,1,0:T(8,128)(2,1)S(1)}, u32[]{:S(2)}, u32[]{:S(2)}) collective-permute-start(bf16[4,2,64,128]{3,2,1,0:T(8,128)(2,1)S(1)} %get-tuple-element.49), channel_id=1, source_target_pairs={{0,28},{4,0},{8,4},{12,8},{16,12},{20,16},{24,20},{28,24},{1,29},{... | collective-permute-start | bytes 393224 | tf_op jit(solution)/shard_map/ppermute | solution.py:201
  77.8 0.7 collective-permute-done.15
  78.5 2.3 %collective-permute-done.14 = bf16[4,2,64,128]{3,2,1,0:T(8,128)(2,1)S(1)} collective-permute-done((bf16[4,2,64,128]{3,2,1,0:T(8,128)(2,1)S(1)}, bf16[4,2,64,128]{3,2,1,0:T(8,128)(2,1)S(1)}, u32[]{:S(2)}, u32[]{:S(2)}) %collective-permute-start.14) | collective-permute-done | bytes 131104 | tf_op jit(solution)/shard_map/ppermute | solution.py:201
  80.8 0.1 add_convert_fusion
  80.9 1.9 %collective-permute-start.17 = (bf16[2,64,128]{2,1,0:T(8,128)(2,1)S(1)}, bf16[2,64,128]{2,1,0:T(8,128)(2,1)S(1)}, u32[]{:S(2)}, u32[]{:S(2)}) collective-permute-start(bf16[2,64,128]{2,1,0:T(8,128)(2,1)S(1)} %get-tuple-element.71), channel_id=1, source_target_pairs={{0,3},{1,0},{2,1},{3,2},{4,7},{5,4},{6,5},{7,6},{8,11},{9,8},{10,9... | collective-permute-start | bytes 98312 | tf_op jit(solution)/shard_map/ppermute | solution.py:207
  82.8 3.5 %all-to-all-start.1 = ((bf16[4,1280,128]{2,1,0:T(8,128)(2,1)}), bf16[4,1280,128]{2,1,0:T(8,128)(2,1)S(1)}, u32[]{:S(2)}, u32[]{:S(2)}) async-start(bf16[4,1280,128]{2,1,0:T(8,128)(2,1)} %get-tuple-element.47), calls=%async_computation.1 | async-start | bytes 2621440 | tf_op jit(solution)/shard_map/all_to_all | solution.py:204
  86.3 3.5 %collective-permute-start.18 = (bf16[2,64,128]{2,1,0:T(8,128)(2,1)S(1)}, bf16[2,64,128]{2,1,0:T(8,128)(2,1)S(1)}, u32[]{:S(2)}, u32[]{:S(2)}) collective-permute-start(bf16[2,64,128]{2,1,0:T(8,128)(2,1)S(1)} %get-tuple-element.70), channel_id=1, source_target_pairs={{0,2},{1,3},{2,0},{3,1},{4,6},{5,7},{6,4},{7,5},{8,10},{9,11},{10,... | collective-permute-start | bytes 98312 | tf_op jit(solution)/shard_map/ppermute | solution.py:207
  89.8 0.6 collective-permute-start.19
  90.4 8.9 %collective-permute-done.18 = bf16[2,64,128]{2,1,0:T(8,128)(2,1)S(1)} collective-permute-done((bf16[2,64,128]{2,1,0:T(8,128)(2,1)S(1)}, bf16[2,64,128]{2,1,0:T(8,128)(2,1)S(1)}, u32[]{:S(2)}, u32[]{:S(2)}) %collective-permute-start.18) | collective-permute-done | bytes 32800 | tf_op jit(solution)/shard_map/ppermute | solution.py:207
  99.4 0.7 copy.23
  100.1 0.7 copy.24
  100.8 0.1 fusion.1
  100.9 0.2 copy.19
  101.1 1.0 broadcast_select_fusion
  102.1 1.0 copy.20
  103.1 0.8 copy.21
  103.8 0.8 copy.22
  (36 shorter events, 0.3 us)
Async XLA Ops:
  0.6 3.0 %copy-start = (bf16[1,128,16,128]{3,2,1,0:T(8,128)(2,1)S(1)}, bf16[1,128,16,128]{3,2,1,0:T(8,128)(2,1)}, u32[]{:S(2)}) copy-start(bf16[1,128,16,128]{3,2,1,0:T(8,128)(2,1)} %param.13) | copy-start | bytes 1572868
  5.1 4.6 %copy-start.1 = (bf16[64,4,128]{2,1,0:T(4,128)(2,1)S(1)}, bf16[64,4,128]{2,1,0:T(4,128)(2,1)}, u32[]{:S(2)}) copy-start(bf16[64,4,128]{2,1,0:T(4,128)(2,1)} %param.11) | copy-start | bytes 196612
  5.1 4.6 %copy-start.2 = (bf16[64,4,128]{2,1,0:T(4,128)(2,1)S(1)}, bf16[64,4,128]{2,1,0:T(4,128)(2,1)}, u32[]{:S(2)}) copy-start(bf16[64,4,128]{2,1,0:T(4,128)(2,1)} %param.10) | copy-start | bytes 196612
  5.1 39.7 %all-to-all-start = ((bf16[4,1280,128]{2,1,0:T(8,128)(2,1)}), bf16[4,1280,128]{2,1,0:T(8,128)(2,1)S(1)}, u32[]{:S(2)}, u32[]{:S(2)}) async-start(bf16[4,1280,128]{2,1,0:T(8,128)(2,1)} %pad_maximum_fusion), calls=%async_computation | async-start | bytes 2621440 | tf_op jit(solution)/shard_map/all_to_all | solution.py:204
  9.8 17.3 %collective-permute-start.2 = (bf16[2,64,128]{2,1,0:T(8,128)(2,1)S(1)}, bf16[2,64,128]{2,1,0:T(8,128)(2,1)S(1)}, u32[]{:S(2)}, u32[]{:S(2)}) collective-permute-start(bf16[2,64,128]{2,1,0:T(8,128)(2,1)S(1)} %get-tuple-element.75), channel_id=1, source_target_pairs={{0,3},{1,0},{2,1},{3,2},{4,7},{5,4},{6,5},{7,6},{8,11},{9,8},{10,9... | collective-permute-start | bytes 98312 | tf_op jit(solution)/shard_map/ppermute | solution.py:207
  13.1 15.6 %collective-permute-start.1 = (bf16[2,64,128]{2,1,0:T(8,128)(2,1)S(1)}, bf16[2,64,128]{2,1,0:T(8,128)(2,1)S(1)}, u32[]{:S(2)}, u32[]{:S(2)}) collective-permute-start(bf16[2,64,128]{2,1,0:T(8,128)(2,1)S(1)} %get-tuple-element.73), channel_id=1, source_target_pairs={{0,2},{1,3},{2,0},{3,1},{4,6},{5,7},{6,4},{7,5},{8,10},{9,11},{10,... | collective-permute-start | bytes 98312 | tf_op jit(solution)/shard_map/ppermute | solution.py:207
  14.0 14.7 %collective-permute-start = (bf16[2,64,128]{2,1,0:T(8,128)(2,1)S(1)}, bf16[2,64,128]{2,1,0:T(8,128)(2,1)S(1)}, u32[]{:S(2)}, u32[]{:S(2)}) collective-permute-start(bf16[2,64,128]{2,1,0:T(8,128)(2,1)S(1)} %get-tuple-element.74), channel_id=1, source_target_pairs={{0,1},{1,2},{2,3},{3,0},{4,5},{5,6},{6,7},{7,4},{8,9},{9,10},{10,1... | collective-permute-start | bytes 98312 | tf_op jit(solution)/shard_map/ppermute | solution.py:207
  28.7 11.4 %collective-permute-start.3 = (bf16[4,2,64,128]{3,2,1,0:T(8,128)(2,1)S(1)}, bf16[4,2,64,128]{3,2,1,0:T(8,128)(2,1)S(1)}, u32[]{:S(2)}, u32[]{:S(2)}) collective-permute-start(bf16[4,2,64,128]{3,2,1,0:T(8,128)(2,1)S(1)} %pad_maximum_fusion.1.kv0), channel_id=1, source_target_pairs={{0,8},{4,12},{8,16},{12,20},{16,24},{20,28},{24,0},{28,4},{1,9},{5... | collective-permute-start | bytes 393224 | tf_op jit(solution)/shard_map/ppermute | solution.py:201
  32.1 10.3 %collective-permute-start.5 = (bf16[4,2,64,128]{3,2,1,0:T(8,128)(2,1)S(1)}, bf16[4,2,64,128]{3,2,1,0:T(8,128)(2,1)S(1)}, u32[]{:S(2)}, u32[]{:S(2)}) collective-permute-start(bf16[4,2,64,128]{3,2,1,0:T(8,128)(2,1)S(1)} %pad_maximum_fusion.1.kv0), channel_id=1, source_target_pairs={{0,24},{4,28},{8,0},{12,4},{16,8},{20,12},{24,16},{28,20},{1,25},{... | collective-permute-start | bytes 393224 | tf_op jit(solution)/shard_map/ppermute | solution.py:201
  35.2 9.6 %collective-permute-start.8 = (bf16[4,2,64,128]{3,2,1,0:T(8,128)(2,1)S(1)}, bf16[4,2,64,128]{3,2,1,0:T(8,128)(2,1)S(1)}, u32[]{:S(2)}, u32[]{:S(2)}) collective-permute-start(bf16[4,2,64,128]{3,2,1,0:T(8,128)(2,1)S(1)} %pad_maximum_fusion.1.kv0), channel_id=1, source_target_pairs={{0,4},{4,8},{8,12},{12,16},{16,20},{20,24},{24,28},{28,0},{1,5},{5... | collective-permute-start | bytes 393224 | tf_op jit(solution)/shard_map/ppermute | solution.py:201
  36.2 8.6 %collective-permute-start.9 = (bf16[4,2,64,128]{3,2,1,0:T(8,128)(2,1)S(1)}, bf16[4,2,64,128]{3,2,1,0:T(8,128)(2,1)S(1)}, u32[]{:S(2)}, u32[]{:S(2)}) collective-permute-start(bf16[4,2,64,128]{3,2,1,0:T(8,128)(2,1)S(1)} %pad_maximum_fusion.1.kv0), channel_id=1, source_target_pairs={{0,28},{4,0},{8,4},{12,8},{16,12},{20,16},{24,20},{28,24},{1,29},{... | collective-permute-start | bytes 393224 | tf_op jit(solution)/shard_map/ppermute | solution.py:201
  40.1 9.7 %collective-permute-start.4 = (bf16[4,2,64,128]{3,2,1,0:T(8,128)(2,1)S(1)}, bf16[4,2,64,128]{3,2,1,0:T(8,128)(2,1)S(1)}, u32[]{:S(2)}, u32[]{:S(2)}) collective-permute-start(bf16[4,2,64,128]{3,2,1,0:T(8,128)(2,1)S(1)} %collective-permute-done.3.kv3), channel_id=1, source_target_pairs={{0,4},{4,8},{8,12},{12,16},{16,20},{20,24},{24,28},{28,0},{1,5},{5... | collective-permute-start | bytes 393224 | tf_op jit(solution)/shard_map/ppermute | solution.py:201
  41.9 9.1 %collective-permute-start.7 = (bf16[4,2,64,128]{3,2,1,0:T(8,128)(2,1)S(1)}, bf16[4,2,64,128]{3,2,1,0:T(8,128)(2,1)S(1)}, u32[]{:S(2)}, u32[]{:S(2)}) collective-permute-start(bf16[4,2,64,128]{3,2,1,0:T(8,128)(2,1)S(1)} %collective-permute-done.3.kv3), channel_id=1, source_target_pairs={{0,8},{4,12},{8,16},{12,20},{16,24},{20,28},{24,0},{28,4},{1,9},{5... | collective-permute-start | bytes 393224 | tf_op jit(solution)/shard_map/ppermute | solution.py:201
  42.4 7.5 %collective-permute-start.6 = (bf16[4,2,64,128]{3,2,1,0:T(8,128)(2,1)S(1)}, bf16[4,2,64,128]{3,2,1,0:T(8,128)(2,1)S(1)}, u32[]{:S(2)}, u32[]{:S(2)}) collective-permute-start(bf16[4,2,64,128]{3,2,1,0:T(8,128)(2,1)S(1)} %collective-permute-done.5.kv4), channel_id=1, source_target_pairs={{0,28},{4,0},{8,4},{12,8},{16,12},{20,16},{24,20},{28,24},{1,29},{... | collective-permute-start | bytes 393224 | tf_op jit(solution)/shard_map/ppermute | solution.py:201
  57.5 12.7 %collective-permute-start.10 = (bf16[4,2,64,128]{3,2,1,0:T(8,128)(2,1)S(1)}, bf16[4,2,64,128]{3,2,1,0:T(8,128)(2,1)S(1)}, u32[]{:S(2)}, u32[]{:S(2)}) collective-permute-start(bf16[4,2,64,128]{3,2,1,0:T(8,128)(2,1)S(1)} %get-tuple-element.33), channel_id=1, source_target_pairs={{0,24},{4,28},{8,0},{12,4},{16,8},{20,12},{24,16},{28,20},{1,25},{... | collective-permute-start | bytes 393224 | tf_op jit(solution)/shard_map/ppermute | solution.py:201
  59.2 11.0 %collective-permute-start.11 = (bf16[4,2,64,128]{3,2,1,0:T(8,128)(2,1)S(1)}, bf16[4,2,64,128]{3,2,1,0:T(8,128)(2,1)S(1)}, u32[]{:S(2)}, u32[]{:S(2)}) collective-permute-start(bf16[4,2,64,128]{3,2,1,0:T(8,128)(2,1)S(1)} %get-tuple-element.34), channel_id=1, source_target_pairs={{0,28},{4,0},{8,4},{12,8},{16,12},{20,16},{24,20},{28,24},{1,29},{... | collective-permute-start | bytes 393224 | tf_op jit(solution)/shard_map/ppermute | solution.py:201
  62.4 7.8 %collective-permute-start.12 = (bf16[4,2,64,128]{3,2,1,0:T(8,128)(2,1)S(1)}, bf16[4,2,64,128]{3,2,1,0:T(8,128)(2,1)S(1)}, u32[]{:S(2)}, u32[]{:S(2)}) collective-permute-start(bf16[4,2,64,128]{3,2,1,0:T(8,128)(2,1)S(1)} %get-tuple-element.35), channel_id=1, source_target_pairs={{0,4},{4,8},{8,12},{12,16},{16,20},{20,24},{24,28},{28,0},{1,5},{5... | collective-permute-start | bytes 393224 | tf_op jit(solution)/shard_map/ppermute | solution.py:201
  70.2 7.6 %collective-permute-start.16 = (bf16[4,2,64,128]{3,2,1,0:T(8,128)(2,1)S(1)}, bf16[4,2,64,128]{3,2,1,0:T(8,128)(2,1)S(1)}, u32[]{:S(2)}, u32[]{:S(2)}) collective-permute-start(bf16[4,2,64,128]{3,2,1,0:T(8,128)(2,1)S(1)} %add_convert_fusion.1), channel_id=1, source_target_pairs={{0,8},{4,12},{8,16},{12,20},{16,24},{20,28},{24,0},{28,4},{1,9},{5... | collective-permute-start | bytes 393224 | tf_op jit(solution)/shard_map/ppermute | solution.py:201
  70.6 7.9 %collective-permute-start.15 = (bf16[4,2,64,128]{3,2,1,0:T(8,128)(2,1)S(1)}, bf16[4,2,64,128]{3,2,1,0:T(8,128)(2,1)S(1)}, u32[]{:S(2)}, u32[]{:S(2)}) collective-permute-start(bf16[4,2,64,128]{3,2,1,0:T(8,128)(2,1)S(1)} %add_convert_fusion.2), channel_id=1, source_target_pairs={{0,24},{4,28},{8,0},{12,4},{16,8},{20,12},{24,16},{28,20},{1,25},{... | collective-permute-start | bytes 393224 | tf_op jit(solution)/shard_map/ppermute | solution.py:201
  74.6 6.2 %collective-permute-start.14 = (bf16[4,2,64,128]{3,2,1,0:T(8,128)(2,1)S(1)}, bf16[4,2,64,128]{3,2,1,0:T(8,128)(2,1)S(1)}, u32[]{:S(2)}, u32[]{:S(2)}) collective-permute-start(bf16[4,2,64,128]{3,2,1,0:T(8,128)(2,1)S(1)} %get-tuple-element.50), channel_id=1, source_target_pairs={{0,4},{4,8},{8,12},{12,16},{16,20},{20,24},{24,28},{28,0},{1,5},{5... | collective-permute-start | bytes 393224 | tf_op jit(solution)/shard_map/ppermute | solution.py:201
  75.4 5.4 %collective-permute-start.13 = (bf16[4,2,64,128]{3,2,1,0:T(8,128)(2,1)S(1)}, bf16[4,2,64,128]{3,2,1,0:T(8,128)(2,1)S(1)}, u32[]{:S(2)}, u32[]{:S(2)}) collective-permute-start(bf16[4,2,64,128]{3,2,1,0:T(8,128)(2,1)S(1)} %get-tuple-element.49), channel_id=1, source_target_pairs={{0,28},{4,0},{8,4},{12,8},{16,12},{20,16},{24,20},{28,24},{1,29},{... | collective-permute-start | bytes 393224 | tf_op jit(solution)/shard_map/ppermute | solution.py:201
  80.9 9.5 %collective-permute-start.17 = (bf16[2,64,128]{2,1,0:T(8,128)(2,1)S(1)}, bf16[2,64,128]{2,1,0:T(8,128)(2,1)S(1)}, u32[]{:S(2)}, u32[]{:S(2)}) collective-permute-start(bf16[2,64,128]{2,1,0:T(8,128)(2,1)S(1)} %get-tuple-element.71), channel_id=1, source_target_pairs={{0,3},{1,0},{2,1},{3,2},{4,7},{5,4},{6,5},{7,6},{8,11},{9,8},{10,9... | collective-permute-start | bytes 98312 | tf_op jit(solution)/shard_map/ppermute | solution.py:207
  82.8 18.0 %all-to-all-start.1 = ((bf16[4,1280,128]{2,1,0:T(8,128)(2,1)}), bf16[4,1280,128]{2,1,0:T(8,128)(2,1)S(1)}, u32[]{:S(2)}, u32[]{:S(2)}) async-start(bf16[4,1280,128]{2,1,0:T(8,128)(2,1)} %get-tuple-element.47), calls=%async_computation.1 | async-start | bytes 2621440 | tf_op jit(solution)/shard_map/all_to_all | solution.py:204
  86.3 13.0 %collective-permute-start.18 = (bf16[2,64,128]{2,1,0:T(8,128)(2,1)S(1)}, bf16[2,64,128]{2,1,0:T(8,128)(2,1)S(1)}, u32[]{:S(2)}, u32[]{:S(2)}) collective-permute-start(bf16[2,64,128]{2,1,0:T(8,128)(2,1)S(1)} %get-tuple-element.70), channel_id=1, source_target_pairs={{0,2},{1,3},{2,0},{3,1},{4,6},{5,7},{6,4},{7,5},{8,10},{9,11},{10,... | collective-permute-start | bytes 98312 | tf_op jit(solution)/shard_map/ppermute | solution.py:207
  89.8 9.5 %collective-permute-start.19 = (bf16[2,64,128]{2,1,0:T(8,128)(2,1)S(1)}, bf16[2,64,128]{2,1,0:T(8,128)(2,1)S(1)}, u32[]{:S(2)}, u32[]{:S(2)}) collective-permute-start(bf16[2,64,128]{2,1,0:T(8,128)(2,1)S(1)} %get-tuple-element.68), channel_id=1, source_target_pairs={{0,1},{1,2},{2,3},{3,0},{4,5},{5,6},{6,7},{7,4},{8,9},{9,10},{10,1... | collective-permute-start | bytes 98312 | tf_op jit(solution)/shard_map/ppermute | solution.py:207

commit v5 on v3

--- a/solution.py
+++ b/solution.py
@@ -8,15 +8,77 @@
 from jax.sharding import Mesh, PartitionSpec as P
 
 LOG2E = 1.4426950408889634
-CHUNK = 512
+CHUNK = 768
+FORWARD_CHUNK = 256
 f32 = jnp.float32
 bf16 = jnp.bfloat16
 NT = (((1,), (1,)), ((), ()))
 NN = (((1,), (0,)), ((), ()))
+TN = (((0,), (0,)), ((), ()))
 
 
 def dot(a, b, dims):
     return lax.dot_general(a, b, dims, preferred_element_type=f32)
+
+
+def sorting(n, token_rows, head_rows):
+    per_head = n // 4
+    o = lax.broadcasted_iota(jnp.int32, (n, n), 0)
+    i = lax.broadcasted_iota(jnp.int32, (n, n), 1)
+    head = o // per_head
+    rest = o % per_head
+    source = (rest // head_rows) * token_rows + head * head_rows + rest % head_rows
+    return jnp.where(i == source, 1.0, 0.0).astype(bf16)
+
+
+def sort_rows(order, x):
+    return dot(order, x, NN).astype(bf16)
+
+
+def unsort_rows(order, x):
+    return lax.dot_general(order, x, TN, preferred_element_type=f32).astype(bf16)
+
+
+def pack_prompt(k_ref, v_ref, out):
+    n = k_ref.shape[0]
+    order = sorting(n, 4, 1)
+    for j, ref in enumerate((k_ref, v_ref)):
+        x = sort_rows(order, ref[...])
+        for h in range(4):
+            out[h, j] = x[h * (n // 4):(h + 1) * (n // 4), :]
+
+
+def pack_rows(length, q, g, k, v, out, *, T, G):
+    R = T * G
+    n = 256
+    order = sorting(n, 4 * G, G)
+    part = n // 4
+    row_pos = lax.broadcasted_iota(jnp.int32, (part, 128), 0) // G
+    live = length[0]
+    for b in range(4 * R // n):
+        x = sort_rows(order, q[b * n:(b + 1) * n, :])
+        y = sort_rows(order, g[b * n:(b + 1) * n, :])
+        alive = row_pos + b * (part // G) < live
+        for h in range(4):
+            at = slice(b * part, (b + 1) * part)
+            out[h, at, :] = x[h * part:(h + 1) * part, :]
+            z = y[h * part:(h + 1) * part, :]
+            out[h, slice(R + b * part, R + (b + 1) * part), :] = jnp.where(alive, z, jnp.zeros_like(z))
+    order = sorting(n, 4, 1)
+    for b in range(4 * T // n):
+        x = sort_rows(order, k[b * n:(b + 1) * n, :])
+        y = sort_rows(order, v[b * n:(b + 1) * n, :])
+        for h in range(4):
+            at = 2 * R + b * part
+            out[h, at:at + part, :] = x[h * part:(h + 1) * part, :]
+            out[h, at + T:at + T + part, :] = y[h * part:(h + 1) * part, :]
+
+
+def unpack_prompt(x, k_out, v_out):
+    n = k_out.shape[0]
+    order = sorting(n, 4, 1)
+    for j, ref in enumerate((k_out, v_out)):
+        ref[...] = unsort_rows(order, jnp.concatenate([x[h, j] for h in range(4)], axis=0))
 
 
 def spans(total, size):
@@ -62,26 +124,40 @@
     key_pos = lax.broadcasted_iota(jnp.int32, (T, R), 0)
     row_pos = lax.broadcasted_iota(jnp.int32, (T, R), 1) // G
     own = slice(nk, nk + T)
+    parts = spans(nk, FORWARD_CHUNK) + [own]
+
+    def score(r, ks, top):
+        qr = pack[r, 0:R, :]
+        if ks is own:
+            s = dot(pack[r, 2 * R:2 * R + T, :], qr, NT)
+            s = jnp.where(key_pos <= row_pos, s, -1e30)
+        else:
+            s = dot(K[ks, :], qr, NT)
+        S[r % 2, ks, :] = s
+        return jnp.maximum(top, jnp.max(s.reshape(s.shape[0] // 8, 8, R), axis=0))
+
+    low = jnp.full((8, R), -jnp.inf, f32)
+    top = low
+    for ks in parts:
+        top = score(0, ks, top)
     for r in range(4):
         rows = slice(r * R, (r + 1) * R)
-        qr = pack[r, 0:R, :]
-        kr = pack[r, 2 * R:2 * R + T, :]
-        vr = pack[r, 2 * R + T:2 * R + 2 * T, :]
-        top = jnp.full((8, R), -jnp.inf, f32)
-        for ks in spans(nk, CHUNK):
-            top = scores_into(S, ks, dot(K[ks, :], qr, NT), top)
-        s = jnp.where(key_pos <= row_pos, dot(kr, qr, NT), -1e30)
-        top = scores_into(S, own, s, top)
         top = jnp.max(top, axis=0, keepdims=True) * (C * LOG2E)
         top_ref[0:1, rows] = top
-        p = jnp.exp2(S[own, :] * (C * LOG2E) - top).astype(bf16)
-        Pm[own, rows] = p
-        acc = dot(jnp.concatenate([vr.T, jnp.ones((16, T), bf16)], axis=0), p, NN)
-        for ks in spans(nk, CHUNK):
-            p = jnp.exp2(S[ks, :] * (C * LOG2E) - top).astype(bf16)
+        vr = pack[r, 2 * R + T:2 * R + 2 * T, :]
+        acc = jnp.zeros((D + 16, R), f32)
+        later = low
+        for ks in parts:
+            if r < 3:
+                later = score(r + 1, ks, later)
+            p = jnp.exp2(S[r % 2, ks, :] * (C * LOG2E) - top).astype(bf16)
             Pm[ks, rows] = p
-            acc = acc + dot(VT[:, ks], p, NN)
+            if ks is own:
+                acc = acc + dot(jnp.concatenate([vr.T, jnp.ones((16, T), bf16)], axis=0), p, NN)
+            else:
+                acc = acc + dot(VT[:, ks], p, NN)
         acc_ref[:, rows] = acc
+        top = later
 
 
 def far_both(
@@ -178,6 +254,19 @@
         out[r, R:2 * R, :] = dq.T.astype(bf16)
 
 
+VMEM_REF = pl.BlockSpec(memory_space=pltpu.VMEM)
+
+
+def small_call(body, name, out_shape, in_specs, *args):
+    return pl.pallas_call(
+        body,
+        out_shape=out_shape,
+        in_specs=in_specs,
+        compiler_params=pltpu.CompilerParams(vmem_limit_bytes=16 * 2**20),
+        name=name,
+    )(*args)
+
+
 def call(body, name, out_shape, scratch, flops, *args):
     return pl.pallas_call(
         body,
@@ -203,24 +292,27 @@
     def swap_y(x):
         return lax.all_to_all(x, "y", 0, 0, tiled=True)
 
-    kv = jnp.stack([prompt_keys, prompt_value_rows], axis=0)
-    kv = swap_y(jnp.transpose(kv, (2, 0, 1, 3)))
+    spots = prompt_keys.shape[0]
+
+    def flat(x):
+        return x.reshape(-1, D)
+
+    kv = small_call(
+        pack_prompt,
+        "pack_prompt",
+        jax.ShapeDtypeStruct((KH, 2, spots, D), bf16),
+        [VMEM_REF] * 2,
+        flat(prompt_keys), flat(prompt_value_rows),
+    )
+    kv = swap_y(kv)
 
     live = (jnp.arange(T) < lengths[0])[:, None, None]
-    masked = jnp.where(live, grad_out[0], jnp.zeros((), bf16))
-
-    def by_head(x, n):
-        x = x.reshape(T, KH, n, D)
-        return jnp.transpose(x, (1, 0, 2, 3)).reshape(KH, T * n, D)
-
-    pack = jnp.concatenate(
-        [
-            by_head(queries, G),
-            by_head(masked, G),
-            by_head(response_keys, 1),
-            by_head(response_values, 1),
-        ],
-        axis=1,
+    pack = small_call(
+        functools.partial(pack_rows, T=T, G=G),
+        "pack_rows",
+        jax.ShapeDtypeStruct((KH, 2 * R + 2 * T, D), bf16),
+        [pl.BlockSpec(memory_space=pltpu.SMEM)] + [VMEM_REF] * 4,
+        lengths, flat(queries), flat(grad_out), flat(response_keys), flat(response_values),
     )
     kv, pack = lax.optimization_barrier((kv, pack))
     pack = swap_y(pack)
@@ -235,7 +327,6 @@
     near = (kv, from_1, from_m1, from_2, from_m2)
     far = (from_3, from_m3, from_4)
     block = jax.ShapeDtypeStruct(kv.shape, bf16)
-    spots = kv.shape[2]
     near_keys = 5 * 4 * spots
     far_keys = 3 * 4 * spots
     rows = 4 * R
@@ -257,7 +348,7 @@
         [
             pltpu.VMEM((near_keys, D), bf16),
             pltpu.VMEM((near_keys, D), bf16),
-            pltpu.VMEM((near_keys + T, R), f32),
+            pltpu.VMEM((2, near_keys + T, R), f32),
             pltpu.VMEM((D + 16, near_keys), bf16),
         ],
         cost(2, near_keys + T),
@@ -316,6 +407,14 @@
     total, home = lax.optimization_barrier((total.astype(bf16), home))
     total = swap_y(total)
 
+    grad_k, grad_v = small_call(
+        unpack_prompt,
+        "unpack_prompt",
+        (jax.ShapeDtypeStruct((spots * KH, D), bf16),) * 2,
+        [VMEM_REF],
+        total,
+    )
+
     def by_token(x, n):
         x = x.reshape(KH, T, n, D)
         return jnp.transpose(x, (1, 0, 2, 3)).reshape(1, T, KH * n, D)
@@ -327,8 +426,8 @@
         by_token(home[:, R:2 * R], G),
         by_token(home[:, 2 * R:2 * R + T], 1),
         by_token(home[:, 2 * R + T:2 * R + 2 * T], 1),
-        jnp.transpose(total[:, 0], (1, 0, 2)),
-        jnp.transpose(total[:, 1], (1, 0, 2)),
+        grad_k.reshape(spots, KH, D),
+        grad_v.reshape(spots, KH, D),
     )
 
 

time: 90.4 us -> 92.8 us (1.027)
  starting transfers between devices: 42.6 us -> 45.5 us
  waiting for transfers between devices: 16.2 us -> 13.3 us
  Pallas kernels: 19.2 us -> 21.8 us
  other arithmetic: 3.96 us -> 1.84 us
  local copies, waits for them, and re-layouts: 6.37 us -> 8.32 us
    unnamed x10 -> x14, local copies, waits for them, and re-layouts: 2.89 us -> 7.07 us
    pallas_call x0 -> x3, Pallas kernels: none -> 3.71 us  [small_call(): pl.pallas_call(body, out_shape=out_shape, in_specs=in_specs, compiler_par...]
    ppermute x14, starting transfers between devices: 27.7 us -> 29.4 us  [over_z(): return lax.ppermute(x, 'z', [(i, (i + k) % 8) for i in range(8)])]
    all_to_all x4, waiting for transfers between devices: 7.48 us -> 5.88 us  [swap_y(): return lax.all_to_all(x, 'y', 0, 0, tiled=True)]
    ppermute x14, waiting for transfers between devices: 8.76 us -> 7.37 us  [over_z(): return lax.ppermute(x, 'z', [(i, (i + k) % 8) for i in range(8)])]
    reshape x2 -> x0, local copies, waits for them, and re-layouts: 1.26 us -> none  [the longest x1 1.23 us: by_head(): x = x.reshape(T, KH, n, D)]
    all_to_all x4, starting transfers between devices: 14.9 us -> 16.1 us  [swap_y(): return lax.all_to_all(x, 'y', 0, 0, tiled=True)]
    concatenate x1 -> x0, other arithmetic: 1.17 us -> none  [on_device(): jnp.concatenate([by_head(queries, G), by_head(masked, G), by_head(respons...]
  transfers between devices with their start and end apart: 18 -> 18, of which waited for: 10 -> 9; matrix products, arithmetic and copies ran while one was open for 8% -> 5% of each run, Pallas kernels for 14% -> 15%
where the time goes in v5:
time: 92.8 us; the launch traced here: 92.1 us
  starting transfers between devices  45.5 us (49%)
  Pallas kernels  21.8 us (23%)
  waiting for transfers between devices  13.3 us (14%)
  local copies, waits for them, and re-layouts  8.32 us (9%)
  other arithmetic  1.84 us (2%)
  between operations  1.4 us (2%)
    ppermute x14, starting transfers between devices, over_z(): return lax.ppermute(x, 'z', [(i, (i + k) % 8) for i in range(8)])  29.4 us
    pallas_call x3, Pallas kernels, call(): pl.pallas_call(body, out_shape=out_shape, scratch_shapes=scratch, compile...  18.1 us
    all_to_all x4, starting transfers between devices, swap_y(): return lax.all_to_all(x, 'y', 0, 0, tiled=True)  16.1 us
    ppermute x14, waiting for transfers between devices, over_z(): return lax.ppermute(x, 'z', [(i, (i + k) % 8) for i in range(8)])  7.37 us
    unnamed x14, local copies, waits for them, and re-layouts  7.07 us
    all_to_all x4, waiting for transfers between devices, swap_y(): return lax.all_to_all(x, 'y', 0, 0, tiled=True)  5.88 us
    pallas_call x3, Pallas kernels, small_call(): pl.pallas_call(body, out_shape=out_shape, in_specs=in_specs, compiler_par...  3.71 us
  transfers between devices with their start and end apart: 18, of which 9 were waited for; matrix products, arithmetic and copies ran while one was open for 5% of the time, Pallas kernels for 15%

profile of v5, /device:TPU:4, one launch (start us, length us, event | category | flops | bytes accessed | tf_op | source)
XLA Modules:
  0.0 92.1 jit_solution(4551561568355432494)
XLA Ops:
  0.6 0.8 copy-done.4
  1.5 0.8 copy-done.5
  2.3 0.9 pack_prompt.1
  3.2 4.5 %all-to-all-start = ((bf16[4,2,64,128]{3,2,1,0:T(8,128)(2,1)}), bf16[4,2,64,128]{3,2,1,0:T(8,128)(2,1)S(1)}, u32[]{:S(2)}, u32[]{:S(2)}) async-start(bf16[4,2,64,128]{3,2,1,0:T(8,128)(2,1)} %pack_prompt.1), calls=%async_computation | async-start | bytes 262144 | tf_op jit(solution)/shard_map/all_to_all | solution.py:293
  8.3 0.0 copy-start
  8.3 1.0 %copy-done = bf16[1,128,16,128]{3,2,1,0:T(8,128)(2,1)S(1)} copy-done((bf16[1,128,16,128]{3,2,1,0:T(8,128)(2,1)S(1)}, bf16[1,128,16,128]{3,2,1,0:T(8,128)(2,1)}, u32[]{:S(2)}) %copy-start) | copy-done | bytes 524312
  9.3 1.0 %copy-done.1 = bf16[1,128,16,128]{3,2,1,0:T(8,128)(2,1)S(1)} copy-done((bf16[1,128,16,128]{3,2,1,0:T(8,128)(2,1)S(1)}, bf16[1,128,16,128]{3,2,1,0:T(8,128)(2,1)}, u32[]{:S(2)}) %copy-start.1) | copy-done | bytes 524312
  10.4 0.9 copy-done.2
  11.3 0.9 copy-done.3
  12.2 1.9 %pack_rows.1 = bf16[4,1280,128]{2,1,0:T(8,128)(2,1)} custom-call(s32[1]{0:T(128)} %copy.17.length, bf16[2048,128]{1,0:T(8,128)(2,1)S(1)} %bitcast.30, bf16[2048,128]{1,0:T(8,128)(2,1)S(1)} %bitcast.31, bf16[512,128]{1,0:T(8,128)(2,1)S(1)} %bitcast.32, bf16[512,128]{1,0:T(8,128)(2,1)S(1)} %bitcast.33), custom_call_target="tpu_custom_call" | custom-call | tf_op jit(solution)/shard_map/pack_rows/pallas_call | solution.py:261
  14.1 4.8 %all-to-all-start.1 = ((bf16[4,1280,128]{2,1,0:T(8,128)(2,1)}), bf16[4,1280,128]{2,1,0:T(8,128)(2,1)S(1)}, u32[]{:S(2)}, u32[]{:S(2)}) async-start(bf16[4,1280,128]{2,1,0:T(8,128)(2,1)} %pack_rows.1), calls=%async_computation.1 | async-start | bytes 2621440 | tf_op jit(solution)/shard_map/all_to_all | solution.py:293
  18.9 3.3 %collective-permute-start.2 = (bf16[4,2,64,128]{3,2,1,0:T(8,128)(2,1)S(1)}, bf16[4,2,64,128]{3,2,1,0:T(8,128)(2,1)S(1)}, u32[]{:S(2)}, u32[]{:S(2)}) collective-permute-start(bf16[4,2,64,128]{3,2,1,0:T(8,128)(2,1)S(1)} %all-to-all-done.kv0), channel_id=1, source_target_pairs={{0,8},{4,12},{8,16},{12,20},{16,24},{20,28},{24,0},{28,4},{1,9},{5... | collective-permute-start | bytes 393224 | tf_op jit(solution)/shard_map/ppermute | solution.py:290
  22.2 3.0 %collective-permute-start.3 = (bf16[4,2,64,128]{3,2,1,0:T(8,128)(2,1)S(1)}, bf16[4,2,64,128]{3,2,1,0:T(8,128)(2,1)S(1)}, u32[]{:S(2)}, u32[]{:S(2)}) collective-permute-start(bf16[4,2,64,128]{3,2,1,0:T(8,128)(2,1)S(1)} %all-to-all-done.kv0), channel_id=1, source_target_pairs={{0,24},{4,28},{8,0},{12,4},{16,8},{20,12},{24,16},{28,20},{1,25},{... | collective-permute-start | bytes 393224 | tf_op jit(solution)/shard_map/ppermute | solution.py:290
  25.2 2.5 %collective-permute-start.1 = (bf16[4,2,64,128]{3,2,1,0:T(8,128)(2,1)S(1)}, bf16[4,2,64,128]{3,2,1,0:T(8,128)(2,1)S(1)}, u32[]{:S(2)}, u32[]{:S(2)}) collective-permute-start(bf16[4,2,64,128]{3,2,1,0:T(8,128)(2,1)S(1)} %all-to-all-done.kv0), channel_id=1, source_target_pairs={{0,28},{4,0},{8,4},{12,8},{16,12},{20,16},{24,20},{28,24},{1,29},{... | collective-permute-start | bytes 393224 | tf_op jit(solution)/shard_map/ppermute | solution.py:290
  27.7 0.0 collective-permute-start
  27.7 0.9 %collective-permute-done.2.kv3 = bf16[4,2,64,128]{3,2,1,0:T(8,128)(2,1)S(1)} collective-permute-done((bf16[4,2,64,128]{3,2,1,0:T(8,128)(2,1)S(1)}, bf16[4,2,64,128]{3,2,1,0:T(8,128)(2,1)S(1)}, u32[]{:S(2)}, u32[]{:S(2)}) %collective-permute-start.2) | collective-permute-done | bytes 131104 | tf_op jit(solution)/shard_map/ppermute | solution.py:290
  28.6 3.5 %collective-permute-start.6 = (bf16[4,2,64,128]{3,2,1,0:T(8,128)(2,1)S(1)}, bf16[4,2,64,128]{3,2,1,0:T(8,128)(2,1)S(1)}, u32[]{:S(2)}, u32[]{:S(2)}) collective-permute-start(bf16[4,2,64,128]{3,2,1,0:T(8,128)(2,1)S(1)} %collective-permute-done.2.kv3), channel_id=1, source_target_pairs={{0,8},{4,12},{8,16},{12,20},{16,24},{20,28},{24,0},{28,4},{1,9},{5... | collective-permute-start | bytes 393224 | tf_op jit(solution)/shard_map/ppermute | solution.py:290
  32.1 0.4 collective-permute-start.4
  32.5 3.0 %collective-permute-start.5 = (bf16[4,2,64,128]{3,2,1,0:T(8,128)(2,1)S(1)}, bf16[4,2,64,128]{3,2,1,0:T(8,128)(2,1)S(1)}, u32[]{:S(2)}, u32[]{:S(2)}) collective-permute-start(bf16[4,2,64,128]{3,2,1,0:T(8,128)(2,1)S(1)} %collective-permute-done.3.kv4), channel_id=1, source_target_pairs={{0,28},{4,0},{8,4},{12,8},{16,12},{20,16},{24,20},{28,24},{1,29},{... | collective-permute-start | bytes 393224 | tf_op jit(solution)/shard_map/ppermute | solution.py:290
  35.5 0.2 collective-permute-done.kv1
  35.7 0.5 all-to-all-done.1.pack
  36.3 4.7 %near_forward.1 = (bf16[1408,2048]{1,0:T(8,128)(2,1)S(1)}, f32[144,2048]{1,0:T(8,128)S(1)}, f32[8,2048]{1,0:T(8,128)S(1)}) custom-call(bf16[4,1280,128]{2,1,0:T(8,128)(2,1)S(1)} %all-to-all-done.1.pack, bf16[4,2,64,128]{3,2,1,0:T(8,128)(2,1)S(1)} %all-to-all-done.kv0, bf16[4,2,64,128]{3,2,1,0:T(8,128)(2,1)S(1)} %collective-permute-done.kv1, ...), custom_call_target="tpu_custom_call" | custom-call | flops 1476395008 | bytes 4194304 | tf_op jit(solution)/shard_map/near_forward/pallas_call | solution.py:271
  41.0 1.0 %collective-permute-done.4.kv0 = bf16[4,2,64,128]{3,2,1,0:T(8,128)(2,1)S(1)} collective-permute-done((bf16[4,2,64,128]{3,2,1,0:T(8,128)(2,1)S(1)}, bf16[4,2,64,128]{3,2,1,0:T(8,128)(2,1)S(1)}, u32[]{:S(2)}, u32[]{:S(2)}) %collective-permute-start.4) | collective-permute-done | bytes 131104 | tf_op jit(solution)/shard_map/ppermute | solution.py:290
  42.0 6.0 %far_both.1 = (bf16[4,512,128]{2,1,0:T(8,128)(2,1)S(1)}, f32[8,2048]{1,0:T(8,128)S(1)}, bf16[2048,128]{1,0:T(8,128)(2,1)S(1)}, bf16[2048,128]{1,0:T(8,128)(2,1)S...) custom-call(bf16[4,1280,128]{2,1,0:T(8,128)(2,1)S(1)} %all-to-all-do, ...), custom_call_target="tpu_custom_call" | custom-call | flops 2415919104 | bytes 4194304 | tf_op jit(solution)/shard_map/far_both/pallas_call | solution.py:271
  48.0 5.4 %collective-permute-start.7 = (bf16[4,2,64,128]{3,2,1,0:T(8,128)(2,1)S(1)}, bf16[4,2,64,128]{3,2,1,0:T(8,128)(2,1)S(1)}, u32[]{:S(2)}, u32[]{:S(2)}) collective-permute-start(bf16[4,2,64,128]{3,2,1,0:T(8,128)(2,1)S(1)} %get-tuple-element.48), channel_id=1, source_target_pairs={{0,24},{4,28},{8,0},{12,4},{16,8},{20,12},{24,16},{28,20},{1,25},{... | collective-permute-start | bytes 393224 | tf_op jit(solution)/shard_map/ppermute | solution.py:290
  53.4 1.0 %collective-permute-start.8 = (bf16[4,2,64,128]{3,2,1,0:T(8,128)(2,1)S(1)}, bf16[4,2,64,128]{3,2,1,0:T(8,128)(2,1)S(1)}, u32[]{:S(2)}, u32[]{:S(2)}) collective-permute-start(bf16[4,2,64,128]{3,2,1,0:T(8,128)(2,1)S(1)} %get-tuple-element.49), channel_id=1, source_target_pairs={{0,28},{4,0},{8,4},{12,8},{16,12},{20,16},{24,20},{28,24},{1,29},{... | collective-permute-start | bytes 393224 | tf_op jit(solution)/shard_map/ppermute | solution.py:290
  54.4 1.0 %collective-permute-start.9 = (bf16[4,2,64,128]{3,2,1,0:T(8,128)(2,1)S(1)}, bf16[4,2,64,128]{3,2,1,0:T(8,128)(2,1)S(1)}, u32[]{:S(2)}, u32[]{:S(2)}) collective-permute-start(bf16[4,2,64,128]{3,2,1,0:T(8,128)(2,1)S(1)} %get-tuple-element.50), channel_id=1, source_target_pairs={{0,4},{4,8},{8,12},{12,16},{16,20},{20,24},{24,28},{28,0},{1,5},{5... | collective-permute-start | bytes 393224 | tf_op jit(solution)/shard_map/ppermute | solution.py:290
  55.4 7.3 %near_backward.1 = (bf16[4,1280,128]{2,1,0:T(8,128)(2,1)}, bf16[4,2,64,128]{3,2,1,0:T(8,128)(2,1)S(1)}, bf16[4,2,64,128]{3,2,1,0:T(8,128)(2,1)S(1)}, bf16[4,2,64...) custom-call(bf16[4,1280,128]{2,1,0:T(8,128)(2,1)S(1)} %all-to-all-done.1.pack, ...), custom_call_target="tpu_custom_call" | custom-call | flops 2952790016 | bytes 4194304 | tf_op jit(solution)/shard_map/near_backward/pallas_call | solution.py:271
  62.8 3.6 %all-to-all-start.2 = ((bf16[4,1280,128]{2,1,0:T(8,128)(2,1)}), bf16[4,1280,128]{2,1,0:T(8,128)(2,1)S(1)}, u32[]{:S(2)}, u32[]{:S(2)}) async-start(bf16[4,1280,128]{2,1,0:T(8,128)(2,1)} %get-tuple-element.63), calls=%async_computation.2 | async-start | bytes 2621440 | tf_op jit(solution)/shard_map/all_to_all | solution.py:293
  66.4 0.5 collective-permute-start.13
  66.9 0.1 add_convert_fusion.2
  67.0 3.8 %collective-permute-start.12 = (bf16[4,2,64,128]{3,2,1,0:T(8,128)(2,1)S(1)}, bf16[4,2,64,128]{3,2,1,0:T(8,128)(2,1)S(1)}, u32[]{:S(2)}, u32[]{:S(2)}) collective-permute-start(bf16[4,2,64,128]{3,2,1,0:T(8,128)(2,1)S(1)} %add_convert_fusion.2), channel_id=1, source_target_pairs={{0,24},{4,28},{8,0},{12,4},{16,8},{20,12},{24,16},{28,20},{1,25},{... | collective-permute-start | bytes 393224 | tf_op jit(solution)/shard_map/ppermute | solution.py:290
  70.8 1.0 %collective-permute-start.10 = (bf16[4,2,64,128]{3,2,1,0:T(8,128)(2,1)S(1)}, bf16[4,2,64,128]{3,2,1,0:T(8,128)(2,1)S(1)}, u32[]{:S(2)}, u32[]{:S(2)}) collective-permute-start(bf16[4,2,64,128]{3,2,1,0:T(8,128)(2,1)S(1)} %get-tuple-element.56), channel_id=1, source_target_pairs={{0,28},{4,0},{8,4},{12,8},{16,12},{20,16},{24,20},{28,24},{1,29},{... | collective-permute-start | bytes 393224 | tf_op jit(solution)/shard_map/ppermute | solution.py:290
  71.8 1.0 %collective-permute-start.11 = (bf16[4,2,64,128]{3,2,1,0:T(8,128)(2,1)S(1)}, bf16[4,2,64,128]{3,2,1,0:T(8,128)(2,1)S(1)}, u32[]{:S(2)}, u32[]{:S(2)}) collective-permute-start(bf16[4,2,64,128]{3,2,1,0:T(8,128)(2,1)S(1)} %get-tuple-element.57), channel_id=1, source_target_pairs={{0,4},{4,8},{8,12},{12,16},{16,20},{20,24},{24,28},{28,0},{1,5},{5... | collective-permute-start | bytes 393224 | tf_op jit(solution)/shard_map/ppermute | solution.py:290
  72.8 2.6 %collective-permute-done.13 = bf16[4,2,64,128]{3,2,1,0:T(8,128)(2,1)S(1)} collective-permute-done((bf16[4,2,64,128]{3,2,1,0:T(8,128)(2,1)S(1)}, bf16[4,2,64,128]{3,2,1,0:T(8,128)(2,1)S(1)}, u32[]{:S(2)}, u32[]{:S(2)}) %collective-permute-start.13) | collective-permute-done | bytes 131104 | tf_op jit(solution)/shard_map/ppermute | solution.py:290
  75.4 2.0 %collective-permute-done.10 = bf16[4,2,64,128]{3,2,1,0:T(8,128)(2,1)S(1)} collective-permute-done((bf16[4,2,64,128]{3,2,1,0:T(8,128)(2,1)S(1)}, bf16[4,2,64,128]{3,2,1,0:T(8,128)(2,1)S(1)}, u32[]{:S(2)}, u32[]{:S(2)}) %collective-permute-start.10) | collective-permute-done | bytes 131104 | tf_op jit(solution)/shard_map/ppermute | solution.py:290
  77.3 0.6 collective-permute-done.11
  77.9 0.7 add_convert_fusion
  78.7 3.2 %all-to-all-done.2 = bf16[4,1280,128]{2,1,0:T(8,128)(2,1)S(1)} async-done(((bf16[4,1280,128]{2,1,0:T(8,128)(2,1)}), bf16[4,1280,128]{2,1,0:T(8,128)(2,1)S(1)}, u32[]{:S(2)}, u32[]{:S(2)}) %all-to-all-start.2) | async-done | bytes 1310752 | tf_op jit(solution)/shard_map/all_to_all | solution.py:293
  81.9 3.3 %all-to-all-start.3 = ((bf16[4,2,64,128]{3,2,1,0:T(8,128)(2,1)}), bf16[4,2,64,128]{3,2,1,0:T(8,128)(2,1)S(1)}, u32[]{:S(2)}, u32[]{:S(2)}) async-start(bf16[4,2,64,128]{3,2,1,0:T(8,128)(2,1)} %add_convert_fusion), calls=%async_computation.3 | async-start | bytes 262144 | tf_op jit(solution)/shard_map/all_to_all | solution.py:293
  85.2 0.1 fusion
  85.3 0.2 copy.13
  85.5 1.0 %broadcast_select_fusion = bf16[1,128,16,128]{3,2,1,0:T(8,128)(2,1)} fusion(bf16[1,128,16,128]{3,2,1,0:T(8,128)(2,1)S(1)} %bitcast.36, pred[128]{0:T(512)(128)(4,1)S(1)} %iota_compare_fusion), kind=kLoop, calls=%fused_computation | loop fusion | flops 262144 | bytes 1048704 | tf_op jit(solution)/shard_map/jit(_where)/select_n | solution.py:423
  86.5 1.0 %copy.14 = bf16[128,4,4,128]{3,2,1,0:T(4,128)(2,1)} copy(bf16[128,4,4,128]{3,2,0,1:T(4,128)(2,1)S(1)} %bitcast.37) | data formatting | bytes 1048576 | tf_op jit(solution)/shard_map/transpose | solution.py:420
  87.5 0.8 copy.16
  88.3 0.8 copy.15
  89.0 2.2 %all-to-all-done.3.x = bf16[4,2,64,128]{3,2,1,0:T(8,128)(2,1)S(1)} async-done(((bf16[4,2,64,128]{3,2,1,0:T(8,128)(2,1)}), bf16[4,2,64,128]{3,2,1,0:T(8,128)(2,1)S(1)}, u32[]{:S(2)}, u32[]{:S(2)}) %all-to-all-start.3) | async-done | bytes 131104 | tf_op jit(solution)/shard_map/all_to_all | solution.py:293
  91.2 0.9 %unpack_prompt.1 = (bf16[256,128]{1,0:T(8,128)(2,1)}, bf16[256,128]{1,0:T(8,128)(2,1)}) custom-call(bf16[4,2,64,128]{3,2,1,0:T(8,128)(2,1)S(1)} %all-to-all-done.3.x), custom_call_target="tpu_custom_call" | custom-call | tf_op jit(solution)/shard_map/unpack_prompt/pallas_call | solution.py:261
  (17 shorter events, 0.1 us)
Async XLA Ops:
  0.6 0.8 copy-start.4
  1.5 0.8 copy-start.5
  3.2 10.9 %all-to-all-start = ((bf16[4,2,64,128]{3,2,1,0:T(8,128)(2,1)}), bf16[4,2,64,128]{3,2,1,0:T(8,128)(2,1)S(1)}, u32[]{:S(2)}, u32[]{:S(2)}) async-start(bf16[4,2,64,128]{3,2,1,0:T(8,128)(2,1)} %pack_prompt.1), calls=%async_computation | async-start | bytes 262144 | tf_op jit(solution)/shard_map/all_to_all | solution.py:293
  8.3 1.0 %copy-start = (bf16[1,128,16,128]{3,2,1,0:T(8,128)(2,1)S(1)}, bf16[1,128,16,128]{3,2,1,0:T(8,128)(2,1)}, u32[]{:S(2)}) copy-start(bf16[1,128,16,128]{3,2,1,0:T(8,128)(2,1)} %param.7) | copy-start | bytes 1572868
  9.3 1.0 %copy-start.1 = (bf16[1,128,16,128]{3,2,1,0:T(8,128)(2,1)S(1)}, bf16[1,128,16,128]{3,2,1,0:T(8,128)(2,1)}, u32[]{:S(2)}) copy-start(bf16[1,128,16,128]{3,2,1,0:T(8,128)(2,1)} %param.13) | copy-start | bytes 1572868
  10.4 0.9 copy-start.2
  11.3 0.9 copy-start.3
  14.1 22.1 %all-to-all-start.1 = ((bf16[4,1280,128]{2,1,0:T(8,128)(2,1)}), bf16[4,1280,128]{2,1,0:T(8,128)(2,1)S(1)}, u32[]{:S(2)}, u32[]{:S(2)}) async-start(bf16[4,1280,128]{2,1,0:T(8,128)(2,1)} %pack_rows.1), calls=%async_computation.1 | async-start | bytes 2621440 | tf_op jit(solution)/shard_map/all_to_all | solution.py:293
  18.9 9.7 %collective-permute-start.2 = (bf16[4,2,64,128]{3,2,1,0:T(8,128)(2,1)S(1)}, bf16[4,2,64,128]{3,2,1,0:T(8,128)(2,1)S(1)}, u32[]{:S(2)}, u32[]{:S(2)}) collective-permute-start(bf16[4,2,64,128]{3,2,1,0:T(8,128)(2,1)S(1)} %all-to-all-done.kv0), channel_id=1, source_target_pairs={{0,8},{4,12},{8,16},{12,20},{16,24},{20,28},{24,0},{28,4},{1,9},{5... | collective-permute-start | bytes 393224 | tf_op jit(solution)/shard_map/ppermute | solution.py:290
  22.2 10.3 %collective-permute-start.3 = (bf16[4,2,64,128]{3,2,1,0:T(8,128)(2,1)S(1)}, bf16[4,2,64,128]{3,2,1,0:T(8,128)(2,1)S(1)}, u32[]{:S(2)}, u32[]{:S(2)}) collective-permute-start(bf16[4,2,64,128]{3,2,1,0:T(8,128)(2,1)S(1)} %all-to-all-done.kv0), channel_id=1, source_target_pairs={{0,24},{4,28},{8,0},{12,4},{16,8},{20,12},{24,16},{28,20},{1,25},{... | collective-permute-start | bytes 393224 | tf_op jit(solution)/shard_map/ppermute | solution.py:290
  25.2 10.3 %collective-permute-start.1 = (bf16[4,2,64,128]{3,2,1,0:T(8,128)(2,1)S(1)}, bf16[4,2,64,128]{3,2,1,0:T(8,128)(2,1)S(1)}, u32[]{:S(2)}, u32[]{:S(2)}) collective-permute-start(bf16[4,2,64,128]{3,2,1,0:T(8,128)(2,1)S(1)} %all-to-all-done.kv0), channel_id=1, source_target_pairs={{0,28},{4,0},{8,4},{12,8},{16,12},{20,16},{24,20},{28,24},{1,29},{... | collective-permute-start | bytes 393224 | tf_op jit(solution)/shard_map/ppermute | solution.py:290
  27.7 8.1 %collective-permute-start = (bf16[4,2,64,128]{3,2,1,0:T(8,128)(2,1)S(1)}, bf16[4,2,64,128]{3,2,1,0:T(8,128)(2,1)S(1)}, u32[]{:S(2)}, u32[]{:S(2)}) collective-permute-start(bf16[4,2,64,128]{3,2,1,0:T(8,128)(2,1)S(1)} %all-to-all-done.kv0), channel_id=1, source_target_pairs={{0,4},{4,8},{8,12},{12,16},{16,20},{20,24},{24,28},{28,0},{1,5},{5... | collective-permute-start | bytes 393224 | tf_op jit(solution)/shard_map/ppermute | solution.py:290
  28.6 12.4 %collective-permute-start.6 = (bf16[4,2,64,128]{3,2,1,0:T(8,128)(2,1)S(1)}, bf16[4,2,64,128]{3,2,1,0:T(8,128)(2,1)S(1)}, u32[]{:S(2)}, u32[]{:S(2)}) collective-permute-start(bf16[4,2,64,128]{3,2,1,0:T(8,128)(2,1)S(1)} %collective-permute-done.2.kv3), channel_id=1, source_target_pairs={{0,8},{4,12},{8,16},{12,20},{16,24},{20,28},{24,0},{28,4},{1,9},{5... | collective-permute-start | bytes 393224 | tf_op jit(solution)/shard_map/ppermute | solution.py:290
  32.1 9.9 %collective-permute-start.4 = (bf16[4,2,64,128]{3,2,1,0:T(8,128)(2,1)S(1)}, bf16[4,2,64,128]{3,2,1,0:T(8,128)(2,1)S(1)}, u32[]{:S(2)}, u32[]{:S(2)}) collective-permute-start(bf16[4,2,64,128]{3,2,1,0:T(8,128)(2,1)S(1)} %collective-permute-done.2.kv3), channel_id=1, source_target_pairs={{0,4},{4,8},{8,12},{12,16},{16,20},{20,24},{24,28},{28,0},{1,5},{5... | collective-permute-start | bytes 393224 | tf_op jit(solution)/shard_map/ppermute | solution.py:290
  32.5 8.5 %collective-permute-start.5 = (bf16[4,2,64,128]{3,2,1,0:T(8,128)(2,1)S(1)}, bf16[4,2,64,128]{3,2,1,0:T(8,128)(2,1)S(1)}, u32[]{:S(2)}, u32[]{:S(2)}) collective-permute-start(bf16[4,2,64,128]{3,2,1,0:T(8,128)(2,1)S(1)} %collective-permute-done.3.kv4), channel_id=1, source_target_pairs={{0,28},{4,0},{8,4},{12,8},{16,12},{20,16},{24,20},{28,24},{1,29},{... | collective-permute-start | bytes 393224 | tf_op jit(solution)/shard_map/ppermute | solution.py:290
  48.0 14.7 %collective-permute-start.7 = (bf16[4,2,64,128]{3,2,1,0:T(8,128)(2,1)S(1)}, bf16[4,2,64,128]{3,2,1,0:T(8,128)(2,1)S(1)}, u32[]{:S(2)}, u32[]{:S(2)}) collective-permute-start(bf16[4,2,64,128]{3,2,1,0:T(8,128)(2,1)S(1)} %get-tuple-element.48), channel_id=1, source_target_pairs={{0,24},{4,28},{8,0},{12,4},{16,8},{20,12},{24,16},{28,20},{1,25},{... | collective-permute-start | bytes 393224 | tf_op jit(solution)/shard_map/ppermute | solution.py:290
  53.4 9.4 %collective-permute-start.8 = (bf16[4,2,64,128]{3,2,1,0:T(8,128)(2,1)S(1)}, bf16[4,2,64,128]{3,2,1,0:T(8,128)(2,1)S(1)}, u32[]{:S(2)}, u32[]{:S(2)}) collective-permute-start(bf16[4,2,64,128]{3,2,1,0:T(8,128)(2,1)S(1)} %get-tuple-element.49), channel_id=1, source_target_pairs={{0,28},{4,0},{8,4},{12,8},{16,12},{20,16},{24,20},{28,24},{1,29},{... | collective-permute-start | bytes 393224 | tf_op jit(solution)/shard_map/ppermute | solution.py:290
  54.4 8.4 %collective-permute-start.9 = (bf16[4,2,64,128]{3,2,1,0:T(8,128)(2,1)S(1)}, bf16[4,2,64,128]{3,2,1,0:T(8,128)(2,1)S(1)}, u32[]{:S(2)}, u32[]{:S(2)}) collective-permute-start(bf16[4,2,64,128]{3,2,1,0:T(8,128)(2,1)S(1)} %get-tuple-element.50), channel_id=1, source_target_pairs={{0,4},{4,8},{8,12},{12,16},{16,20},{20,24},{24,28},{28,0},{1,5},{5... | collective-permute-start | bytes 393224 | tf_op jit(solution)/shard_map/ppermute | solution.py:290
  62.8 19.1 %all-to-all-start.2 = ((bf16[4,1280,128]{2,1,0:T(8,128)(2,1)}), bf16[4,1280,128]{2,1,0:T(8,128)(2,1)S(1)}, u32[]{:S(2)}, u32[]{:S(2)}) async-start(bf16[4,1280,128]{2,1,0:T(8,128)(2,1)} %get-tuple-element.63), calls=%async_computation.2 | async-start | bytes 2621440 | tf_op jit(solution)/shard_map/all_to_all | solution.py:293
  66.4 9.0 %collective-permute-start.13 = (bf16[4,2,64,128]{3,2,1,0:T(8,128)(2,1)S(1)}, bf16[4,2,64,128]{3,2,1,0:T(8,128)(2,1)S(1)}, u32[]{:S(2)}, u32[]{:S(2)}) collective-permute-start(bf16[4,2,64,128]{3,2,1,0:T(8,128)(2,1)S(1)} %add_convert_fusion.1), channel_id=1, source_target_pairs={{0,8},{4,12},{8,16},{12,20},{16,24},{20,28},{24,0},{28,4},{1,9},{5... | collective-permute-start | bytes 393224 | tf_op jit(solution)/shard_map/ppermute | solution.py:290
  67.0 8.4 %collective-permute-start.12 = (bf16[4,2,64,128]{3,2,1,0:T(8,128)(2,1)S(1)}, bf16[4,2,64,128]{3,2,1,0:T(8,128)(2,1)S(1)}, u32[]{:S(2)}, u32[]{:S(2)}) collective-permute-start(bf16[4,2,64,128]{3,2,1,0:T(8,128)(2,1)S(1)} %add_convert_fusion.2), channel_id=1, source_target_pairs={{0,24},{4,28},{8,0},{12,4},{16,8},{20,12},{24,16},{28,20},{1,25},{... | collective-permute-start | bytes 393224 | tf_op jit(solution)/shard_map/ppermute | solution.py:290
  70.8 6.6 %collective-permute-start.10 = (bf16[4,2,64,128]{3,2,1,0:T(8,128)(2,1)S(1)}, bf16[4,2,64,128]{3,2,1,0:T(8,128)(2,1)S(1)}, u32[]{:S(2)}, u32[]{:S(2)}) collective-permute-start(bf16[4,2,64,128]{3,2,1,0:T(8,128)(2,1)S(1)} %get-tuple-element.56), channel_id=1, source_target_pairs={{0,28},{4,0},{8,4},{12,8},{16,12},{20,16},{24,20},{28,24},{1,29},{... | collective-permute-start | bytes 393224 | tf_op jit(solution)/shard_map/ppermute | solution.py:290
  71.8 6.2 %collective-permute-start.11 = (bf16[4,2,64,128]{3,2,1,0:T(8,128)(2,1)S(1)}, bf16[4,2,64,128]{3,2,1,0:T(8,128)(2,1)S(1)}, u32[]{:S(2)}, u32[]{:S(2)}) collective-permute-start(bf16[4,2,64,128]{3,2,1,0:T(8,128)(2,1)S(1)} %get-tuple-element.57), channel_id=1, source_target_pairs={{0,4},{4,8},{8,12},{12,16},{16,20},{20,24},{24,28},{28,0},{1,5},{5... | collective-permute-start | bytes 393224 | tf_op jit(solution)/shard_map/ppermute | solution.py:290
  81.9 9.3 %all-to-all-start.3 = ((bf16[4,2,64,128]{3,2,1,0:T(8,128)(2,1)}), bf16[4,2,64,128]{3,2,1,0:T(8,128)(2,1)S(1)}, u32[]{:S(2)}, u32[]{:S(2)}) async-start(bf16[4,2,64,128]{3,2,1,0:T(8,128)(2,1)} %add_convert_fusion), calls=%async_computation.3 | async-start | bytes 262144 | tf_op jit(solution)/shard_map/all_to_all | solution.py:293

commit v6 on v5

--- a/solution.py
+++ b/solution.py
@@ -39,22 +39,34 @@
     return lax.dot_general(order, x, TN, preferred_element_type=f32).astype(bf16)
 
 
-def pack_prompt(k_ref, v_ref, out):
+def fetch(refs, held, sems):
+    copies = [pltpu.make_async_copy(a, b, sems.at[i]) for i, (a, b) in enumerate(zip(refs, held))]
+    for x in copies:
+        x.start()
+    return copies
+
+
+def pack_prompt(k_ref, v_ref, out, k_held, v_held, sems):
+    copies = fetch((k_ref, v_ref), (k_held, v_held), sems)
     n = k_ref.shape[0]
     order = sorting(n, 4, 1)
-    for j, ref in enumerate((k_ref, v_ref)):
+    for j, ref in enumerate((k_held, v_held)):
+        copies[j].wait()
         x = sort_rows(order, ref[...])
         for h in range(4):
             out[h, j] = x[h * (n // 4):(h + 1) * (n // 4), :]
 
 
-def pack_rows(length, q, g, k, v, out, *, T, G):
+def pack_rows(length, q_ref, g_ref, k_ref, v_ref, out, q, g, k, v, sems, *, T, G):
+    copies = fetch((q_ref, g_ref, k_ref, v_ref), (q, g, k, v), sems)
     R = T * G
     n = 256
     order = sorting(n, 4 * G, G)
     part = n // 4
     row_pos = lax.broadcasted_iota(jnp.int32, (part, 128), 0) // G
     live = length[0]
+    copies[0].wait()
+    copies[1].wait()
     for b in range(4 * R // n):
         x = sort_rows(order, q[b * n:(b + 1) * n, :])
         y = sort_rows(order, g[b * n:(b + 1) * n, :])
@@ -65,6 +77,8 @@
             z = y[h * part:(h + 1) * part, :]
             out[h, slice(R + b * part, R + (b + 1) * part), :] = jnp.where(alive, z, jnp.zeros_like(z))
     order = sorting(n, 4, 1)
+    copies[2].wait()
+    copies[3].wait()
     for b in range(4 * T // n):
         x = sort_rows(order, k[b * n:(b + 1) * n, :])
         y = sort_rows(order, v[b * n:(b + 1) * n, :])
@@ -255,13 +269,15 @@
 
 
 VMEM_REF = pl.BlockSpec(memory_space=pltpu.VMEM)
-
-
-def small_call(body, name, out_shape, in_specs, *args):
+HBM_REF = pl.BlockSpec(memory_space=pltpu.HBM)
+
+
+def small_call(body, name, out_shape, in_specs, scratch, *args):
     return pl.pallas_call(
         body,
         out_shape=out_shape,
         in_specs=in_specs,
+        scratch_shapes=scratch,
         compiler_params=pltpu.CompilerParams(vmem_limit_bytes=16 * 2**20),
         name=name,
     )(*args)
@@ -301,7 +317,8 @@
         pack_prompt,
         "pack_prompt",
         jax.ShapeDtypeStruct((KH, 2, spots, D), bf16),
-        [VMEM_REF] * 2,
+        [HBM_REF] * 2,
+        [pltpu.VMEM((spots * KH, D), bf16)] * 2 + [pltpu.SemaphoreType.DMA((2,))],
         flat(prompt_keys), flat(prompt_value_rows),
     )
     kv = swap_y(kv)
@@ -311,7 +328,14 @@
         functools.partial(pack_rows, T=T, G=G),
         "pack_rows",
         jax.ShapeDtypeStruct((KH, 2 * R + 2 * T, D), bf16),
-        [pl.BlockSpec(memory_space=pltpu.SMEM)] + [VMEM_REF] * 4,
+        [pl.BlockSpec(memory_space=pltpu.SMEM)] + [HBM_REF] * 4,
+        [
+            pltpu.VMEM((T * H, D), bf16),
+            pltpu.VMEM((T * H, D), bf16),
+            pltpu.VMEM((T * KH, D), bf16),
+            pltpu.VMEM((T * KH, D), bf16),
+            pltpu.SemaphoreType.DMA((4,)),
+        ],
         lengths, flat(queries), flat(grad_out), flat(response_keys), flat(response_values),
     )
     kv, pack = lax.optimization_barrier((kv, pack))
@@ -412,6 +436,7 @@
         "unpack_prompt",
         (jax.ShapeDtypeStruct((spots * KH, D), bf16),) * 2,
         [VMEM_REF],
+        [],
         total,
     )
 

time: 92.8 us -> 93.8 us (1.011)
  Pallas kernels: 21.8 us -> 22.8 us
    pallas_call x3, Pallas kernels: 3.71 us -> 4.75 us  [small_call(): pl.pallas_call(body, out_shape=out_shape, in_specs=in_specs, scratch_shap...]
  transfers between devices with their start and end apart: 18 -> 18, of which waited for: 9 -> 9; matrix products, arithmetic and copies ran while one was open for 5% -> 5% of each run, Pallas kernels for 15% -> 16%
where the time goes in v6:
time: 93.8 us; the launch traced here: 93.2 us
  starting transfers between devices  45.5 us (49%)
  Pallas kernels  22.8 us (24%)
  waiting for transfers between devices  13.2 us (14%)
  local copies, waits for them, and re-layouts  8.32 us (9%)
  other arithmetic  1.84 us (2%)
  between operations  1.42 us (2%)
    ppermute x14, starting transfers between devices, over_z(): return lax.ppermute(x, 'z', [(i, (i + k) % 8) for i in range(8)])  29.4 us
    pallas_call x3, Pallas kernels, call(): pl.pallas_call(body, out_shape=out_shape, scratch_shapes=scratch, compile...  18.1 us
    all_to_all x4, starting transfers between devices, swap_y(): return lax.all_to_all(x, 'y', 0, 0, tiled=True)  16.2 us
    ppermute x14, waiting for transfers between devices, over_z(): return lax.ppermute(x, 'z', [(i, (i + k) % 8) for i in range(8)])  7.36 us
    unnamed x14, local copies, waits for them, and re-layouts  7.07 us
    all_to_all x4, waiting for transfers between devices, swap_y(): return lax.all_to_all(x, 'y', 0, 0, tiled=True)  5.89 us
    pallas_call x3, Pallas kernels, small_call(): pl.pallas_call(body, out_shape=out_shape, in_specs=in_specs, scratch_shap...  4.75 us
  transfers between devices with their start and end apart: 18, of which 9 were waited for; matrix products, arithmetic and copies ran while one was open for 5% of the time, Pallas kernels for 16%

profile of v6, /device:TPU:4, one launch (start us, length us, event | category | flops | bytes accessed | tf_op | source)
XLA Modules:
  0.0 93.2 jit_solution(1273190259372790748)
XLA Ops:
  0.6 0.8 copy-done.4
  1.5 0.8 copy-done.5
  2.3 1.3 %pack_prompt.1 = bf16[4,2,64,128]{3,2,1,0:T(8,128)(2,1)} custom-call(bf16[256,128]{1,0:T(8,128)(2,1)S(1)} %bitcast.34, bf16[256,128]{1,0:T(8,128)(2,1)S(1)} %bitcast.35), custom_call_target="tpu_custom_call" | custom-call | tf_op jit(solution)/shard_map/pack_prompt/pallas_call | solution.py:276
  3.6 4.5 %all-to-all-start = ((bf16[4,2,64,128]{3,2,1,0:T(8,128)(2,1)}), bf16[4,2,64,128]{3,2,1,0:T(8,128)(2,1)S(1)}, u32[]{:S(2)}, u32[]{:S(2)}) async-start(bf16[4,2,64,128]{3,2,1,0:T(8,128)(2,1)} %pack_prompt.1), calls=%async_computation | async-start | bytes 262144 | tf_op jit(solution)/shard_map/all_to_all | solution.py:309
  8.7 0.0 copy-start
  8.7 1.0 %copy-done = bf16[1,128,16,128]{3,2,1,0:T(8,128)(2,1)S(1)} copy-done((bf16[1,128,16,128]{3,2,1,0:T(8,128)(2,1)S(1)}, bf16[1,128,16,128]{3,2,1,0:T(8,128)(2,1)}, u32[]{:S(2)}) %copy-start) | copy-done | bytes 524312
  9.8 1.0 %copy-done.1 = bf16[1,128,16,128]{3,2,1,0:T(8,128)(2,1)S(1)} copy-done((bf16[1,128,16,128]{3,2,1,0:T(8,128)(2,1)S(1)}, bf16[1,128,16,128]{3,2,1,0:T(8,128)(2,1)}, u32[]{:S(2)}) %copy-start.1) | copy-done | bytes 524312
  10.8 0.9 copy-done.2
  11.7 0.9 copy-done.3
  12.6 2.6 %pack_rows.1 = bf16[4,1280,128]{2,1,0:T(8,128)(2,1)} custom-call(s32[1]{0:T(128)} %copy.17.length, bf16[2048,128]{1,0:T(8,128)(2,1)S(1)} %bitcast.30, bf16[2048,128]{1,0:T(8,128)(2,1)S(1)} %bitcast.31, bf16[512,128]{1,0:T(8,128)(2,1)S(1)} %bitcast.32, bf16[512,128]{1,0:T(8,128)(2,1)S(1)} %bitcast.33), custom_call_target="tpu_custom_call" | custom-call | tf_op jit(solution)/shard_map/pack_rows/pallas_call | solution.py:276
  15.2 0.0 all-to-all-done.kv0
  15.2 4.8 %all-to-all-start.1 = ((bf16[4,1280,128]{2,1,0:T(8,128)(2,1)}), bf16[4,1280,128]{2,1,0:T(8,128)(2,1)S(1)}, u32[]{:S(2)}, u32[]{:S(2)}) async-start(bf16[4,1280,128]{2,1,0:T(8,128)(2,1)} %pack_rows.1), calls=%async_computation.1 | async-start | bytes 2621440 | tf_op jit(solution)/shard_map/all_to_all | solution.py:309
  20.0 3.3 %collective-permute-start.2 = (bf16[4,2,64,128]{3,2,1,0:T(8,128)(2,1)S(1)}, bf16[4,2,64,128]{3,2,1,0:T(8,128)(2,1)S(1)}, u32[]{:S(2)}, u32[]{:S(2)}) collective-permute-start(bf16[4,2,64,128]{3,2,1,0:T(8,128)(2,1)S(1)} %all-to-all-done.kv0), channel_id=1, source_target_pairs={{0,8},{4,12},{8,16},{12,20},{16,24},{20,28},{24,0},{28,4},{1,9},{5... | collective-permute-start | bytes 393224 | tf_op jit(solution)/shard_map/ppermute | solution.py:306
  23.3 3.0 %collective-permute-start.3 = (bf16[4,2,64,128]{3,2,1,0:T(8,128)(2,1)S(1)}, bf16[4,2,64,128]{3,2,1,0:T(8,128)(2,1)S(1)}, u32[]{:S(2)}, u32[]{:S(2)}) collective-permute-start(bf16[4,2,64,128]{3,2,1,0:T(8,128)(2,1)S(1)} %all-to-all-done.kv0), channel_id=1, source_target_pairs={{0,24},{4,28},{8,0},{12,4},{16,8},{20,12},{24,16},{28,20},{1,25},{... | collective-permute-start | bytes 393224 | tf_op jit(solution)/shard_map/ppermute | solution.py:306
  26.3 2.5 %collective-permute-start.1 = (bf16[4,2,64,128]{3,2,1,0:T(8,128)(2,1)S(1)}, bf16[4,2,64,128]{3,2,1,0:T(8,128)(2,1)S(1)}, u32[]{:S(2)}, u32[]{:S(2)}) collective-permute-start(bf16[4,2,64,128]{3,2,1,0:T(8,128)(2,1)S(1)} %all-to-all-done.kv0), channel_id=1, source_target_pairs={{0,28},{4,0},{8,4},{12,8},{16,12},{20,16},{24,20},{28,24},{1,29},{... | collective-permute-start | bytes 393224 | tf_op jit(solution)/shard_map/ppermute | solution.py:306
  28.8 0.9 %collective-permute-done.2.kv3 = bf16[4,2,64,128]{3,2,1,0:T(8,128)(2,1)S(1)} collective-permute-done((bf16[4,2,64,128]{3,2,1,0:T(8,128)(2,1)S(1)}, bf16[4,2,64,128]{3,2,1,0:T(8,128)(2,1)S(1)}, u32[]{:S(2)}, u32[]{:S(2)}) %collective-permute-start.2) | collective-permute-done | bytes 131104 | tf_op jit(solution)/shard_map/ppermute | solution.py:306
  29.7 3.5 %collective-permute-start.6 = (bf16[4,2,64,128]{3,2,1,0:T(8,128)(2,1)S(1)}, bf16[4,2,64,128]{3,2,1,0:T(8,128)(2,1)S(1)}, u32[]{:S(2)}, u32[]{:S(2)}) collective-permute-start(bf16[4,2,64,128]{3,2,1,0:T(8,128)(2,1)S(1)} %collective-permute-done.2.kv3), channel_id=1, source_target_pairs={{0,8},{4,12},{8,16},{12,20},{16,24},{20,28},{24,0},{28,4},{1,9},{5... | collective-permute-start | bytes 393224 | tf_op jit(solution)/shard_map/ppermute | solution.py:306
  33.2 0.4 collective-permute-start.4
  33.6 3.0 %collective-permute-start.5 = (bf16[4,2,64,128]{3,2,1,0:T(8,128)(2,1)S(1)}, bf16[4,2,64,128]{3,2,1,0:T(8,128)(2,1)S(1)}, u32[]{:S(2)}, u32[]{:S(2)}) collective-permute-start(bf16[4,2,64,128]{3,2,1,0:T(8,128)(2,1)S(1)} %collective-permute-done.3.kv4), channel_id=1, source_target_pairs={{0,28},{4,0},{8,4},{12,8},{16,12},{20,16},{24,20},{28,24},{1,29},{... | collective-permute-start | bytes 393224 | tf_op jit(solution)/shard_map/ppermute | solution.py:306
  36.6 0.2 collective-permute-done.kv1
  36.8 0.5 all-to-all-done.1.pack
  37.3 4.7 %near_forward.1 = (bf16[1408,2048]{1,0:T(8,128)(2,1)S(1)}, f32[144,2048]{1,0:T(8,128)S(1)}, f32[8,2048]{1,0:T(8,128)S(1)}) custom-call(bf16[4,1280,128]{2,1,0:T(8,128)(2,1)S(1)} %all-to-all-done.1.pack, bf16[4,2,64,128]{3,2,1,0:T(8,128)(2,1)S(1)} %all-to-all-done.kv0, bf16[4,2,64,128]{3,2,1,0:T(8,128)(2,1)S(1)} %collective-permute-done.kv1, ...), custom_call_target="tpu_custom_call" | custom-call | flops 1476395008 | bytes 4194304 | tf_op jit(solution)/shard_map/near_forward/pallas_call | solution.py:287
  42.1 1.0 %collective-permute-done.4.kv0 = bf16[4,2,64,128]{3,2,1,0:T(8,128)(2,1)S(1)} collective-permute-done((bf16[4,2,64,128]{3,2,1,0:T(8,128)(2,1)S(1)}, bf16[4,2,64,128]{3,2,1,0:T(8,128)(2,1)S(1)}, u32[]{:S(2)}, u32[]{:S(2)}) %collective-permute-start.4) | collective-permute-done | bytes 131104 | tf_op jit(solution)/shard_map/ppermute | solution.py:306
  43.1 6.0 %far_both.1 = (bf16[4,512,128]{2,1,0:T(8,128)(2,1)S(1)}, f32[8,2048]{1,0:T(8,128)S(1)}, bf16[2048,128]{1,0:T(8,128)(2,1)S(1)}, bf16[2048,128]{1,0:T(8,128)(2,1)S...) custom-call(bf16[4,1280,128]{2,1,0:T(8,128)(2,1)S(1)} %all-to-all-do, ...), custom_call_target="tpu_custom_call" | custom-call | flops 2415919104 | bytes 4194304 | tf_op jit(solution)/shard_map/far_both/pallas_call | solution.py:287
  49.1 5.4 %collective-permute-start.7 = (bf16[4,2,64,128]{3,2,1,0:T(8,128)(2,1)S(1)}, bf16[4,2,64,128]{3,2,1,0:T(8,128)(2,1)S(1)}, u32[]{:S(2)}, u32[]{:S(2)}) collective-permute-start(bf16[4,2,64,128]{3,2,1,0:T(8,128)(2,1)S(1)} %get-tuple-element.48), channel_id=1, source_target_pairs={{0,24},{4,28},{8,0},{12,4},{16,8},{20,12},{24,16},{28,20},{1,25},{... | collective-permute-start | bytes 393224 | tf_op jit(solution)/shard_map/ppermute | solution.py:306
  54.5 1.0 %collective-permute-start.8 = (bf16[4,2,64,128]{3,2,1,0:T(8,128)(2,1)S(1)}, bf16[4,2,64,128]{3,2,1,0:T(8,128)(2,1)S(1)}, u32[]{:S(2)}, u32[]{:S(2)}) collective-permute-start(bf16[4,2,64,128]{3,2,1,0:T(8,128)(2,1)S(1)} %get-tuple-element.49), channel_id=1, source_target_pairs={{0,28},{4,0},{8,4},{12,8},{16,12},{20,16},{24,20},{28,24},{1,29},{... | collective-permute-start | bytes 393224 | tf_op jit(solution)/shard_map/ppermute | solution.py:306
  55.5 1.0 %collective-permute-start.9 = (bf16[4,2,64,128]{3,2,1,0:T(8,128)(2,1)S(1)}, bf16[4,2,64,128]{3,2,1,0:T(8,128)(2,1)S(1)}, u32[]{:S(2)}, u32[]{:S(2)}) collective-permute-start(bf16[4,2,64,128]{3,2,1,0:T(8,128)(2,1)S(1)} %get-tuple-element.50), channel_id=1, source_target_pairs={{0,4},{4,8},{8,12},{12,16},{16,20},{20,24},{24,28},{28,0},{1,5},{5... | collective-permute-start | bytes 393224 | tf_op jit(solution)/shard_map/ppermute | solution.py:306
  56.5 7.3 %near_backward.1 = (bf16[4,1280,128]{2,1,0:T(8,128)(2,1)}, bf16[4,2,64,128]{3,2,1,0:T(8,128)(2,1)S(1)}, bf16[4,2,64,128]{3,2,1,0:T(8,128)(2,1)S(1)}, bf16[4,2,64...) custom-call(bf16[4,1280,128]{2,1,0:T(8,128)(2,1)S(1)} %all-to-all-done.1.pack, ...), custom_call_target="tpu_custom_call" | custom-call | flops 2952790016 | bytes 4194304 | tf_op jit(solution)/shard_map/near_backward/pallas_call | solution.py:287
  63.9 3.6 %all-to-all-start.2 = ((bf16[4,1280,128]{2,1,0:T(8,128)(2,1)}), bf16[4,1280,128]{2,1,0:T(8,128)(2,1)S(1)}, u32[]{:S(2)}, u32[]{:S(2)}) async-start(bf16[4,1280,128]{2,1,0:T(8,128)(2,1)} %get-tuple-element.63), calls=%async_computation.2 | async-start | bytes 2621440 | tf_op jit(solution)/shard_map/all_to_all | solution.py:309
  67.5 0.5 collective-permute-start.13
  68.0 0.1 add_convert_fusion.2
  68.1 3.8 %collective-permute-start.12 = (bf16[4,2,64,128]{3,2,1,0:T(8,128)(2,1)S(1)}, bf16[4,2,64,128]{3,2,1,0:T(8,128)(2,1)S(1)}, u32[]{:S(2)}, u32[]{:S(2)}) collective-permute-start(bf16[4,2,64,128]{3,2,1,0:T(8,128)(2,1)S(1)} %add_convert_fusion.2), channel_id=1, source_target_pairs={{0,24},{4,28},{8,0},{12,4},{16,8},{20,12},{24,16},{28,20},{1,25},{... | collective-permute-start | bytes 393224 | tf_op jit(solution)/shard_map/ppermute | solution.py:306
  71.8 1.0 %collective-permute-start.10 = (bf16[4,2,64,128]{3,2,1,0:T(8,128)(2,1)S(1)}, bf16[4,2,64,128]{3,2,1,0:T(8,128)(2,1)S(1)}, u32[]{:S(2)}, u32[]{:S(2)}) collective-permute-start(bf16[4,2,64,128]{3,2,1,0:T(8,128)(2,1)S(1)} %get-tuple-element.56), channel_id=1, source_target_pairs={{0,28},{4,0},{8,4},{12,8},{16,12},{20,16},{24,20},{28,24},{1,29},{... | collective-permute-start | bytes 393224 | tf_op jit(solution)/shard_map/ppermute | solution.py:306
  72.8 1.0 %collective-permute-start.11 = (bf16[4,2,64,128]{3,2,1,0:T(8,128)(2,1)S(1)}, bf16[4,2,64,128]{3,2,1,0:T(8,128)(2,1)S(1)}, u32[]{:S(2)}, u32[]{:S(2)}) collective-permute-start(bf16[4,2,64,128]{3,2,1,0:T(8,128)(2,1)S(1)} %get-tuple-element.57), channel_id=1, source_target_pairs={{0,4},{4,8},{8,12},{12,16},{16,20},{20,24},{24,28},{28,0},{1,5},{5... | collective-permute-start | bytes 393224 | tf_op jit(solution)/shard_map/ppermute | solution.py:306
  73.9 2.6 %collective-permute-done.13 = bf16[4,2,64,128]{3,2,1,0:T(8,128)(2,1)S(1)} collective-permute-done((bf16[4,2,64,128]{3,2,1,0:T(8,128)(2,1)S(1)}, bf16[4,2,64,128]{3,2,1,0:T(8,128)(2,1)S(1)}, u32[]{:S(2)}, u32[]{:S(2)}) %collective-permute-start.13) | collective-permute-done | bytes 131104 | tf_op jit(solution)/shard_map/ppermute | solution.py:306
  76.5 2.0 %collective-permute-done.10 = bf16[4,2,64,128]{3,2,1,0:T(8,128)(2,1)S(1)} collective-permute-done((bf16[4,2,64,128]{3,2,1,0:T(8,128)(2,1)S(1)}, bf16[4,2,64,128]{3,2,1,0:T(8,128)(2,1)S(1)}, u32[]{:S(2)}, u32[]{:S(2)}) %collective-permute-start.10) | collective-permute-done | bytes 131104 | tf_op jit(solution)/shard_map/ppermute | solution.py:306
  78.4 0.6 collective-permute-done.11
  79.0 0.7 add_convert_fusion
  79.8 3.2 %all-to-all-done.2 = bf16[4,1280,128]{2,1,0:T(8,128)(2,1)S(1)} async-done(((bf16[4,1280,128]{2,1,0:T(8,128)(2,1)}), bf16[4,1280,128]{2,1,0:T(8,128)(2,1)S(1)}, u32[]{:S(2)}, u32[]{:S(2)}) %all-to-all-start.2) | async-done | bytes 1310752 | tf_op jit(solution)/shard_map/all_to_all | solution.py:309
  83.0 3.3 %all-to-all-start.3 = ((bf16[4,2,64,128]{3,2,1,0:T(8,128)(2,1)}), bf16[4,2,64,128]{3,2,1,0:T(8,128)(2,1)S(1)}, u32[]{:S(2)}, u32[]{:S(2)}) async-start(bf16[4,2,64,128]{3,2,1,0:T(8,128)(2,1)} %add_convert_fusion), calls=%async_computation.3 | async-start | bytes 262144 | tf_op jit(solution)/shard_map/all_to_all | solution.py:309
  86.3 0.1 fusion
  86.4 0.2 copy.13
  86.6 1.0 %broadcast_select_fusion = bf16[1,128,16,128]{3,2,1,0:T(8,128)(2,1)} fusion(bf16[1,128,16,128]{3,2,1,0:T(8,128)(2,1)S(1)} %bitcast.36, pred[128]{0:T(512)(128)(4,1)S(1)} %iota_compare_fusion), kind=kLoop, calls=%fused_computation | loop fusion | flops 262144 | bytes 1048704 | tf_op jit(solution)/shard_map/jit(_where)/select_n | solution.py:448
  87.6 1.0 %copy.14 = bf16[128,4,4,128]{3,2,1,0:T(4,128)(2,1)} copy(bf16[128,4,4,128]{3,2,0,1:T(4,128)(2,1)S(1)} %bitcast.37) | data formatting | bytes 1048576 | tf_op jit(solution)/shard_map/transpose | solution.py:445
  88.6 0.8 copy.16
  89.3 0.8 copy.15
  90.1 2.2 %all-to-all-done.3.x = bf16[4,2,64,128]{3,2,1,0:T(8,128)(2,1)S(1)} async-done(((bf16[4,2,64,128]{3,2,1,0:T(8,128)(2,1)}), bf16[4,2,64,128]{3,2,1,0:T(8,128)(2,1)S(1)}, u32[]{:S(2)}, u32[]{:S(2)}) %all-to-all-start.3) | async-done | bytes 131104 | tf_op jit(solution)/shard_map/all_to_all | solution.py:309
  92.3 0.9 unpack_prompt.1
  (17 shorter events, 0.1 us)
Async XLA Ops:
  0.6 0.8 copy-start.4
  1.5 0.8 copy-start.5
  3.6 11.6 %all-to-all-start = ((bf16[4,2,64,128]{3,2,1,0:T(8,128)(2,1)}), bf16[4,2,64,128]{3,2,1,0:T(8,128)(2,1)S(1)}, u32[]{:S(2)}, u32[]{:S(2)}) async-start(bf16[4,2,64,128]{3,2,1,0:T(8,128)(2,1)} %pack_prompt.1), calls=%async_computation | async-start | bytes 262144 | tf_op jit(solution)/shard_map/all_to_all | solution.py:309
  8.7 1.0 %copy-start = (bf16[1,128,16,128]{3,2,1,0:T(8,128)(2,1)S(1)}, bf16[1,128,16,128]{3,2,1,0:T(8,128)(2,1)}, u32[]{:S(2)}) copy-start(bf16[1,128,16,128]{3,2,1,0:T(8,128)(2,1)} %param.7) | copy-start | bytes 1572868
  9.7 1.0 %copy-start.1 = (bf16[1,128,16,128]{3,2,1,0:T(8,128)(2,1)S(1)}, bf16[1,128,16,128]{3,2,1,0:T(8,128)(2,1)}, u32[]{:S(2)}) copy-start(bf16[1,128,16,128]{3,2,1,0:T(8,128)(2,1)} %param.13) | copy-start | bytes 1572868
  10.8 0.9 copy-start.2
  11.7 0.9 copy-start.3
  15.2 22.1 %all-to-all-start.1 = ((bf16[4,1280,128]{2,1,0:T(8,128)(2,1)}), bf16[4,1280,128]{2,1,0:T(8,128)(2,1)S(1)}, u32[]{:S(2)}, u32[]{:S(2)}) async-start(bf16[4,1280,128]{2,1,0:T(8,128)(2,1)} %pack_rows.1), calls=%async_computation.1 | async-start | bytes 2621440 | tf_op jit(solution)/shard_map/all_to_all | solution.py:309
  20.0 9.7 %collective-permute-start.2 = (bf16[4,2,64,128]{3,2,1,0:T(8,128)(2,1)S(1)}, bf16[4,2,64,128]{3,2,1,0:T(8,128)(2,1)S(1)}, u32[]{:S(2)}, u32[]{:S(2)}) collective-permute-start(bf16[4,2,64,128]{3,2,1,0:T(8,128)(2,1)S(1)} %all-to-all-done.kv0), channel_id=1, source_target_pairs={{0,8},{4,12},{8,16},{12,20},{16,24},{20,28},{24,0},{28,4},{1,9},{5... | collective-permute-start | bytes 393224 | tf_op jit(solution)/shard_map/ppermute | solution.py:306
  23.3 10.3 %collective-permute-start.3 = (bf16[4,2,64,128]{3,2,1,0:T(8,128)(2,1)S(1)}, bf16[4,2,64,128]{3,2,1,0:T(8,128)(2,1)S(1)}, u32[]{:S(2)}, u32[]{:S(2)}) collective-permute-start(bf16[4,2,64,128]{3,2,1,0:T(8,128)(2,1)S(1)} %all-to-all-done.kv0), channel_id=1, source_target_pairs={{0,24},{4,28},{8,0},{12,4},{16,8},{20,12},{24,16},{28,20},{1,25},{... | collective-permute-start | bytes 393224 | tf_op jit(solution)/shard_map/ppermute | solution.py:306
  26.3 10.3 %collective-permute-start.1 = (bf16[4,2,64,128]{3,2,1,0:T(8,128)(2,1)S(1)}, bf16[4,2,64,128]{3,2,1,0:T(8,128)(2,1)S(1)}, u32[]{:S(2)}, u32[]{:S(2)}) collective-permute-start(bf16[4,2,64,128]{3,2,1,0:T(8,128)(2,1)S(1)} %all-to-all-done.kv0), channel_id=1, source_target_pairs={{0,28},{4,0},{8,4},{12,8},{16,12},{20,16},{24,20},{28,24},{1,29},{... | collective-permute-start | bytes 393224 | tf_op jit(solution)/shard_map/ppermute | solution.py:306
  28.8 8.0 %collective-permute-start = (bf16[4,2,64,128]{3,2,1,0:T(8,128)(2,1)S(1)}, bf16[4,2,64,128]{3,2,1,0:T(8,128)(2,1)S(1)}, u32[]{:S(2)}, u32[]{:S(2)}) collective-permute-start(bf16[4,2,64,128]{3,2,1,0:T(8,128)(2,1)S(1)} %all-to-all-done.kv0), channel_id=1, source_target_pairs={{0,4},{4,8},{8,12},{12,16},{16,20},{20,24},{24,28},{28,0},{1,5},{5... | collective-permute-start | bytes 393224 | tf_op jit(solution)/shard_map/ppermute | solution.py:306
  29.7 12.4 %collective-permute-start.6 = (bf16[4,2,64,128]{3,2,1,0:T(8,128)(2,1)S(1)}, bf16[4,2,64,128]{3,2,1,0:T(8,128)(2,1)S(1)}, u32[]{:S(2)}, u32[]{:S(2)}) collective-permute-start(bf16[4,2,64,128]{3,2,1,0:T(8,128)(2,1)S(1)} %collective-permute-done.2.kv3), channel_id=1, source_target_pairs={{0,8},{4,12},{8,16},{12,20},{16,24},{20,28},{24,0},{28,4},{1,9},{5... | collective-permute-start | bytes 393224 | tf_op jit(solution)/shard_map/ppermute | solution.py:306
  33.2 9.9 %collective-permute-start.4 = (bf16[4,2,64,128]{3,2,1,0:T(8,128)(2,1)S(1)}, bf16[4,2,64,128]{3,2,1,0:T(8,128)(2,1)S(1)}, u32[]{:S(2)}, u32[]{:S(2)}) collective-permute-start(bf16[4,2,64,128]{3,2,1,0:T(8,128)(2,1)S(1)} %collective-permute-done.2.kv3), channel_id=1, source_target_pairs={{0,4},{4,8},{8,12},{12,16},{16,20},{20,24},{24,28},{28,0},{1,5},{5... | collective-permute-start | bytes 393224 | tf_op jit(solution)/shard_map/ppermute | solution.py:306
  33.6 8.5 %collective-permute-start.5 = (bf16[4,2,64,128]{3,2,1,0:T(8,128)(2,1)S(1)}, bf16[4,2,64,128]{3,2,1,0:T(8,128)(2,1)S(1)}, u32[]{:S(2)}, u32[]{:S(2)}) collective-permute-start(bf16[4,2,64,128]{3,2,1,0:T(8,128)(2,1)S(1)} %collective-permute-done.3.kv4), channel_id=1, source_target_pairs={{0,28},{4,0},{8,4},{12,8},{16,12},{20,16},{24,20},{28,24},{1,29},{... | collective-permute-start | bytes 393224 | tf_op jit(solution)/shard_map/ppermute | solution.py:306
  49.1 14.8 %collective-permute-start.7 = (bf16[4,2,64,128]{3,2,1,0:T(8,128)(2,1)S(1)}, bf16[4,2,64,128]{3,2,1,0:T(8,128)(2,1)S(1)}, u32[]{:S(2)}, u32[]{:S(2)}) collective-permute-start(bf16[4,2,64,128]{3,2,1,0:T(8,128)(2,1)S(1)} %get-tuple-element.48), channel_id=1, source_target_pairs={{0,24},{4,28},{8,0},{12,4},{16,8},{20,12},{24,16},{28,20},{1,25},{... | collective-permute-start | bytes 393224 | tf_op jit(solution)/shard_map/ppermute | solution.py:306
  54.5 9.4 %collective-permute-start.8 = (bf16[4,2,64,128]{3,2,1,0:T(8,128)(2,1)S(1)}, bf16[4,2,64,128]{3,2,1,0:T(8,128)(2,1)S(1)}, u32[]{:S(2)}, u32[]{:S(2)}) collective-permute-start(bf16[4,2,64,128]{3,2,1,0:T(8,128)(2,1)S(1)} %get-tuple-element.49), channel_id=1, source_target_pairs={{0,28},{4,0},{8,4},{12,8},{16,12},{20,16},{24,20},{28,24},{1,29},{... | collective-permute-start | bytes 393224 | tf_op jit(solution)/shard_map/ppermute | solution.py:306
  55.5 8.4 %collective-permute-start.9 = (bf16[4,2,64,128]{3,2,1,0:T(8,128)(2,1)S(1)}, bf16[4,2,64,128]{3,2,1,0:T(8,128)(2,1)S(1)}, u32[]{:S(2)}, u32[]{:S(2)}) collective-permute-start(bf16[4,2,64,128]{3,2,1,0:T(8,128)(2,1)S(1)} %get-tuple-element.50), channel_id=1, source_target_pairs={{0,4},{4,8},{8,12},{12,16},{16,20},{20,24},{24,28},{28,0},{1,5},{5... | collective-permute-start | bytes 393224 | tf_op jit(solution)/shard_map/ppermute | solution.py:306
  63.9 19.1 %all-to-all-start.2 = ((bf16[4,1280,128]{2,1,0:T(8,128)(2,1)}), bf16[4,1280,128]{2,1,0:T(8,128)(2,1)S(1)}, u32[]{:S(2)}, u32[]{:S(2)}) async-start(bf16[4,1280,128]{2,1,0:T(8,128)(2,1)} %get-tuple-element.63), calls=%async_computation.2 | async-start | bytes 2621440 | tf_op jit(solution)/shard_map/all_to_all | solution.py:309
  67.5 9.0 %collective-permute-start.13 = (bf16[4,2,64,128]{3,2,1,0:T(8,128)(2,1)S(1)}, bf16[4,2,64,128]{3,2,1,0:T(8,128)(2,1)S(1)}, u32[]{:S(2)}, u32[]{:S(2)}) collective-permute-start(bf16[4,2,64,128]{3,2,1,0:T(8,128)(2,1)S(1)} %add_convert_fusion.1), channel_id=1, source_target_pairs={{0,8},{4,12},{8,16},{12,20},{16,24},{20,28},{24,0},{28,4},{1,9},{5... | collective-permute-start | bytes 393224 | tf_op jit(solution)/shard_map/ppermute | solution.py:306
  68.1 8.4 %collective-permute-start.12 = (bf16[4,2,64,128]{3,2,1,0:T(8,128)(2,1)S(1)}, bf16[4,2,64,128]{3,2,1,0:T(8,128)(2,1)S(1)}, u32[]{:S(2)}, u32[]{:S(2)}) collective-permute-start(bf16[4,2,64,128]{3,2,1,0:T(8,128)(2,1)S(1)} %add_convert_fusion.2), channel_id=1, source_target_pairs={{0,24},{4,28},{8,0},{12,4},{16,8},{20,12},{24,16},{28,20},{1,25},{... | collective-permute-start | bytes 393224 | tf_op jit(solution)/shard_map/ppermute | solution.py:306
  71.8 6.6 %collective-permute-start.10 = (bf16[4,2,64,128]{3,2,1,0:T(8,128)(2,1)S(1)}, bf16[4,2,64,128]{3,2,1,0:T(8,128)(2,1)S(1)}, u32[]{:S(2)}, u32[]{:S(2)}) collective-permute-start(bf16[4,2,64,128]{3,2,1,0:T(8,128)(2,1)S(1)} %get-tuple-element.56), channel_id=1, source_target_pairs={{0,28},{4,0},{8,4},{12,8},{16,12},{20,16},{24,20},{28,24},{1,29},{... | collective-permute-start | bytes 393224 | tf_op jit(solution)/shard_map/ppermute | solution.py:306
  72.8 6.2 %collective-permute-start.11 = (bf16[4,2,64,128]{3,2,1,0:T(8,128)(2,1)S(1)}, bf16[4,2,64,128]{3,2,1,0:T(8,128)(2,1)S(1)}, u32[]{:S(2)}, u32[]{:S(2)}) collective-permute-start(bf16[4,2,64,128]{3,2,1,0:T(8,128)(2,1)S(1)} %get-tuple-element.57), channel_id=1, source_target_pairs={{0,4},{4,8},{8,12},{12,16},{16,20},{20,24},{24,28},{28,0},{1,5},{5... | collective-permute-start | bytes 393224 | tf_op jit(solution)/shard_map/ppermute | solution.py:306
  83.0 9.3 %all-to-all-start.3 = ((bf16[4,2,64,128]{3,2,1,0:T(8,128)(2,1)}), bf16[4,2,64,128]{3,2,1,0:T(8,128)(2,1)S(1)}, u32[]{:S(2)}, u32[]{:S(2)}) async-start(bf16[4,2,64,128]{3,2,1,0:T(8,128)(2,1)} %add_convert_fusion), calls=%async_computation.3 | async-start | bytes 262144 | tf_op jit(solution)/shard_map/all_to_all | solution.py:309

commit v7 on v5

--- a/solution.py
+++ b/solution.py
@@ -10,6 +10,8 @@
 LOG2E = 1.4426950408889634
 CHUNK = 768
 FORWARD_CHUNK = 256
+FAR_CHUNK = 384
+BACKWARD_CHUNK = 512
 f32 = jnp.float32
 bf16 = jnp.bfloat16
 NT = (((1,), (1,)), ((), ()))
@@ -37,41 +39,6 @@
 
 def unsort_rows(order, x):
     return lax.dot_general(order, x, TN, preferred_element_type=f32).astype(bf16)
-
-
-def pack_prompt(k_ref, v_ref, out):
-    n = k_ref.shape[0]
-    order = sorting(n, 4, 1)
-    for j, ref in enumerate((k_ref, v_ref)):
-        x = sort_rows(order, ref[...])
-        for h in range(4):
-            out[h, j] = x[h * (n // 4):(h + 1) * (n // 4), :]
-
-
-def pack_rows(length, q, g, k, v, out, *, T, G):
-    R = T * G
-    n = 256
-    order = sorting(n, 4 * G, G)
-    part = n // 4
-    row_pos = lax.broadcasted_iota(jnp.int32, (part, 128), 0) // G
-    live = length[0]
-    for b in range(4 * R // n):
-        x = sort_rows(order, q[b * n:(b + 1) * n, :])
-        y = sort_rows(order, g[b * n:(b + 1) * n, :])
-        alive = row_pos + b * (part // G) < live
-        for h in range(4):
-            at = slice(b * part, (b + 1) * part)
-            out[h, at, :] = x[h * part:(h + 1) * part, :]
-            z = y[h * part:(h + 1) * part, :]
-            out[h, slice(R + b * part, R + (b + 1) * part), :] = jnp.where(alive, z, jnp.zeros_like(z))
-    order = sorting(n, 4, 1)
-    for b in range(4 * T // n):
-        x = sort_rows(order, k[b * n:(b + 1) * n, :])
-        y = sort_rows(order, v[b * n:(b + 1) * n, :])
-        for h in range(4):
-            at = 2 * R + b * part
-            out[h, at:at + part, :] = x[h * part:(h + 1) * part, :]
-            out[h, at + T:at + T + part, :] = y[h * part:(h + 1) * part, :]
 
 
 def unpack_prompt(x, k_out, v_out):
@@ -169,19 +136,29 @@
     C = D ** (-0.5)
     nk = K.shape[0]
     load_blocks((kv0, kv1, kv2), K, V, KT, VT)
+
+    def score(r, ks, top):
+        s = dot(K[ks, :], pack[r, 0:R, :], NT)
+        S[r % 2, ks, :] = s
+        return jnp.maximum(top, jnp.max(s.reshape(s.shape[0] // 8, 8, R), axis=0))
+
+    low = jnp.full((8, R), -jnp.inf, f32)
+    later = low
+    for ks in spans(nk, FAR_CHUNK):
+        later = score(0, ks, later)
     for r in range(4):
         rows = slice(r * R, (r + 1) * R)
         qr = pack[r, 0:R, :]
         dof = pack[r, R:2 * R, :].astype(f32)
-        top = jnp.full((8, R), -jnp.inf, f32)
-        for ks in spans(nk, CHUNK):
-            top = scores_into(S, ks, dot(K[ks, :], qr, NT), top)
         near_top = top_ref[0:1, rows]
-        top = jnp.maximum(near_top, jnp.max(top, axis=0, keepdims=True) * (C * LOG2E))
+        top = jnp.maximum(near_top, jnp.max(later, axis=0, keepdims=True) * (C * LOG2E))
         near = jnp.exp2(near_top - top)
         acc = acc_ref[:, rows] * near
-        for ks in spans(nk, CHUNK):
-            p = jnp.exp2(S[ks, :] * (C * LOG2E) - top).astype(bf16)
+        later = low
+        for ks in spans(nk, FAR_CHUNK):
+            if r < 3:
+                later = score(r + 1, ks, later)
+            p = jnp.exp2(S[r % 2, ks, :] * (C * LOG2E) - top).astype(bf16)
             Pm[ks, rows] = p
             acc = acc + dot(VT[:, ks], p, NN)
         inv = 1.0 / acc[D:D + 1, :]
@@ -218,7 +195,7 @@
 
 def near_backward(
     pack, kv0, kv1, kv2, kv3, kv4, Pm, o_ref, stat, Qs, Os, dqt, out, d0, d1, d2, d3, d4,
-    K, V, KT, acc, *, T, G
+    K, V, KT, DS, *, T, G
 ):
     D = K.shape[1]
     R = T * G
@@ -228,30 +205,26 @@
     own = slice(nk, nk + T)
     for r in range(4):
         rows = slice(r * R, (r + 1) * R)
+        dor = pack[r, R:2 * R, :]
         kr = pack[r, 2 * R:2 * R + T, :]
         vr = pack[r, 2 * R + T:2 * R + 2 * T, :]
+        delta = stat[0:1, rows]
         p = Pm[own, rows]
-        ds = (p.astype(f32) * (dot(vr, pack[r, R:2 * R, :], NT) - stat[0:1, rows])).astype(bf16)
+        ds = (p.astype(f32) * (dot(vr, dor, NT) - delta)).astype(bf16)
         out[r, 0:R, :] = o_ref[r]
         out[r, 2 * R:2 * R + T, :] = dot(ds, Qs[rows, :], NN).astype(bf16)
         out[r, 2 * R + T:2 * R + 2 * T, :] = dot(p, Os[rows, :], NN).astype(bf16)
-        acc[:, rows] = dot(kr.T, ds, NN)
-    for ks in spans(nk, CHUNK):
-        dk = jnp.zeros((ks.stop - ks.start, D), f32)
-        dv = jnp.zeros((ks.stop - ks.start, D), f32)
-        for r in range(4):
-            rows = slice(r * R, (r + 1) * R)
-            p = Pm[ks, rows]
-            dp = dot(V[ks, :], pack[r, R:2 * R, :], NT)
-            ds = (p.astype(f32) * (dp - stat[0:1, rows])).astype(bf16)
-            dk = dk + dot(ds, Qs[rows, :], NN)
-            dv = dv + dot(p, Os[rows, :], NN)
-            acc[:, rows] += dot(KT[:, ks], ds, NN)
+        acc = dot(kr.T, ds, NN)
+        for ks in spans(nk, BACKWARD_CHUNK):
+            ds = (Pm[ks, rows].astype(f32) * (dot(V[ks, :], dor, NT) - delta)).astype(bf16)
+            DS[ks, rows] = ds
+        acc = acc + dot(KT[...], DS[:, rows], NN)
+        dq = (dqt[:, rows] + acc * stat[2:3, rows]) * C
+        out[r, R:2 * R, :] = dq.T.astype(bf16)
+    for ks in spans(nk, BACKWARD_CHUNK):
+        dk = dot(DS[ks, :], Qs[...], NN)
+        dv = dot(Pm[ks, :], Os[...], NN)
         store_blocks((d0, d1, d2, d3, d4), ks, dk, dv)
-    for r in range(4):
-        rows = slice(r * R, (r + 1) * R)
-        dq = (dqt[:, rows] + acc[:, rows] * stat[2:3, rows]) * C
-        out[r, R:2 * R, :] = dq.T.astype(bf16)
 
 
 VMEM_REF = pl.BlockSpec(memory_space=pltpu.VMEM)
@@ -292,27 +265,24 @@
     def swap_y(x):
         return lax.all_to_all(x, "y", 0, 0, tiled=True)
 
-    spots = prompt_keys.shape[0]
-
-    def flat(x):
-        return x.reshape(-1, D)
-
-    kv = small_call(
-        pack_prompt,
-        "pack_prompt",
-        jax.ShapeDtypeStruct((KH, 2, spots, D), bf16),
-        [VMEM_REF] * 2,
-        flat(prompt_keys), flat(prompt_value_rows),
-    )
-    kv = swap_y(kv)
+    kv = jnp.stack([prompt_keys, prompt_value_rows], axis=0)
+    kv = swap_y(jnp.transpose(kv, (2, 0, 1, 3)))
 
     live = (jnp.arange(T) < lengths[0])[:, None, None]
-    pack = small_call(
-        functools.partial(pack_rows, T=T, G=G),
-        "pack_rows",
-        jax.ShapeDtypeStruct((KH, 2 * R + 2 * T, D), bf16),
-        [pl.BlockSpec(memory_space=pltpu.SMEM)] + [VMEM_REF] * 4,
-        lengths, flat(queries), flat(grad_out), flat(response_keys), flat(response_values),
+    masked = jnp.where(live, grad_out[0], jnp.zeros((), bf16))
+
+    def by_head(x, n):
+        x = x.reshape(T, KH, n, D)
+        return jnp.transpose(x, (1, 0, 2, 3)).reshape(KH, T * n, D)
+
+    pack = jnp.concatenate(
+        [
+            by_head(queries, G),
+            by_head(masked, G),
+            by_head(response_keys, 1),
+            by_head(response_values, 1),
+        ],
+        axis=1,
     )
     kv, pack = lax.optimization_barrier((kv, pack))
     pack = swap_y(pack)
@@ -327,6 +297,7 @@
     near = (kv, from_1, from_m1, from_2, from_m2)
     far = (from_3, from_m3, from_4)
     block = jax.ShapeDtypeStruct(kv.shape, bf16)
+    spots = kv.shape[2]
     near_keys = 5 * 4 * spots
     far_keys = 3 * 4 * spots
     rows = 4 * R
@@ -368,7 +339,7 @@
         [
             pltpu.VMEM((far_keys, D), bf16),
             pltpu.VMEM((far_keys, D), bf16),
-            pltpu.VMEM((far_keys, R), f32),
+            pltpu.VMEM((2, far_keys, R), f32),
             pltpu.VMEM((far_keys, rows), bf16),
             pltpu.VMEM((D, far_keys), bf16),
             pltpu.VMEM((D + 16, far_keys), bf16),
@@ -386,7 +357,7 @@
             pltpu.VMEM((near_keys, D), bf16),
             pltpu.VMEM((near_keys, D), bf16),
             pltpu.VMEM((D, near_keys), bf16),
-            pltpu.VMEM((D, rows), f32),
+            pltpu.VMEM((near_keys, rows), bf16),
         ],
         cost(4, near_keys + T),
         pack, *near, weights, out, stat, q_near, g_near, dqt,

time: 92.8 us -> 88 us (0.948)
  Pallas kernels: 21.8 us -> 18.3 us
  local copies, waits for them, and re-layouts: 8.32 us -> 5 us
  waiting for transfers between devices: 13.3 us -> 16.6 us
  starting transfers between devices: 45.5 us -> 42.3 us
  other arithmetic: 1.84 us -> 3.96 us
    unnamed x14 -> x8, local copies, waits for them, and re-layouts: 7.07 us -> 1.53 us
    pallas_call x3 -> x1, Pallas kernels: 3.71 us -> 0.92 us  [small_call(): pl.pallas_call(body, out_shape=out_shape, in_specs=in_specs, compiler_par...]
    ppermute x14, starting transfers between devices: 29.4 us -> 27.4 us  [over_z(): return lax.ppermute(x, 'z', [(i, (i + k) % 8) for i in range(8)])]
    ppermute x14, waiting for transfers between devices: 7.37 us -> 9.09 us  [over_z(): return lax.ppermute(x, 'z', [(i, (i + k) % 8) for i in range(8)])]
    all_to_all x4, waiting for transfers between devices: 5.88 us -> 7.46 us  [swap_y(): return lax.all_to_all(x, 'y', 0, 0, tiled=True)]
    reshape x0 -> x2, local copies, waits for them, and re-layouts: none -> 1.26 us  [the longest x1 1.23 us: by_head(): x = x.reshape(T, KH, n, D)]
    all_to_all x4, starting transfers between devices: 16.1 us -> 14.9 us  [swap_y(): return lax.all_to_all(x, 'y', 0, 0, tiled=True)]
    concatenate x0 -> x1, other arithmetic: none -> 1.17 us  [on_device(): jnp.concatenate([by_head(queries, G), by_head(masked, G), by_head(respons...]
  transfers between devices with their start and end apart: 18 -> 18, of which waited for: 9 -> 10; matrix products, arithmetic and copies ran while one was open for 5% -> 8% of each run, Pallas kernels for 15% -> 13%
where the time goes in v7:
time: 88 us; the launch traced here: 87.5 us
  starting transfers between devices  42.3 us (48%)
  Pallas kernels  18.3 us (21%)
  waiting for transfers between devices  16.6 us (19%)
  local copies, waits for them, and re-layouts  5 us (6%)
  other arithmetic  3.96 us (4%)
  between operations  1.47 us (2%)
    ppermute x14, starting transfers between devices, over_z(): return lax.ppermute(x, 'z', [(i, (i + k) % 8) for i in range(8)])  27.4 us
    pallas_call x3, Pallas kernels, call(): pl.pallas_call(body, out_shape=out_shape, scratch_shapes=scratch, compile...  17.3 us
    all_to_all x4, starting transfers between devices, swap_y(): return lax.all_to_all(x, 'y', 0, 0, tiled=True)  14.9 us
    ppermute x14, waiting for transfers between devices, over_z(): return lax.ppermute(x, 'z', [(i, (i + k) % 8) for i in range(8)])  9.09 us
    all_to_all x4, waiting for transfers between devices, swap_y(): return lax.all_to_all(x, 'y', 0, 0, tiled=True)  7.46 us
  transfers between devices with their start and end apart: 18, of which 10 were waited for; matrix products, arithmetic and copies ran while one was open for 8% of the time, Pallas kernels for 13%

profile of v7, /device:TPU:4, one launch (start us, length us, event | category | flops | bytes accessed | tf_op | source)
XLA Modules:
  0.0 87.5 jit_solution(6801864783739568233)
XLA Ops:
  0.7 1.0 %copy_bitcast_fusion.2 = (bf16[1,64,4,128]{3,1,0,2:T(8,128)(2,1)S(1)}, bf16[1,64,4,128]{3,1,0,2:T(8,128)(2,1)S(1)}) fusion(bf16[64,4,128]{2,1,0:T(4,128)(2,1)} %param.11, bf16[64,4,128]{2,1,0:T(4,128)(2,1)} %param.10), kind=kLoop, calls=%fused_computation.11 | loop fusion | bytes 262144 | tf_op jit(solution)/shard_map/stack | solution.py:268
  1.6 0.7 maximum_bitcast_fusion
  2.3 4.5 %all-to-all-start = ((bf16[4,2,64,128]{3,2,1,0:T(8,128)(2,1)}), bf16[4,2,64,128]{3,2,1,0:T(8,128)(2,1)S(1)}, u32[]{:S(2)}, u32[]{:S(2)}) async-start(bf16[4,2,64,128]{3,2,1,0:T(8,128)(2,1)} %maximum_bitcast_fusion), calls=%async_computation | async-start | bytes 262144 | tf_op jit(solution)/shard_map/all_to_all | solution.py:266
  7.4 1.2 %copy.15 = bf16[128,4,4,128]{3,2,0,1:T(4,128)(2,1)S(1)} copy(bf16[128,4,4,128]{3,2,1,0:T(4,128)(2,1)} %bitcast.55) | data formatting | bytes 1048576 | tf_op jit(solution)/shard_map/reshape | solution.py:275
  8.7 0.3 copy_select_fusion
  9.0 1.2 %pad_maximum_fusion = bf16[4,1280,128]{2,1,0:T(8,128)(2,1)} fusion(bf16[4,128,128]{2,1,0:T(8,128)(2,1)S(1)} %get-tuple-element.80, bf16[4,128,128]{2,1,0:T(8,128)(2,1)S(1)} %get-tuple-element.81, bf16[4,512,128]{2,1,0:T(8,128)(2,1)S(1)} %bitcast.51, bf16[4,512,128]{2,1,0:T(8,128)(2,1)S(1)} %bitcast.50), kind=kLoop, calls=%fused_computation | loop fusion | flops 5242880 | bytes 2621440 | tf_op jit(solution)/shard_map/concatenate | solution.py:278
  10.2 2.6 %all-to-all-done.kv0 = bf16[4,2,64,128]{3,2,1,0:T(8,128)(2,1)S(1)} async-done(((bf16[4,2,64,128]{3,2,1,0:T(8,128)(2,1)}), bf16[4,2,64,128]{3,2,1,0:T(8,128)(2,1)S(1)}, u32[]{:S(2)}, u32[]{:S(2)}) %all-to-all-start) | async-done | bytes 131104 | tf_op jit(solution)/shard_map/all_to_all | solution.py:266
  12.7 3.5 %all-to-all-start.1 = ((bf16[4,1280,128]{2,1,0:T(8,128)(2,1)}), bf16[4,1280,128]{2,1,0:T(8,128)(2,1)S(1)}, u32[]{:S(2)}, u32[]{:S(2)}) async-start(bf16[4,1280,128]{2,1,0:T(8,128)(2,1)} %pad_maximum_fusion), calls=%async_computation.1 | async-start | bytes 2621440 | tf_op jit(solution)/shard_map/all_to_all | solution.py:266
  16.3 3.3 %collective-permute-start.2 = (bf16[4,2,64,128]{3,2,1,0:T(8,128)(2,1)S(1)}, bf16[4,2,64,128]{3,2,1,0:T(8,128)(2,1)S(1)}, u32[]{:S(2)}, u32[]{:S(2)}) collective-permute-start(bf16[4,2,64,128]{3,2,1,0:T(8,128)(2,1)S(1)} %all-to-all-done.kv0), channel_id=1, source_target_pairs={{0,8},{4,12},{8,16},{12,20},{16,24},{20,28},{24,0},{28,4},{1,9},{5... | collective-permute-start | bytes 393224 | tf_op jit(solution)/shard_map/ppermute | solution.py:263
  19.6 3.1 %collective-permute-start.3 = (bf16[4,2,64,128]{3,2,1,0:T(8,128)(2,1)S(1)}, bf16[4,2,64,128]{3,2,1,0:T(8,128)(2,1)S(1)}, u32[]{:S(2)}, u32[]{:S(2)}) collective-permute-start(bf16[4,2,64,128]{3,2,1,0:T(8,128)(2,1)S(1)} %all-to-all-done.kv0), channel_id=1, source_target_pairs={{0,24},{4,28},{8,0},{12,4},{16,8},{20,12},{24,16},{28,20},{1,25},{... | collective-permute-start | bytes 393224 | tf_op jit(solution)/shard_map/ppermute | solution.py:263
  22.8 2.4 %collective-permute-start.1 = (bf16[4,2,64,128]{3,2,1,0:T(8,128)(2,1)S(1)}, bf16[4,2,64,128]{3,2,1,0:T(8,128)(2,1)S(1)}, u32[]{:S(2)}, u32[]{:S(2)}) collective-permute-start(bf16[4,2,64,128]{3,2,1,0:T(8,128)(2,1)S(1)} %all-to-all-done.kv0), channel_id=1, source_target_pairs={{0,28},{4,0},{8,4},{12,8},{16,12},{20,16},{24,20},{28,24},{1,29},{... | collective-permute-start | bytes 393224 | tf_op jit(solution)/shard_map/ppermute | solution.py:263
  25.1 0.0 collective-permute-start
  25.1 1.9 %collective-permute-done.2.kv3 = bf16[4,2,64,128]{3,2,1,0:T(8,128)(2,1)S(1)} collective-permute-done((bf16[4,2,64,128]{3,2,1,0:T(8,128)(2,1)S(1)}, bf16[4,2,64,128]{3,2,1,0:T(8,128)(2,1)S(1)}, u32[]{:S(2)}, u32[]{:S(2)}) %collective-permute-start.2) | collective-permute-done | bytes 131104 | tf_op jit(solution)/shard_map/ppermute | solution.py:263
  27.0 1.9 %collective-permute-start.6 = (bf16[4,2,64,128]{3,2,1,0:T(8,128)(2,1)S(1)}, bf16[4,2,64,128]{3,2,1,0:T(8,128)(2,1)S(1)}, u32[]{:S(2)}, u32[]{:S(2)}) collective-permute-start(bf16[4,2,64,128]{3,2,1,0:T(8,128)(2,1)S(1)} %collective-permute-done.2.kv3), channel_id=1, source_target_pairs={{0,8},{4,12},{8,16},{12,20},{16,24},{20,28},{24,0},{28,4},{1,9},{5... | collective-permute-start | bytes 393224 | tf_op jit(solution)/shard_map/ppermute | solution.py:263
  28.9 1.0 %collective-permute-start.4 = (bf16[4,2,64,128]{3,2,1,0:T(8,128)(2,1)S(1)}, bf16[4,2,64,128]{3,2,1,0:T(8,128)(2,1)S(1)}, u32[]{:S(2)}, u32[]{:S(2)}) collective-permute-start(bf16[4,2,64,128]{3,2,1,0:T(8,128)(2,1)S(1)} %collective-permute-done.2.kv3), channel_id=1, source_target_pairs={{0,4},{4,8},{8,12},{12,16},{16,20},{20,24},{24,28},{28,0},{1,5},{5... | collective-permute-start | bytes 393224 | tf_op jit(solution)/shard_map/ppermute | solution.py:263
  30.0 0.0 collective-permute-done.3.kv4
  30.0 2.2 %collective-permute-start.5 = (bf16[4,2,64,128]{3,2,1,0:T(8,128)(2,1)S(1)}, bf16[4,2,64,128]{3,2,1,0:T(8,128)(2,1)S(1)}, u32[]{:S(2)}, u32[]{:S(2)}) collective-permute-start(bf16[4,2,64,128]{3,2,1,0:T(8,128)(2,1)S(1)} %collective-permute-done.3.kv4), channel_id=1, source_target_pairs={{0,28},{4,0},{8,4},{12,8},{16,12},{20,16},{24,20},{28,24},{1,29},{... | collective-permute-start | bytes 393224 | tf_op jit(solution)/shard_map/ppermute | solution.py:263
  32.2 0.0 collective-permute-done.1.kv2
  32.2 0.7 collective-permute-done.kv1
  32.9 0.1 all-to-all-done.1.pack
  33.0 4.7 %near_forward.1 = (bf16[1408,2048]{1,0:T(8,128)(2,1)S(1)}, f32[144,2048]{1,0:T(8,128)S(1)}, f32[8,2048]{1,0:T(8,128)S(1)}) custom-call(bf16[4,1280,128]{2,1,0:T(8,128)(2,1)S(1)} %all-to-all-done.1.pack, bf16[4,2,64,128]{3,2,1,0:T(8,128)(2,1)S(1)} %all-to-all-done.kv0, bf16[4,2,64,128]{3,2,1,0:T(8,128)(2,1)S(1)} %collective-permute-done.kv1, ...), custom_call_target="tpu_custom_call" | custom-call | flops 1476395008 | bytes 4194304 | tf_op jit(solution)/shard_map/near_forward/pallas_call | solution.py:244
  37.8 1.4 %collective-permute-done.4.kv0 = bf16[4,2,64,128]{3,2,1,0:T(8,128)(2,1)S(1)} collective-permute-done((bf16[4,2,64,128]{3,2,1,0:T(8,128)(2,1)S(1)}, bf16[4,2,64,128]{3,2,1,0:T(8,128)(2,1)S(1)}, u32[]{:S(2)}, u32[]{:S(2)}) %collective-permute-start.4) | collective-permute-done | bytes 131104 | tf_op jit(solution)/shard_map/ppermute | solution.py:263
  39.2 5.6 %far_both.1 = (bf16[4,512,128]{2,1,0:T(8,128)(2,1)S(1)}, f32[8,2048]{1,0:T(8,128)S(1)}, bf16[2048,128]{1,0:T(8,128)(2,1)S(1)}, bf16[2048,128]{1,0:T(8,128)(2,1)S...) custom-call(bf16[4,1280,128]{2,1,0:T(8,128)(2,1)S(1)} %all-to-all-do, ...), custom_call_target="tpu_custom_call" | custom-call | flops 2415919104 | bytes 4194304 | tf_op jit(solution)/shard_map/far_both/pallas_call | solution.py:244
  44.8 5.0 %collective-permute-start.7 = (bf16[4,2,64,128]{3,2,1,0:T(8,128)(2,1)S(1)}, bf16[4,2,64,128]{3,2,1,0:T(8,128)(2,1)S(1)}, u32[]{:S(2)}, u32[]{:S(2)}) collective-permute-start(bf16[4,2,64,128]{3,2,1,0:T(8,128)(2,1)S(1)} %get-tuple-element.48), channel_id=1, source_target_pairs={{0,24},{4,28},{8,0},{12,4},{16,8},{20,12},{24,16},{28,20},{1,25},{... | collective-permute-start | bytes 393224 | tf_op jit(solution)/shard_map/ppermute | solution.py:263
  49.8 1.0 %collective-permute-start.8 = (bf16[4,2,64,128]{3,2,1,0:T(8,128)(2,1)S(1)}, bf16[4,2,64,128]{3,2,1,0:T(8,128)(2,1)S(1)}, u32[]{:S(2)}, u32[]{:S(2)}) collective-permute-start(bf16[4,2,64,128]{3,2,1,0:T(8,128)(2,1)S(1)} %get-tuple-element.49), channel_id=1, source_target_pairs={{0,28},{4,0},{8,4},{12,8},{16,12},{20,16},{24,20},{28,24},{1,29},{... | collective-permute-start | bytes 393224 | tf_op jit(solution)/shard_map/ppermute | solution.py:263
  50.8 1.0 %collective-permute-start.9 = (bf16[4,2,64,128]{3,2,1,0:T(8,128)(2,1)S(1)}, bf16[4,2,64,128]{3,2,1,0:T(8,128)(2,1)S(1)}, u32[]{:S(2)}, u32[]{:S(2)}) collective-permute-start(bf16[4,2,64,128]{3,2,1,0:T(8,128)(2,1)S(1)} %get-tuple-element.50), channel_id=1, source_target_pairs={{0,4},{4,8},{8,12},{12,16},{16,20},{20,24},{24,28},{28,0},{1,5},{5... | collective-permute-start | bytes 393224 | tf_op jit(solution)/shard_map/ppermute | solution.py:263
  51.8 7.0 %near_backward.1 = (bf16[4,1280,128]{2,1,0:T(8,128)(2,1)}, bf16[4,2,64,128]{3,2,1,0:T(8,128)(2,1)S(1)}, bf16[4,2,64,128]{3,2,1,0:T(8,128)(2,1)S(1)}, bf16[4,2,64...) custom-call(bf16[4,1280,128]{2,1,0:T(8,128)(2,1)S(1)} %all-to-all-done.1.pack, ...), custom_call_target="tpu_custom_call" | custom-call | flops 2952790016 | bytes 4194304 | tf_op jit(solution)/shard_map/near_backward/pallas_call | solution.py:244
  58.8 3.6 %all-to-all-start.2 = ((bf16[4,1280,128]{2,1,0:T(8,128)(2,1)}), bf16[4,1280,128]{2,1,0:T(8,128)(2,1)S(1)}, u32[]{:S(2)}, u32[]{:S(2)}) async-start(bf16[4,1280,128]{2,1,0:T(8,128)(2,1)} %get-tuple-element.63), calls=%async_computation.2 | async-start | bytes 2621440 | tf_op jit(solution)/shard_map/all_to_all | solution.py:266
  62.4 0.5 collective-permute-start.13
  63.0 0.1 add_convert_fusion.2
  63.0 3.8 %collective-permute-start.12 = (bf16[4,2,64,128]{3,2,1,0:T(8,128)(2,1)S(1)}, bf16[4,2,64,128]{3,2,1,0:T(8,128)(2,1)S(1)}, u32[]{:S(2)}, u32[]{:S(2)}) collective-permute-start(bf16[4,2,64,128]{3,2,1,0:T(8,128)(2,1)S(1)} %add_convert_fusion.2), channel_id=1, source_target_pairs={{0,24},{4,28},{8,0},{12,4},{16,8},{20,12},{24,16},{28,20},{1,25},{... | collective-permute-start | bytes 393224 | tf_op jit(solution)/shard_map/ppermute | solution.py:263
  66.8 1.0 %collective-permute-start.10 = (bf16[4,2,64,128]{3,2,1,0:T(8,128)(2,1)S(1)}, bf16[4,2,64,128]{3,2,1,0:T(8,128)(2,1)S(1)}, u32[]{:S(2)}, u32[]{:S(2)}) collective-permute-start(bf16[4,2,64,128]{3,2,1,0:T(8,128)(2,1)S(1)} %get-tuple-element.56), channel_id=1, source_target_pairs={{0,28},{4,0},{8,4},{12,8},{16,12},{20,16},{24,20},{28,24},{1,29},{... | collective-permute-start | bytes 393224 | tf_op jit(solution)/shard_map/ppermute | solution.py:263
  67.8 1.0 %collective-permute-start.11 = (bf16[4,2,64,128]{3,2,1,0:T(8,128)(2,1)S(1)}, bf16[4,2,64,128]{3,2,1,0:T(8,128)(2,1)S(1)}, u32[]{:S(2)}, u32[]{:S(2)}) collective-permute-start(bf16[4,2,64,128]{3,2,1,0:T(8,128)(2,1)S(1)} %get-tuple-element.57), channel_id=1, source_target_pairs={{0,4},{4,8},{8,12},{12,16},{16,20},{20,24},{24,28},{28,0},{1,5},{5... | collective-permute-start | bytes 393224 | tf_op jit(solution)/shard_map/ppermute | solution.py:263
  68.8 1.7 %collective-permute-done.13 = bf16[4,2,64,128]{3,2,1,0:T(8,128)(2,1)S(1)} collective-permute-done((bf16[4,2,64,128]{3,2,1,0:T(8,128)(2,1)S(1)}, bf16[4,2,64,128]{3,2,1,0:T(8,128)(2,1)S(1)}, u32[]{:S(2)}, u32[]{:S(2)}) %collective-permute-start.13) | collective-permute-done | bytes 131104 | tf_op jit(solution)/shard_map/ppermute | solution.py:263
  70.4 0.0 collective-permute-done.12
  70.5 2.8 %collective-permute-done.10 = bf16[4,2,64,128]{3,2,1,0:T(8,128)(2,1)S(1)} collective-permute-done((bf16[4,2,64,128]{3,2,1,0:T(8,128)(2,1)S(1)}, bf16[4,2,64,128]{3,2,1,0:T(8,128)(2,1)S(1)}, u32[]{:S(2)}, u32[]{:S(2)}) %collective-permute-start.10) | collective-permute-done | bytes 131104 | tf_op jit(solution)/shard_map/ppermute | solution.py:263
  73.2 0.7 collective-permute-done.11
  74.0 0.7 add_convert_fusion
  74.7 2.6 %all-to-all-done.2 = bf16[4,1280,128]{2,1,0:T(8,128)(2,1)S(1)} async-done(((bf16[4,1280,128]{2,1,0:T(8,128)(2,1)}), bf16[4,1280,128]{2,1,0:T(8,128)(2,1)S(1)}, u32[]{:S(2)}, u32[]{:S(2)}) %all-to-all-start.2) | async-done | bytes 1310752 | tf_op jit(solution)/shard_map/all_to_all | solution.py:266
  77.3 3.3 %all-to-all-start.3 = ((bf16[4,2,64,128]{3,2,1,0:T(8,128)(2,1)}), bf16[4,2,64,128]{3,2,1,0:T(8,128)(2,1)S(1)}, u32[]{:S(2)}, u32[]{:S(2)}) async-start(bf16[4,2,64,128]{3,2,1,0:T(8,128)(2,1)} %add_convert_fusion), calls=%async_computation.3 | async-start | bytes 262144 | tf_op jit(solution)/shard_map/all_to_all | solution.py:266
  80.7 0.1 fusion
  80.7 0.2 copy.19
  80.9 1.0 %broadcast_select_fusion = bf16[1,128,16,128]{3,2,1,0:T(8,128)(2,1)} fusion(bf16[1,128,16,128]{3,2,1,0:T(8,128)(2,1)S(1)} %bitcast.52, pred[128]{0:T(512)(128)(4,1)S(1)} %iota_compare_fusion), kind=kLoop, calls=%fused_computation.2 | loop fusion | flops 262144 | bytes 1048704 | tf_op jit(solution)/shard_map/jit(_where)/select_n | solution.py:394
  81.9 1.0 %copy.20 = bf16[128,4,4,128]{3,2,1,0:T(4,128)(2,1)} copy(bf16[128,4,4,128]{3,2,0,1:T(4,128)(2,1)S(1)} %bitcast.53) | data formatting | bytes 1048576 | tf_op jit(solution)/shard_map/transpose | solution.py:391
  82.9 0.8 copy.22
  83.7 0.8 copy.21
  84.4 2.2 %all-to-all-done.3.x = bf16[4,2,64,128]{3,2,1,0:T(8,128)(2,1)S(1)} async-done(((bf16[4,2,64,128]{3,2,1,0:T(8,128)(2,1)}), bf16[4,2,64,128]{3,2,1,0:T(8,128)(2,1)S(1)}, u32[]{:S(2)}, u32[]{:S(2)}) %all-to-all-start.3) | async-done | bytes 131104 | tf_op jit(solution)/shard_map/all_to_all | solution.py:266
  86.6 0.9 %unpack_prompt.1 = (bf16[256,128]{1,0:T(8,128)(2,1)}, bf16[256,128]{1,0:T(8,128)(2,1)}) custom-call(bf16[4,2,64,128]{3,2,1,0:T(8,128)(2,1)S(1)} %all-to-all-done.3.x), custom_call_target="tpu_custom_call" | custom-call | tf_op jit(solution)/shard_map/unpack_prompt/pallas_call | solution.py:234
  (15 shorter events, 0.1 us)
Async XLA Ops:
  0.6 8.0 %copy-start.1 = (bf16[1,128,4,128]{3,2,1,0:T(4,128)(2,1)S(1)}, bf16[1,128,4,128]{3,2,1,0:T(4,128)(2,1)}, u32[]{:S(2)}) copy-start(bf16[1,128,4,128]{3,2,1,0:T(4,128)(2,1)} %param.9) | copy-start | bytes 393220
  0.6 8.0 %copy-start.2 = (bf16[1,128,4,128]{3,2,1,0:T(4,128)(2,1)S(1)}, bf16[1,128,4,128]{3,2,1,0:T(4,128)(2,1)}, u32[]{:S(2)}) copy-start(bf16[1,128,4,128]{3,2,1,0:T(4,128)(2,1)} %param.8) | copy-start | bytes 393220
  0.7 8.1 %copy-start = (bf16[1,128,16,128]{3,2,1,0:T(8,128)(2,1)S(1)}, bf16[1,128,16,128]{3,2,1,0:T(8,128)(2,1)}, u32[]{:S(2)}) copy-start(bf16[1,128,16,128]{3,2,1,0:T(8,128)(2,1)} %param.13) | copy-start | bytes 1572868
  2.3 10.4 %all-to-all-start = ((bf16[4,2,64,128]{3,2,1,0:T(8,128)(2,1)}), bf16[4,2,64,128]{3,2,1,0:T(8,128)(2,1)S(1)}, u32[]{:S(2)}, u32[]{:S(2)}) async-start(bf16[4,2,64,128]{3,2,1,0:T(8,128)(2,1)} %maximum_bitcast_fusion), calls=%async_computation | async-start | bytes 262144 | tf_op jit(solution)/shard_map/all_to_all | solution.py:266
  12.7 20.3 %all-to-all-start.1 = ((bf16[4,1280,128]{2,1,0:T(8,128)(2,1)}), bf16[4,1280,128]{2,1,0:T(8,128)(2,1)S(1)}, u32[]{:S(2)}, u32[]{:S(2)}) async-start(bf16[4,1280,128]{2,1,0:T(8,128)(2,1)} %pad_maximum_fusion), calls=%async_computation.1 | async-start | bytes 2621440 | tf_op jit(solution)/shard_map/all_to_all | solution.py:266
  16.3 10.7 %collective-permute-start.2 = (bf16[4,2,64,128]{3,2,1,0:T(8,128)(2,1)S(1)}, bf16[4,2,64,128]{3,2,1,0:T(8,128)(2,1)S(1)}, u32[]{:S(2)}, u32[]{:S(2)}) collective-permute-start(bf16[4,2,64,128]{3,2,1,0:T(8,128)(2,1)S(1)} %all-to-all-done.kv0), channel_id=1, source_target_pairs={{0,8},{4,12},{8,16},{12,20},{16,24},{20,28},{24,0},{28,4},{1,9},{5... | collective-permute-start | bytes 393224 | tf_op jit(solution)/shard_map/ppermute | solution.py:263
  19.6 10.3 %collective-permute-start.3 = (bf16[4,2,64,128]{3,2,1,0:T(8,128)(2,1)S(1)}, bf16[4,2,64,128]{3,2,1,0:T(8,128)(2,1)S(1)}, u32[]{:S(2)}, u32[]{:S(2)}) collective-permute-start(bf16[4,2,64,128]{3,2,1,0:T(8,128)(2,1)S(1)} %all-to-all-done.kv0), channel_id=1, source_target_pairs={{0,24},{4,28},{8,0},{12,4},{16,8},{20,12},{24,16},{28,20},{1,25},{... | collective-permute-start | bytes 393224 | tf_op jit(solution)/shard_map/ppermute | solution.py:263
  22.8 9.5 %collective-permute-start.1 = (bf16[4,2,64,128]{3,2,1,0:T(8,128)(2,1)S(1)}, bf16[4,2,64,128]{3,2,1,0:T(8,128)(2,1)S(1)}, u32[]{:S(2)}, u32[]{:S(2)}) collective-permute-start(bf16[4,2,64,128]{3,2,1,0:T(8,128)(2,1)S(1)} %all-to-all-done.kv0), channel_id=1, source_target_pairs={{0,28},{4,0},{8,4},{12,8},{16,12},{20,16},{24,20},{28,24},{1,29},{... | collective-permute-start | bytes 393224 | tf_op jit(solution)/shard_map/ppermute | solution.py:263
  25.1 7.7 %collective-permute-start = (bf16[4,2,64,128]{3,2,1,0:T(8,128)(2,1)S(1)}, bf16[4,2,64,128]{3,2,1,0:T(8,128)(2,1)S(1)}, u32[]{:S(2)}, u32[]{:S(2)}) collective-permute-start(bf16[4,2,64,128]{3,2,1,0:T(8,128)(2,1)S(1)} %all-to-all-done.kv0), channel_id=1, source_target_pairs={{0,4},{4,8},{8,12},{12,16},{16,20},{20,24},{24,28},{28,0},{1,5},{5... | collective-permute-start | bytes 393224 | tf_op jit(solution)/shard_map/ppermute | solution.py:263
  27.0 10.8 %collective-permute-start.6 = (bf16[4,2,64,128]{3,2,1,0:T(8,128)(2,1)S(1)}, bf16[4,2,64,128]{3,2,1,0:T(8,128)(2,1)S(1)}, u32[]{:S(2)}, u32[]{:S(2)}) collective-permute-start(bf16[4,2,64,128]{3,2,1,0:T(8,128)(2,1)S(1)} %collective-permute-done.2.kv3), channel_id=1, source_target_pairs={{0,8},{4,12},{8,16},{12,20},{16,24},{20,28},{24,0},{28,4},{1,9},{5... | collective-permute-start | bytes 393224 | tf_op jit(solution)/shard_map/ppermute | solution.py:263
  28.9 10.2 %collective-permute-start.4 = (bf16[4,2,64,128]{3,2,1,0:T(8,128)(2,1)S(1)}, bf16[4,2,64,128]{3,2,1,0:T(8,128)(2,1)S(1)}, u32[]{:S(2)}, u32[]{:S(2)}) collective-permute-start(bf16[4,2,64,128]{3,2,1,0:T(8,128)(2,1)S(1)} %collective-permute-done.2.kv3), channel_id=1, source_target_pairs={{0,4},{4,8},{8,12},{12,16},{16,20},{20,24},{24,28},{28,0},{1,5},{5... | collective-permute-start | bytes 393224 | tf_op jit(solution)/shard_map/ppermute | solution.py:263
  30.0 7.8 %collective-permute-start.5 = (bf16[4,2,64,128]{3,2,1,0:T(8,128)(2,1)S(1)}, bf16[4,2,64,128]{3,2,1,0:T(8,128)(2,1)S(1)}, u32[]{:S(2)}, u32[]{:S(2)}) collective-permute-start(bf16[4,2,64,128]{3,2,1,0:T(8,128)(2,1)S(1)} %collective-permute-done.3.kv4), channel_id=1, source_target_pairs={{0,28},{4,0},{8,4},{12,8},{16,12},{20,16},{24,20},{28,24},{1,29},{... | collective-permute-start | bytes 393224 | tf_op jit(solution)/shard_map/ppermute | solution.py:263
  44.8 14.0 %collective-permute-start.7 = (bf16[4,2,64,128]{3,2,1,0:T(8,128)(2,1)S(1)}, bf16[4,2,64,128]{3,2,1,0:T(8,128)(2,1)S(1)}, u32[]{:S(2)}, u32[]{:S(2)}) collective-permute-start(bf16[4,2,64,128]{3,2,1,0:T(8,128)(2,1)S(1)} %get-tuple-element.48), channel_id=1, source_target_pairs={{0,24},{4,28},{8,0},{12,4},{16,8},{20,12},{24,16},{28,20},{1,25},{... | collective-permute-start | bytes 393224 | tf_op jit(solution)/shard_map/ppermute | solution.py:263
  49.8 9.0 %collective-permute-start.8 = (bf16[4,2,64,128]{3,2,1,0:T(8,128)(2,1)S(1)}, bf16[4,2,64,128]{3,2,1,0:T(8,128)(2,1)S(1)}, u32[]{:S(2)}, u32[]{:S(2)}) collective-permute-start(bf16[4,2,64,128]{3,2,1,0:T(8,128)(2,1)S(1)} %get-tuple-element.49), channel_id=1, source_target_pairs={{0,28},{4,0},{8,4},{12,8},{16,12},{20,16},{24,20},{28,24},{1,29},{... | collective-permute-start | bytes 393224 | tf_op jit(solution)/shard_map/ppermute | solution.py:263
  50.8 8.0 %collective-permute-start.9 = (bf16[4,2,64,128]{3,2,1,0:T(8,128)(2,1)S(1)}, bf16[4,2,64,128]{3,2,1,0:T(8,128)(2,1)S(1)}, u32[]{:S(2)}, u32[]{:S(2)}) collective-permute-start(bf16[4,2,64,128]{3,2,1,0:T(8,128)(2,1)S(1)} %get-tuple-element.50), channel_id=1, source_target_pairs={{0,4},{4,8},{8,12},{12,16},{16,20},{20,24},{24,28},{28,0},{1,5},{5... | collective-permute-start | bytes 393224 | tf_op jit(solution)/shard_map/ppermute | solution.py:263
  58.8 18.5 %all-to-all-start.2 = ((bf16[4,1280,128]{2,1,0:T(8,128)(2,1)}), bf16[4,1280,128]{2,1,0:T(8,128)(2,1)S(1)}, u32[]{:S(2)}, u32[]{:S(2)}) async-start(bf16[4,1280,128]{2,1,0:T(8,128)(2,1)} %get-tuple-element.63), calls=%async_computation.2 | async-start | bytes 2621440 | tf_op jit(solution)/shard_map/all_to_all | solution.py:266
  62.4 8.0 %collective-permute-start.13 = (bf16[4,2,64,128]{3,2,1,0:T(8,128)(2,1)S(1)}, bf16[4,2,64,128]{3,2,1,0:T(8,128)(2,1)S(1)}, u32[]{:S(2)}, u32[]{:S(2)}) collective-permute-start(bf16[4,2,64,128]{3,2,1,0:T(8,128)(2,1)S(1)} %add_convert_fusion.1), channel_id=1, source_target_pairs={{0,8},{4,12},{8,16},{12,20},{16,24},{20,28},{24,0},{28,4},{1,9},{5... | collective-permute-start | bytes 393224 | tf_op jit(solution)/shard_map/ppermute | solution.py:263
  63.0 7.4 %collective-permute-start.12 = (bf16[4,2,64,128]{3,2,1,0:T(8,128)(2,1)S(1)}, bf16[4,2,64,128]{3,2,1,0:T(8,128)(2,1)S(1)}, u32[]{:S(2)}, u32[]{:S(2)}) collective-permute-start(bf16[4,2,64,128]{3,2,1,0:T(8,128)(2,1)S(1)} %add_convert_fusion.2), channel_id=1, source_target_pairs={{0,24},{4,28},{8,0},{12,4},{16,8},{20,12},{24,16},{28,20},{1,25},{... | collective-permute-start | bytes 393224 | tf_op jit(solution)/shard_map/ppermute | solution.py:263
  66.8 6.5 %collective-permute-start.10 = (bf16[4,2,64,128]{3,2,1,0:T(8,128)(2,1)S(1)}, bf16[4,2,64,128]{3,2,1,0:T(8,128)(2,1)S(1)}, u32[]{:S(2)}, u32[]{:S(2)}) collective-permute-start(bf16[4,2,64,128]{3,2,1,0:T(8,128)(2,1)S(1)} %get-tuple-element.56), channel_id=1, source_target_pairs={{0,28},{4,0},{8,4},{12,8},{16,12},{20,16},{24,20},{28,24},{1,29},{... | collective-permute-start | bytes 393224 | tf_op jit(solution)/shard_map/ppermute | solution.py:263
  67.8 6.2 %collective-permute-start.11 = (bf16[4,2,64,128]{3,2,1,0:T(8,128)(2,1)S(1)}, bf16[4,2,64,128]{3,2,1,0:T(8,128)(2,1)S(1)}, u32[]{:S(2)}, u32[]{:S(2)}) collective-permute-start(bf16[4,2,64,128]{3,2,1,0:T(8,128)(2,1)S(1)} %get-tuple-element.57), channel_id=1, source_target_pairs={{0,4},{4,8},{8,12},{12,16},{16,20},{20,24},{24,28},{28,0},{1,5},{5... | collective-permute-start | bytes 393224 | tf_op jit(solution)/shard_map/ppermute | solution.py:263
  77.3 9.3 %all-to-all-start.3 = ((bf16[4,2,64,128]{3,2,1,0:T(8,128)(2,1)}), bf16[4,2,64,128]{3,2,1,0:T(8,128)(2,1)S(1)}, u32[]{:S(2)}, u32[]{:S(2)}) async-start(bf16[4,2,64,128]{3,2,1,0:T(8,128)(2,1)} %add_convert_fusion), calls=%async_computation.3 | async-start | bytes 262144 | tf_op jit(solution)/shard_map/all_to_all | solution.py:266

commit v8 on v7

--- a/solution.py
+++ b/solution.py
@@ -68,13 +68,13 @@
         VT[D:D + 16, :] = jnp.ones((16, K.shape[0]), bf16)
 
 
-def store_blocks(out_kvs, ks, dk, dv):
-    spots = out_kvs[0].shape[2]
+def store_blocks(places, ks, dk, dv):
+    spots = places[0][0].shape[2]
     for j in range((ks.stop - ks.start) // spots):
-        block = ks.start // spots + j
+        out, at = places[ks.start // spots + j]
         part = slice(j * spots, (j + 1) * spots)
-        out_kvs[block // 4][block % 4, 0] = dk[part, :].astype(bf16)
-        out_kvs[block // 4][block % 4, 1] = dv[part, :].astype(bf16)
+        out[at, 0] = dk[part, :].astype(bf16)
+        out[at, 1] = dv[part, :].astype(bf16)
 
 
 def scores_into(S, at, s, top):
@@ -128,7 +128,7 @@
 
 
 def far_both(
-    pack, kv0, kv1, kv2, acc_ref, top_ref, o_ref, stat, Qs, Os, dqt, d0, d1, d2,
+    pack, kv0, kv1, kv2, acc_ref, top_ref, o_ref, stat, Qs, Os, dqt, low_out, high_out,
     K, V, S, Pm, KT, VT, Qn, On, *, T, G
 ):
     D = K.shape[1]
@@ -136,6 +136,8 @@
     C = D ** (-0.5)
     nk = K.shape[0]
     load_blocks((kv0, kv1, kv2), K, V, KT, VT)
+    places = [(low_out, i) for i in range(4)] + [(high_out, i) for i in range(4)]
+    places += [(low_out, 4), (low_out, 5), (high_out, 4), (high_out, 5)]
 
     def score(r, ks, top):
         s = dot(K[ks, :], pack[r, 0:R, :], NT)
@@ -190,7 +192,7 @@
                 dqt[:, rows] = part
             else:
                 dqt[:, rows] += part
-        store_blocks((d0, d1, d2), ks, dk, dv)
+        store_blocks(places, ks, dk, dv)
 
 
 def near_backward(
@@ -202,6 +204,7 @@
     C = D ** (-0.5)
     nk = K.shape[0]
     load_blocks((kv0, kv1, kv2, kv3, kv4), K, V, KT, None)
+    places = [(x, i) for x in (d0, d1, d2, d3, d4) for i in range(4)]
     own = slice(nk, nk + T)
     for r in range(4):
         rows = slice(r * R, (r + 1) * R)
@@ -224,7 +227,7 @@
     for ks in spans(nk, BACKWARD_CHUNK):
         dk = dot(DS[ks, :], Qs[...], NN)
         dv = dot(Pm[ks, :], Os[...], NN)
-        store_blocks((d0, d1, d2, d3, d4), ks, dk, dv)
+        store_blocks(places, ks, dk, dv)
 
 
 VMEM_REF = pl.BlockSpec(memory_space=pltpu.VMEM)
@@ -325,7 +328,7 @@
         cost(2, near_keys + T),
         pack, *near,
     )
-    out, stat, q_near, g_near, dqt, d3, dm3, d4 = call(
+    out, stat, q_near, g_near, dqt, down, up = call(
         functools.partial(far_both, T=T, G=G),
         "far_both",
         (
@@ -334,7 +337,8 @@
             shape((rows, D), bf16),
             shape((rows, D), bf16),
             shape((D, rows), f32),
-            block, block, block,
+            shape((6,) + kv.shape[1:], bf16),
+            shape((6,) + kv.shape[1:], bf16),
         ),
         [
             pltpu.VMEM((far_keys, D), bf16),
@@ -362,16 +366,22 @@
         cost(4, near_keys + T),
         pack, *near, weights, out, stat, q_near, g_near, dqt,
     )
-    via_2 = over_z(d4, -2)
-    via_1 = over_z(d3, -1)
-    via_m1 = over_z(dm3, 1)
-    (via_2, via_1, via_m1, home, d1, dm1, d2, dm2) = lax.optimization_barrier(
-        (via_2, via_1, via_m1, home, d1, dm1, d2, dm2)
+    via_down = over_z(down, -2)
+    via_up = over_z(up, 2)
+    (via_down, via_up, d1, dm1, d2, dm2) = lax.optimization_barrier(
+        (via_down, via_up, d1, dm1, d2, dm2)
     )
     home = swap_y(home)
-    far = (d2.astype(f32) + via_1.astype(f32) + via_2.astype(f32)).astype(bf16)
-    far_m = (dm2.astype(f32) + via_m1.astype(f32)).astype(bf16)
-    parts = [over_z(d1, -1), over_z(dm1, 1), over_z(far, -2), over_z(far_m, 2)]
+
+    def add(x, y):
+        return (x.astype(f32) + y.astype(f32)).astype(bf16)
+
+    parts = [
+        over_z(jnp.concatenate([add(d2[0:2], via_down[4:6]), d2[2:4]]), -2),
+        over_z(jnp.concatenate([dm2[0:2], add(dm2[2:4], via_up[4:6])]), 2),
+        over_z(add(d1, via_down[0:4]), -1),
+        over_z(add(dm1, via_up[0:4]), 1),
+    ]
     total = d0.astype(f32)
     for x in parts:
         total = total + x.astype(f32)

time: 88 us -> 86.6 us (0.984)
  starting transfers between devices: 42.3 us -> 40.7 us
    ppermute x14 -> x13, starting transfers between devices: 27.4 us -> 25.8 us  [over_z(): return lax.ppermute(x, 'z', [(i, (i + k) % 8) for i in range(8)])]
    ppermute x14 -> x13, waiting for transfers between devices: 9.09 us -> 9.05 us  [over_z(): return lax.ppermute(x, 'z', [(i, (i + k) % 8) for i in range(8)])]
  transfers between devices with their start and end apart: 18 -> 17, of which waited for: 10 -> 10; matrix products, arithmetic and copies ran while one was open for 8% -> 9% of each run, Pallas kernels for 13% -> 14%
where the time goes in v8:
time: 86.6 us; the launch traced here: 86 us
  starting transfers between devices  40.7 us (47%)
  Pallas kernels  18.3 us (21%)
  waiting for transfers between devices  16.5 us (19%)
  local copies, waits for them, and re-layouts  5.01 us (6%)
  other arithmetic  4.02 us (5%)
  between operations  1.53 us (2%)
    ppermute x13, starting transfers between devices, over_z(): return lax.ppermute(x, 'z', [(i, (i + k) % 8) for i in range(8)])  25.8 us
    pallas_call x3, Pallas kernels, call(): pl.pallas_call(body, out_shape=out_shape, scratch_shapes=scratch, compile...  17.4 us
    all_to_all x4, starting transfers between devices, swap_y(): return lax.all_to_all(x, 'y', 0, 0, tiled=True)  14.9 us
    ppermute x13, waiting for transfers between devices, over_z(): return lax.ppermute(x, 'z', [(i, (i + k) % 8) for i in range(8)])  9.05 us
    all_to_all x4, waiting for transfers between devices, swap_y(): return lax.all_to_all(x, 'y', 0, 0, tiled=True)  7.47 us
  transfers between devices with their start and end apart: 17, of which 10 were waited for; matrix products, arithmetic and copies ran while one was open for 9% of the time, Pallas kernels for 14%

profile of v8, /device:TPU:4, one launch (start us, length us, event | category | flops | bytes accessed | tf_op | source)
XLA Modules:
  0.0 86.0 jit_solution(2691590181818684321)
XLA Ops:
  0.7 1.0 %copy_bitcast_fusion.2 = (bf16[1,64,4,128]{3,1,0,2:T(8,128)(2,1)S(1)}, bf16[1,64,4,128]{3,1,0,2:T(8,128)(2,1)S(1)}) fusion(bf16[64,4,128]{2,1,0:T(4,128)(2,1)} %param.11, bf16[64,4,128]{2,1,0:T(4,128)(2,1)} %param.10), kind=kLoop, calls=%fused_computation.15 | loop fusion | bytes 262144 | tf_op jit(solution)/shard_map/stack | solution.py:271
  1.6 0.7 maximum_bitcast_fusion
  2.3 4.5 %all-to-all-start = ((bf16[4,2,64,128]{3,2,1,0:T(8,128)(2,1)}), bf16[4,2,64,128]{3,2,1,0:T(8,128)(2,1)S(1)}, u32[]{:S(2)}, u32[]{:S(2)}) async-start(bf16[4,2,64,128]{3,2,1,0:T(8,128)(2,1)} %maximum_bitcast_fusion), calls=%async_computation | async-start | bytes 262144 | tf_op jit(solution)/shard_map/all_to_all | solution.py:269
  7.4 1.2 %copy.15 = bf16[128,4,4,128]{3,2,0,1:T(4,128)(2,1)S(1)} copy(bf16[128,4,4,128]{3,2,1,0:T(4,128)(2,1)} %bitcast.55) | data formatting | bytes 1048576 | tf_op jit(solution)/shard_map/reshape | solution.py:278
  8.7 0.3 copy_select_fusion
  9.0 1.2 %pad_maximum_fusion = bf16[4,1280,128]{2,1,0:T(8,128)(2,1)} fusion(bf16[4,128,128]{2,1,0:T(8,128)(2,1)S(1)} %get-tuple-element.74, bf16[4,128,128]{2,1,0:T(8,128)(2,1)S(1)} %get-tuple-element.75, bf16[4,512,128]{2,1,0:T(8,128)(2,1)S(1)} %bitcast.51, bf16[4,512,128]{2,1,0:T(8,128)(2,1)S(1)} %bitcast.50), kind=kLoop, calls=%fused_computation | loop fusion | flops 5242880 | bytes 2621440 | tf_op jit(solution)/shard_map/concatenate | solution.py:281
  10.2 2.5 %all-to-all-done.kv0 = bf16[4,2,64,128]{3,2,1,0:T(8,128)(2,1)S(1)} async-done(((bf16[4,2,64,128]{3,2,1,0:T(8,128)(2,1)}), bf16[4,2,64,128]{3,2,1,0:T(8,128)(2,1)S(1)}, u32[]{:S(2)}, u32[]{:S(2)}) %all-to-all-start) | async-done | bytes 131104 | tf_op jit(solution)/shard_map/all_to_all | solution.py:269
  12.7 3.5 %all-to-all-start.1 = ((bf16[4,1280,128]{2,1,0:T(8,128)(2,1)}), bf16[4,1280,128]{2,1,0:T(8,128)(2,1)S(1)}, u32[]{:S(2)}, u32[]{:S(2)}) async-start(bf16[4,1280,128]{2,1,0:T(8,128)(2,1)} %pad_maximum_fusion), calls=%async_computation.1 | async-start | bytes 2621440 | tf_op jit(solution)/shard_map/all_to_all | solution.py:269
  16.3 3.3 %collective-permute-start.2 = (bf16[4,2,64,128]{3,2,1,0:T(8,128)(2,1)S(1)}, bf16[4,2,64,128]{3,2,1,0:T(8,128)(2,1)S(1)}, u32[]{:S(2)}, u32[]{:S(2)}) collective-permute-start(bf16[4,2,64,128]{3,2,1,0:T(8,128)(2,1)S(1)} %all-to-all-done.kv0), channel_id=1, source_target_pairs={{0,8},{4,12},{8,16},{12,20},{16,24},{20,28},{24,0},{28,4},{1,9},{5... | collective-permute-start | bytes 393224 | tf_op jit(solution)/shard_map/ppermute | solution.py:266
  19.6 3.1 %collective-permute-start.3 = (bf16[4,2,64,128]{3,2,1,0:T(8,128)(2,1)S(1)}, bf16[4,2,64,128]{3,2,1,0:T(8,128)(2,1)S(1)}, u32[]{:S(2)}, u32[]{:S(2)}) collective-permute-start(bf16[4,2,64,128]{3,2,1,0:T(8,128)(2,1)S(1)} %all-to-all-done.kv0), channel_id=1, source_target_pairs={{0,24},{4,28},{8,0},{12,4},{16,8},{20,12},{24,16},{28,20},{1,25},{... | collective-permute-start | bytes 393224 | tf_op jit(solution)/shard_map/ppermute | solution.py:266
  22.8 2.4 %collective-permute-start.1 = (bf16[4,2,64,128]{3,2,1,0:T(8,128)(2,1)S(1)}, bf16[4,2,64,128]{3,2,1,0:T(8,128)(2,1)S(1)}, u32[]{:S(2)}, u32[]{:S(2)}) collective-permute-start(bf16[4,2,64,128]{3,2,1,0:T(8,128)(2,1)S(1)} %all-to-all-done.kv0), channel_id=1, source_target_pairs={{0,28},{4,0},{8,4},{12,8},{16,12},{20,16},{24,20},{28,24},{1,29},{... | collective-permute-start | bytes 393224 | tf_op jit(solution)/shard_map/ppermute | solution.py:266
  25.1 0.0 collective-permute-start
  25.1 1.9 %collective-permute-done.2.kv3 = bf16[4,2,64,128]{3,2,1,0:T(8,128)(2,1)S(1)} collective-permute-done((bf16[4,2,64,128]{3,2,1,0:T(8,128)(2,1)S(1)}, bf16[4,2,64,128]{3,2,1,0:T(8,128)(2,1)S(1)}, u32[]{:S(2)}, u32[]{:S(2)}) %collective-permute-start.2) | collective-permute-done | bytes 131104 | tf_op jit(solution)/shard_map/ppermute | solution.py:266
  27.0 1.9 %collective-permute-start.6 = (bf16[4,2,64,128]{3,2,1,0:T(8,128)(2,1)S(1)}, bf16[4,2,64,128]{3,2,1,0:T(8,128)(2,1)S(1)}, u32[]{:S(2)}, u32[]{:S(2)}) collective-permute-start(bf16[4,2,64,128]{3,2,1,0:T(8,128)(2,1)S(1)} %collective-permute-done.2.kv3), channel_id=1, source_target_pairs={{0,8},{4,12},{8,16},{12,20},{16,24},{20,28},{24,0},{28,4},{1,9},{5... | collective-permute-start | bytes 393224 | tf_op jit(solution)/shard_map/ppermute | solution.py:266
  28.9 1.0 %collective-permute-start.4 = (bf16[4,2,64,128]{3,2,1,0:T(8,128)(2,1)S(1)}, bf16[4,2,64,128]{3,2,1,0:T(8,128)(2,1)S(1)}, u32[]{:S(2)}, u32[]{:S(2)}) collective-permute-start(bf16[4,2,64,128]{3,2,1,0:T(8,128)(2,1)S(1)} %collective-permute-done.2.kv3), channel_id=1, source_target_pairs={{0,4},{4,8},{8,12},{12,16},{16,20},{20,24},{24,28},{28,0},{1,5},{5... | collective-permute-start | bytes 393224 | tf_op jit(solution)/shard_map/ppermute | solution.py:266
  30.0 0.0 collective-permute-done.3.kv4
  30.0 2.2 %collective-permute-start.5 = (bf16[4,2,64,128]{3,2,1,0:T(8,128)(2,1)S(1)}, bf16[4,2,64,128]{3,2,1,0:T(8,128)(2,1)S(1)}, u32[]{:S(2)}, u32[]{:S(2)}) collective-permute-start(bf16[4,2,64,128]{3,2,1,0:T(8,128)(2,1)S(1)} %collective-permute-done.3.kv4), channel_id=1, source_target_pairs={{0,28},{4,0},{8,4},{12,8},{16,12},{20,16},{24,20},{28,24},{1,29},{... | collective-permute-start | bytes 393224 | tf_op jit(solution)/shard_map/ppermute | solution.py:266
  32.2 0.0 collective-permute-done.1.kv2
  32.2 0.7 collective-permute-done.kv1
  32.9 0.1 all-to-all-done.1.pack
  33.0 4.7 %near_forward.1 = (bf16[1408,2048]{1,0:T(8,128)(2,1)S(1)}, f32[144,2048]{1,0:T(8,128)S(1)}, f32[8,2048]{1,0:T(8,128)S(1)}) custom-call(bf16[4,1280,128]{2,1,0:T(8,128)(2,1)S(1)} %all-to-all-done.1.pack, bf16[4,2,64,128]{3,2,1,0:T(8,128)(2,1)S(1)} %all-to-all-done.kv0, bf16[4,2,64,128]{3,2,1,0:T(8,128)(2,1)S(1)} %collective-permute-done.kv1, ...), custom_call_target="tpu_custom_call" | custom-call | flops 1476395008 | bytes 4194304 | tf_op jit(solution)/shard_map/near_forward/pallas_call | solution.py:247
  37.8 0.0 collective-permute-done.5.kv1
  37.8 0.0 collective-permute-done.6.kv2
  37.8 1.4 %collective-permute-done.4.kv0 = bf16[4,2,64,128]{3,2,1,0:T(8,128)(2,1)S(1)} collective-permute-done((bf16[4,2,64,128]{3,2,1,0:T(8,128)(2,1)S(1)}, bf16[4,2,64,128]{3,2,1,0:T(8,128)(2,1)S(1)}, u32[]{:S(2)}, u32[]{:S(2)}) %collective-permute-start.4) | collective-permute-done | bytes 131104 | tf_op jit(solution)/shard_map/ppermute | solution.py:266
  39.2 5.6 %far_both.1 = (bf16[4,512,128]{2,1,0:T(8,128)(2,1)S(1)}, f32[8,2048]{1,0:T(8,128)S(1)}, bf16[2048,128]{1,0:T(8,128)(2,1)S(1)}, bf16[2048,128]{1,0:T(8,128)(2,1)S...) custom-call(bf16[4,1280,128]{2,1,0:T(8,128)(2,1)S(1)} %all-to-all-done.1.pack, ...), custom_call_target="tpu_custom_call" | custom-call | flops 2415919104 | bytes 4194304 | tf_op jit(solution)/shard_map/far_both/pallas_call | solution.py:247
  44.8 5.0 %collective-permute-start.7 = (bf16[6,2,64,128]{3,2,1,0:T(8,128)(2,1)S(1)}, bf16[6,2,64,128]{3,2,1,0:T(8,128)(2,1)S(1)}, u32[]{:S(2)}, u32[]{:S(2)}) collective-permute-start(bf16[6,2,64,128]{3,2,1,0:T(8,128)(2,1)S(1)} %get-tuple-element.45), channel_id=1, source_target_pairs={{0,24},{4,28},{8,0},{12,4},{16,8},{20,12},{24,16},{28,20},{1,25},{... | collective-permute-start | bytes 589832 | tf_op jit(solution)/shard_map/ppermute | solution.py:266
  49.8 0.0 collective-permute-start.8
  49.8 7.0 %near_backward.1 = (bf16[4,1280,128]{2,1,0:T(8,128)(2,1)}, bf16[4,2,64,128]{3,2,1,0:T(8,128)(2,1)S(1)}, bf16[4,2,64,128]{3,2,1,0:T(8,128)(2,1)S(1)}, bf16[4,2,64...) custom-call(bf16[4,1280,128]{2,1,0:T(8,128)(2,1)S(1)} %all-to-all-done.1.pack, ...), custom_call_target="tpu_custom_call" | custom-call | flops 2952790016 | bytes 4194304 | tf_op jit(solution)/shard_map/near_backward/pallas_call | solution.py:247
  56.8 3.5 %all-to-all-start.2 = ((bf16[4,1280,128]{2,1,0:T(8,128)(2,1)}), bf16[4,1280,128]{2,1,0:T(8,128)(2,1)S(1)}, u32[]{:S(2)}, u32[]{:S(2)}) async-start(bf16[4,1280,128]{2,1,0:T(8,128)(2,1)} %get-tuple-element.57), calls=%async_computation.2 | async-start | bytes 2621440 | tf_op jit(solution)/shard_map/all_to_all | solution.py:269
  60.3 0.0 collective-permute-done.8
  60.5 2.6 %collective-permute-start.10 = (bf16[4,2,64,128]{3,2,1,0:T(8,128)(2,1)S(1)}, bf16[4,2,64,128]{3,2,1,0:T(8,128)(2,1)S(1)}, u32[]{:S(2)}, u32[]{:S(2)}) collective-permute-start(bf16[4,2,64,128]{3,2,1,0:T(8,128)(2,1)S(1)} %pad_maximum_fusion.2), channel_id=1, source_target_pairs={{0,8},{4,12},{8,16},{12,20},{16,24},{20,28},{24,0},{28,4},{1,9},{5... | collective-permute-start | bytes 393224 | tf_op jit(solution)/shard_map/ppermute | solution.py:266
  63.1 0.5 collective-permute-start.12
  63.7 2.3 %collective-permute-start.9 = (bf16[4,2,64,128]{3,2,1,0:T(8,128)(2,1)S(1)}, bf16[4,2,64,128]{3,2,1,0:T(8,128)(2,1)S(1)}, u32[]{:S(2)}, u32[]{:S(2)}) collective-permute-start(bf16[4,2,64,128]{3,2,1,0:T(8,128)(2,1)S(1)} %pad_maximum_fusion.1), channel_id=1, source_target_pairs={{0,24},{4,28},{8,0},{12,4},{16,8},{20,12},{24,16},{28,20},{1,25},{... | collective-permute-start | bytes 393224 | tf_op jit(solution)/shard_map/ppermute | solution.py:266
  66.0 1.4 %collective-permute-start.11 = (bf16[4,2,64,128]{3,2,1,0:T(8,128)(2,1)S(1)}, bf16[4,2,64,128]{3,2,1,0:T(8,128)(2,1)S(1)}, u32[]{:S(2)}, u32[]{:S(2)}) collective-permute-start(bf16[4,2,64,128]{3,2,1,0:T(8,128)(2,1)S(1)} %add_convert_fusion.2), channel_id=1, source_target_pairs={{0,28},{4,0},{8,4},{12,8},{16,12},{20,16},{24,20},{28,24},{1,29},{... | collective-permute-start | bytes 393224 | tf_op jit(solution)/shard_map/ppermute | solution.py:266
  67.3 0.8 collective-permute-done.10
  68.1 2.3 %collective-permute-done.12 = bf16[4,2,64,128]{3,2,1,0:T(8,128)(2,1)S(1)} collective-permute-done((bf16[4,2,64,128]{3,2,1,0:T(8,128)(2,1)S(1)}, bf16[4,2,64,128]{3,2,1,0:T(8,128)(2,1)S(1)}, u32[]{:S(2)}, u32[]{:S(2)}) %collective-permute-start.12) | collective-permute-done | bytes 131104 | tf_op jit(solution)/shard_map/ppermute | solution.py:266
  70.5 2.0 %collective-permute-done.11 = bf16[4,2,64,128]{3,2,1,0:T(8,128)(2,1)S(1)} collective-permute-done((bf16[4,2,64,128]{3,2,1,0:T(8,128)(2,1)S(1)}, bf16[4,2,64,128]{3,2,1,0:T(8,128)(2,1)S(1)}, u32[]{:S(2)}, u32[]{:S(2)}) %collective-permute-start.11) | collective-permute-done | bytes 131104 | tf_op jit(solution)/shard_map/ppermute | solution.py:266
  72.5 0.7 add_convert_fusion
  73.2 2.6 %all-to-all-done.2 = bf16[4,1280,128]{2,1,0:T(8,128)(2,1)S(1)} async-done(((bf16[4,1280,128]{2,1,0:T(8,128)(2,1)}), bf16[4,1280,128]{2,1,0:T(8,128)(2,1)S(1)}, u32[]{:S(2)}, u32[]{:S(2)}) %all-to-all-start.2) | async-done | bytes 1310752 | tf_op jit(solution)/shard_map/all_to_all | solution.py:269
  75.9 3.3 %all-to-all-start.3 = ((bf16[4,2,64,128]{3,2,1,0:T(8,128)(2,1)}), bf16[4,2,64,128]{3,2,1,0:T(8,128)(2,1)S(1)}, u32[]{:S(2)}, u32[]{:S(2)}) async-start(bf16[4,2,64,128]{3,2,1,0:T(8,128)(2,1)} %add_convert_fusion), calls=%async_computation.3 | async-start | bytes 262144 | tf_op jit(solution)/shard_map/all_to_all | solution.py:269
  79.2 0.1 fusion
  79.3 0.2 copy.19
  79.5 1.0 %broadcast_select_fusion = bf16[1,128,16,128]{3,2,1,0:T(8,128)(2,1)} fusion(bf16[1,128,16,128]{3,2,1,0:T(8,128)(2,1)S(1)} %bitcast.52, pred[128]{0:T(512)(128)(4,1)S(1)} %iota_compare_fusion), kind=kLoop, calls=%fused_computation.2 | loop fusion | flops 262144 | bytes 1048704 | tf_op jit(solution)/shard_map/jit(_where)/select_n | solution.py:404
  80.5 1.0 %copy.20 = bf16[128,4,4,128]{3,2,1,0:T(4,128)(2,1)} copy(bf16[128,4,4,128]{3,2,0,1:T(4,128)(2,1)S(1)} %bitcast.53) | data formatting | bytes 1048576 | tf_op jit(solution)/shard_map/transpose | solution.py:401
  81.4 0.8 copy.22
  82.2 0.8 copy.21
  83.0 2.2 %all-to-all-done.3.x = bf16[4,2,64,128]{3,2,1,0:T(8,128)(2,1)S(1)} async-done(((bf16[4,2,64,128]{3,2,1,0:T(8,128)(2,1)}), bf16[4,2,64,128]{3,2,1,0:T(8,128)(2,1)S(1)}, u32[]{:S(2)}, u32[]{:S(2)}) %all-to-all-start.3) | async-done | bytes 131104 | tf_op jit(solution)/shard_map/all_to_all | solution.py:269
  85.1 0.9 %unpack_prompt.1 = (bf16[256,128]{1,0:T(8,128)(2,1)}, bf16[256,128]{1,0:T(8,128)(2,1)}) custom-call(bf16[4,2,64,128]{3,2,1,0:T(8,128)(2,1)S(1)} %all-to-all-done.3.x), custom_call_target="tpu_custom_call" | custom-call | tf_op jit(solution)/shard_map/unpack_prompt/pallas_call | solution.py:237
  (19 shorter events, 0.2 us)
Async XLA Ops:
  0.6 8.0 %copy-start.1 = (bf16[1,128,4,128]{3,2,1,0:T(4,128)(2,1)S(1)}, bf16[1,128,4,128]{3,2,1,0:T(4,128)(2,1)}, u32[]{:S(2)}) copy-start(bf16[1,128,4,128]{3,2,1,0:T(4,128)(2,1)} %param.9) | copy-start | bytes 393220
  0.6 8.0 %copy-start.2 = (bf16[1,128,4,128]{3,2,1,0:T(4,128)(2,1)S(1)}, bf16[1,128,4,128]{3,2,1,0:T(4,128)(2,1)}, u32[]{:S(2)}) copy-start(bf16[1,128,4,128]{3,2,1,0:T(4,128)(2,1)} %param.8) | copy-start | bytes 393220
  0.7 8.1 %copy-start = (bf16[1,128,16,128]{3,2,1,0:T(8,128)(2,1)S(1)}, bf16[1,128,16,128]{3,2,1,0:T(8,128)(2,1)}, u32[]{:S(2)}) copy-start(bf16[1,128,16,128]{3,2,1,0:T(8,128)(2,1)} %param.13) | copy-start | bytes 1572868
  2.3 10.4 %all-to-all-start = ((bf16[4,2,64,128]{3,2,1,0:T(8,128)(2,1)}), bf16[4,2,64,128]{3,2,1,0:T(8,128)(2,1)S(1)}, u32[]{:S(2)}, u32[]{:S(2)}) async-start(bf16[4,2,64,128]{3,2,1,0:T(8,128)(2,1)} %maximum_bitcast_fusion), calls=%async_computation | async-start | bytes 262144 | tf_op jit(solution)/shard_map/all_to_all | solution.py:269
  12.7 20.3 %all-to-all-start.1 = ((bf16[4,1280,128]{2,1,0:T(8,128)(2,1)}), bf16[4,1280,128]{2,1,0:T(8,128)(2,1)S(1)}, u32[]{:S(2)}, u32[]{:S(2)}) async-start(bf16[4,1280,128]{2,1,0:T(8,128)(2,1)} %pad_maximum_fusion), calls=%async_computation.1 | async-start | bytes 2621440 | tf_op jit(solution)/shard_map/all_to_all | solution.py:269
  16.3 10.7 %collective-permute-start.2 = (bf16[4,2,64,128]{3,2,1,0:T(8,128)(2,1)S(1)}, bf16[4,2,64,128]{3,2,1,0:T(8,128)(2,1)S(1)}, u32[]{:S(2)}, u32[]{:S(2)}) collective-permute-start(bf16[4,2,64,128]{3,2,1,0:T(8,128)(2,1)S(1)} %all-to-all-done.kv0), channel_id=1, source_target_pairs={{0,8},{4,12},{8,16},{12,20},{16,24},{20,28},{24,0},{28,4},{1,9},{5... | collective-permute-start | bytes 393224 | tf_op jit(solution)/shard_map/ppermute | solution.py:266
  19.6 10.3 %collective-permute-start.3 = (bf16[4,2,64,128]{3,2,1,0:T(8,128)(2,1)S(1)}, bf16[4,2,64,128]{3,2,1,0:T(8,128)(2,1)S(1)}, u32[]{:S(2)}, u32[]{:S(2)}) collective-permute-start(bf16[4,2,64,128]{3,2,1,0:T(8,128)(2,1)S(1)} %all-to-all-done.kv0), channel_id=1, source_target_pairs={{0,24},{4,28},{8,0},{12,4},{16,8},{20,12},{24,16},{28,20},{1,25},{... | collective-permute-start | bytes 393224 | tf_op jit(solution)/shard_map/ppermute | solution.py:266
  22.8 9.5 %collective-permute-start.1 = (bf16[4,2,64,128]{3,2,1,0:T(8,128)(2,1)S(1)}, bf16[4,2,64,128]{3,2,1,0:T(8,128)(2,1)S(1)}, u32[]{:S(2)}, u32[]{:S(2)}) collective-permute-start(bf16[4,2,64,128]{3,2,1,0:T(8,128)(2,1)S(1)} %all-to-all-done.kv0), channel_id=1, source_target_pairs={{0,28},{4,0},{8,4},{12,8},{16,12},{20,16},{24,20},{28,24},{1,29},{... | collective-permute-start | bytes 393224 | tf_op jit(solution)/shard_map/ppermute | solution.py:266
  25.1 7.7 %collective-permute-start = (bf16[4,2,64,128]{3,2,1,0:T(8,128)(2,1)S(1)}, bf16[4,2,64,128]{3,2,1,0:T(8,128)(2,1)S(1)}, u32[]{:S(2)}, u32[]{:S(2)}) collective-permute-start(bf16[4,2,64,128]{3,2,1,0:T(8,128)(2,1)S(1)} %all-to-all-done.kv0), channel_id=1, source_target_pairs={{0,4},{4,8},{8,12},{12,16},{16,20},{20,24},{24,28},{28,0},{1,5},{5... | collective-permute-start | bytes 393224 | tf_op jit(solution)/shard_map/ppermute | solution.py:266
  27.0 10.8 %collective-permute-start.6 = (bf16[4,2,64,128]{3,2,1,0:T(8,128)(2,1)S(1)}, bf16[4,2,64,128]{3,2,1,0:T(8,128)(2,1)S(1)}, u32[]{:S(2)}, u32[]{:S(2)}) collective-permute-start(bf16[4,2,64,128]{3,2,1,0:T(8,128)(2,1)S(1)} %collective-permute-done.2.kv3), channel_id=1, source_target_pairs={{0,8},{4,12},{8,16},{12,20},{16,24},{20,28},{24,0},{28,4},{1,9},{5... | collective-permute-start | bytes 393224 | tf_op jit(solution)/shard_map/ppermute | solution.py:266
  28.9 10.2 %collective-permute-start.4 = (bf16[4,2,64,128]{3,2,1,0:T(8,128)(2,1)S(1)}, bf16[4,2,64,128]{3,2,1,0:T(8,128)(2,1)S(1)}, u32[]{:S(2)}, u32[]{:S(2)}) collective-permute-start(bf16[4,2,64,128]{3,2,1,0:T(8,128)(2,1)S(1)} %collective-permute-done.2.kv3), channel_id=1, source_target_pairs={{0,4},{4,8},{8,12},{12,16},{16,20},{20,24},{24,28},{28,0},{1,5},{5... | collective-permute-start | bytes 393224 | tf_op jit(solution)/shard_map/ppermute | solution.py:266
  30.0 7.8 %collective-permute-start.5 = (bf16[4,2,64,128]{3,2,1,0:T(8,128)(2,1)S(1)}, bf16[4,2,64,128]{3,2,1,0:T(8,128)(2,1)S(1)}, u32[]{:S(2)}, u32[]{:S(2)}) collective-permute-start(bf16[4,2,64,128]{3,2,1,0:T(8,128)(2,1)S(1)} %collective-permute-done.3.kv4), channel_id=1, source_target_pairs={{0,28},{4,0},{8,4},{12,8},{16,12},{20,16},{24,20},{28,24},{1,29},{... | collective-permute-start | bytes 393224 | tf_op jit(solution)/shard_map/ppermute | solution.py:266
  44.8 15.5 %collective-permute-start.7 = (bf16[6,2,64,128]{3,2,1,0:T(8,128)(2,1)S(1)}, bf16[6,2,64,128]{3,2,1,0:T(8,128)(2,1)S(1)}, u32[]{:S(2)}, u32[]{:S(2)}) collective-permute-start(bf16[6,2,64,128]{3,2,1,0:T(8,128)(2,1)S(1)} %get-tuple-element.45), channel_id=1, source_target_pairs={{0,24},{4,28},{8,0},{12,4},{16,8},{20,12},{24,16},{28,20},{1,25},{... | collective-permute-start | bytes 589832 | tf_op jit(solution)/shard_map/ppermute | solution.py:266
  49.8 10.5 %collective-permute-start.8 = (bf16[6,2,64,128]{3,2,1,0:T(8,128)(2,1)S(1)}, bf16[6,2,64,128]{3,2,1,0:T(8,128)(2,1)S(1)}, u32[]{:S(2)}, u32[]{:S(2)}) collective-permute-start(bf16[6,2,64,128]{3,2,1,0:T(8,128)(2,1)S(1)} %get-tuple-element.46), channel_id=1, source_target_pairs={{0,8},{4,12},{8,16},{12,20},{16,24},{20,28},{24,0},{28,4},{1,9},{5... | collective-permute-start | bytes 589832 | tf_op jit(solution)/shard_map/ppermute | solution.py:266
  56.8 19.1 %all-to-all-start.2 = ((bf16[4,1280,128]{2,1,0:T(8,128)(2,1)}), bf16[4,1280,128]{2,1,0:T(8,128)(2,1)S(1)}, u32[]{:S(2)}, u32[]{:S(2)}) async-start(bf16[4,1280,128]{2,1,0:T(8,128)(2,1)} %get-tuple-element.57), calls=%async_computation.2 | async-start | bytes 2621440 | tf_op jit(solution)/shard_map/all_to_all | solution.py:269
  60.5 7.6 %collective-permute-start.10 = (bf16[4,2,64,128]{3,2,1,0:T(8,128)(2,1)S(1)}, bf16[4,2,64,128]{3,2,1,0:T(8,128)(2,1)S(1)}, u32[]{:S(2)}, u32[]{:S(2)}) collective-permute-start(bf16[4,2,64,128]{3,2,1,0:T(8,128)(2,1)S(1)} %pad_maximum_fusion.2), channel_id=1, source_target_pairs={{0,8},{4,12},{8,16},{12,20},{16,24},{20,28},{24,0},{28,4},{1,9},{5... | collective-permute-start | bytes 393224 | tf_op jit(solution)/shard_map/ppermute | solution.py:266
  63.1 7.4 %collective-permute-start.12 = (bf16[4,2,64,128]{3,2,1,0:T(8,128)(2,1)S(1)}, bf16[4,2,64,128]{3,2,1,0:T(8,128)(2,1)S(1)}, u32[]{:S(2)}, u32[]{:S(2)}) collective-permute-start(bf16[4,2,64,128]{3,2,1,0:T(8,128)(2,1)S(1)} %add_convert_fusion.1), channel_id=1, source_target_pairs={{0,4},{4,8},{8,12},{12,16},{16,20},{20,24},{24,28},{28,0},{1,5},{5... | collective-permute-start | bytes 393224 | tf_op jit(solution)/shard_map/ppermute | solution.py:266
  63.7 6.8 %collective-permute-start.9 = (bf16[4,2,64,128]{3,2,1,0:T(8,128)(2,1)S(1)}, bf16[4,2,64,128]{3,2,1,0:T(8,128)(2,1)S(1)}, u32[]{:S(2)}, u32[]{:S(2)}) collective-permute-start(bf16[4,2,64,128]{3,2,1,0:T(8,128)(2,1)S(1)} %pad_maximum_fusion.1), channel_id=1, source_target_pairs={{0,24},{4,28},{8,0},{12,4},{16,8},{20,12},{24,16},{28,20},{1,25},{... | collective-permute-start | bytes 393224 | tf_op jit(solution)/shard_map/ppermute | solution.py:266
  66.0 6.5 %collective-permute-start.11 = (bf16[4,2,64,128]{3,2,1,0:T(8,128)(2,1)S(1)}, bf16[4,2,64,128]{3,2,1,0:T(8,128)(2,1)S(1)}, u32[]{:S(2)}, u32[]{:S(2)}) collective-permute-start(bf16[4,2,64,128]{3,2,1,0:T(8,128)(2,1)S(1)} %add_convert_fusion.2), channel_id=1, source_target_pairs={{0,28},{4,0},{8,4},{12,8},{16,12},{20,16},{24,20},{28,24},{1,29},{... | collective-permute-start | bytes 393224 | tf_op jit(solution)/shard_map/ppermute | solution.py:266
  75.9 9.3 %all-to-all-start.3 = ((bf16[4,2,64,128]{3,2,1,0:T(8,128)(2,1)}), bf16[4,2,64,128]{3,2,1,0:T(8,128)(2,1)S(1)}, u32[]{:S(2)}, u32[]{:S(2)}) async-start(bf16[4,2,64,128]{3,2,1,0:T(8,128)(2,1)} %add_convert_fusion), calls=%async_computation.3 | async-start | bytes 262144 | tf_op jit(solution)/shard_map/all_to_all | solution.py:269

commit v9 on v8

--- a/solution.py
+++ b/solution.py
@@ -268,8 +268,18 @@
     def swap_y(x):
         return lax.all_to_all(x, "y", 0, 0, tiled=True)
 
-    kv = jnp.stack([prompt_keys, prompt_value_rows], axis=0)
-    kv = swap_y(jnp.transpose(kv, (2, 0, 1, 3)))
+    my_y = lax.axis_index("y")
+
+    def over_y(x, k):
+        return lax.ppermute(x, "y", [(i, (i + k) % 4) for i in range(4)])
+
+    def of_head(k):
+        h = (my_y + k) % KH
+        return jnp.stack(
+            [lax.dynamic_index_in_dim(x, h, 1, False) for x in (prompt_keys, prompt_value_rows)]
+        )
+
+    kv = jnp.stack([of_head(0)] + [over_y(of_head(4 - m), -m) for m in (1, 2, 3)])
 
     live = (jnp.arange(T) < lengths[0])[:, None, None]
     masked = jnp.where(live, grad_out[0], jnp.zeros((), bf16))
@@ -385,7 +395,9 @@
     total = d0.astype(f32)
     for x in parts:
         total = total + x.astype(f32)
-    total, home = lax.optimization_barrier((total.astype(bf16), home))
+    total = total.astype(bf16)
+    total = lax.dynamic_slice_in_dim(jnp.concatenate([total, total]), (4 - my_y) % 4, 4, 0)
+    total, home = lax.optimization_barrier((total, home))
     total = swap_y(total)
 
     grad_k, grad_v = small_call(

time: 86.6 us -> 85 us (0.982)
  waiting for transfers between devices: 16.5 us -> 14.7 us
  starting transfers between devices: 40.7 us -> 42 us
    ppermute x0 -> x3, starting transfers between devices: none -> 5.46 us  [over_y(): return lax.ppermute(x, 'y', [(i, (i + k) % 4) for i in range(4)])]
    all_to_all x4 -> x3, starting transfers between devices: 14.9 us -> 10.4 us  [swap_y(): return lax.all_to_all(x, 'y', 0, 0, tiled=True)]
    all_to_all x4 -> x3, waiting for transfers between devices: 7.47 us -> 4.43 us  [swap_y(): return lax.all_to_all(x, 'y', 0, 0, tiled=True)]
    ppermute x0 -> x3, waiting for transfers between devices: none -> 1.72 us  [over_y(): return lax.ppermute(x, 'y', [(i, (i + k) % 4) for i in range(4)])]
    dynamic_slice x0 -> x1, local copies, waits for them, and re-layouts: none -> 1.43 us  [of_head(): lax.dynamic_index_in_dim(x, h, 1, False)]
    reshape x1, local copies, waits for them, and re-layouts: 1.23 us -> 0.18 us  [by_head(): x = x.reshape(T, KH, n, D)]
    another operation x1 -> x0, local copies, waits for them, and re-layouts: 0.96 us -> none  [on_device(): kv = jnp.stack([prompt_keys, prompt_value_rows], axis=0)]
  transfers between devices with their start and end apart: 17 -> 19, of which waited for: 10 -> 10; matrix products, arithmetic and copies ran while one was open for 9% -> 8% of each run, Pallas kernels for 14% -> 14%
where the time goes in v9:
time: 85 us; the launch traced here: 84.6 us
  starting transfers between devices  42 us (49%)
  Pallas kernels  18.3 us (22%)
  waiting for transfers between devices  14.7 us (17%)
  local copies, waits for them, and re-layouts  4.48 us (5%)
  other arithmetic  3.45 us (4%)
  between operations  1.68 us (2%)
    ppermute x13, starting transfers between devices, over_z(): return lax.ppermute(x, 'z', [(i, (i + k) % 8) for i in range(8)])  26.2 us
    pallas_call x3, Pallas kernels, call(): pl.pallas_call(body, out_shape=out_shape, scratch_shapes=scratch, compile...  17.3 us
    all_to_all x3, starting transfers between devices, swap_y(): return lax.all_to_all(x, 'y', 0, 0, tiled=True)  10.4 us
    ppermute x13, waiting for transfers between devices, over_z(): return lax.ppermute(x, 'z', [(i, (i + k) % 8) for i in range(8)])  8.56 us
    ppermute x3, starting transfers between devices, over_y(): return lax.ppermute(x, 'y', [(i, (i + k) % 4) for i in range(4)])  5.46 us
    all_to_all x3, waiting for transfers between devices, swap_y(): return lax.all_to_all(x, 'y', 0, 0, tiled=True)  4.43 us
    ppermute x3, waiting for transfers between devices, over_y(): return lax.ppermute(x, 'y', [(i, (i + k) % 4) for i in range(4)])  1.72 us
  transfers between devices with their start and end apart: 19, of which 10 were waited for; matrix products, arithmetic and copies ran while one was open for 8% of the time, Pallas kernels for 14%

profile of v9, /device:TPU:4, one launch (start us, length us, event | category | flops | bytes accessed | tf_op | source)
XLA Modules:
  0.0 84.6 jit_solution(10661361217936183324)
XLA Ops:
  0.7 1.4 %constant_dynamic-slice_fusion.6 = (bf16[64,1,128]{2,1,0:T(2,128)(2,1)S(1)}, bf16[64,1,128]{2,1,0:T(2,128)(2,1)S(1)}, bf16[64,1,128]{2,1,0:T(2,128)(2,1)S(1)}, b...) fusion(bf16[64,4,128]{2,1,0:T(4,128)(2,1)} %param.11, ...), kind=kLoop, calls=%fused_computation.36 | loop fusion | bytes 262160 | tf_op jit(solution)/shard_map/jit(dynamic_index_in_dim)/dynamic_slice | solution.py:279
  2.2 3.3 %collective-permute-start.1 = (bf16[2,64,128]{2,1,0:T(8,128)(2,1)S(1)}, bf16[2,64,128]{2,1,0:T(8,128)(2,1)S(1)}, u32[]{:S(2)}, u32[]{:S(2)}) collective-permute-start(bf16[2,64,128]{2,1,0:T(8,128)(2,1)S(1)} %pad_maximum_fusion.5), channel_id=1, source_target_pairs={{0,2},{1,3},{2,0},{3,1},{4,6},{5,7},{6,4},{7,5},{8,10},{9,11},{10,... | collective-permute-start | bytes 98312 | tf_op jit(solution)/shard_map/ppermute | solution.py:274
  5.5 1.1 %collective-permute-start = (bf16[2,64,128]{2,1,0:T(8,128)(2,1)S(1)}, bf16[2,64,128]{2,1,0:T(8,128)(2,1)S(1)}, u32[]{:S(2)}, u32[]{:S(2)}) collective-permute-start(bf16[2,64,128]{2,1,0:T(8,128)(2,1)S(1)} %pad_maximum_fusion.4), channel_id=1, source_target_pairs={{0,3},{1,0},{2,1},{3,2},{4,7},{5,4},{6,5},{7,6},{8,11},{9,8},{10,9... | collective-permute-start | bytes 98312 | tf_op jit(solution)/shard_map/ppermute | solution.py:274
  6.7 1.0 %collective-permute-start.2 = (bf16[2,64,128]{2,1,0:T(8,128)(2,1)S(1)}, bf16[2,64,128]{2,1,0:T(8,128)(2,1)S(1)}, u32[]{:S(2)}, u32[]{:S(2)}) collective-permute-start(bf16[2,64,128]{2,1,0:T(8,128)(2,1)S(1)} %pad_maximum_fusion.6), channel_id=1, source_target_pairs={{0,1},{1,2},{2,3},{3,0},{4,5},{5,6},{6,7},{7,4},{8,9},{9,10},{10,1... | collective-permute-start | bytes 98312 | tf_op jit(solution)/shard_map/ppermute | solution.py:274
  8.4 0.2 copy.29
  8.7 0.3 copy_select_fusion
  9.0 1.2 %pad_maximum_fusion = bf16[4,1280,128]{2,1,0:T(8,128)(2,1)} fusion(bf16[4,128,128]{2,1,0:T(8,128)(2,1)S(1)} %get-tuple-element.90, bf16[4,128,128]{2,1,0:T(8,128)(2,1)S(1)} %get-tuple-element.91, bf16[4,512,128]{2,1,0:T(8,128)(2,1)S(1)} %bitcast.74, bf16[4,512,128]{2,1,0:T(8,128)(2,1)S(1)} %bitcast.73), kind=kLoop, calls=%fused_computation | loop fusion | flops 5242880 | bytes 2621440 | tf_op jit(solution)/shard_map/concatenate | solution.py:291
  10.2 0.0 collective-permute-done
  10.2 1.7 %collective-permute-done.2 = bf16[2,64,128]{2,1,0:T(8,128)(2,1)S(1)} collective-permute-done((bf16[2,64,128]{2,1,0:T(8,128)(2,1)S(1)}, bf16[2,64,128]{2,1,0:T(8,128)(2,1)S(1)}, u32[]{:S(2)}, u32[]{:S(2)}) %collective-permute-start.2) | collective-permute-done | bytes 32800 | tf_op jit(solution)/shard_map/ppermute | solution.py:274
  11.9 3.6 %all-to-all-start = ((bf16[4,1280,128]{2,1,0:T(8,128)(2,1)}), bf16[4,1280,128]{2,1,0:T(8,128)(2,1)S(1)}, u32[]{:S(2)}, u32[]{:S(2)}) async-start(bf16[4,1280,128]{2,1,0:T(8,128)(2,1)} %pad_maximum_fusion), calls=%async_computation | async-start | bytes 2621440 | tf_op jit(solution)/shard_map/all_to_all | solution.py:269
  15.5 3.3 %collective-permute-start.5 = (bf16[4,2,64,128]{3,2,1,0:T(8,128)(2,1)S(1)}, bf16[4,2,64,128]{3,2,1,0:T(8,128)(2,1)S(1)}, u32[]{:S(2)}, u32[]{:S(2)}) collective-permute-start(bf16[4,2,64,128]{3,2,1,0:T(8,128)(2,1)S(1)} %pad_maximum_fusion.1.kv0), channel_id=1, source_target_pairs={{0,8},{4,12},{8,16},{12,20},{16,24},{20,28},{24,0},{28,4},{1,9},{5... | collective-permute-start | bytes 393224 | tf_op jit(solution)/shard_map/ppermute | solution.py:266
  18.8 3.1 %collective-permute-start.6 = (bf16[4,2,64,128]{3,2,1,0:T(8,128)(2,1)S(1)}, bf16[4,2,64,128]{3,2,1,0:T(8,128)(2,1)S(1)}, u32[]{:S(2)}, u32[]{:S(2)}) collective-permute-start(bf16[4,2,64,128]{3,2,1,0:T(8,128)(2,1)S(1)} %pad_maximum_fusion.1.kv0), channel_id=1, source_target_pairs={{0,24},{4,28},{8,0},{12,4},{16,8},{20,12},{24,16},{28,20},{1,25},{... | collective-permute-start | bytes 393224 | tf_op jit(solution)/shard_map/ppermute | solution.py:266
  21.9 2.4 %collective-permute-start.4 = (bf16[4,2,64,128]{3,2,1,0:T(8,128)(2,1)S(1)}, bf16[4,2,64,128]{3,2,1,0:T(8,128)(2,1)S(1)}, u32[]{:S(2)}, u32[]{:S(2)}) collective-permute-start(bf16[4,2,64,128]{3,2,1,0:T(8,128)(2,1)S(1)} %pad_maximum_fusion.1.kv0), channel_id=1, source_target_pairs={{0,28},{4,0},{8,4},{12,8},{16,12},{20,16},{24,20},{28,24},{1,29},{... | collective-permute-start | bytes 393224 | tf_op jit(solution)/shard_map/ppermute | solution.py:266
  24.3 0.0 collective-permute-start.3
  24.3 2.2 %collective-permute-done.5.kv3 = bf16[4,2,64,128]{3,2,1,0:T(8,128)(2,1)S(1)} collective-permute-done((bf16[4,2,64,128]{3,2,1,0:T(8,128)(2,1)S(1)}, bf16[4,2,64,128]{3,2,1,0:T(8,128)(2,1)S(1)}, u32[]{:S(2)}, u32[]{:S(2)}) %collective-permute-start.5) | collective-permute-done | bytes 131104 | tf_op jit(solution)/shard_map/ppermute | solution.py:266
  26.5 2.4 %collective-permute-start.9 = (bf16[4,2,64,128]{3,2,1,0:T(8,128)(2,1)S(1)}, bf16[4,2,64,128]{3,2,1,0:T(8,128)(2,1)S(1)}, u32[]{:S(2)}, u32[]{:S(2)}) collective-permute-start(bf16[4,2,64,128]{3,2,1,0:T(8,128)(2,1)S(1)} %collective-permute-done.5.kv3), channel_id=1, source_target_pairs={{0,8},{4,12},{8,16},{12,20},{16,24},{20,28},{24,0},{28,4},{1,9},{5... | collective-permute-start | bytes 393224 | tf_op jit(solution)/shard_map/ppermute | solution.py:266
  28.9 0.0 collective-permute-start.7
  28.9 0.2 collective-permute-done.6.kv4
  29.1 3.1 %collective-permute-start.8 = (bf16[4,2,64,128]{3,2,1,0:T(8,128)(2,1)S(1)}, bf16[4,2,64,128]{3,2,1,0:T(8,128)(2,1)S(1)}, u32[]{:S(2)}, u32[]{:S(2)}) collective-permute-start(bf16[4,2,64,128]{3,2,1,0:T(8,128)(2,1)S(1)} %collective-permute-done.6.kv4), channel_id=1, source_target_pairs={{0,28},{4,0},{8,4},{12,8},{16,12},{20,16},{24,20},{28,24},{1,29},{... | collective-permute-start | bytes 393224 | tf_op jit(solution)/shard_map/ppermute | solution.py:266
  32.2 0.0 collective-permute-done.4.kv2
  32.2 0.7 collective-permute-done.3.kv1
  32.8 4.7 %near_forward.1 = (bf16[1408,2048]{1,0:T(8,128)(2,1)S(1)}, f32[144,2048]{1,0:T(8,128)S(1)}, f32[8,2048]{1,0:T(8,128)S(1)}) custom-call(bf16[4,1280,128]{2,1,0:T(8,128)(2,1)S(1)} %all-to-all-done.pack, bf16[4,2,64,128]{3,2,1,0:T(8,128)(2,1)S(1)} %pad_maximum_fusion.1.kv0, bf16[4,2,64,128]{3,2,1,0:T(8,128)(2,1)S(1)} %collective-permute-done.3.kv1, ...), custom_call_target="tpu_custom_call" | custom-call | flops 1476395008 | bytes 4194304 | tf_op jit(solution)/shard_map/near_forward/pallas_call | solution.py:247
  37.6 0.0 collective-permute-done.8.kv1
  37.6 0.4 collective-permute-done.7.kv0
  38.0 5.6 %far_both.1 = (bf16[4,512,128]{2,1,0:T(8,128)(2,1)S(1)}, f32[8,2048]{1,0:T(8,128)S(1)}, bf16[2048,128]{1,0:T(8,128)(2,1)S(1)}, bf16[2048,128]{1,0:T(8,128)(2,1)S...) custom-call(bf16[4,1280,128]{2,1,0:T(8,128)(2,1)S(1)} %all-to-all-done.pack, ...), custom_call_target="tpu_custom_call" | custom-call | flops 2415919104 | bytes 4194304 | tf_op jit(solution)/shard_map/far_both/pallas_call | solution.py:247
  43.6 5.1 %collective-permute-start.10 = (bf16[6,2,64,128]{3,2,1,0:T(8,128)(2,1)S(1)}, bf16[6,2,64,128]{3,2,1,0:T(8,128)(2,1)S(1)}, u32[]{:S(2)}, u32[]{:S(2)}) collective-permute-start(bf16[6,2,64,128]{3,2,1,0:T(8,128)(2,1)S(1)} %get-tuple-element.45), channel_id=1, source_target_pairs={{0,24},{4,28},{8,0},{12,4},{16,8},{20,12},{24,16},{28,20},{1,25},{... | collective-permute-start | bytes 589832 | tf_op jit(solution)/shard_map/ppermute | solution.py:266
  48.7 0.0 collective-permute-start.11
  48.7 7.0 %near_backward.1 = (bf16[4,1280,128]{2,1,0:T(8,128)(2,1)}, bf16[4,2,64,128]{3,2,1,0:T(8,128)(2,1)S(1)}, bf16[4,2,64,128]{3,2,1,0:T(8,128)(2,1)S(1)}, bf16[4,2,64...) custom-call(bf16[4,1280,128]{2,1,0:T(8,128)(2,1)S(1)} %all-to-all-done.pack, ...), custom_call_target="tpu_custom_call" | custom-call | flops 2952790016 | bytes 4194304 | tf_op jit(solution)/shard_map/near_backward/pallas_call | solution.py:247
  55.7 3.5 %all-to-all-start.1 = ((bf16[4,1280,128]{2,1,0:T(8,128)(2,1)}), bf16[4,1280,128]{2,1,0:T(8,128)(2,1)S(1)}, u32[]{:S(2)}, u32[]{:S(2)}) async-start(bf16[4,1280,128]{2,1,0:T(8,128)(2,1)} %get-tuple-element.57), calls=%async_computation.1 | async-start | bytes 2621440 | tf_op jit(solution)/shard_map/all_to_all | solution.py:269
  59.4 2.5 %collective-permute-start.13 = (bf16[4,2,64,128]{3,2,1,0:T(8,128)(2,1)S(1)}, bf16[4,2,64,128]{3,2,1,0:T(8,128)(2,1)S(1)}, u32[]{:S(2)}, u32[]{:S(2)}) collective-permute-start(bf16[4,2,64,128]{3,2,1,0:T(8,128)(2,1)S(1)} %pad_maximum_fusion.3), channel_id=1, source_target_pairs={{0,8},{4,12},{8,16},{12,20},{16,24},{20,28},{24,0},{28,4},{1,9},{5... | collective-permute-start | bytes 393224 | tf_op jit(solution)/shard_map/ppermute | solution.py:266
  61.8 0.6 collective-permute-start.15
  62.6 2.3 %collective-permute-start.12 = (bf16[4,2,64,128]{3,2,1,0:T(8,128)(2,1)S(1)}, bf16[4,2,64,128]{3,2,1,0:T(8,128)(2,1)S(1)}, u32[]{:S(2)}, u32[]{:S(2)}) collective-permute-start(bf16[4,2,64,128]{3,2,1,0:T(8,128)(2,1)S(1)} %pad_maximum_fusion.2), channel_id=1, source_target_pairs={{0,24},{4,28},{8,0},{12,4},{16,8},{20,12},{24,16},{28,20},{1,25},{... | collective-permute-start | bytes 393224 | tf_op jit(solution)/shard_map/ppermute | solution.py:266
  64.8 1.4 %collective-permute-start.14 = (bf16[4,2,64,128]{3,2,1,0:T(8,128)(2,1)S(1)}, bf16[4,2,64,128]{3,2,1,0:T(8,128)(2,1)S(1)}, u32[]{:S(2)}, u32[]{:S(2)}) collective-permute-start(bf16[4,2,64,128]{3,2,1,0:T(8,128)(2,1)S(1)} %add_convert_fusion.2), channel_id=1, source_target_pairs={{0,28},{4,0},{8,4},{12,8},{16,12},{20,16},{24,20},{28,24},{1,29},{... | collective-permute-start | bytes 393224 | tf_op jit(solution)/shard_map/ppermute | solution.py:266
  66.2 0.6 collective-permute-done.13
  66.8 2.2 %collective-permute-done.15 = bf16[4,2,64,128]{3,2,1,0:T(8,128)(2,1)S(1)} collective-permute-done((bf16[4,2,64,128]{3,2,1,0:T(8,128)(2,1)S(1)}, bf16[4,2,64,128]{3,2,1,0:T(8,128)(2,1)S(1)}, u32[]{:S(2)}, u32[]{:S(2)}) %collective-permute-start.15) | collective-permute-done | bytes 131104 | tf_op jit(solution)/shard_map/ppermute | solution.py:266
  69.1 2.3 %collective-permute-done.14 = bf16[4,2,64,128]{3,2,1,0:T(8,128)(2,1)S(1)} collective-permute-done((bf16[4,2,64,128]{3,2,1,0:T(8,128)(2,1)S(1)}, bf16[4,2,64,128]{3,2,1,0:T(8,128)(2,1)S(1)}, u32[]{:S(2)}, u32[]{:S(2)}) %collective-permute-start.14) | collective-permute-done | bytes 131104 | tf_op jit(solution)/shard_map/ppermute | solution.py:266
  71.4 0.1 add_convert_fusion
  71.5 0.7 fusion
  72.2 2.3 %all-to-all-done.1 = bf16[4,1280,128]{2,1,0:T(8,128)(2,1)S(1)} async-done(((bf16[4,1280,128]{2,1,0:T(8,128)(2,1)}), bf16[4,1280,128]{2,1,0:T(8,128)(2,1)S(1)}, u32[]{:S(2)}, u32[]{:S(2)}) %all-to-all-start.1) | async-done | bytes 1310752 | tf_op jit(solution)/shard_map/all_to_all | solution.py:269
  74.4 3.3 %all-to-all-start.2 = ((bf16[4,2,64,128]{3,2,1,0:T(8,128)(2,1)}), bf16[4,2,64,128]{3,2,1,0:T(8,128)(2,1)S(1)}, u32[]{:S(2)}, u32[]{:S(2)}) async-start(bf16[4,2,64,128]{3,2,1,0:T(8,128)(2,1)} %fusion), calls=%async_computation.2 | async-start | bytes 262144 | tf_op jit(solution)/shard_map/all_to_all | solution.py:269
  77.8 0.1 fusion.1
  77.8 0.2 copy.33
  78.0 1.0 %broadcast_select_fusion = bf16[1,128,16,128]{3,2,1,0:T(8,128)(2,1)} fusion(bf16[1,128,16,128]{3,2,1,0:T(8,128)(2,1)S(1)} %bitcast.75, pred[128]{0:T(512)(128)(4,1)S(1)} %iota_compare_fusion), kind=kLoop, calls=%fused_computation.2 | loop fusion | flops 262144 | bytes 1048704 | tf_op jit(solution)/shard_map/jit(_where)/select_n | solution.py:416
  79.1 1.0 %copy.34 = bf16[128,4,4,128]{3,2,1,0:T(4,128)(2,1)} copy(bf16[128,4,4,128]{3,2,0,1:T(4,128)(2,1)S(1)} %bitcast.76) | data formatting | bytes 1048576 | tf_op jit(solution)/shard_map/transpose | solution.py:413
  80.0 0.8 copy.36
  80.8 0.8 copy.35
  81.5 2.2 %all-to-all-done.2.x = bf16[4,2,64,128]{3,2,1,0:T(8,128)(2,1)S(1)} async-done(((bf16[4,2,64,128]{3,2,1,0:T(8,128)(2,1)}), bf16[4,2,64,128]{3,2,1,0:T(8,128)(2,1)S(1)}, u32[]{:S(2)}, u32[]{:S(2)}) %all-to-all-start.2) | async-done | bytes 131104 | tf_op jit(solution)/shard_map/all_to_all | solution.py:269
  83.7 0.9 %unpack_prompt.1 = (bf16[256,128]{1,0:T(8,128)(2,1)}, bf16[256,128]{1,0:T(8,128)(2,1)}) custom-call(bf16[4,2,64,128]{3,2,1,0:T(8,128)(2,1)S(1)} %all-to-all-done.2.x), custom_call_target="tpu_custom_call" | custom-call | tf_op jit(solution)/shard_map/unpack_prompt/pallas_call | solution.py:237
  (38 shorter events, 0.3 us)
Async XLA Ops:
  0.6 7.8 %copy-start = (bf16[1,128,16,128]{3,2,1,0:T(8,128)(2,1)S(1)}, bf16[1,128,16,128]{3,2,1,0:T(8,128)(2,1)}, u32[]{:S(2)}) copy-start(bf16[1,128,16,128]{3,2,1,0:T(8,128)(2,1)} %param.7) | copy-start | bytes 1572868
  0.6 8.0 %copy-start.2 = (bf16[1,128,4,128]{3,2,1,0:T(4,128)(2,1)S(1)}, bf16[1,128,4,128]{3,2,1,0:T(4,128)(2,1)}, u32[]{:S(2)}) copy-start(bf16[1,128,4,128]{3,2,1,0:T(4,128)(2,1)} %param.9) | copy-start | bytes 393220
  0.7 8.0 %copy-start.3 = (bf16[1,128,4,128]{3,2,1,0:T(4,128)(2,1)S(1)}, bf16[1,128,4,128]{3,2,1,0:T(4,128)(2,1)}, u32[]{:S(2)}) copy-start(bf16[1,128,4,128]{3,2,1,0:T(4,128)(2,1)} %param.8) | copy-start | bytes 393220
  0.7 8.0 %copy-start.1 = (bf16[1,128,16,128]{3,2,1,0:T(8,128)(2,1)S(1)}, bf16[1,128,16,128]{3,2,1,0:T(8,128)(2,1)}, u32[]{:S(2)}) copy-start(bf16[1,128,16,128]{3,2,1,0:T(8,128)(2,1)} %param.13) | copy-start | bytes 1572868
  2.2 7.9 %collective-permute-start.1 = (bf16[2,64,128]{2,1,0:T(8,128)(2,1)S(1)}, bf16[2,64,128]{2,1,0:T(8,128)(2,1)S(1)}, u32[]{:S(2)}, u32[]{:S(2)}) collective-permute-start(bf16[2,64,128]{2,1,0:T(8,128)(2,1)S(1)} %pad_maximum_fusion.5), channel_id=1, source_target_pairs={{0,2},{1,3},{2,0},{3,1},{4,6},{5,7},{6,4},{7,5},{8,10},{9,11},{10,... | collective-permute-start | bytes 98312 | tf_op jit(solution)/shard_map/ppermute | solution.py:274
  5.5 4.6 %collective-permute-start = (bf16[2,64,128]{2,1,0:T(8,128)(2,1)S(1)}, bf16[2,64,128]{2,1,0:T(8,128)(2,1)S(1)}, u32[]{:S(2)}, u32[]{:S(2)}) collective-permute-start(bf16[2,64,128]{2,1,0:T(8,128)(2,1)S(1)} %pad_maximum_fusion.4), channel_id=1, source_target_pairs={{0,3},{1,0},{2,1},{3,2},{4,7},{5,4},{6,5},{7,6},{8,11},{9,8},{10,9... | collective-permute-start | bytes 98312 | tf_op jit(solution)/shard_map/ppermute | solution.py:274
  6.7 5.2 %collective-permute-start.2 = (bf16[2,64,128]{2,1,0:T(8,128)(2,1)S(1)}, bf16[2,64,128]{2,1,0:T(8,128)(2,1)S(1)}, u32[]{:S(2)}, u32[]{:S(2)}) collective-permute-start(bf16[2,64,128]{2,1,0:T(8,128)(2,1)S(1)} %pad_maximum_fusion.6), channel_id=1, source_target_pairs={{0,1},{1,2},{2,3},{3,0},{4,5},{5,6},{6,7},{7,4},{8,9},{9,10},{10,1... | collective-permute-start | bytes 98312 | tf_op jit(solution)/shard_map/ppermute | solution.py:274
  11.9 20.9 %all-to-all-start = ((bf16[4,1280,128]{2,1,0:T(8,128)(2,1)}), bf16[4,1280,128]{2,1,0:T(8,128)(2,1)S(1)}, u32[]{:S(2)}, u32[]{:S(2)}) async-start(bf16[4,1280,128]{2,1,0:T(8,128)(2,1)} %pad_maximum_fusion), calls=%async_computation | async-start | bytes 2621440 | tf_op jit(solution)/shard_map/all_to_all | solution.py:269
  15.5 11.0 %collective-permute-start.5 = (bf16[4,2,64,128]{3,2,1,0:T(8,128)(2,1)S(1)}, bf16[4,2,64,128]{3,2,1,0:T(8,128)(2,1)S(1)}, u32[]{:S(2)}, u32[]{:S(2)}) collective-permute-start(bf16[4,2,64,128]{3,2,1,0:T(8,128)(2,1)S(1)} %pad_maximum_fusion.1.kv0), channel_id=1, source_target_pairs={{0,8},{4,12},{8,16},{12,20},{16,24},{20,28},{24,0},{28,4},{1,9},{5... | collective-permute-start | bytes 393224 | tf_op jit(solution)/shard_map/ppermute | solution.py:266
  18.8 10.3 %collective-permute-start.6 = (bf16[4,2,64,128]{3,2,1,0:T(8,128)(2,1)S(1)}, bf16[4,2,64,128]{3,2,1,0:T(8,128)(2,1)S(1)}, u32[]{:S(2)}, u32[]{:S(2)}) collective-permute-start(bf16[4,2,64,128]{3,2,1,0:T(8,128)(2,1)S(1)} %pad_maximum_fusion.1.kv0), channel_id=1, source_target_pairs={{0,24},{4,28},{8,0},{12,4},{16,8},{20,12},{24,16},{28,20},{1,25},{... | collective-permute-start | bytes 393224 | tf_op jit(solution)/shard_map/ppermute | solution.py:266
  21.9 10.2 %collective-permute-start.4 = (bf16[4,2,64,128]{3,2,1,0:T(8,128)(2,1)S(1)}, bf16[4,2,64,128]{3,2,1,0:T(8,128)(2,1)S(1)}, u32[]{:S(2)}, u32[]{:S(2)}) collective-permute-start(bf16[4,2,64,128]{3,2,1,0:T(8,128)(2,1)S(1)} %pad_maximum_fusion.1.kv0), channel_id=1, source_target_pairs={{0,28},{4,0},{8,4},{12,8},{16,12},{20,16},{24,20},{28,24},{1,29},{... | collective-permute-start | bytes 393224 | tf_op jit(solution)/shard_map/ppermute | solution.py:266
  24.3 8.5 %collective-permute-start.3 = (bf16[4,2,64,128]{3,2,1,0:T(8,128)(2,1)S(1)}, bf16[4,2,64,128]{3,2,1,0:T(8,128)(2,1)S(1)}, u32[]{:S(2)}, u32[]{:S(2)}) collective-permute-start(bf16[4,2,64,128]{3,2,1,0:T(8,128)(2,1)S(1)} %pad_maximum_fusion.1.kv0), channel_id=1, source_target_pairs={{0,4},{4,8},{8,12},{12,16},{16,20},{20,24},{24,28},{28,0},{1,5},{5... | collective-permute-start | bytes 393224 | tf_op jit(solution)/shard_map/ppermute | solution.py:266
  26.5 11.1 %collective-permute-start.9 = (bf16[4,2,64,128]{3,2,1,0:T(8,128)(2,1)S(1)}, bf16[4,2,64,128]{3,2,1,0:T(8,128)(2,1)S(1)}, u32[]{:S(2)}, u32[]{:S(2)}) collective-permute-start(bf16[4,2,64,128]{3,2,1,0:T(8,128)(2,1)S(1)} %collective-permute-done.5.kv3), channel_id=1, source_target_pairs={{0,8},{4,12},{8,16},{12,20},{16,24},{20,28},{24,0},{28,4},{1,9},{5... | collective-permute-start | bytes 393224 | tf_op jit(solution)/shard_map/ppermute | solution.py:266
  28.9 9.1 %collective-permute-start.7 = (bf16[4,2,64,128]{3,2,1,0:T(8,128)(2,1)S(1)}, bf16[4,2,64,128]{3,2,1,0:T(8,128)(2,1)S(1)}, u32[]{:S(2)}, u32[]{:S(2)}) collective-permute-start(bf16[4,2,64,128]{3,2,1,0:T(8,128)(2,1)S(1)} %collective-permute-done.5.kv3), channel_id=1, source_target_pairs={{0,4},{4,8},{8,12},{12,16},{16,20},{20,24},{24,28},{28,0},{1,5},{5... | collective-permute-start | bytes 393224 | tf_op jit(solution)/shard_map/ppermute | solution.py:266
  29.1 8.5 %collective-permute-start.8 = (bf16[4,2,64,128]{3,2,1,0:T(8,128)(2,1)S(1)}, bf16[4,2,64,128]{3,2,1,0:T(8,128)(2,1)S(1)}, u32[]{:S(2)}, u32[]{:S(2)}) collective-permute-start(bf16[4,2,64,128]{3,2,1,0:T(8,128)(2,1)S(1)} %collective-permute-done.6.kv4), channel_id=1, source_target_pairs={{0,28},{4,0},{8,4},{12,8},{16,12},{20,16},{24,20},{28,24},{1,29},{... | collective-permute-start | bytes 393224 | tf_op jit(solution)/shard_map/ppermute | solution.py:266
  43.6 15.6 %collective-permute-start.10 = (bf16[6,2,64,128]{3,2,1,0:T(8,128)(2,1)S(1)}, bf16[6,2,64,128]{3,2,1,0:T(8,128)(2,1)S(1)}, u32[]{:S(2)}, u32[]{:S(2)}) collective-permute-start(bf16[6,2,64,128]{3,2,1,0:T(8,128)(2,1)S(1)} %get-tuple-element.45), channel_id=1, source_target_pairs={{0,24},{4,28},{8,0},{12,4},{16,8},{20,12},{24,16},{28,20},{1,25},{... | collective-permute-start | bytes 589832 | tf_op jit(solution)/shard_map/ppermute | solution.py:266
  48.7 10.5 %collective-permute-start.11 = (bf16[6,2,64,128]{3,2,1,0:T(8,128)(2,1)S(1)}, bf16[6,2,64,128]{3,2,1,0:T(8,128)(2,1)S(1)}, u32[]{:S(2)}, u32[]{:S(2)}) collective-permute-start(bf16[6,2,64,128]{3,2,1,0:T(8,128)(2,1)S(1)} %get-tuple-element.46), channel_id=1, source_target_pairs={{0,8},{4,12},{8,16},{12,20},{16,24},{20,28},{24,0},{28,4},{1,9},{5... | collective-permute-start | bytes 589832 | tf_op jit(solution)/shard_map/ppermute | solution.py:266
  55.7 18.8 %all-to-all-start.1 = ((bf16[4,1280,128]{2,1,0:T(8,128)(2,1)}), bf16[4,1280,128]{2,1,0:T(8,128)(2,1)S(1)}, u32[]{:S(2)}, u32[]{:S(2)}) async-start(bf16[4,1280,128]{2,1,0:T(8,128)(2,1)} %get-tuple-element.57), calls=%async_computation.1 | async-start | bytes 2621440 | tf_op jit(solution)/shard_map/all_to_all | solution.py:269
  59.4 7.5 %collective-permute-start.13 = (bf16[4,2,64,128]{3,2,1,0:T(8,128)(2,1)S(1)}, bf16[4,2,64,128]{3,2,1,0:T(8,128)(2,1)S(1)}, u32[]{:S(2)}, u32[]{:S(2)}) collective-permute-start(bf16[4,2,64,128]{3,2,1,0:T(8,128)(2,1)S(1)} %pad_maximum_fusion.3), channel_id=1, source_target_pairs={{0,8},{4,12},{8,16},{12,20},{16,24},{20,28},{24,0},{28,4},{1,9},{5... | collective-permute-start | bytes 393224 | tf_op jit(solution)/shard_map/ppermute | solution.py:266
  61.8 7.2 %collective-permute-start.15 = (bf16[4,2,64,128]{3,2,1,0:T(8,128)(2,1)S(1)}, bf16[4,2,64,128]{3,2,1,0:T(8,128)(2,1)S(1)}, u32[]{:S(2)}, u32[]{:S(2)}) collective-permute-start(bf16[4,2,64,128]{3,2,1,0:T(8,128)(2,1)S(1)} %add_convert_fusion.1), channel_id=1, source_target_pairs={{0,4},{4,8},{8,12},{12,16},{16,20},{20,24},{24,28},{28,0},{1,5},{5... | collective-permute-start | bytes 393224 | tf_op jit(solution)/shard_map/ppermute | solution.py:266
  62.6 6.5 %collective-permute-start.12 = (bf16[4,2,64,128]{3,2,1,0:T(8,128)(2,1)S(1)}, bf16[4,2,64,128]{3,2,1,0:T(8,128)(2,1)S(1)}, u32[]{:S(2)}, u32[]{:S(2)}) collective-permute-start(bf16[4,2,64,128]{3,2,1,0:T(8,128)(2,1)S(1)} %pad_maximum_fusion.2), channel_id=1, source_target_pairs={{0,24},{4,28},{8,0},{12,4},{16,8},{20,12},{24,16},{28,20},{1,25},{... | collective-permute-start | bytes 393224 | tf_op jit(solution)/shard_map/ppermute | solution.py:266
  64.8 6.5 %collective-permute-start.14 = (bf16[4,2,64,128]{3,2,1,0:T(8,128)(2,1)S(1)}, bf16[4,2,64,128]{3,2,1,0:T(8,128)(2,1)S(1)}, u32[]{:S(2)}, u32[]{:S(2)}) collective-permute-start(bf16[4,2,64,128]{3,2,1,0:T(8,128)(2,1)S(1)} %add_convert_fusion.2), channel_id=1, source_target_pairs={{0,28},{4,0},{8,4},{12,8},{16,12},{20,16},{24,20},{28,24},{1,29},{... | collective-permute-start | bytes 393224 | tf_op jit(solution)/shard_map/ppermute | solution.py:266
  74.4 9.3 %all-to-all-start.2 = ((bf16[4,2,64,128]{3,2,1,0:T(8,128)(2,1)}), bf16[4,2,64,128]{3,2,1,0:T(8,128)(2,1)S(1)}, u32[]{:S(2)}, u32[]{:S(2)}) async-start(bf16[4,2,64,128]{3,2,1,0:T(8,128)(2,1)} %fusion), calls=%async_computation.2 | async-start | bytes 262144 | tf_op jit(solution)/shard_map/all_to_all | solution.py:269

commit v10 on v9

--- a/solution.py
+++ b/solution.py
@@ -41,11 +41,45 @@
     return lax.dot_general(order, x, TN, preferred_element_type=f32).astype(bf16)
 
 
-def unpack_prompt(x, k_out, v_out):
+def unpack_rows(length, home, o, dq, dk, dv, *, T, G):
+    R = T * G
+    n = 256
+    part = n // 4
+
+    def order(token_rows, head_rows):
+        i = lax.broadcasted_iota(jnp.int32, (n, n), 0)
+        j = lax.broadcasted_iota(jnp.int32, (n, n), 1)
+        in_token = i % token_rows
+        block = in_token // head_rows
+        source = block * part + (i // token_rows) * head_rows + in_token % head_rows
+        return jnp.where(j == source, 1.0, 0.0).astype(bf16)
+
+    def rows(at):
+        return jnp.concatenate([home[k, at:at + part, :] for k in range(4)], axis=0)
+
+    by_group = order(4 * G, G)
+    token = lax.broadcasted_iota(jnp.int32, (n, 128), 0) // (4 * G)
+    live = length[0]
+    for b in range(R // part):
+        x = sort_rows(by_group, rows(b * part))
+        alive = token + b * (n // (4 * G)) < live
+        o[b * n:(b + 1) * n, :] = jnp.where(alive, x, jnp.zeros_like(x))
+        dq[b * n:(b + 1) * n, :] = sort_rows(by_group, rows(R + b * part))
+    by_one = order(4, 1)
+    for b in range(T // part):
+        dk[b * n:(b + 1) * n, :] = sort_rows(by_one, rows(2 * R + b * part))
+        dv[b * n:(b + 1) * n, :] = sort_rows(by_one, rows(2 * R + T + b * part))
+
+
+def unpack_prompt(place, b0, b1, b2, b3, k_out, v_out):
     n = k_out.shape[0]
-    order = sorting(n, 4, 1)
-    for j, ref in enumerate((k_out, v_out)):
-        ref[...] = unsort_rows(order, jnp.concatenate([x[h, j] for h in range(4)], axis=0))
+    i = lax.broadcasted_iota(jnp.int32, (n, n), 0)
+    j = lax.broadcasted_iota(jnp.int32, (n, n), 1)
+    source = ((place[0] + 4 - i % 4) % 4) * (n // 4) + i // 4
+    order = jnp.where(j == source, 1.0, 0.0).astype(bf16)
+    for which, ref in enumerate((k_out, v_out)):
+        x = jnp.concatenate([x[which] for x in (b0, b1, b2, b3)], axis=0)
+        ref[...] = sort_rows(order, x)
 
 
 def spans(total, size):
@@ -396,29 +430,31 @@
     for x in parts:
         total = total + x.astype(f32)
     total = total.astype(bf16)
-    total = lax.dynamic_slice_in_dim(jnp.concatenate([total, total]), (4 - my_y) % 4, 4, 0)
     total, home = lax.optimization_barrier((total, home))
-    total = swap_y(total)
+    blocks = [total[0]] + [over_y(total[m], m) for m in (1, 2, 3)]
+    blocks[1], home = lax.optimization_barrier((blocks[1], home))
 
     grad_k, grad_v = small_call(
         unpack_prompt,
         "unpack_prompt",
         (jax.ShapeDtypeStruct((spots * KH, D), bf16),) * 2,
-        [VMEM_REF],
-        total,
-    )
-
-    def by_token(x, n):
-        x = x.reshape(KH, T, n, D)
-        return jnp.transpose(x, (1, 0, 2, 3)).reshape(1, T, KH * n, D)
-
-    attended = by_token(home[:, 0:R], G)
-    attended = jnp.where(live, attended, jnp.zeros((), bf16))
+        [pl.BlockSpec(memory_space=pltpu.SMEM)] + [VMEM_REF] * 4,
+        my_y.astype(jnp.int32)[None], *blocks,
+    )
+
+    attended, grad_query, grad_rk, grad_rv = small_call(
+        functools.partial(unpack_rows, T=T, G=G),
+        "unpack_rows",
+        (jax.ShapeDtypeStruct((T * H, D), bf16),) * 2
+        + (jax.ShapeDtypeStruct((T * KH, D), bf16),) * 2,
+        [pl.BlockSpec(memory_space=pltpu.SMEM), VMEM_REF],
+        lengths, home,
+    )
     return (
-        attended,
-        by_token(home[:, R:2 * R], G),
-        by_token(home[:, 2 * R:2 * R + T], 1),
-        by_token(home[:, 2 * R + T:2 * R + 2 * T], 1),
+        attended.reshape(1, T, H, D),
+        grad_query.reshape(1, T, H, D),
+        grad_rk.reshape(1, T, KH, D),
+        grad_rv.reshape(1, T, KH, D),
         grad_k.reshape(spots, KH, D),
         grad_v.reshape(spots, KH, D),
     )

time: 85 us -> 84.7 us (level)
  local copies, waits for them, and re-layouts: 4.48 us -> 1.73 us
  waiting for transfers between devices: 14.7 us -> 17.3 us
  other arithmetic: 3.45 us -> 1.74 us
  Pallas kernels: 18.3 us -> 20 us
    ppermute x3 -> x6, waiting for transfers between devices: 1.72 us -> 5.37 us  [over_y(): return lax.ppermute(x, 'y', [(i, (i + k) % 4) for i in range(4)])]
    all_to_all x3 -> x2, starting transfers between devices: 10.4 us -> 7.09 us  [swap_y(): return lax.all_to_all(x, 'y', 0, 0, tiled=True)]
    ppermute x3 -> x6, starting transfers between devices: 5.46 us -> 8.78 us  [over_y(): return lax.ppermute(x, 'y', [(i, (i + k) % 4) for i in range(4)])]
    pallas_call x1 -> x2, Pallas kernels: 0.92 us -> 2.63 us  [small_call(): pl.pallas_call(body, out_shape=out_shape, in_specs=in_specs, compiler_par...]
    unnamed x18 -> x16, local copies, waits for them, and re-layouts: 1.57 us -> 0.06 us
    transpose x2 -> x0, local copies, waits for them, and re-layouts: 1.16 us -> none  [by_token(): return jnp.transpose(x, (1, 0, 2, 3)).reshape(1, T, KH * n, D)]
    all_to_all x3 -> x2, waiting for transfers between devices: 4.43 us -> 3.39 us  [swap_y(): return lax.all_to_all(x, 'y', 0, 0, tiled=True)]
    select_n x1 -> x0, other arithmetic: 1 us -> none  [on_device(): attended = jnp.where(live, attended, jnp.zeros((), bf16))]
  transfers between devices with their start and end apart: 19 -> 21, of which waited for: 10 -> 11; matrix products, arithmetic and copies ran while one was open for 8% -> 2% of each run, Pallas kernels for 14% -> 16%
where the time goes in v10:
time: 84.7 us; the launch traced here: 84.5 us
  starting transfers between devices  42 us (50%)
  Pallas kernels  20 us (24%)
  waiting for transfers between devices  17.3 us (20%)
  other arithmetic  1.74 us (2%)
  local copies, waits for them, and re-layouts  1.73 us (2%)
  between operations  1.66 us (2%)
    ppermute x13, starting transfers between devices, over_z(): return lax.ppermute(x, 'z', [(i, (i + k) % 8) for i in range(8)])  26.2 us
    pallas_call x3, Pallas kernels, call(): pl.pallas_call(body, out_shape=out_shape, scratch_shapes=scratch, compile...  17.3 us
    ppermute x6, starting transfers between devices, over_y(): return lax.ppermute(x, 'y', [(i, (i + k) % 4) for i in range(4)])  8.78 us
    ppermute x13, waiting for transfers between devices, over_z(): return lax.ppermute(x, 'z', [(i, (i + k) % 8) for i in range(8)])  8.56 us
    all_to_all x2, starting transfers between devices, swap_y(): return lax.all_to_all(x, 'y', 0, 0, tiled=True)  7.09 us
    ppermute x6, waiting for transfers between devices, over_y(): return lax.ppermute(x, 'y', [(i, (i + k) % 4) for i in range(4)])  5.37 us
    all_to_all x2, waiting for transfers between devices, swap_y(): return lax.all_to_all(x, 'y', 0, 0, tiled=True)  3.39 us
    pallas_call x2, Pallas kernels, small_call(): pl.pallas_call(body, out_shape=out_shape, in_specs=in_specs, compiler_par...  2.63 us
  transfers between devices with their start and end apart: 21, of which 11 were waited for; matrix products, arithmetic and copies ran while one was open for 2% of the time, Pallas kernels for 16%

profile of v10, /device:TPU:4, one launch (start us, length us, event | category | flops | bytes accessed | tf_op | source)
XLA Modules:
  0.0 84.5 jit_solution(4911469571499929231)
XLA Ops:
  0.7 1.4 %constant_dynamic-slice_fusion.6 = (bf16[64,1,128]{2,1,0:T(2,128)(2,1)S(1)}, bf16[64,1,128]{2,1,0:T(2,128)(2,1)S(1)}, bf16[64,1,128]{2,1,0:T(2,128)(2,1)S(1)}, b...) fusion(bf16[64,4,128]{2,1,0:T(4,128)(2,1)} %param.11, ...), kind=kLoop, calls=%fused_computation.34 | loop fusion | bytes 262160 | tf_op jit(solution)/shard_map/jit(dynamic_index_in_dim)/dynamic_slice | solution.py:313
  2.2 3.3 %collective-permute-start.1 = (bf16[2,64,128]{2,1,0:T(8,128)(2,1)S(1)}, bf16[2,64,128]{2,1,0:T(8,128)(2,1)S(1)}, u32[]{:S(2)}, u32[]{:S(2)}) collective-permute-start(bf16[2,64,128]{2,1,0:T(8,128)(2,1)S(1)} %pad_maximum_fusion.5), channel_id=1, source_target_pairs={{0,2},{1,3},{2,0},{3,1},{4,6},{5,7},{6,4},{7,5},{8,10},{9,11},{10,... | collective-permute-start | bytes 98312 | tf_op jit(solution)/shard_map/ppermute | solution.py:308
  5.5 1.1 %collective-permute-start = (bf16[2,64,128]{2,1,0:T(8,128)(2,1)S(1)}, bf16[2,64,128]{2,1,0:T(8,128)(2,1)S(1)}, u32[]{:S(2)}, u32[]{:S(2)}) collective-permute-start(bf16[2,64,128]{2,1,0:T(8,128)(2,1)S(1)} %pad_maximum_fusion.4), channel_id=1, source_target_pairs={{0,3},{1,0},{2,1},{3,2},{4,7},{5,4},{6,5},{7,6},{8,11},{9,8},{10,9... | collective-permute-start | bytes 98312 | tf_op jit(solution)/shard_map/ppermute | solution.py:308
  6.7 1.0 %collective-permute-start.2 = (bf16[2,64,128]{2,1,0:T(8,128)(2,1)S(1)}, bf16[2,64,128]{2,1,0:T(8,128)(2,1)S(1)}, u32[]{:S(2)}, u32[]{:S(2)}) collective-permute-start(bf16[2,64,128]{2,1,0:T(8,128)(2,1)S(1)} %pad_maximum_fusion.6), channel_id=1, source_target_pairs={{0,1},{1,2},{2,3},{3,0},{4,5},{5,6},{6,7},{7,4},{8,9},{9,10},{10,1... | collective-permute-start | bytes 98312 | tf_op jit(solution)/shard_map/ppermute | solution.py:308
  8.4 0.2 copy.25
  8.7 0.3 copy_select_fusion
  9.0 1.2 %pad_maximum_fusion = bf16[4,1280,128]{2,1,0:T(8,128)(2,1)} fusion(bf16[4,128,128]{2,1,0:T(8,128)(2,1)S(1)} %get-tuple-element.90, bf16[4,128,128]{2,1,0:T(8,128)(2,1)S(1)} %get-tuple-element.91, bf16[4,512,128]{2,1,0:T(8,128)(2,1)S(1)} %bitcast.67, bf16[4,512,128]{2,1,0:T(8,128)(2,1)S(1)} %bitcast.66), kind=kLoop, calls=%fused_computation | loop fusion | flops 5242880 | bytes 2621440 | tf_op jit(solution)/shard_map/concatenate | solution.py:325
  10.1 0.0 collective-permute-done.1
  10.2 0.0 collective-permute-done
  10.2 1.7 %collective-permute-done.2 = bf16[2,64,128]{2,1,0:T(8,128)(2,1)S(1)} collective-permute-done((bf16[2,64,128]{2,1,0:T(8,128)(2,1)S(1)}, bf16[2,64,128]{2,1,0:T(8,128)(2,1)S(1)}, u32[]{:S(2)}, u32[]{:S(2)}) %collective-permute-start.2) | collective-permute-done | bytes 32800 | tf_op jit(solution)/shard_map/ppermute | solution.py:308
  11.9 3.6 %all-to-all-start = ((bf16[4,1280,128]{2,1,0:T(8,128)(2,1)}), bf16[4,1280,128]{2,1,0:T(8,128)(2,1)S(1)}, u32[]{:S(2)}, u32[]{:S(2)}) async-start(bf16[4,1280,128]{2,1,0:T(8,128)(2,1)} %pad_maximum_fusion), calls=%async_computation | async-start | bytes 2621440 | tf_op jit(solution)/shard_map/all_to_all | solution.py:303
  15.5 3.3 %collective-permute-start.5 = (bf16[4,2,64,128]{3,2,1,0:T(8,128)(2,1)S(1)}, bf16[4,2,64,128]{3,2,1,0:T(8,128)(2,1)S(1)}, u32[]{:S(2)}, u32[]{:S(2)}) collective-permute-start(bf16[4,2,64,128]{3,2,1,0:T(8,128)(2,1)S(1)} %pad_maximum_fusion.1.kv0), channel_id=1, source_target_pairs={{0,8},{4,12},{8,16},{12,20},{16,24},{20,28},{24,0},{28,4},{1,9},{5... | collective-permute-start | bytes 393224 | tf_op jit(solution)/shard_map/ppermute | solution.py:300
  18.8 3.1 %collective-permute-start.6 = (bf16[4,2,64,128]{3,2,1,0:T(8,128)(2,1)S(1)}, bf16[4,2,64,128]{3,2,1,0:T(8,128)(2,1)S(1)}, u32[]{:S(2)}, u32[]{:S(2)}) collective-permute-start(bf16[4,2,64,128]{3,2,1,0:T(8,128)(2,1)S(1)} %pad_maximum_fusion.1.kv0), channel_id=1, source_target_pairs={{0,24},{4,28},{8,0},{12,4},{16,8},{20,12},{24,16},{28,20},{1,25},{... | collective-permute-start | bytes 393224 | tf_op jit(solution)/shard_map/ppermute | solution.py:300
  21.9 2.4 %collective-permute-start.4 = (bf16[4,2,64,128]{3,2,1,0:T(8,128)(2,1)S(1)}, bf16[4,2,64,128]{3,2,1,0:T(8,128)(2,1)S(1)}, u32[]{:S(2)}, u32[]{:S(2)}) collective-permute-start(bf16[4,2,64,128]{3,2,1,0:T(8,128)(2,1)S(1)} %pad_maximum_fusion.1.kv0), channel_id=1, source_target_pairs={{0,28},{4,0},{8,4},{12,8},{16,12},{20,16},{24,20},{28,24},{1,29},{... | collective-permute-start | bytes 393224 | tf_op jit(solution)/shard_map/ppermute | solution.py:300
  24.3 0.0 collective-permute-start.3
  24.3 2.2 %collective-permute-done.5.kv3 = bf16[4,2,64,128]{3,2,1,0:T(8,128)(2,1)S(1)} collective-permute-done((bf16[4,2,64,128]{3,2,1,0:T(8,128)(2,1)S(1)}, bf16[4,2,64,128]{3,2,1,0:T(8,128)(2,1)S(1)}, u32[]{:S(2)}, u32[]{:S(2)}) %collective-permute-start.5) | collective-permute-done | bytes 131104 | tf_op jit(solution)/shard_map/ppermute | solution.py:300
  26.5 2.4 %collective-permute-start.9 = (bf16[4,2,64,128]{3,2,1,0:T(8,128)(2,1)S(1)}, bf16[4,2,64,128]{3,2,1,0:T(8,128)(2,1)S(1)}, u32[]{:S(2)}, u32[]{:S(2)}) collective-permute-start(bf16[4,2,64,128]{3,2,1,0:T(8,128)(2,1)S(1)} %collective-permute-done.5.kv3), channel_id=1, source_target_pairs={{0,8},{4,12},{8,16},{12,20},{16,24},{20,28},{24,0},{28,4},{1,9},{5... | collective-permute-start | bytes 393224 | tf_op jit(solution)/shard_map/ppermute | solution.py:300
  28.9 0.0 collective-permute-start.7
  28.9 0.2 collective-permute-done.6.kv4
  29.1 3.1 %collective-permute-start.8 = (bf16[4,2,64,128]{3,2,1,0:T(8,128)(2,1)S(1)}, bf16[4,2,64,128]{3,2,1,0:T(8,128)(2,1)S(1)}, u32[]{:S(2)}, u32[]{:S(2)}) collective-permute-start(bf16[4,2,64,128]{3,2,1,0:T(8,128)(2,1)S(1)} %collective-permute-done.6.kv4), channel_id=1, source_target_pairs={{0,28},{4,0},{8,4},{12,8},{16,12},{20,16},{24,20},{28,24},{1,29},{... | collective-permute-start | bytes 393224 | tf_op jit(solution)/shard_map/ppermute | solution.py:300
  32.2 0.0 collective-permute-done.4.kv2
  32.2 0.7 collective-permute-done.3.kv1
  32.8 0.0 all-to-all-done.pack
  32.8 4.7 %near_forward.1 = (bf16[1408,2048]{1,0:T(8,128)(2,1)S(1)}, f32[144,2048]{1,0:T(8,128)S(1)}, f32[8,2048]{1,0:T(8,128)S(1)}) custom-call(bf16[4,1280,128]{2,1,0:T(8,128)(2,1)S(1)} %all-to-all-done.pack, bf16[4,2,64,128]{3,2,1,0:T(8,128)(2,1)S(1)} %pad_maximum_fusion.1.kv0, bf16[4,2,64,128]{3,2,1,0:T(8,128)(2,1)S(1)} %collective-permute-done.3.kv1, ...), custom_call_target="tpu_custom_call" | custom-call | flops 1476395008 | bytes 4194304 | tf_op jit(solution)/shard_map/near_forward/pallas_call | solution.py:281
  37.6 0.0 collective-permute-done.8.kv1
  37.6 0.0 collective-permute-done.9.kv2
  37.6 0.4 collective-permute-done.7.kv0
  38.0 5.6 %far_both.1 = (bf16[4,512,128]{2,1,0:T(8,128)(2,1)S(1)}, f32[8,2048]{1,0:T(8,128)S(1)}, bf16[2048,128]{1,0:T(8,128)(2,1)S(1)}, bf16[2048,128]{1,0:T(8,128)(2,1)S...) custom-call(bf16[4,1280,128]{2,1,0:T(8,128)(2,1)S(1)} %all-to-all-done.pack, ...), custom_call_target="tpu_custom_call" | custom-call | flops 2415919104 | bytes 4194304 | tf_op jit(solution)/shard_map/far_both/pallas_call | solution.py:281
  43.6 5.1 %collective-permute-start.10 = (bf16[6,2,64,128]{3,2,1,0:T(8,128)(2,1)S(1)}, bf16[6,2,64,128]{3,2,1,0:T(8,128)(2,1)S(1)}, u32[]{:S(2)}, u32[]{:S(2)}) collective-permute-start(bf16[6,2,64,128]{3,2,1,0:T(8,128)(2,1)S(1)} %get-tuple-element.51), channel_id=1, source_target_pairs={{0,24},{4,28},{8,0},{12,4},{16,8},{20,12},{24,16},{28,20},{1,25},{... | collective-permute-start | bytes 589832 | tf_op jit(solution)/shard_map/ppermute | solution.py:300
  48.7 0.0 collective-permute-start.11
  48.7 7.0 %near_backward.1 = (bf16[4,1280,128]{2,1,0:T(8,128)(2,1)}, bf16[4,2,64,128]{3,2,1,0:T(8,128)(2,1)S(1)}, bf16[4,2,64,128]{3,2,1,0:T(8,128)(2,1)S(1)}, bf16[4,2,64...) custom-call(bf16[4,1280,128]{2,1,0:T(8,128)(2,1)S(1)} %all-to-all-done.pack, ...), custom_call_target="tpu_custom_call" | custom-call | flops 2952790016 | bytes 4194304 | tf_op jit(solution)/shard_map/near_backward/pallas_call | solution.py:281
  55.7 3.5 %all-to-all-start.1 = ((bf16[4,1280,128]{2,1,0:T(8,128)(2,1)}), bf16[4,1280,128]{2,1,0:T(8,128)(2,1)S(1)}, u32[]{:S(2)}, u32[]{:S(2)}) async-start(bf16[4,1280,128]{2,1,0:T(8,128)(2,1)} %get-tuple-element.63), calls=%async_computation.1 | async-start | bytes 2621440 | tf_op jit(solution)/shard_map/all_to_all | solution.py:303
  59.2 0.0 collective-permute-done.10
  59.4 2.5 %collective-permute-start.13 = (bf16[4,2,64,128]{3,2,1,0:T(8,128)(2,1)S(1)}, bf16[4,2,64,128]{3,2,1,0:T(8,128)(2,1)S(1)}, u32[]{:S(2)}, u32[]{:S(2)}) collective-permute-start(bf16[4,2,64,128]{3,2,1,0:T(8,128)(2,1)S(1)} %pad_maximum_fusion.3), channel_id=1, source_target_pairs={{0,8},{4,12},{8,16},{12,20},{16,24},{20,28},{24,0},{28,4},{1,9},{5... | collective-permute-start | bytes 393224 | tf_op jit(solution)/shard_map/ppermute | solution.py:300
  61.8 0.6 collective-permute-start.15
  62.6 2.3 %collective-permute-start.12 = (bf16[4,2,64,128]{3,2,1,0:T(8,128)(2,1)S(1)}, bf16[4,2,64,128]{3,2,1,0:T(8,128)(2,1)S(1)}, u32[]{:S(2)}, u32[]{:S(2)}) collective-permute-start(bf16[4,2,64,128]{3,2,1,0:T(8,128)(2,1)S(1)} %pad_maximum_fusion.2), channel_id=1, source_target_pairs={{0,24},{4,28},{8,0},{12,4},{16,8},{20,12},{24,16},{28,20},{1,25},{... | collective-permute-start | bytes 393224 | tf_op jit(solution)/shard_map/ppermute | solution.py:300
  64.9 1.4 %collective-permute-start.14 = (bf16[4,2,64,128]{3,2,1,0:T(8,128)(2,1)S(1)}, bf16[4,2,64,128]{3,2,1,0:T(8,128)(2,1)S(1)}, u32[]{:S(2)}, u32[]{:S(2)}) collective-permute-start(bf16[4,2,64,128]{3,2,1,0:T(8,128)(2,1)S(1)} %add_convert_fusion.2), channel_id=1, source_target_pairs={{0,28},{4,0},{8,4},{12,8},{16,12},{20,16},{24,20},{28,24},{1,29},{... | collective-permute-start | bytes 393224 | tf_op jit(solution)/shard_map/ppermute | solution.py:300
  66.2 0.6 collective-permute-done.13
  66.8 2.2 %collective-permute-done.15 = bf16[4,2,64,128]{3,2,1,0:T(8,128)(2,1)S(1)} collective-permute-done((bf16[4,2,64,128]{3,2,1,0:T(8,128)(2,1)S(1)}, bf16[4,2,64,128]{3,2,1,0:T(8,128)(2,1)S(1)}, u32[]{:S(2)}, u32[]{:S(2)}) %collective-permute-start.15) | collective-permute-done | bytes 131104 | tf_op jit(solution)/shard_map/ppermute | solution.py:300
  69.1 2.3 %collective-permute-done.14 = bf16[4,2,64,128]{3,2,1,0:T(8,128)(2,1)S(1)} collective-permute-done((bf16[4,2,64,128]{3,2,1,0:T(8,128)(2,1)S(1)}, bf16[4,2,64,128]{3,2,1,0:T(8,128)(2,1)S(1)}, u32[]{:S(2)}, u32[]{:S(2)}) %collective-permute-start.14) | collective-permute-done | bytes 131104 | tf_op jit(solution)/shard_map/ppermute | solution.py:300
  71.4 0.1 add_convert_fusion
  71.5 3.4 %all-to-all-done.1.home = bf16[4,1280,128]{2,1,0:T(8,128)(2,1)S(1)} async-done(((bf16[4,1280,128]{2,1,0:T(8,128)(2,1)}), bf16[4,1280,128]{2,1,0:T(8,128)(2,1)S(1)}, u32[]{:S(2)}, u32[]{:S(2)}) %all-to-all-start.1) | async-done | bytes 1310752 | tf_op jit(solution)/shard_map/all_to_all | solution.py:303
  74.9 0.3 collective-permute-start.16
  75.2 3.0 %collective-permute-start.18 = (bf16[2,64,128]{2,1,0:T(8,128)(2,1)S(1)}, bf16[2,64,128]{2,1,0:T(8,128)(2,1)S(1)}, u32[]{:S(2)}, u32[]{:S(2)}) collective-permute-start(bf16[2,64,128]{2,1,0:T(8,128)(2,1)S(1)} %get-tuple-element.74), channel_id=1, source_target_pairs={{0,3},{1,0},{2,1},{3,2},{4,7},{5,4},{6,5},{7,6},{8,11},{9,8},{10,9... | collective-permute-start | bytes 98312 | tf_op jit(solution)/shard_map/ppermute | solution.py:308
  78.2 1.9 %collective-permute-done.16.b1 = bf16[2,64,128]{2,1,0:T(8,128)(2,1)S(1)} collective-permute-done((bf16[2,64,128]{2,1,0:T(8,128)(2,1)S(1)}, bf16[2,64,128]{2,1,0:T(8,128)(2,1)S(1)}, u32[]{:S(2)}, u32[]{:S(2)}) %collective-permute-start.16) | collective-permute-done | bytes 32800 | tf_op jit(solution)/shard_map/ppermute | solution.py:308
  80.1 1.8 %unpack_rows.1 = (bf16[2048,128]{1,0:T(8,128)(2,1)}, bf16[2048,128]{1,0:T(8,128)(2,1)}, bf16[512,128]{1,0:T(8,128)(2,1)}, bf16[512,128]{1,0:T(8,128)(2,1)}) custom-call(s32[1]{0:T(128)} %copy.56.length, bf16[4,1280,128]{2,1,0:T(8,128)(2,1)S(1)} %all-to-all-done.1.home), custom_call_target="tpu_custom_call" | custom-call | tf_op jit(solution)/shard_map/unpack_rows/pallas_call | solution.py:271
  81.8 1.8 %collective-permute-done.17.b2 = bf16[2,64,128]{2,1,0:T(8,128)(2,1)S(1)} collective-permute-done((bf16[2,64,128]{2,1,0:T(8,128)(2,1)S(1)}, bf16[2,64,128]{2,1,0:T(8,128)(2,1)S(1)}, u32[]{:S(2)}, u32[]{:S(2)}) %collective-permute-start.17) | collective-permute-done | bytes 32800 | tf_op jit(solution)/shard_map/ppermute | solution.py:308
  83.6 0.9 %unpack_prompt.1 = (bf16[256,128]{1,0:T(8,128)(2,1)}, bf16[256,128]{1,0:T(8,128)(2,1)}) custom-call(s32[1]{0:T(128)} %bitcast.30.place, bf16[2,64,128]{2,1,0:T(8,128)(2,1)S(1)} %get-tuple-element.76.b0, bf16[2,64,128]{2,1,0:T(8,128)(2,1)S(1)} %collective-permute-done.16.b1, bf16[2,64,128]{2,1,0:T(8,128)(2,1)S(1)} %collective-permute-done.17.b2, ...), custom_call_target="tpu_custom_call" | custom-call | tf_op jit(solution)/shard_map/unpack_prompt/pallas_call | solution.py:271
  (36 shorter events, 0.3 us)
Async XLA Ops:
  0.6 7.8 %copy-start = (bf16[1,128,16,128]{3,2,1,0:T(8,128)(2,1)S(1)}, bf16[1,128,16,128]{3,2,1,0:T(8,128)(2,1)}, u32[]{:S(2)}) copy-start(bf16[1,128,16,128]{3,2,1,0:T(8,128)(2,1)} %param.7) | copy-start | bytes 1572868
  0.6 8.0 %copy-start.2 = (bf16[1,128,4,128]{3,2,1,0:T(4,128)(2,1)S(1)}, bf16[1,128,4,128]{3,2,1,0:T(4,128)(2,1)}, u32[]{:S(2)}) copy-start(bf16[1,128,4,128]{3,2,1,0:T(4,128)(2,1)} %param.9) | copy-start | bytes 393220
  0.7 8.0 %copy-start.3 = (bf16[1,128,4,128]{3,2,1,0:T(4,128)(2,1)S(1)}, bf16[1,128,4,128]{3,2,1,0:T(4,128)(2,1)}, u32[]{:S(2)}) copy-start(bf16[1,128,4,128]{3,2,1,0:T(4,128)(2,1)} %param.8) | copy-start | bytes 393220
  0.7 8.0 %copy-start.1 = (bf16[1,128,16,128]{3,2,1,0:T(8,128)(2,1)S(1)}, bf16[1,128,16,128]{3,2,1,0:T(8,128)(2,1)}, u32[]{:S(2)}) copy-start(bf16[1,128,16,128]{3,2,1,0:T(8,128)(2,1)} %param.13) | copy-start | bytes 1572868
  2.2 7.9 %collective-permute-start.1 = (bf16[2,64,128]{2,1,0:T(8,128)(2,1)S(1)}, bf16[2,64,128]{2,1,0:T(8,128)(2,1)S(1)}, u32[]{:S(2)}, u32[]{:S(2)}) collective-permute-start(bf16[2,64,128]{2,1,0:T(8,128)(2,1)S(1)} %pad_maximum_fusion.5), channel_id=1, source_target_pairs={{0,2},{1,3},{2,0},{3,1},{4,6},{5,7},{6,4},{7,5},{8,10},{9,11},{10,... | collective-permute-start | bytes 98312 | tf_op jit(solution)/shard_map/ppermute | solution.py:308
  5.5 4.6 %collective-permute-start = (bf16[2,64,128]{2,1,0:T(8,128)(2,1)S(1)}, bf16[2,64,128]{2,1,0:T(8,128)(2,1)S(1)}, u32[]{:S(2)}, u32[]{:S(2)}) collective-permute-start(bf16[2,64,128]{2,1,0:T(8,128)(2,1)S(1)} %pad_maximum_fusion.4), channel_id=1, source_target_pairs={{0,3},{1,0},{2,1},{3,2},{4,7},{5,4},{6,5},{7,6},{8,11},{9,8},{10,9... | collective-permute-start | bytes 98312 | tf_op jit(solution)/shard_map/ppermute | solution.py:308
  6.7 5.2 %collective-permute-start.2 = (bf16[2,64,128]{2,1,0:T(8,128)(2,1)S(1)}, bf16[2,64,128]{2,1,0:T(8,128)(2,1)S(1)}, u32[]{:S(2)}, u32[]{:S(2)}) collective-permute-start(bf16[2,64,128]{2,1,0:T(8,128)(2,1)S(1)} %pad_maximum_fusion.6), channel_id=1, source_target_pairs={{0,1},{1,2},{2,3},{3,0},{4,5},{5,6},{6,7},{7,4},{8,9},{9,10},{10,1... | collective-permute-start | bytes 98312 | tf_op jit(solution)/shard_map/ppermute | solution.py:308
  11.9 20.9 %all-to-all-start = ((bf16[4,1280,128]{2,1,0:T(8,128)(2,1)}), bf16[4,1280,128]{2,1,0:T(8,128)(2,1)S(1)}, u32[]{:S(2)}, u32[]{:S(2)}) async-start(bf16[4,1280,128]{2,1,0:T(8,128)(2,1)} %pad_maximum_fusion), calls=%async_computation | async-start | bytes 2621440 | tf_op jit(solution)/shard_map/all_to_all | solution.py:303
  15.5 11.0 %collective-permute-start.5 = (bf16[4,2,64,128]{3,2,1,0:T(8,128)(2,1)S(1)}, bf16[4,2,64,128]{3,2,1,0:T(8,128)(2,1)S(1)}, u32[]{:S(2)}, u32[]{:S(2)}) collective-permute-start(bf16[4,2,64,128]{3,2,1,0:T(8,128)(2,1)S(1)} %pad_maximum_fusion.1.kv0), channel_id=1, source_target_pairs={{0,8},{4,12},{8,16},{12,20},{16,24},{20,28},{24,0},{28,4},{1,9},{5... | collective-permute-start | bytes 393224 | tf_op jit(solution)/shard_map/ppermute | solution.py:300
  18.8 10.3 %collective-permute-start.6 = (bf16[4,2,64,128]{3,2,1,0:T(8,128)(2,1)S(1)}, bf16[4,2,64,128]{3,2,1,0:T(8,128)(2,1)S(1)}, u32[]{:S(2)}, u32[]{:S(2)}) collective-permute-start(bf16[4,2,64,128]{3,2,1,0:T(8,128)(2,1)S(1)} %pad_maximum_fusion.1.kv0), channel_id=1, source_target_pairs={{0,24},{4,28},{8,0},{12,4},{16,8},{20,12},{24,16},{28,20},{1,25},{... | collective-permute-start | bytes 393224 | tf_op jit(solution)/shard_map/ppermute | solution.py:300
  21.9 10.2 %collective-permute-start.4 = (bf16[4,2,64,128]{3,2,1,0:T(8,128)(2,1)S(1)}, bf16[4,2,64,128]{3,2,1,0:T(8,128)(2,1)S(1)}, u32[]{:S(2)}, u32[]{:S(2)}) collective-permute-start(bf16[4,2,64,128]{3,2,1,0:T(8,128)(2,1)S(1)} %pad_maximum_fusion.1.kv0), channel_id=1, source_target_pairs={{0,28},{4,0},{8,4},{12,8},{16,12},{20,16},{24,20},{28,24},{1,29},{... | collective-permute-start | bytes 393224 | tf_op jit(solution)/shard_map/ppermute | solution.py:300
  24.3 8.5 %collective-permute-start.3 = (bf16[4,2,64,128]{3,2,1,0:T(8,128)(2,1)S(1)}, bf16[4,2,64,128]{3,2,1,0:T(8,128)(2,1)S(1)}, u32[]{:S(2)}, u32[]{:S(2)}) collective-permute-start(bf16[4,2,64,128]{3,2,1,0:T(8,128)(2,1)S(1)} %pad_maximum_fusion.1.kv0), channel_id=1, source_target_pairs={{0,4},{4,8},{8,12},{12,16},{16,20},{20,24},{24,28},{28,0},{1,5},{5... | collective-permute-start | bytes 393224 | tf_op jit(solution)/shard_map/ppermute | solution.py:300
  26.5 11.1 %collective-permute-start.9 = (bf16[4,2,64,128]{3,2,1,0:T(8,128)(2,1)S(1)}, bf16[4,2,64,128]{3,2,1,0:T(8,128)(2,1)S(1)}, u32[]{:S(2)}, u32[]{:S(2)}) collective-permute-start(bf16[4,2,64,128]{3,2,1,0:T(8,128)(2,1)S(1)} %collective-permute-done.5.kv3), channel_id=1, source_target_pairs={{0,8},{4,12},{8,16},{12,20},{16,24},{20,28},{24,0},{28,4},{1,9},{5... | collective-permute-start | bytes 393224 | tf_op jit(solution)/shard_map/ppermute | solution.py:300
  28.9 9.1 %collective-permute-start.7 = (bf16[4,2,64,128]{3,2,1,0:T(8,128)(2,1)S(1)}, bf16[4,2,64,128]{3,2,1,0:T(8,128)(2,1)S(1)}, u32[]{:S(2)}, u32[]{:S(2)}) collective-permute-start(bf16[4,2,64,128]{3,2,1,0:T(8,128)(2,1)S(1)} %collective-permute-done.5.kv3), channel_id=1, source_target_pairs={{0,4},{4,8},{8,12},{12,16},{16,20},{20,24},{24,28},{28,0},{1,5},{5... | collective-permute-start | bytes 393224 | tf_op jit(solution)/shard_map/ppermute | solution.py:300
  29.1 8.5 %collective-permute-start.8 = (bf16[4,2,64,128]{3,2,1,0:T(8,128)(2,1)S(1)}, bf16[4,2,64,128]{3,2,1,0:T(8,128)(2,1)S(1)}, u32[]{:S(2)}, u32[]{:S(2)}) collective-permute-start(bf16[4,2,64,128]{3,2,1,0:T(8,128)(2,1)S(1)} %collective-permute-done.6.kv4), channel_id=1, source_target_pairs={{0,28},{4,0},{8,4},{12,8},{16,12},{20,16},{24,20},{28,24},{1,29},{... | collective-permute-start | bytes 393224 | tf_op jit(solution)/shard_map/ppermute | solution.py:300
  43.6 15.6 %collective-permute-start.10 = (bf16[6,2,64,128]{3,2,1,0:T(8,128)(2,1)S(1)}, bf16[6,2,64,128]{3,2,1,0:T(8,128)(2,1)S(1)}, u32[]{:S(2)}, u32[]{:S(2)}) collective-permute-start(bf16[6,2,64,128]{3,2,1,0:T(8,128)(2,1)S(1)} %get-tuple-element.51), channel_id=1, source_target_pairs={{0,24},{4,28},{8,0},{12,4},{16,8},{20,12},{24,16},{28,20},{1,25},{... | collective-permute-start | bytes 589832 | tf_op jit(solution)/shard_map/ppermute | solution.py:300
  48.7 10.5 %collective-permute-start.11 = (bf16[6,2,64,128]{3,2,1,0:T(8,128)(2,1)S(1)}, bf16[6,2,64,128]{3,2,1,0:T(8,128)(2,1)S(1)}, u32[]{:S(2)}, u32[]{:S(2)}) collective-permute-start(bf16[6,2,64,128]{3,2,1,0:T(8,128)(2,1)S(1)} %get-tuple-element.52), channel_id=1, source_target_pairs={{0,8},{4,12},{8,16},{12,20},{16,24},{20,28},{24,0},{28,4},{1,9},{5... | collective-permute-start | bytes 589832 | tf_op jit(solution)/shard_map/ppermute | solution.py:300
  55.7 19.2 %all-to-all-start.1 = ((bf16[4,1280,128]{2,1,0:T(8,128)(2,1)}), bf16[4,1280,128]{2,1,0:T(8,128)(2,1)S(1)}, u32[]{:S(2)}, u32[]{:S(2)}) async-start(bf16[4,1280,128]{2,1,0:T(8,128)(2,1)} %get-tuple-element.63), calls=%async_computation.1 | async-start | bytes 2621440 | tf_op jit(solution)/shard_map/all_to_all | solution.py:303
  59.4 7.5 %collective-permute-start.13 = (bf16[4,2,64,128]{3,2,1,0:T(8,128)(2,1)S(1)}, bf16[4,2,64,128]{3,2,1,0:T(8,128)(2,1)S(1)}, u32[]{:S(2)}, u32[]{:S(2)}) collective-permute-start(bf16[4,2,64,128]{3,2,1,0:T(8,128)(2,1)S(1)} %pad_maximum_fusion.3), channel_id=1, source_target_pairs={{0,8},{4,12},{8,16},{12,20},{16,24},{20,28},{24,0},{28,4},{1,9},{5... | collective-permute-start | bytes 393224 | tf_op jit(solution)/shard_map/ppermute | solution.py:300
  61.8 7.2 %collective-permute-start.15 = (bf16[4,2,64,128]{3,2,1,0:T(8,128)(2,1)S(1)}, bf16[4,2,64,128]{3,2,1,0:T(8,128)(2,1)S(1)}, u32[]{:S(2)}, u32[]{:S(2)}) collective-permute-start(bf16[4,2,64,128]{3,2,1,0:T(8,128)(2,1)S(1)} %add_convert_fusion.1), channel_id=1, source_target_pairs={{0,4},{4,8},{8,12},{12,16},{16,20},{20,24},{24,28},{28,0},{1,5},{5... | collective-permute-start | bytes 393224 | tf_op jit(solution)/shard_map/ppermute | solution.py:300
  62.6 6.5 %collective-permute-start.12 = (bf16[4,2,64,128]{3,2,1,0:T(8,128)(2,1)S(1)}, bf16[4,2,64,128]{3,2,1,0:T(8,128)(2,1)S(1)}, u32[]{:S(2)}, u32[]{:S(2)}) collective-permute-start(bf16[4,2,64,128]{3,2,1,0:T(8,128)(2,1)S(1)} %pad_maximum_fusion.2), channel_id=1, source_target_pairs={{0,24},{4,28},{8,0},{12,4},{16,8},{20,12},{24,16},{28,20},{1,25},{... | collective-permute-start | bytes 393224 | tf_op jit(solution)/shard_map/ppermute | solution.py:300
  64.9 6.5 %collective-permute-start.14 = (bf16[4,2,64,128]{3,2,1,0:T(8,128)(2,1)S(1)}, bf16[4,2,64,128]{3,2,1,0:T(8,128)(2,1)S(1)}, u32[]{:S(2)}, u32[]{:S(2)}) collective-permute-start(bf16[4,2,64,128]{3,2,1,0:T(8,128)(2,1)S(1)} %add_convert_fusion.2), channel_id=1, source_target_pairs={{0,28},{4,0},{8,4},{12,8},{16,12},{20,16},{24,20},{28,24},{1,29},{... | collective-permute-start | bytes 393224 | tf_op jit(solution)/shard_map/ppermute | solution.py:300
  74.9 5.2 %collective-permute-start.16 = (bf16[2,64,128]{2,1,0:T(8,128)(2,1)S(1)}, bf16[2,64,128]{2,1,0:T(8,128)(2,1)S(1)}, u32[]{:S(2)}, u32[]{:S(2)}) collective-permute-start(bf16[2,64,128]{2,1,0:T(8,128)(2,1)S(1)} %get-tuple-element.77), channel_id=1, source_target_pairs={{0,1},{1,2},{2,3},{3,0},{4,5},{5,6},{6,7},{7,4},{8,9},{9,10},{10,1... | collective-permute-start | bytes 98312 | tf_op jit(solution)/shard_map/ppermute | solution.py:308
  75.2 6.6 %collective-permute-start.18 = (bf16[2,64,128]{2,1,0:T(8,128)(2,1)S(1)}, bf16[2,64,128]{2,1,0:T(8,128)(2,1)S(1)}, u32[]{:S(2)}, u32[]{:S(2)}) collective-permute-start(bf16[2,64,128]{2,1,0:T(8,128)(2,1)S(1)} %get-tuple-element.74), channel_id=1, source_target_pairs={{0,3},{1,0},{2,1},{3,2},{4,7},{5,4},{6,5},{7,6},{8,11},{9,8},{10,9... | collective-permute-start | bytes 98312 | tf_op jit(solution)/shard_map/ppermute | solution.py:308
  78.2 5.4 %collective-permute-start.17 = (bf16[2,64,128]{2,1,0:T(8,128)(2,1)S(1)}, bf16[2,64,128]{2,1,0:T(8,128)(2,1)S(1)}, u32[]{:S(2)}, u32[]{:S(2)}) collective-permute-start(bf16[2,64,128]{2,1,0:T(8,128)(2,1)S(1)} %get-tuple-element.75), channel_id=1, source_target_pairs={{0,2},{1,3},{2,0},{3,1},{4,6},{5,7},{6,4},{7,5},{8,10},{9,11},{10,... | collective-permute-start | bytes 98312 | tf_op jit(solution)/shard_map/ppermute | solution.py:308
